TPU v7x, 32 devices: a whole 2x2x4 slice. The times are simulated.
32 devices in a mesh: section: 4 (over x, core), dp: 8 (over z, y).
Axes of the slice: x: 2, y: 2, z: 4, core: 2. Of those that a mesh axis runs over, the one named last changes fastest.
Arguments:
- stash: bfloat16 [4, 1024, 2048], P('section', 'dp'), may hold values from -6 to 6
- cotangent: bfloat16 [1024, 2048], P('dp', 'section'), may hold values from -6 to 6
- gate_weight: bfloat16 [4, 2048, 512], P('section', 'dp'), may hold values from -0.125 to 0.125
- up_weight: bfloat16 [4, 2048, 512], P('section', 'dp'), may hold values from -0.125 to 0.125
- down_weight: bfloat16 [4, 512, 2048], P('section'), may hold values from -0.25 to 0.25
- shared_gate: bfloat16 [4, 2048], P('section'), may hold values from -0.125 to 0.125
Outputs:
- grad_inputs: bfloat16 [4, 1024, 2048], P('section', 'dp')
- down_grad: float32 [4, 512, 2048], P('section', 'dp')
All inputs are finite; a program needn't handle non-finite values.
Results may differ from a plain program's by a relative error of at most 0.029.
Values may be sent and summed in bfloat16 or wider, within the bound.
No kernel may reach another device: no remote copies, remote signals or barrier semaphores. Data moves between devices by JAX's collectives and lax.ppermute only.
A program may use at most 64 MiB of HBM per device.

v0:
```python
import jax
import jax.numpy as jnp
from jax import lax
from jax.sharding import PartitionSpec as P

ROWS = 64
MICRO = 2


def from_partner(x, axis, stride):
    return lax.ppermute(x, axis, [(i, i ^ 1 << stride) for i in range(lax.axis_size(axis))])


def shifted(x, axis, by):
    size = lax.axis_size(axis)
    pairs = [(i, i + by) for i in range(size) if 0 <= i + by < size]
    return lax.ppermute(x, axis, pairs)


def chain_rows(grad_rows, projected, gate_score, hidden, joined, down_full, gate_vector):
    hidden_units = down_full.shape[0]
    gate_pre = projected[:, :hidden_units]
    up_pre = projected[:, hidden_units:]
    gate_sig = jax.nn.sigmoid(gate_pre)
    activated = gate_pre * gate_sig
    back_proj = lax.dot_general(
        grad_rows, down_full, (((1,), (1,)), ((), ())), preferred_element_type=jnp.float32
    )
    gate_sum = jnp.sum(back_proj * hidden.astype(jnp.float32), axis=1, keepdims=True)
    hidden_grad = gate_score * back_proj
    gate_grad = hidden_grad * up_pre * gate_sig * (1.0 + gate_pre * (1.0 - gate_sig))
    up_grad = hidden_grad * activated
    pair_grad = jnp.concatenate([gate_grad, up_grad], axis=1).astype(jnp.bfloat16)
    through = lax.dot_general(
        pair_grad, joined, (((1,), (1,)), ((), ())), preferred_element_type=jnp.float32
    )
    logit_grad = gate_sum * gate_score * (1.0 - gate_score)
    return (
        grad_rows.astype(jnp.float32)
        + through
        + logit_grad * gate_vector.astype(jnp.float32)[None, :]
    ).astype(jnp.bfloat16)


def on_device(stash, cotangent, gate_weight, up_weight, down_weight, shared_gate):
    sections = lax.axis_size("section")
    replicas = lax.axis_size("dp")
    section_index = lax.axis_index("section")
    local_rows = stash.shape[1]
    model_width = stash.shape[2]
    own_rows = stash[0]
    for bit_place in range(sections.bit_length() - 1):
        own_rows = from_partner(own_rows, "section", bit_place)
    seeded = lax.all_gather(cotangent, "section", axis=1, tiled=True)
    gate_full, up_full = (
        lax.all_gather(gate_weight[0], "dp", axis=0, tiled=True),
        lax.all_gather(up_weight[0], "dp", axis=0, tiled=True),
    )
    joined = jnp.concatenate([gate_full, up_full], axis=1)
    down_full = down_weight[0]
    gate_vector = shared_gate[0]
    hidden_units = down_full.shape[0]
    projected_all = jnp.dot(own_rows, joined, preferred_element_type=jnp.float32)
    score_all = jax.nn.sigmoid(jnp.dot(own_rows, gate_vector, preferred_element_type=jnp.float32))[
        :, None
    ]
    gate_all = projected_all[:, :hidden_units]
    hidden_all = (gate_all * jax.nn.sigmoid(gate_all) * projected_all[:, hidden_units:]).astype(
        jnp.bfloat16
    )
    tick_count = sections + MICRO - 1
    is_last = section_index == sections - 1
    offset = sections - 1 - section_index

    def advance(tick_now, received):
        micro_index = tick_now - offset
        active = jnp.logical_and(micro_index >= 0, micro_index < MICRO)
        row_start = jnp.clip(micro_index, 0, MICRO - 1) * ROWS
        seed_rows = lax.dynamic_slice_in_dim(seeded, row_start, ROWS, 0)
        grad_rows = jnp.where(is_last, seed_rows, received)
        pieces = (
            grad_rows,
            lax.dynamic_slice_in_dim(projected_all, row_start, ROWS, 0),
            lax.dynamic_slice_in_dim(score_all, row_start, ROWS, 0),
            lax.dynamic_slice_in_dim(hidden_all, row_start, ROWS, 0),
        )

        def compute(operands):
            return chain_rows(
                operands[0], operands[1], operands[2], operands[3], joined, down_full, gate_vector
            )

        def skip_step(operands):
            return jnp.zeros_like(operands[0])

        return (lax.cond(active, compute, skip_step, pieces), grad_rows)

    def one_tick(received, tick_now):
        outgoing, grad_rows = advance(tick_now, received)
        passed = shifted(outgoing, "section", -1)
        return (passed, (outgoing, grad_rows))

    start_rows = jnp.zeros((ROWS, model_width), jnp.bfloat16)
    received, (outs_seen, grads_seen) = lax.scan(
        one_tick, start_rows, jnp.arange(tick_count - 1, dtype=jnp.int32)
    )
    last_out, last_grad = advance(tick_count - 1, received)
    outs_seen = jnp.concatenate([outs_seen, last_out[None]], axis=0)
    grads_seen = jnp.concatenate([grads_seen, last_grad[None]], axis=0)
    results = lax.dynamic_slice_in_dim(outs_seen, offset, MICRO, 0).reshape(local_rows, model_width)
    grad_all = lax.dynamic_slice_in_dim(grads_seen, offset, MICRO, 0).reshape(
        local_rows, model_width
    )
    scaled_all = (score_all * grad_all.astype(jnp.float32)).astype(jnp.bfloat16)
    norm_factor = (local_rows * replicas) ** (-0.5)
    weight_part = lax.dot_general(
        hidden_all, scaled_all, (((0,), (0,)), ((), ())), preferred_element_type=jnp.float32
    )
    summed = lax.psum_scatter(
        weight_part.astype(jnp.bfloat16), "dp", scatter_dimension=0, tiled=True
    ).astype(jnp.float32)
    return (results[None], (summed * norm_factor)[None])


def solution(mesh):
    placed = (
        P("section", "dp", None),
        P("dp", "section"),
        P("section", "dp", None),
        P("section", "dp", None),
        P("section", None, None),
        P("section", None),
    )
    return jax.shard_map(
        on_device,
        mesh=mesh,
        in_specs=placed,
        out_specs=(P("section", "dp", None), P("section", "dp", None)),
        check_vma=False,
    )
```

profile of v0, /device:TPU:1, one launch (start us, length us, event | category | flops | bytes accessed | tf_op | source)
XLA Modules:
  0.0 256.4 jit_solution(17409450213400630852)
XLA Ops:
  8.8 2.1 collective-permute-done.1
  10.9 2.3 collective-permute-start.2
  14.0 16.1 %all_gather.9 = bf16[128,2048]{1,0:T(8,128)(2,1)} all-gather(bf16[128,512]{1,0:T(8,128)(2,1)} %param.13), channel_id=1, replica_groups=mesh['section'=4,'dp'=8] {'section'}, dimensions={1}, use_global_device_ids=true | all-gather | bytes 655360 | tf_op jit(solution)/shard_map/all_gather | solution.py:54
  31.0 29.4 %all-gather.5.cloned.1.call-done = bf16[1,2048,512]{2,1,0:T(8,128)(2,1)} async-done(((bf16[1,256,512]{2,1,0:T(8,128)(2,1)}), bf16[1,2048,512]{2,1,0:T(8,128)(2,1)}) %all-gather.5.cloned.1.call-update) | async-done | bytes 2097168 | tf_op jit(solution)/shard_map/all_gather | solution.py:56
  60.4 49.9 %all-gather.7.cloned.1.call-done = bf16[1,2048,512]{2,1,0:T(8,128)(2,1)} async-done(((bf16[1,256,512]{2,1,0:T(8,128)(2,1)}), bf16[1,2048,512]{2,1,0:T(8,128)(2,1)}) %all-gather.7.cloned.1.call-update) | async-done | bytes 2097168 | tf_op jit(solution)/shard_map/all_gather | solution.py:57
  110.3 2.8 %pad_maximum_fusion = bf16[2048,1024]{1,0:T(8,128)(2,1)S(1)} fusion(bf16[2048,512]{1,0:T(8,128)(2,1)} %bitcast.63, bf16[2048,512]{1,0:T(8,128)(2,1)} %bitcast.62), kind=kLoop, calls=%fused_computation.35 | loop fusion | flops 8388608 | bytes 8388608 | tf_op jit(solution)/shard_map/concatenate | solution.py:59
  114.0 1.3 copy-done
  115.3 1.0 copy-done.1
  116.3 63.1 %while.14 = (s32[]{:T(128)}, bf16[64,2048]{1,0:T(8,128)(2,1)S(1)}, bf16[4,64,2048]{2,1,0:T(8,128)(2,1)}, bf16[4,64,2048]{2,1,0:T(8,128)(2,1)}, s32[4]{0:T(128)S(...) while((s32[]{:T(128)}, bf16[64,2048]{1,0:T(8,128)(2,1)S(1)}, ...), condition=%wide.region_4.5_spmd, body=%wide.region_0.4_spmd.sunk | while | flops 404260992 | bytes 10837449 | solution.py:104
  117.5 1.7 bitcast_dynamic-update-slice_fusion.2
  120.0 3.7 %collective-permute-start = (bf16[64,2048]{1,0:T(8,128)(2,1)}, bf16[64,2048]{1,0:T(8,128)(2,1)S(1)}, u32[]{:S(2)}, u32[]{:S(2)}) collective-permute-start(bf16[64,2048]{1,0:T(8,128)(2,1)} %get-tuple-element.350), channel_id=1, source_target_pairs={{8,0},{16,8},{24,16},{9,1},{17,9},{25,17},{10,2},{18,10},{26,18},{... | collective-permute-start | bytes 786440 | tf_op jit(solution)/shard_map/while/body/eval_jaxpr/ppermute | solution.py:17
  124.4 4.6 %collective-permute-done = bf16[64,2048]{1,0:T(8,128)(2,1)S(1)} collective-permute-done((bf16[64,2048]{1,0:T(8,128)(2,1)}, bf16[64,2048]{1,0:T(8,128)(2,1)S(1)}, u32[]{:S(2)}, u32[]{:S(2)}) %collective-permute-start) | collective-permute-done | bytes 262176 | tf_op jit(solution)/shard_map/while/body/eval_jaxpr/ppermute | solution.py:17
  130.3 1.7 bitcast_dynamic-update-slice_fusion.2
  132.8 1.9 collective-permute-start
  135.4 9.6 %collective-permute-done = bf16[64,2048]{1,0:T(8,128)(2,1)S(1)} collective-permute-done((bf16[64,2048]{1,0:T(8,128)(2,1)}, bf16[64,2048]{1,0:T(8,128)(2,1)S(1)}, u32[]{:S(2)}, u32[]{:S(2)}) %collective-permute-start) | collective-permute-done | bytes 262176 | tf_op jit(solution)/shard_map/while/body/eval_jaxpr/ppermute | solution.py:17
  146.3 1.8 bitcast_dynamic-update-slice_fusion.2
  148.1 6.3 %conditional.4 = (bf16[64,2048]{1,0:T(8,128)(2,1)}, bf16[1,64,2048]{2,1,0:T(8,128)(2,1)S(1)}) conditional(s32[]{:T(128)} %convert_element_type.92, () %tuple.60, (bf16[64,2048]{1,0:T(8,128)(2,1)S(1)}, f32[128,1]{0,1:T(1,128)S(1)}, s32[]{:T(128)}, bf16[512,2048]{1,0:T(8,128)(2,1)S(1)}, f32[128,1024]{1,0:T(8,128)S(1)}, ...), branch_computations={%region_1.1_spmd, %region_2.3_spmd} | conditional | flops 404129920 | bytes 8214572 | solution.py:96
  149.1 4.3 %fusion.1 = bf16[64,2048]{1,0:T(8,128)(2,1)} fusion(bf16[2048,1024]{1,0:T(8,128)(2,1)} %get-tuple-element.185, bf16[64,2048]{1,0:T(8,128)(2,1)S(1)} %get-tuple-element.180, f32[2048]{0:T(1024)S(1)} %convert_element_type.56, f32[64]{0:T(128)S(1)} %fusion.9, bf16[64,512]{1,0:T(8,128)(2,1)S(1)} %get-tuple-element.254, bf16[64,512]{1,0:T(8,128)(2,1)S(1)} %get-tuple-element.253), kind=kOutput, calls=%fused_computation.2 | convolution fusion | flops 269352960 | bytes 4858112 | tf_op jit(solution)/shard_map/while/body/eval_jaxpr/cond/branch_1_fun/dot_general | solution.py:34
  153.4 0.9 copy.12
  154.3 1.9 collective-permute-start
  157.0 5.2 %collective-permute-done = bf16[64,2048]{1,0:T(8,128)(2,1)S(1)} collective-permute-done((bf16[64,2048]{1,0:T(8,128)(2,1)}, bf16[64,2048]{1,0:T(8,128)(2,1)S(1)}, u32[]{:S(2)}, u32[]{:S(2)}) %collective-permute-start) | collective-permute-done | bytes 262176 | tf_op jit(solution)/shard_map/while/body/eval_jaxpr/ppermute | solution.py:17
  163.5 1.7 bitcast_dynamic-update-slice_fusion.2
  165.2 6.3 %conditional.4 = (bf16[64,2048]{1,0:T(8,128)(2,1)}, bf16[1,64,2048]{2,1,0:T(8,128)(2,1)S(1)}) conditional(s32[]{:T(128)} %convert_element_type.92, () %tuple.60, (bf16[64,2048]{1,0:T(8,128)(2,1)S(1)}, f32[128,1]{0,1:T(1,128)S(1)}, s32[]{:T(128)}, bf16[512,2048]{1,0:T(8,128)(2,1)S(1)}, f32[128,1024]{1,0:T(8,128)S(1)}, ...), branch_computations={%region_1.1_spmd, %region_2.3_spmd} | conditional | flops 404129920 | bytes 8214572 | solution.py:96
  166.3 4.3 %fusion.1 = bf16[64,2048]{1,0:T(8,128)(2,1)} fusion(bf16[2048,1024]{1,0:T(8,128)(2,1)} %get-tuple-element.185, bf16[64,2048]{1,0:T(8,128)(2,1)S(1)} %get-tuple-element.180, f32[2048]{0:T(1024)S(1)} %convert_element_type.56, f32[64]{0:T(128)S(1)} %fusion.9, bf16[64,512]{1,0:T(8,128)(2,1)S(1)} %get-tuple-element.254, bf16[64,512]{1,0:T(8,128)(2,1)S(1)} %get-tuple-element.253), kind=kOutput, calls=%fused_computation.2 | convolution fusion | flops 269352960 | bytes 4858112 | tf_op jit(solution)/shard_map/while/body/eval_jaxpr/cond/branch_1_fun/dot_general | solution.py:34
  171.5 1.9 collective-permute-start
  174.1 5.2 %collective-permute-done = bf16[64,2048]{1,0:T(8,128)(2,1)S(1)} collective-permute-done((bf16[64,2048]{1,0:T(8,128)(2,1)}, bf16[64,2048]{1,0:T(8,128)(2,1)S(1)}, u32[]{:S(2)}, u32[]{:S(2)}) %collective-permute-start) | collective-permute-done | bytes 262176 | tf_op jit(solution)/shard_map/while/body/eval_jaxpr/ppermute | solution.py:17
  179.4 1.0 dynamic-slice_select_fusion.1
  180.4 1.2 fusion.25
  181.6 2.1 convolution_convert_fusion
  183.8 2.0 fusion.26
  185.9 62.3 %reduce-scatter.2.cloned.1.call-done = bf16[64,2048]{1,0:T(8,128)(2,1)} async-done(((bf16[512,2048]{1,0:T(8,128)(2,1)}), bf16[64,2048]{1,0:T(8,128)(2,1)}) %reduce-scatter.2.cloned.1.call-update) | async-done | bytes 262160 | tf_op jit(solution)/shard_map/reduce_scatter | solution.py:119
  248.1 1.8 multiply_bitcast_fusion
  (44 shorter events, 15.4 us)
Async XLA Ops:
  7.2 53.2 %all-gather.5.cloned.1.call-start = ((), (), s32[]{:S(2)}) async-start(), calls=%async_computation.2 | async-start | bytes 2359296 | tf_op jit(solution)/shard_map/all_gather | solution.py:56
  7.9 102.4 %all-gather.7.cloned.1.call-start = ((), (), s32[]{:S(2)}) async-start(), calls=%async_computation.3 | async-start | bytes 2359296 | tf_op jit(solution)/shard_map/all_gather | solution.py:57
  8.6 239.5 %reduce-scatter.2.cloned.1.call-start = ((), (), s32[]{:S(2)}) async-start(), calls=%async_computation.1 | async-start | bytes 2359296 | tf_op jit(solution)/shard_map/reduce_scatter | solution.py:119
  8.7 2.2 collective-permute-start.1
  10.9 19.2 %collective-permute-start.2 = (bf16[128,2048]{1,0:T(8,128)(2,1)S(1)}, bf16[128,2048]{1,0:T(8,128)(2,1)S(1)}, u32[]{:S(2)}, u32[]{:S(2)}) collective-permute-start(bf16[128,2048]{1,0:T(8,128)(2,1)S(1)} %collective-permute-done.1), channel_id=1, source_target_pairs={{0,16},{8,24},{16,0},{24,8},{1,17},{9,25},{17,1},{25,9},{2,18},{10... | collective-permute-start | bytes 1572872 | tf_op jit(solution)/shard_map/ppermute | solution.py:11
  113.1 2.1 copy-start
  113.1 3.1 %copy-start.1 = (bf16[1,512,2048]{2,1,0:T(8,128)(2,1)S(1)}, bf16[1,512,2048]{2,1,0:T(8,128)(2,1)}, u32[]{:S(2)}) copy-start(bf16[1,512,2048]{2,1,0:T(8,128)(2,1)} %param.16) | copy-start | bytes 6291460
  120.0 9.0 %collective-permute-start = (bf16[64,2048]{1,0:T(8,128)(2,1)}, bf16[64,2048]{1,0:T(8,128)(2,1)S(1)}, u32[]{:S(2)}, u32[]{:S(2)}) collective-permute-start(bf16[64,2048]{1,0:T(8,128)(2,1)} %get-tuple-element.350), channel_id=1, source_target_pairs={{8,0},{16,8},{24,16},{9,1},{17,9},{25,17},{10,2},{18,10},{26,18},{... | collective-permute-start | bytes 786440 | tf_op jit(solution)/shard_map/while/body/eval_jaxpr/ppermute | solution.py:17
  132.8 12.3 %collective-permute-start = (bf16[64,2048]{1,0:T(8,128)(2,1)}, bf16[64,2048]{1,0:T(8,128)(2,1)S(1)}, u32[]{:S(2)}, u32[]{:S(2)}) collective-permute-start(bf16[64,2048]{1,0:T(8,128)(2,1)} %get-tuple-element.350), channel_id=1, source_target_pairs={{8,0},{16,8},{24,16},{9,1},{17,9},{25,17},{10,2},{18,10},{26,18},{... | collective-permute-start | bytes 786440 | tf_op jit(solution)/shard_map/while/body/eval_jaxpr/ppermute | solution.py:17
  154.3 7.9 %collective-permute-start = (bf16[64,2048]{1,0:T(8,128)(2,1)}, bf16[64,2048]{1,0:T(8,128)(2,1)S(1)}, u32[]{:S(2)}, u32[]{:S(2)}) collective-permute-start(bf16[64,2048]{1,0:T(8,128)(2,1)} %get-tuple-element.350), channel_id=1, source_target_pairs={{8,0},{16,8},{24,16},{9,1},{17,9},{25,17},{10,2},{18,10},{26,18},{... | collective-permute-start | bytes 786440 | tf_op jit(solution)/shard_map/while/body/eval_jaxpr/ppermute | solution.py:17
  171.5 7.9 %collective-permute-start = (bf16[64,2048]{1,0:T(8,128)(2,1)}, bf16[64,2048]{1,0:T(8,128)(2,1)S(1)}, u32[]{:S(2)}, u32[]{:S(2)}) collective-permute-start(bf16[64,2048]{1,0:T(8,128)(2,1)} %get-tuple-element.350), channel_id=1, source_target_pairs={{8,0},{16,8},{24,16},{9,1},{17,9},{25,17},{10,2},{18,10},{26,18},{... | collective-permute-start | bytes 786440 | tf_op jit(solution)/shard_map/while/body/eval_jaxpr/ppermute | solution.py:17
Sparse Core Ops, SparseCore 0:
  10.1 50.2 all-gather.4
  62.5 47.7 all-gather.6
  183.9 64.1 reduce-scatter.1
where the time goes:
time: 259 us; the launch traced here: 256 us
  waiting for transfers between devices  170 us (66%)
  other arithmetic  16.7 us (6%)
  blocking collectives  16.1 us (6%)
  matrix products  14.1 us (5%)
  between operations  13.8 us (5%)
  starting transfers between devices  12 us (5%)
  local copies, waits for them, and re-layouts  11.1 us (4%)
  loops' own time  2.77 us (1%)
    reduce_scatter x1, waiting for transfers between devices, on_device(): lax.psum_scatter(weight_part.astype(jnp.bfloat16), 'dp', scatter_dimensio...  62.3 us
    all_gather x1, waiting for transfers between devices, on_device(): lax.all_gather(up_weight[0], 'dp', axis=0, tiled=True)  49.9 us
    all_gather x1, waiting for transfers between devices, on_device(): lax.all_gather(gate_weight[0], 'dp', axis=0, tiled=True)  29.4 us
    ppermute x4, waiting for transfers between devices, shifted(): return lax.ppermute(x, axis, pairs)  24.7 us
    all_gather x1, blocking collectives, on_device(): seeded = lax.all_gather(cotangent, 'section', axis=1, tiled=True)  16.1 us
    ppermute x4, starting transfers between devices, shifted(): return lax.ppermute(x, axis, pairs)  9.43 us
    dot_general x2, matrix products, chain_rows(): lax.dot_general(pair_grad, joined, (((1,), (1,)), ((), ())), preferred_el...  8.59 us
    dynamic_update_slice x4, other arithmetic, on_device(): lax.scan(one_tick, start_rows, jnp.arange(tick_count - 1, dtype=jnp.int32))  6.96 us
  transfers between devices with their start and end apart: 9, of which 8 were waited for; matrix products, arithmetic and copies ran while one was open for 3% of the time, Pallas kernels for 0%

commit v1 on v0

v1 whole, which is shorter than its diff:
```python
import jax
import jax.numpy as jnp
from jax import lax
from jax.sharding import PartitionSpec as P


def to_next(x, axis, pairs):
    return lax.ppermute(x, axis, pairs)


def ring_order(size):
    return [i for i in range(0, size, 2)] + [i for i in range(1, size, 2)][::-1]


def gather_ring(arrays, axis):
    size = lax.axis_size(axis)
    order = ring_order(size)
    ahead = [(order[i], order[(i + 1) % size]) for i in range(size)]
    back = [(b, a) for a, b in ahead]
    pieces = [list(arrays)]
    offsets = [0]
    from_back, from_ahead = list(arrays), list(arrays)
    for step in range(1, (size - 1) // 2 + 1):
        from_back = [to_next(v, axis, ahead) for v in from_back]
        from_ahead = [to_next(v, axis, back) for v in from_ahead]
        pieces += [from_back, from_ahead]
        offsets += [-step, step]
    if size % 2 == 0 and size > 1:
        half = len(arrays) // 2
        last = [
            to_next(v if i < half else w, axis, ahead if i < half else back)
            for i, (v, w) in enumerate(zip(from_back, from_ahead))
        ]
        pieces.append(last)
        offsets.append(size // 2)
    return pieces, offsets


def block_owner(offset, axis):
    size = lax.axis_size(axis)
    order = ring_order(size)
    place = [order.index(i) for i in range(size)]
    table = jnp.array([order[(place[i] + offset) % size] for i in range(size)], jnp.int32)
    return table[lax.axis_index(axis)]


def gather_to_last(x, axis):
    size = lax.axis_size(axis)
    width = 1
    while width < size:
        pairs = [(i, i + width) for i in range(width - 1, size - width, 2 * width)]
        x = jnp.concatenate([to_next(x, axis, pairs), x], axis=1)
        width *= 2
    return x


def reduce_rows(hidden, rows, axis):
    size = lax.axis_size(axis)
    inner = 2 if size % 2 == 0 else 1
    outer = size // inner
    me = lax.axis_index(axis)
    units = hidden.shape[1] // size
    width = rows.shape[1]
    cut = width * 11 // 16 // 128 * 128
    swap = [(i, i ^ 1) for i in range(size)]

    def turn(k):
        return [(i, (i + k * inner) % size) for i in range(size)]

    def block(k, j):
        place = (me // inner + k) % outer * inner + (me + j) % inner
        return lax.dynamic_slice_in_dim(hidden, place * units, units, 1)

    def product(blocks, columns):
        left = jnp.concatenate(blocks, axis=1)
        return lax.dot_general(
            left, columns, (((0,), (0,)), ((), ())), preferred_element_type=jnp.float32
        )

    first, second = rows[:, :cut], rows[:, cut:]
    send_a = product([block(k, 1) for k in range(outer)], first).astype(jnp.bfloat16)
    got_a = to_next(send_a, axis, swap)
    sums_b = product([block(0, j) for j in range(inner)], second)
    for k in range(1, outer):
        send = product([block(k, j) for j in range(inner)], second).astype(jnp.bfloat16)
        sums_b += to_next(send, axis, turn(k)).astype(jnp.float32)
    keep_a = product([block(k, 0) for k in range(outer)], first) + got_a.astype(jnp.float32)
    total_a = keep_a[:units]
    for k in range(1, outer):
        send = keep_a[k * units : (k + 1) * units].astype(jnp.bfloat16)
        total_a += to_next(send, axis, turn(k)).astype(jnp.float32)
    got_b = to_next(sums_b[units:].astype(jnp.bfloat16), axis, swap)
    total_b = sums_b[:units] + got_b.astype(jnp.float32)
    return jnp.concatenate([total_a, total_b], axis=1)


def on_device(stash, cotangent, gate_weight, up_weight, down_weight, shared_gate):
    sections = lax.axis_size("section")
    replicas = lax.axis_size("dp")
    section_index = lax.axis_index("section")
    local_rows = stash.shape[1]
    depth = gate_weight.shape[1]
    down_full = down_weight[0]
    gate_vector = shared_gate[0]
    hidden_units = down_full.shape[0]

    own_rows = to_next(stash[0], "section", [(i, sections - 1 - i) for i in range(sections)])
    seeded = gather_to_last(cotangent, "section")
    pieces, offsets = gather_ring([gate_weight[0], up_weight[0]], "dp")
    owners = [block_owner(offset, "dp") for offset in offsets]

    score = jax.nn.sigmoid(jnp.dot(own_rows, gate_vector, preferred_element_type=jnp.float32))[:, None]
    joined = jnp.zeros((depth * replicas, 2 * hidden_units), jnp.bfloat16)
    for owner, piece in zip(owners, pieces):
        joined = lax.dynamic_update_slice(
            joined, jnp.concatenate(piece, axis=1), (owner * depth, 0)
        )
    projected = jnp.dot(own_rows, joined, preferred_element_type=jnp.float32)
    gate_pre, up_pre = projected[:, :hidden_units], projected[:, hidden_units:]
    gate_sig = jax.nn.sigmoid(gate_pre)
    activated = gate_pre * gate_sig
    hidden = (activated * up_pre).astype(jnp.bfloat16)
    gate_scale = score * up_pre * gate_sig * (1.0 + gate_pre * (1.0 - gate_sig))
    up_scale = score * activated

    grad_rows = seeded
    results = grads = None
    for tick in range(sections):
        back_proj = lax.dot_general(
            grad_rows, down_full, (((1,), (1,)), ((), ())), preferred_element_type=jnp.float32
        )
        gate_sum = jnp.sum(back_proj * hidden.astype(jnp.float32), axis=1, keepdims=True)
        pair_grad = jnp.concatenate([back_proj * gate_scale, back_proj * up_scale], axis=1).astype(
            jnp.bfloat16
        )
        through = lax.dot_general(
            pair_grad, joined, (((1,), (1,)), ((), ())), preferred_element_type=jnp.float32
        )
        logit_grad = gate_sum * score * (1.0 - score)
        outgoing = (
            grad_rows.astype(jnp.float32)
            + through
            + logit_grad * gate_vector.astype(jnp.float32)[None, :]
        ).astype(jnp.bfloat16)
        here = section_index == sections - 1 - tick
        results = outgoing if tick == 0 else jnp.where(here, outgoing, results)
        grads = grad_rows if tick == 0 else jnp.where(here, grad_rows, grads)
        if tick < sections - 1:
            pairs = [(i, i - 1) for i in range(1, sections)]
            grad_rows = to_next(outgoing, "section", pairs)

    scaled = (score * grads.astype(jnp.float32)).astype(jnp.bfloat16)
    summed = reduce_rows(hidden, scaled, "dp")
    norm_factor = (local_rows * replicas) ** (-0.5)
    return (results[None], (summed * norm_factor)[None])


def solution(mesh):
    placed = (
        P("section", "dp", None),
        P("dp", "section"),
        P("section", "dp", None),
        P("section", "dp", None),
        P("section", None, None),
        P("section", None),
    )
    return jax.shard_map(
        on_device,
        mesh=mesh,
        in_specs=placed,
        out_specs=(P("section", "dp", None), P("section", "dp", None)),
        check_vma=False,
    )
```

time: 259 us -> 149 us (0.58)
  waiting for transfers between devices: 170 us -> 67.1 us
  starting transfers between devices: 12 us -> 30 us
  blocking collectives: 16.1 us -> 0 us
  matrix products: 14.1 us -> 27 us
  between operations: 13.8 us -> 5.84 us
  other arithmetic: 16.7 us -> 11.2 us
  local copies, waits for them, and re-layouts: 11.1 us -> 7.19 us
  loops' own time: 2.77 us -> 0 us
    all_gather x2 -> x0, waiting for transfers between devices: 79.3 us -> none  [the longest x1 49.9 us: on_device(): lax.all_gather(up_weight[0], 'dp', axis=0, tiled=True)]
    reduce_scatter x1 -> x0, waiting for transfers between devices: 62.3 us -> none  [on_device(): lax.psum_scatter(weight_part.astype(jnp.bfloat16), 'dp', scatter_dimensio...]
    ppermute x6 -> x28, waiting for transfers between devices: 26.8 us -> 67.1 us  [to_next(): return lax.ppermute(x, axis, pairs)]
    ppermute x6 -> x28, starting transfers between devices: 11.9 us -> 30 us  [to_next(): return lax.ppermute(x, axis, pairs)]
    all_gather x1 -> x0, blocking collectives: 16.1 us -> none  [on_device(): seeded = lax.all_gather(cotangent, 'section', axis=1, tiled=True)]
    dot_general x6 -> x15, matrix products: 13.2 us -> 26.8 us  [the longest x4 16.9 us: on_device(): lax.dot_general(pair_grad, joined, (((1,), (1,)), ((), ())), preferred_el...]
    concatenate x3, other arithmetic: 6.01 us -> 1.03 us  [the longest x1 0.92 us: gather_to_last(): x = jnp.concatenate([to_next(x, axis, pairs), x], axis=1)]
    dynamic_update_slice x4 -> x0, local copies, waits for them, and re-layouts: 2.91 us -> none  [on_device(): lax.scan(one_tick, start_rows, jnp.arange(tick_count - 1, dtype=jnp.int32))]
  transfers between devices with their start and end apart: 9 -> 28, of which waited for: 8 -> 14; matrix products, arithmetic and copies ran while one was open for 3% -> 16% of each run, Pallas kernels for 0% -> 0%
where the time goes in v1:
time: 149 us; the launch traced here: 148 us
  waiting for transfers between devices  67.1 us (45%)
  starting transfers between devices  30 us (20%)
  matrix products  27 us (18%)
  other arithmetic  11.2 us (8%)
  local copies, waits for them, and re-layouts  7.19 us (5%)
  between operations  5.84 us (4%)
    ppermute x28, waiting for transfers between devices, to_next(): return lax.ppermute(x, axis, pairs)  67.1 us
    ppermute x28, starting transfers between devices, to_next(): return lax.ppermute(x, axis, pairs)  30 us
    dot_general x4, matrix products, on_device(): lax.dot_general(pair_grad, joined, (((1,), (1,)), ((), ())), preferred_el...  16.9 us
    dynamic_update_slice x8, other arithmetic, on_device(): lax.dynamic_update_slice(joined, jnp.concatenate(piece, axis=1), (owner *...  8.98 us
    dot_general x4, matrix products, on_device(): lax.dot_general(grad_rows, down_full, (((1,), (1,)), ((), ())), preferred...  4.88 us
    dynamic_slice x7, local copies, waits for them, and re-layouts, block_owner(): return table[lax.axis_index(axis)]  4.31 us
  transfers between devices with their start and end apart: 28, of which 14 were waited for; matrix products, arithmetic and copies ran while one was open for 16% of the time, Pallas kernels for 0%

profile of v1, /device:TPU:1, one launch (start us, length us, event | category | flops | bytes accessed | tf_op | source)
XLA Modules:
  0.0 148.4 jit_solution(4770098205025295620)
XLA Ops:
  0.8 1.4 collective-permute-start
  2.2 2.2 %collective-permute-start.4 = (bf16[256,512]{1,0:T(8,128)(2,1)}, bf16[256,512]{1,0:T(8,128)(2,1)}, u32[]{:S(2)}, u32[]{:S(2)}) collective-permute-start(bf16[256,512]{1,0:T(8,128)(2,1)} %bitcast.59), channel_id=1, source_target_pairs={{0,2},{2,4},{4,6},{6,7},{7,5},{5,3},{3,1},{1,0},{8,10},{10,12},{12... | collective-permute-start | bytes 786440 | tf_op jit(solution)/shard_map/ppermute | solution.py:8
  6.8 3.4 %collective-permute-start.1 = (bf16[128,1024]{1,0:T(8,128)(2,1)S(1)}, bf16[128,1024]{1,0:T(8,128)(2,1)S(1)}, u32[]{:S(2)}, u32[]{:S(2)}) collective-permute-start(bf16[128,1024]{1,0:T(8,128)(2,1)S(1)} %pad_maximum_fusion), channel_id=1, source_target_pairs={{8,24},{9,25},{10,26},{11,27},{12,28},{13,29},{14,30},{15,31}} | collective-permute-start | bytes 786440 | tf_op jit(solution)/shard_map/ppermute | solution.py:8
  10.2 2.5 %broadcast_in_dim.4 = bf16[2048,1024]{1,0:T(8,128)(2,1)} broadcast(bf16[]{:T(256)} %constant.173.clone.1), dimensions={} | broadcast | bytes 4194306 | tf_op jit(solution)/shard_map/broadcast_in_dim | solution.py:113
  24.9 1.9 %maximum_dynamic-update-slice_fusion.1 = bf16[2048,1024]{1,0:T(8,128)(2,1)} fusion(bf16[2048,1024]{1,0:T(8,128)(2,1)} %maximum_dynamic-update-slice_fusion, s32[]{:T(128)S(6)} %select_n.199, bf16[256,512]{1,0:T(8,128)(2,1)} %collective-permute-done.4, bf16[256,512]{1,0:T(8,128)(2,1)} %collective-permute-done.3), kind=kLoop, calls=%fused_computation.35 | loop fusion | flops 1048576 | bytes 1048580 | tf_op jit(solution)/shard_map/dynamic_update_slice | solution.py:115
  28.2 1.9 %maximum_dynamic-update-slice_fusion.2 = bf16[2048,1024]{1,0:T(8,128)(2,1)} fusion(bf16[2048,1024]{1,0:T(8,128)(2,1)} %maximum_dynamic-update-slice_fusion.1, s32[]{:T(128)S(6)} %select_n.200, bf16[256,512]{1,0:T(8,128)(2,1)} %collective-permute-done.6, bf16[256,512]{1,0:T(8,128)(2,1)} %collective-permute-done.5), kind=kLoop, calls=%fused_computation.36 | loop fusion | flops 1048576 | bytes 1048580 | tf_op jit(solution)/shard_map/dynamic_update_slice | solution.py:115
  30.3 1.7 %collective-permute-done.8 = bf16[256,512]{1,0:T(8,128)(2,1)S(1)} collective-permute-done((bf16[256,512]{1,0:T(8,128)(2,1)}, bf16[256,512]{1,0:T(8,128)(2,1)S(1)}, u32[]{:S(2)}, u32[]{:S(2)}) %collective-permute-start.8) | collective-permute-done | bytes 262176 | tf_op jit(solution)/shard_map/ppermute | solution.py:8
  33.3 4.3 %collective-permute-done.7 = bf16[256,512]{1,0:T(8,128)(2,1)S(1)} collective-permute-done((bf16[256,512]{1,0:T(8,128)(2,1)}, bf16[256,512]{1,0:T(8,128)(2,1)S(1)}, u32[]{:S(2)}, u32[]{:S(2)}) %collective-permute-start.7) | collective-permute-done | bytes 262176 | tf_op jit(solution)/shard_map/ppermute | solution.py:8
  39.1 3.1 %collective-permute-done.9 = bf16[256,512]{1,0:T(8,128)(2,1)S(1)} collective-permute-done((bf16[256,512]{1,0:T(8,128)(2,1)}, bf16[256,512]{1,0:T(8,128)(2,1)S(1)}, u32[]{:S(2)}, u32[]{:S(2)}) %collective-permute-start.9) | collective-permute-done | bytes 262176 | tf_op jit(solution)/shard_map/ppermute | solution.py:8
  43.5 4.3 %collective-permute-done.14 = bf16[256,512]{1,0:T(8,128)(2,1)S(1)} collective-permute-done((bf16[256,512]{1,0:T(8,128)(2,1)S(1)}, bf16[256,512]{1,0:T(8,128)(2,1)S(1)}, u32[]{:S(2)}, u32[]{:S(2)}) %collective-permute-start.14) | collective-permute-done | bytes 262176 | tf_op jit(solution)/shard_map/ppermute | solution.py:8
  48.3 1.4 collective-permute-start.15
  51.4 2.0 %collective-permute-done.13 = bf16[256,512]{1,0:T(8,128)(2,1)S(1)} collective-permute-done((bf16[256,512]{1,0:T(8,128)(2,1)S(1)}, bf16[256,512]{1,0:T(8,128)(2,1)S(1)}, u32[]{:S(2)}, u32[]{:S(2)}) %collective-permute-start.13) | collective-permute-done | bytes 262176 | tf_op jit(solution)/shard_map/ppermute | solution.py:8
  54.3 4.8 %collective-permute-done.16 = bf16[256,512]{1,0:T(8,128)(2,1)S(1)} collective-permute-done((bf16[256,512]{1,0:T(8,128)(2,1)S(1)}, bf16[256,512]{1,0:T(8,128)(2,1)S(1)}, u32[]{:S(2)}, u32[]{:S(2)}) %collective-permute-start.16) | collective-permute-done | bytes 262176 | tf_op jit(solution)/shard_map/ppermute | solution.py:8
  59.9 2.9 %convolution_bitcast_fusion = f32[128,1024]{1,0:T(8,128)S(1)} fusion(bf16[128,2048]{1,0:T(8,128)(2,1)S(1)} %collective-permute-done.2, bf16[2048,1024]{1,0:T(8,128)(2,1)} %maximum_dynamic-update-slice_fusion.7), kind=kOutput, calls=%fused_computation.24 | convolution fusion | flops 536870912 | bytes 5242880 | tf_op jit(solution)/shard_map/dot_general | solution.py:118
  63.9 3.7 %fusion.4 = bf16[128,2048]{1,0:T(8,128)(2,1)S(1)} fusion(bf16[2048,1024]{1,0:T(8,128)(2,1)} %maximum_dynamic-update-slice_fusion.7, bf16[128,2048]{1,0:T(8,128)(2,1)S(1)} %constant_dynamic-update-slice_fusion, f32[2048]{0:T(1024)S(1)} %mul.301, f32[128]{0:T(128)S(1)} %multiply_multiply_fusion.3, bf16[128,512]{1,0:T(8,128)(2,1)S(1)} %get-tuple-element.6, ...), kind=kOutput, calls=%fused_computation.9 | convolution fusion | flops 538705920 | bytes 5513728 | tf_op jit(solution)/shard_map/dot_general | solution.py:136
  67.6 2.3 %collective-permute-start.17 = (bf16[128,2048]{1,0:T(8,128)(2,1)S(1)}, bf16[128,2048]{1,0:T(8,128)(2,1)S(1)}, u32[]{:S(2)}, u32[]{:S(2)}) collective-permute-start(bf16[128,2048]{1,0:T(8,128)(2,1)S(1)} %fusion.4), channel_id=1, source_target_pairs={{8,0},{16,8},{24,16},{9,1},{17,9},{25,17},{10,2},{18,10},{26,18},{... | collective-permute-start | bytes 1572872 | tf_op jit(solution)/shard_map/ppermute | solution.py:8
  70.0 8.2 %collective-permute-done.17 = bf16[128,2048]{1,0:T(8,128)(2,1)S(1)} collective-permute-done((bf16[128,2048]{1,0:T(8,128)(2,1)S(1)}, bf16[128,2048]{1,0:T(8,128)(2,1)S(1)}, u32[]{:S(2)}, u32[]{:S(2)}) %collective-permute-start.17) | collective-permute-done | bytes 524320 | tf_op jit(solution)/shard_map/ppermute | solution.py:8
  79.1 3.7 %fusion.5 = bf16[128,2048]{1,0:T(8,128)(2,1)S(1)} fusion(bf16[2048,1024]{1,0:T(8,128)(2,1)} %maximum_dynamic-update-slice_fusion.7, bf16[128,2048]{1,0:T(8,128)(2,1)S(1)} %collective-permute-done.17, f32[128]{0:T(128)S(1)} %multiply_multiply_fusion.2, f32[2048]{0:T(1024)S(1)} %mul.301, bf16[128,512]{1,0:T(8,128)(2,1)S(1)} %get-tuple-element.20, ...), kind=kOutput, calls=%fused_computation.10 | convolution fusion | flops 538705920 | bytes 5513728 | tf_op jit(solution)/shard_map/dot_general | solution.py:136
  82.9 1.9 %collective-permute-start.18 = (bf16[128,2048]{1,0:T(8,128)(2,1)S(1)}, bf16[128,2048]{1,0:T(8,128)(2,1)S(1)}, u32[]{:S(2)}, u32[]{:S(2)}) collective-permute-start(bf16[128,2048]{1,0:T(8,128)(2,1)S(1)} %fusion.5), channel_id=1, source_target_pairs={{8,0},{16,8},{24,16},{9,1},{17,9},{25,17},{10,2},{18,10},{26,18},{... | collective-permute-start | bytes 1572872 | tf_op jit(solution)/shard_map/ppermute | solution.py:8
  84.8 8.6 %collective-permute-done.18 = bf16[128,2048]{1,0:T(8,128)(2,1)S(1)} collective-permute-done((bf16[128,2048]{1,0:T(8,128)(2,1)S(1)}, bf16[128,2048]{1,0:T(8,128)(2,1)S(1)}, u32[]{:S(2)}, u32[]{:S(2)}) %collective-permute-start.18) | collective-permute-done | bytes 524320 | tf_op jit(solution)/shard_map/ppermute | solution.py:8
  94.3 4.5 %fusion.6 = bf16[128,2048]{1,0:T(8,128)(2,1)} fusion(bf16[2048,1024]{1,0:T(8,128)(2,1)} %maximum_dynamic-update-slice_fusion.7, bf16[128,2048]{1,0:T(8,128)(2,1)S(1)} %collective-permute-done.18, f32[128]{0:T(128)S(1)} %multiply_multiply_fusion.1, f32[2048]{0:T(1024)S(1)} %mul.301, bf16[128,512]{1,0:T(8,128)(2,1)S(1)} %get-tuple-element.17, ...), kind=kOutput, calls=%fused_computation.11 | convolution fusion | flops 538705920 | bytes 5513728 | tf_op jit(solution)/shard_map/dot_general | solution.py:136
  98.8 1.9 %collective-permute-start.19 = (bf16[128,2048]{1,0:T(8,128)(2,1)}, bf16[128,2048]{1,0:T(8,128)(2,1)}, u32[]{:S(2)}, u32[]{:S(2)}) collective-permute-start(bf16[128,2048]{1,0:T(8,128)(2,1)} %fusion.6), channel_id=1, source_target_pairs={{8,0},{16,8},{24,16},{9,1},{17,9},{25,17},{10,2},{18,10},{26,18},{... | collective-permute-start | bytes 1572872 | tf_op jit(solution)/shard_map/ppermute | solution.py:8
  101.1 8.5 %collective-permute-done.19 = bf16[128,2048]{1,0:T(8,128)(2,1)} collective-permute-done((bf16[128,2048]{1,0:T(8,128)(2,1)}, bf16[128,2048]{1,0:T(8,128)(2,1)}, u32[]{:S(2)}, u32[]{:S(2)}) %collective-permute-start.19) | collective-permute-done | bytes 524320 | tf_op jit(solution)/shard_map/ppermute | solution.py:8
  109.6 2.0 %multiply_convert_fusion.2 = (bf16[128,512]{1,0:T(8,128)(2,1)S(1)}, f32[128]{0:T(128)S(1)}, bf16[128,512]{1,0:T(8,128)(2,1)S(1)}) fusion(f32[128,512]{1,0:T(8,128)S(1)} %get-tuple-element.3, bf16[128,512]{1,0:T(8,128)(2,1)S(1)} %get-tuple-element.8, f32[128,1024]{1,0:T(8,128)} %copy-done.3, f32[128]{0:T(128)S(1)} %fusion.21, ...), kind=kOutput, calls=%fused_computation.73 | convolution fusion | flops 269221760 | bytes 3539968 | tf_op jit(solution)/shard_map/dot_general | solution.py:129
  112.2 2.7 %collective-permute-start.26 = (bf16[128,640]{1,0:T(8,128)(2,1)S(1)}, bf16[128,640]{1,0:T(8,128)(2,1)S(1)}, u32[]{:S(2)}, u32[]{:S(2)}) collective-permute-start(bf16[128,640]{1,0:T(8,128)(2,1)S(1)} %convolution_convert_fusion.1), channel_id=1, source_target_pairs={{0,6},{1,7},{2,0},{3,1},{4,2},{5,3},{6,4},{7,5},{8,14},{9,15},{10,... | collective-permute-start | bytes 491528 | tf_op jit(solution)/shard_map/ppermute | solution.py:8
  115.6 1.3 collective-permute-start.24
  117.5 4.9 %fusion.9 = bf16[1,128,2048]{2,1,0:T(8,128)(2,1)} fusion(bf16[2048,1024]{1,0:T(8,128)(2,1)} %maximum_dynamic-update-slice_fusion.7, bf16[128,2048]{1,0:T(8,128)(2,1)} %collective-permute-done.19, bf16[128,2048]{1,0:T(8,128)(2,1)} %fusion.6, bf16[128,2048]{1,0:T(8,128)(2,1)S(1)} %copy-done.8, bf16[128,2048]{1,0:T(8,128)(2,1)S(1)} %copy-done.6, ...), kind=kOutput, calls=%fused_computation.14 | convolution fusion | flops 539492352 | bytes 7086595 | tf_op jit(solution)/shard_map/dot_general | solution.py:136
  122.7 2.9 %collective-permute-done.25 = bf16[128,640]{1,0:T(8,128)(2,1)S(1)} collective-permute-done((bf16[128,640]{1,0:T(8,128)(2,1)S(1)}, bf16[128,640]{1,0:T(8,128)(2,1)S(1)}, u32[]{:S(2)}, u32[]{:S(2)}) %collective-permute-start.25) | collective-permute-done | bytes 163872 | tf_op jit(solution)/shard_map/ppermute | solution.py:8
  125.8 6.4 %collective-permute-done.20 = bf16[256,1408]{1,0:T(8,128)(2,1)S(1)} collective-permute-done((bf16[256,1408]{1,0:T(8,128)(2,1)S(1)}, bf16[256,1408]{1,0:T(8,128)(2,1)S(1)}, u32[]{:S(2)}, u32[]{:S(2)}) %collective-permute-start.20) | collective-permute-done | bytes 720928 | tf_op jit(solution)/shard_map/ppermute | solution.py:8
  132.7 2.0 %collective-permute-start.23 = (bf16[64,1408]{1,0:T(8,128)(2,1)S(1)}, bf16[64,1408]{1,0:T(8,128)(2,1)S(1)}, u32[]{:S(2)}, u32[]{:S(2)}) collective-permute-start(bf16[64,1408]{1,0:T(8,128)(2,1)S(1)} %get-tuple-element.10), channel_id=1, source_target_pairs={{0,6},{1,7},{2,0},{3,1},{4,2},{5,3},{6,4},{7,5},{8,14},{9,15},{10,... | collective-permute-start | bytes 540680 | tf_op jit(solution)/shard_map/ppermute | solution.py:8
  135.5 5.0 %collective-permute-done.23 = bf16[64,1408]{1,0:T(8,128)(2,1)S(1)} collective-permute-done((bf16[64,1408]{1,0:T(8,128)(2,1)S(1)}, bf16[64,1408]{1,0:T(8,128)(2,1)S(1)}, u32[]{:S(2)}, u32[]{:S(2)}) %collective-permute-start.23) | collective-permute-done | bytes 180256 | tf_op jit(solution)/shard_map/ppermute | solution.py:8
  140.5 7.0 %collective-permute-done.22 = bf16[64,1408]{1,0:T(8,128)(2,1)S(1)} collective-permute-done((bf16[64,1408]{1,0:T(8,128)(2,1)S(1)}, bf16[64,1408]{1,0:T(8,128)(2,1)S(1)}, u32[]{:S(2)}, u32[]{:S(2)}) %collective-permute-start.22) | collective-permute-done | bytes 180256 | tf_op jit(solution)/shard_map/ppermute | solution.py:8
  (112 shorter events, 27.1 us)
Async XLA Ops:
  0.6 62.2 %copy-start = (bf16[1,512,2048]{2,1,0:T(8,128)(2,1)S(1)}, bf16[1,512,2048]{2,1,0:T(8,128)(2,1)}, u32[]{:S(2)}) copy-start(bf16[1,512,2048]{2,1,0:T(8,128)(2,1)} %param.18) | copy-start | bytes 6291460
  0.8 21.7 %copy-start.11 = (bf16[1,2048]{1,0:T(2,128)(2,1)S(1)}, bf16[1,2048]{1,0:T(2,128)(2,1)}, u32[]{:S(2)}) copy-start(bf16[1,2048]{1,0:T(2,128)(2,1)} %param.19) | copy-start | bytes 12292
  0.8 5.1 %collective-permute-start = (bf16[128,512]{1,0:T(8,128)(2,1)}, bf16[128,512]{1,0:T(8,128)(2,1)S(1)}, u32[]{:S(2)}, u32[]{:S(2)}) collective-permute-start(bf16[128,512]{1,0:T(8,128)(2,1)} %param.15), channel_id=1, source_target_pairs={{0,8},{16,24},{1,9},{17,25},{2,10},{18,26},{3,11},{19,27},{4,12},{... | collective-permute-start | bytes 393224 | tf_op jit(solution)/shard_map/ppermute | solution.py:8
  2.2 20.4 %collective-permute-start.4 = (bf16[256,512]{1,0:T(8,128)(2,1)}, bf16[256,512]{1,0:T(8,128)(2,1)}, u32[]{:S(2)}, u32[]{:S(2)}) collective-permute-start(bf16[256,512]{1,0:T(8,128)(2,1)} %bitcast.59), channel_id=1, source_target_pairs={{0,2},{2,4},{4,6},{6,7},{7,5},{5,3},{3,1},{1,0},{8,10},{10,12},{12... | collective-permute-start | bytes 786440 | tf_op jit(solution)/shard_map/ppermute | solution.py:8
  4.4 19.2 %collective-permute-start.3 = (bf16[256,512]{1,0:T(8,128)(2,1)}, bf16[256,512]{1,0:T(8,128)(2,1)}, u32[]{:S(2)}, u32[]{:S(2)}) collective-permute-start(bf16[256,512]{1,0:T(8,128)(2,1)} %bitcast.62), channel_id=1, source_target_pairs={{0,2},{2,4},{4,6},{6,7},{7,5},{5,3},{3,1},{1,0},{8,10},{10,12},{12... | collective-permute-start | bytes 786440 | tf_op jit(solution)/shard_map/ppermute | solution.py:8
  5.7 21.1 %collective-permute-start.6 = (bf16[256,512]{1,0:T(8,128)(2,1)}, bf16[256,512]{1,0:T(8,128)(2,1)}, u32[]{:S(2)}, u32[]{:S(2)}) collective-permute-start(bf16[256,512]{1,0:T(8,128)(2,1)} %bitcast.60), channel_id=1, source_target_pairs={{2,0},{4,2},{6,4},{7,6},{5,7},{3,5},{1,3},{0,1},{10,8},{12,10},{14... | collective-permute-start | bytes 786440 | tf_op jit(solution)/shard_map/ppermute | solution.py:8
  5.8 22.2 %collective-permute-start.5 = (bf16[256,512]{1,0:T(8,128)(2,1)}, bf16[256,512]{1,0:T(8,128)(2,1)}, u32[]{:S(2)}, u32[]{:S(2)}) collective-permute-start(bf16[256,512]{1,0:T(8,128)(2,1)} %bitcast.63), channel_id=1, source_target_pairs={{2,0},{4,2},{6,4},{7,6},{5,7},{3,5},{1,3},{0,1},{10,8},{12,10},{14... | collective-permute-start | bytes 786440 | tf_op jit(solution)/shard_map/ppermute | solution.py:8
  6.8 23.5 %copy-start.4 = (bf16[128,512]{1,0:T(8,128)(2,1)S(1)}, bf16[128,512]{1,0:T(8,128)(2,1)}, u32[]{:S(2)}) copy-start(bf16[128,512]{1,0:T(8,128)(2,1)} %param.15) | copy-start | bytes 393220
  6.8 23.3 %collective-permute-start.1 = (bf16[128,1024]{1,0:T(8,128)(2,1)S(1)}, bf16[128,1024]{1,0:T(8,128)(2,1)S(1)}, u32[]{:S(2)}, u32[]{:S(2)}) collective-permute-start(bf16[128,1024]{1,0:T(8,128)(2,1)S(1)} %pad_maximum_fusion), channel_id=1, source_target_pairs={{8,24},{9,25},{10,26},{11,27},{12,28},{13,29},{14,30},{15,31}} | collective-permute-start | bytes 786440 | tf_op jit(solution)/shard_map/ppermute | solution.py:8
  22.6 19.8 %collective-permute-start.2 = (bf16[128,2048]{1,0:T(8,128)(2,1)}, bf16[128,2048]{1,0:T(8,128)(2,1)S(1)}, u32[]{:S(2)}, u32[]{:S(2)}) collective-permute-start(bf16[128,2048]{1,0:T(8,128)(2,1)} %bitcast.65), channel_id=1, source_target_pairs={{0,24},{8,16},{16,8},{24,0},{1,25},{9,17},{17,9},{25,1},{2,26},{10... | collective-permute-start | bytes 1572872 | tf_op jit(solution)/shard_map/ppermute | solution.py:8
  23.6 8.5 %collective-permute-start.8 = (bf16[256,512]{1,0:T(8,128)(2,1)}, bf16[256,512]{1,0:T(8,128)(2,1)S(1)}, u32[]{:S(2)}, u32[]{:S(2)}) collective-permute-start(bf16[256,512]{1,0:T(8,128)(2,1)} %collective-permute-done.4), channel_id=1, source_target_pairs={{0,2},{2,4},{4,6},{6,7},{7,5},{5,3},{3,1},{1,0},{8,10},{10,12},{12... | collective-permute-start | bytes 786440 | tf_op jit(solution)/shard_map/ppermute | solution.py:8
  26.8 10.9 %collective-permute-start.7 = (bf16[256,512]{1,0:T(8,128)(2,1)}, bf16[256,512]{1,0:T(8,128)(2,1)S(1)}, u32[]{:S(2)}, u32[]{:S(2)}) collective-permute-start(bf16[256,512]{1,0:T(8,128)(2,1)} %collective-permute-done.3), channel_id=1, source_target_pairs={{0,2},{2,4},{4,6},{6,7},{7,5},{5,3},{3,1},{1,0},{8,10},{10,12},{12... | collective-permute-start | bytes 786440 | tf_op jit(solution)/shard_map/ppermute | solution.py:8
  28.1 10.9 %collective-permute-start.10 = (bf16[256,512]{1,0:T(8,128)(2,1)}, bf16[256,512]{1,0:T(8,128)(2,1)S(1)}, u32[]{:S(2)}, u32[]{:S(2)}) collective-permute-start(bf16[256,512]{1,0:T(8,128)(2,1)} %collective-permute-done.6), channel_id=1, source_target_pairs={{2,0},{4,2},{6,4},{7,6},{5,7},{3,5},{1,3},{0,1},{10,8},{12,10},{14... | collective-permute-start | bytes 786440 | tf_op jit(solution)/shard_map/ppermute | solution.py:8
  30.1 12.1 %collective-permute-start.9 = (bf16[256,512]{1,0:T(8,128)(2,1)}, bf16[256,512]{1,0:T(8,128)(2,1)S(1)}, u32[]{:S(2)}, u32[]{:S(2)}) collective-permute-start(bf16[256,512]{1,0:T(8,128)(2,1)} %collective-permute-done.5), channel_id=1, source_target_pairs={{2,0},{4,2},{6,4},{7,6},{5,7},{3,5},{1,3},{0,1},{10,8},{12,10},{14... | collective-permute-start | bytes 786440 | tf_op jit(solution)/shard_map/ppermute | solution.py:8
  32.1 18.5 %collective-permute-start.12 = (bf16[256,512]{1,0:T(8,128)(2,1)S(1)}, bf16[256,512]{1,0:T(8,128)(2,1)S(1)}, u32[]{:S(2)}, u32[]{:S(2)}) collective-permute-start(bf16[256,512]{1,0:T(8,128)(2,1)S(1)} %collective-permute-done.8), channel_id=1, source_target_pairs={{0,2},{2,4},{4,6},{6,7},{7,5},{5,3},{3,1},{1,0},{8,10},{10,12},{12... | collective-permute-start | bytes 786440 | tf_op jit(solution)/shard_map/ppermute | solution.py:8
  37.7 10.6 %collective-permute-start.11 = (bf16[256,512]{1,0:T(8,128)(2,1)S(1)}, bf16[256,512]{1,0:T(8,128)(2,1)S(1)}, u32[]{:S(2)}, u32[]{:S(2)}) collective-permute-start(bf16[256,512]{1,0:T(8,128)(2,1)S(1)} %collective-permute-done.7), channel_id=1, source_target_pairs={{0,2},{2,4},{4,6},{6,7},{7,5},{5,3},{3,1},{1,0},{8,10},{10,12},{12... | collective-permute-start | bytes 786440 | tf_op jit(solution)/shard_map/ppermute | solution.py:8
  39.0 8.9 %collective-permute-start.14 = (bf16[256,512]{1,0:T(8,128)(2,1)S(1)}, bf16[256,512]{1,0:T(8,128)(2,1)S(1)}, u32[]{:S(2)}, u32[]{:S(2)}) collective-permute-start(bf16[256,512]{1,0:T(8,128)(2,1)S(1)} %collective-permute-done.10), channel_id=1, source_target_pairs={{2,0},{4,2},{6,4},{7,6},{5,7},{3,5},{1,3},{0,1},{10,8},{12,10},{14... | collective-permute-start | bytes 786440 | tf_op jit(solution)/shard_map/ppermute | solution.py:8
  42.2 11.2 %collective-permute-start.13 = (bf16[256,512]{1,0:T(8,128)(2,1)S(1)}, bf16[256,512]{1,0:T(8,128)(2,1)S(1)}, u32[]{:S(2)}, u32[]{:S(2)}) collective-permute-start(bf16[256,512]{1,0:T(8,128)(2,1)S(1)} %collective-permute-done.9), channel_id=1, source_target_pairs={{2,0},{4,2},{6,4},{7,6},{5,7},{3,5},{1,3},{0,1},{10,8},{12,10},{14... | collective-permute-start | bytes 786440 | tf_op jit(solution)/shard_map/ppermute | solution.py:8
  47.8 11.2 %collective-permute-start.16 = (bf16[256,512]{1,0:T(8,128)(2,1)S(1)}, bf16[256,512]{1,0:T(8,128)(2,1)S(1)}, u32[]{:S(2)}, u32[]{:S(2)}) collective-permute-start(bf16[256,512]{1,0:T(8,128)(2,1)S(1)} %collective-permute-done.14), channel_id=1, source_target_pairs={{2,0},{4,2},{6,4},{7,6},{5,7},{3,5},{1,3},{0,1},{10,8},{12,10},{14... | collective-permute-start | bytes 786440 | tf_op jit(solution)/shard_map/ppermute | solution.py:8
  48.3 10.8 %collective-permute-start.15 = (bf16[256,512]{1,0:T(8,128)(2,1)S(1)}, bf16[256,512]{1,0:T(8,128)(2,1)S(1)}, u32[]{:S(2)}, u32[]{:S(2)}) collective-permute-start(bf16[256,512]{1,0:T(8,128)(2,1)S(1)} %collective-permute-done.11), channel_id=1, source_target_pairs={{0,2},{2,4},{4,6},{6,7},{7,5},{5,3},{3,1},{1,0},{8,10},{10,12},{12... | collective-permute-start | bytes 786440 | tf_op jit(solution)/shard_map/ppermute | solution.py:8
  62.9 30.5 %copy-start.3 = (f32[128,1024]{1,0:T(8,128)}, f32[128,1024]{1,0:T(8,128)S(1)}, u32[]{:S(2)}) copy-start(f32[128,1024]{1,0:T(8,128)S(1)} %convolution_bitcast_fusion) | copy-start | bytes 1572868
  67.6 10.5 %collective-permute-start.17 = (bf16[128,2048]{1,0:T(8,128)(2,1)S(1)}, bf16[128,2048]{1,0:T(8,128)(2,1)S(1)}, u32[]{:S(2)}, u32[]{:S(2)}) collective-permute-start(bf16[128,2048]{1,0:T(8,128)(2,1)S(1)} %fusion.4), channel_id=1, source_target_pairs={{8,0},{16,8},{24,16},{9,1},{17,9},{25,17},{10,2},{18,10},{26,18},{... | collective-permute-start | bytes 1572872 | tf_op jit(solution)/shard_map/ppermute | solution.py:8
  82.9 10.5 %collective-permute-start.18 = (bf16[128,2048]{1,0:T(8,128)(2,1)S(1)}, bf16[128,2048]{1,0:T(8,128)(2,1)S(1)}, u32[]{:S(2)}, u32[]{:S(2)}) collective-permute-start(bf16[128,2048]{1,0:T(8,128)(2,1)S(1)} %fusion.5), channel_id=1, source_target_pairs={{8,0},{16,8},{24,16},{9,1},{17,9},{25,17},{10,2},{18,10},{26,18},{... | collective-permute-start | bytes 1572872 | tf_op jit(solution)/shard_map/ppermute | solution.py:8
  98.8 10.8 %collective-permute-start.19 = (bf16[128,2048]{1,0:T(8,128)(2,1)}, bf16[128,2048]{1,0:T(8,128)(2,1)}, u32[]{:S(2)}, u32[]{:S(2)}) collective-permute-start(bf16[128,2048]{1,0:T(8,128)(2,1)} %fusion.6), channel_id=1, source_target_pairs={{8,0},{16,8},{24,16},{9,1},{17,9},{25,17},{10,2},{18,10},{26,18},{... | collective-permute-start | bytes 1572872 | tf_op jit(solution)/shard_map/ppermute | solution.py:8
  112.2 10.4 %collective-permute-start.26 = (bf16[128,640]{1,0:T(8,128)(2,1)S(1)}, bf16[128,640]{1,0:T(8,128)(2,1)S(1)}, u32[]{:S(2)}, u32[]{:S(2)}) collective-permute-start(bf16[128,640]{1,0:T(8,128)(2,1)S(1)} %convolution_convert_fusion.1), channel_id=1, source_target_pairs={{0,6},{1,7},{2,0},{3,1},{4,2},{5,3},{6,4},{7,5},{8,14},{9,15},{10,... | collective-permute-start | bytes 491528 | tf_op jit(solution)/shard_map/ppermute | solution.py:8
  115.2 10.4 %collective-permute-start.25 = (bf16[128,640]{1,0:T(8,128)(2,1)S(1)}, bf16[128,640]{1,0:T(8,128)(2,1)S(1)}, u32[]{:S(2)}, u32[]{:S(2)}) collective-permute-start(bf16[128,640]{1,0:T(8,128)(2,1)S(1)} %convolution_convert_fusion.2), channel_id=1, source_target_pairs={{0,4},{1,5},{2,6},{3,7},{4,0},{5,1},{6,2},{7,3},{8,12},{9,13},{10,... | collective-permute-start | bytes 491528 | tf_op jit(solution)/shard_map/ppermute | solution.py:8
  115.6 10.0 %collective-permute-start.24 = (bf16[128,640]{1,0:T(8,128)(2,1)S(1)}, bf16[128,640]{1,0:T(8,128)(2,1)S(1)}, u32[]{:S(2)}, u32[]{:S(2)}) collective-permute-start(bf16[128,640]{1,0:T(8,128)(2,1)S(1)} %convolution_convert_fusion.3), channel_id=1, source_target_pairs={{0,2},{1,3},{2,4},{3,5},{4,6},{5,7},{6,0},{7,1},{8,10},{9,11},{10,... | collective-permute-start | bytes 491528 | tf_op jit(solution)/shard_map/ppermute | solution.py:8
  117.4 14.8 %collective-permute-start.20 = (bf16[256,1408]{1,0:T(8,128)(2,1)S(1)}, bf16[256,1408]{1,0:T(8,128)(2,1)S(1)}, u32[]{:S(2)}, u32[]{:S(2)}) collective-permute-start(bf16[256,1408]{1,0:T(8,128)(2,1)S(1)} %convolution_convert_fusion), channel_id=1, source_target_pairs={{0,1},{1,0},{2,3},{3,2},{4,5},{5,4},{6,7},{7,6},{8,9},{9,8},{10,11... | collective-permute-start | bytes 2162696 | tf_op jit(solution)/shard_map/ppermute | solution.py:8
  125.7 9.7 %collective-permute-start.27 = (bf16[64,640]{1,0:T(8,128)(2,1)S(1)}, bf16[64,640]{1,0:T(8,128)(2,1)S(1)}, u32[]{:S(2)}, u32[]{:S(2)}) collective-permute-start(bf16[64,640]{1,0:T(8,128)(2,1)S(1)} %slice.93), channel_id=1, source_target_pairs={{0,1},{1,0},{2,3},{3,2},{4,5},{5,4},{6,7},{7,6},{8,9},{9,8},{10,11... | collective-permute-start | bytes 245768 | tf_op jit(solution)/shard_map/ppermute | solution.py:8
  132.7 7.8 %collective-permute-start.23 = (bf16[64,1408]{1,0:T(8,128)(2,1)S(1)}, bf16[64,1408]{1,0:T(8,128)(2,1)S(1)}, u32[]{:S(2)}, u32[]{:S(2)}) collective-permute-start(bf16[64,1408]{1,0:T(8,128)(2,1)S(1)} %get-tuple-element.10), channel_id=1, source_target_pairs={{0,6},{1,7},{2,0},{3,1},{4,2},{5,3},{6,4},{7,5},{8,14},{9,15},{10,... | collective-permute-start | bytes 540680 | tf_op jit(solution)/shard_map/ppermute | solution.py:8
  134.7 12.7 %collective-permute-start.22 = (bf16[64,1408]{1,0:T(8,128)(2,1)S(1)}, bf16[64,1408]{1,0:T(8,128)(2,1)S(1)}, u32[]{:S(2)}, u32[]{:S(2)}) collective-permute-start(bf16[64,1408]{1,0:T(8,128)(2,1)S(1)} %get-tuple-element.11), channel_id=1, source_target_pairs={{0,4},{1,5},{2,6},{3,7},{4,0},{5,1},{6,2},{7,3},{8,12},{9,13},{10,... | collective-permute-start | bytes 540680 | tf_op jit(solution)/shard_map/ppermute | solution.py:8
  135.5 12.0 %collective-permute-start.21 = (bf16[64,1408]{1,0:T(8,128)(2,1)S(1)}, bf16[64,1408]{1,0:T(8,128)(2,1)S(1)}, u32[]{:S(2)}, u32[]{:S(2)}) collective-permute-start(bf16[64,1408]{1,0:T(8,128)(2,1)S(1)} %get-tuple-element.9), channel_id=1, source_target_pairs={{0,2},{1,3},{2,4},{3,5},{4,6},{5,7},{6,0},{7,1},{8,10},{9,11},{10,... | collective-permute-start | bytes 540680 | tf_op jit(solution)/shard_map/ppermute | solution.py:8
  (15 other events, 217.5 us)

commit v2 on v1

v2 whole, which is shorter than its diff:
```python
import functools

import jax
import jax.numpy as jnp
from jax import lax
from jax.experimental import pallas as pl
from jax.experimental.pallas import tpu as pltpu
from jax.sharding import PartitionSpec as P

F32, BF16 = jnp.float32, jnp.bfloat16
PLAIN = (((1,), (0,)), ((), ()))
TURNED = (((1,), (1,)), ((), ()))
VMEM = pl.BlockSpec(memory_space=pltpu.VMEM)
LIMIT = 16 * 2**20


def dot(left, right, dims):
    return lax.dot_general(left, right, dims, preferred_element_type=F32)


def params():
    return pltpu.CompilerParams(vmem_limit_bytes=LIMIT)


def cost(macs, *arrays):
    moved = sum(a.size * a.dtype.itemsize for a in arrays)
    return pl.CostEstimate(flops=2 * macs, bytes_accessed=moved, transcendentals=0)


def ring_place(index, size):
    return jnp.where(index % 2 == 0, index // 2, size - 1 - index // 2)


def ring_member(place, size):
    return jnp.where(place < (size + 1) // 2, 2 * place, 2 * (size - 1 - place) + 1)


def ring_pairs(size):
    order = list(range(0, size, 2)) + list(range(1, size, 2))[::-1]
    ahead = [(order[i], order[(i + 1) % size]) for i in range(size)]
    return ahead, [(b, a) for a, b in ahead]


def gather_ring(arrays, axis):
    size = lax.axis_size(axis)
    ahead, back = ring_pairs(size)
    pieces, offsets = [list(arrays)], [0]
    from_back, from_ahead = list(arrays), list(arrays)
    for step in range(1, (size - 1) // 2 + 1):
        from_back = [lax.ppermute(v, axis, ahead) for v in from_back]
        from_ahead = [lax.ppermute(v, axis, back) for v in from_ahead]
        pieces += [from_back, from_ahead]
        offsets += [-step, step]
    if size % 2 == 0:
        pieces.append(
            [lax.ppermute(from_back[0], axis, ahead), lax.ppermute(from_ahead[1], axis, back)]
        )
        offsets.append(size // 2)
    return pieces, offsets


def gather_to_ends(x, axis):
    size = lax.axis_size(axis)
    steps = [1 << place for place in range(size.bit_length() - 1)]
    needed = [{0, size - 1}]
    for stride in steps[::-1]:
        needed.append(needed[-1] | {i ^ stride for i in needed[-1]})
    held = [x]
    for stride, wanted in zip(steps, needed[-2::-1]):
        pairs = [(i ^ stride, i) for i in sorted(wanted)]
        held = held + [lax.ppermute(v, axis, pairs) for v in held]
    return held


def after(values, *others):
    return lax.optimization_barrier((values, others))[0]


def piece_columns(offset, axis, depth):
    if offset is None:
        return slice(0, depth)
    size = lax.axis_size(axis)
    place = (ring_place(lax.axis_index(axis), size) + (offset + size)) % size
    return pl.ds(pl.multiple_of(ring_member(place, size) * depth, depth), depth)


def push_back(grad_ref, back_proj, scales, gate_vector, pieces, columns, out_ref):
    gate_scale, up_scale, logit_scale = scales
    logit = jnp.sum(back_proj * logit_scale[...], axis=1, keepdims=True)
    gate_grad = (back_proj * gate_scale[...]).astype(BF16)
    up_grad = (back_proj * up_scale[...]).astype(BF16)
    for where, (gate, up) in zip(columns, pieces):
        through = dot(gate_grad, gate[...], TURNED) + dot(up_grad, up[...], TURNED)
        out_ref[:, where] = (
            grad_ref[:, where].astype(F32) + through + logit * gate_vector[:, where].astype(F32)
        ).astype(BF16)


def pair_up(refs):
    return [refs[i : i + 2] for i in range(0, len(refs), 2)]


def prepare_kernel(rows, gate_vector, down, *rest):
    blocks, (seeded, score, back_proj) = rest[:-3], rest[-3:]
    sections = lax.axis_size("section")
    is_last = lax.axis_index("section") == sections - 1
    width = blocks[0].shape[1]

    def lay(order):
        for place, block in enumerate(order):
            seeded[:, place * width : (place + 1) * width] = block[...]

    pl.when(is_last)(lambda: lay(blocks[::-1]))
    pl.when(jnp.logical_not(is_last))(lambda: lay(blocks))
    logit = jnp.sum(
        rows[...].astype(F32) * gate_vector[...].astype(F32), axis=1, keepdims=True
    )
    score[...] = jax.nn.sigmoid(logit)
    back_proj[...] = dot(seeded[...], down[...], TURNED)


def first_kernel(offsets, rows, score, back_proj, grad, gate_vector, *rest):
    pieces = pair_up(rest[: 2 * len(offsets)])
    out, gate_scale, up_scale, logit_scale, scored = rest[2 * len(offsets) :]
    depth = pieces[0][0].shape[0]
    columns = [piece_columns(offset, "dp", depth) for offset in offsets]
    gate_pre = up_pre = 0.0
    for where, (gate, up) in zip(columns, pieces):
        block = rows[:, where]
        gate_pre += dot(block, gate[...], PLAIN)
        up_pre += dot(block, up[...], PLAIN)
    gate_sig = jax.nn.sigmoid(gate_pre)
    activated = gate_pre * gate_sig
    hidden = (activated * up_pre).astype(BF16).astype(F32)
    share = score[...]
    gate_scale[...] = share * up_pre * gate_sig * (1.0 + gate_pre * (1.0 - gate_sig))
    up_scale[...] = share * activated
    logit_scale[...] = hidden * (share * (1.0 - share))
    scored[...] = (hidden * share).astype(BF16)
    scales = gate_scale, up_scale, logit_scale
    push_back(grad, back_proj[...], scales, gate_vector, pieces, columns, out)


def tick_kernel(offsets, section, grad, held, down, gate_vector, a, b, c, *rest):
    pieces, out = pair_up(rest[:-1]), rest[-1]

    here = lax.axis_index("section") == section

    @pl.when(jnp.logical_not(here))
    def _():
        out[...] = held[...]

    @pl.when(here)
    def _():
        depth = pieces[0][0].shape[0]
        columns = [piece_columns(offset, "dp", depth) for offset in offsets]
        back_proj = dot(grad[...], down[...], TURNED)
        push_back(grad, back_proj, (a, b, c), gate_vector, pieces, columns, out)


def products_kernel(inner, cut, scored, grad, first_grad, keep_a, keep_b, send_a, *rest):
    send_b, turned = rest[:-1], rest[-1]
    size = lax.axis_size("dp")
    outer = size // inner
    units = scored.shape[1] // size
    me = lax.axis_index("dp")
    turned[...] = scored[...].T

    def block(k, j):
        place = (me // inner + k) % outer * inner + (me + j) % inner
        return turned[pl.ds(pl.multiple_of(place * units, units), units), :]

    def work(source):
        for k in range(outer):
            rows = slice(k * units, (k + 1) * units)
            send_a[rows, :] = dot(block(k, 1), source[:, :cut], PLAIN).astype(BF16)
            keep_a[rows, :] = dot(block(k, 0), source[:, :cut], PLAIN)
            for j in range(inner):
                rows = slice(j * units, (j + 1) * units)
                found = dot(block(k, j), source[:, cut:], PLAIN)
                if k == 0:
                    keep_b[rows, :] = found
                else:
                    send_b[k - 1][rows, :] = found.astype(BF16)

    is_first = lax.axis_index("section") == 0
    pl.when(is_first)(lambda: work(first_grad))
    pl.when(jnp.logical_not(is_first))(lambda: work(grad))


def reduce_rows(scored, grad, first_grad, axis):
    size = lax.axis_size(axis)
    inner = 2
    outer = size // inner
    tokens, hidden_units = scored.shape
    units = hidden_units // size
    width = grad.shape[1]
    cut = width * 11 // 16 // 128 * 128
    swap = [(i, i ^ 1) for i in range(size)]

    def turn(k):
        return [(i, (i + k * inner) % size) for i in range(size)]

    shape = jax.ShapeDtypeStruct
    keep_a, sum_b, send_a, *send_b = pl.pallas_call(
        functools.partial(products_kernel, inner, cut),
        out_shape=[
            shape((outer * units, cut), F32),
            shape((inner * units, width - cut), F32),
            shape((outer * units, cut), BF16),
        ]
        + [shape((inner * units, width - cut), BF16)] * (outer - 1),
        in_specs=[VMEM] * 3,
        out_specs=[VMEM] * (outer + 2),
        scratch_shapes=[pltpu.VMEM((hidden_units, tokens), BF16)],
        compiler_params=params(),
        cost_estimate=cost(tokens * hidden_units * width, scored, grad),
        name="products",
    )(scored, grad, first_grad)
    sum_a = keep_a + lax.ppermute(send_a, axis, swap).astype(F32)
    for k in range(1, outer):
        sum_b += lax.ppermute(send_b[k - 1], axis, turn(k)).astype(F32)
    total_a = sum_a[:units]
    for k in range(1, outer):
        send = sum_a[k * units : (k + 1) * units].astype(BF16)
        total_a += lax.ppermute(send, axis, turn(k)).astype(F32)
    got_b = lax.ppermute(sum_b[units:].astype(BF16), axis, swap)
    total_b = sum_b[:units] + got_b.astype(F32)
    return jnp.concatenate([total_a, total_b], axis=1)


def on_device(stash, cotangent, gate_weight, up_weight, down_weight, shared_gate):
    sections = lax.axis_size("section")
    replicas = lax.axis_size("dp")
    local_rows, model_width = stash.shape[1:]
    depth = gate_weight.shape[1]
    down_full = down_weight[0]
    hidden_units = down_full.shape[0]

    pieces, offsets = gather_ring([gate_weight[0], up_weight[0]], "dp")
    stash, cotangent = after((stash, cotangent), pieces[min(1, len(pieces) - 1)])
    own_rows = lax.ppermute(stash[0], "section", [(i, sections - 1 - i) for i in range(sections)])
    blocks = gather_to_ends(cotangent, "section")
    shape = jax.ShapeDtypeStruct
    small = shape((local_rows, hidden_units), F32)
    seeded, score, back_proj = pl.pallas_call(
        prepare_kernel,
        out_shape=[shape((local_rows, model_width), BF16), shape((local_rows, 1), F32), small],
        in_specs=[VMEM] * (3 + len(blocks)),
        out_specs=[VMEM] * 3,
        compiler_params=params(),
        cost_estimate=cost(local_rows * model_width * hidden_units, down_full, own_rows),
        name="prepare",
    )(own_rows, shared_gate, down_full, *blocks)

    if depth % 128:
        size = replicas
        place = ring_place(lax.axis_index("dp"), size)
        joined = [jnp.zeros((depth * replicas, hidden_units), BF16)] * 2
        for offset, piece in zip(offsets, pieces):
            start = ring_member((place + offset + size) % size, size) * depth
            joined = [lax.dynamic_update_slice(j, p, (start, 0)) for j, p in zip(joined, piece)]
        pieces, offsets = [joined], [None]
    flat = [v for piece in pieces for v in piece]

    outgoing, *scales, scored = pl.pallas_call(
        functools.partial(first_kernel, offsets),
        out_shape=[
            shape((local_rows, model_width), BF16),
            small,
            small,
            small,
            shape((local_rows, hidden_units), BF16),
        ],
        in_specs=[VMEM] * (5 + len(flat)),
        out_specs=[VMEM] * 5,
        compiler_params=params(),
        cost_estimate=cost(4 * local_rows * model_width * hidden_units, *flat),
        name="first_tick",
    )(own_rows, score, back_proj, seeded, shared_gate, *flat)
    scored = lax.ppermute(scored, "section", [(i, (i + 1) % sections) for i in range(sections)])

    def tick(section, grad, held):
        return pl.pallas_call(
            functools.partial(tick_kernel, offsets, section),
            out_shape=shape((local_rows, model_width), BF16),
            in_specs=[VMEM] * (7 + len(flat)),
            out_specs=VMEM,
            compiler_params=params(),
            cost_estimate=cost(3 * local_rows * model_width * hidden_units, *flat),
            name="tick",
        )(grad, held, down_full, shared_gate, *scales, *flat)

    for section in range(sections - 2, -1, -1):
        if section == 0:
            summed = reduce_rows(scored, outgoing, seeded, "dp")
        grad = lax.ppermute(outgoing, "section", [(section + 1, section)])
        outgoing = tick(section, grad, outgoing)

    summed = lax.ppermute(
        summed.astype(BF16), "section", [(i, (i - 1) % sections) for i in range(sections)]
    ).astype(F32)
    norm_factor = (local_rows * replicas) ** (-0.5)
    return (outgoing[None], (summed * norm_factor)[None])


def solution(mesh):
    placed = (
        P("section", "dp", None),
        P("dp", "section"),
        P("section", "dp", None),
        P("section", "dp", None),
        P("section", None, None),
        P("section", None),
    )
    return jax.shard_map(
        on_device,
        mesh=mesh,
        in_specs=placed,
        out_specs=(P("section", "dp", None), P("section", "dp", None)),
        check_vma=False,
    )
```

time: 149 us -> 108 us (0.72)
  matrix products: 27 us -> 0 us
  waiting for transfers between devices: 67.1 us -> 47.8 us
  starting transfers between devices: 30 us -> 47.7 us
  other arithmetic: 11.2 us -> 1.21 us
  Pallas kernels: 0 us -> 7.09 us
  between operations: 5.84 us -> 0.88 us
  local copies, waits for them, and re-layouts: 7.19 us -> 3.26 us
    dot_general x16 -> x0, matrix products: 27 us -> none  [the longest x4 16.9 us: on_device(): lax.dot_general(pair_grad, joined, (((1,), (1,)), ((), ())), preferred_el...]
    ppermute x28 -> x31, waiting for transfers between devices: 67.1 us -> 47.8 us  [the longest x6 9.67 us: gather_ring(): from_back = [lax.ppermute(v, axis, ahead) for v in from_back]]
    ppermute x28 -> x31, starting transfers between devices: 30 us -> 47.7 us  [the longest x6 8.03 us: gather_ring(): from_back = [lax.ppermute(v, axis, ahead) for v in from_back]]
    dynamic_update_slice x8 -> x0, other arithmetic: 8.98 us -> none  [on_device(): lax.dynamic_update_slice(joined, jnp.concatenate(piece, axis=1), (owner *...]
    pallas_call x0 -> x6, Pallas kernels: none -> 7.09 us  [the longest x3 3.16 us: tick(): pl.pallas_call(functools.partial(tick_kernel, offsets, section), out_shap...]
    dynamic_slice x8 -> x0, local copies, waits for them, and re-layouts: 4.47 us -> none  [the longest x7 4.31 us: block_owner(): return table[lax.axis_index(axis)]]
    unnamed x40 -> x14, local copies, waits for them, and re-layouts: 0.14 us -> 3.21 us
    broadcast_in_dim x1 -> x0, local copies, waits for them, and re-layouts: 2.52 us -> none  [on_device(): joined = jnp.zeros((depth * replicas, 2 * hidden_units), jnp.bfloat16)]
  transfers between devices with their start and end apart: 28 -> 31, of which waited for: 14 -> 14; matrix products, arithmetic and copies ran while one was open for 16% -> 0% of each run, Pallas kernels for 0% -> 4%
where the time goes in v2:
time: 108 us
  waiting for transfers between devices  47.8 us (44%)
  starting transfers between devices  47.7 us (44%)
  Pallas kernels  7.09 us (7%)
  local copies, waits for them, and re-layouts  3.26 us (3%)
  other arithmetic  1.21 us (1%)
    ppermute x6, waiting for transfers between devices, gather_ring(): from_back = [lax.ppermute(v, axis, ahead) for v in from_back]  9.67 us
    ppermute x6, starting transfers between devices, gather_ring(): from_back = [lax.ppermute(v, axis, ahead) for v in from_back]  8.03 us
    ppermute x3, starting transfers between devices, gather_to_ends(): held = held + [lax.ppermute(v, axis, pairs) for v in held]  7.73 us
    ppermute x1, starting transfers between devices, on_device(): lax.ppermute(scored, 'section', [(i, (i + 1) % sections) for i in range(s...  7.53 us
    ppermute x3, waiting for transfers between devices, on_device(): grad = lax.ppermute(outgoing, 'section', [(section + 1, section)])  7.06 us
    ppermute x3, waiting for transfers between devices, reduce_rows(): sum_b += lax.ppermute(send_b[k - 1], axis, turn(k)).astype(F32)  7.05 us
    ppermute x3, starting transfers between devices, reduce_rows(): total_a += lax.ppermute(send, axis, turn(k)).astype(F32)  7.02 us
    ppermute x3, waiting for transfers between devices, reduce_rows(): total_a += lax.ppermute(send, axis, turn(k)).astype(F32)  6.89 us
  transfers between devices with their start and end apart: 31, of which 14 were waited for; matrix products, arithmetic and copies ran while one was open for 0% of the time, Pallas kernels for 4%

profile of v2, /device:TPU:1, one launch (start us, length us, event | category | flops | bytes accessed | tf_op | source)
XLA Modules:
  0.0 107.9 jit_solution(10694685612311884889)
XLA Ops:
  0.6 2.2 %collective-permute-start = (bf16[256,512]{1,0:T(8,128)(2,1)}, bf16[256,512]{1,0:T(8,128)(2,1)S(1)}, u32[]{:S(2)}, u32[]{:S(2)}) collective-permute-start(bf16[256,512]{1,0:T(8,128)(2,1)} %bitcast.11), channel_id=1, source_target_pairs={{0,2},{2,4},{4,6},{6,7},{7,5},{5,3},{3,1},{1,0},{8,10},{10,12},{12... | collective-permute-start | bytes 786440 | tf_op jit(solution)/shard_map/ppermute | solution.py:50
  2.8 1.5 %collective-permute-start.1 = (bf16[256,512]{1,0:T(8,128)(2,1)}, bf16[256,512]{1,0:T(8,128)(2,1)S(1)}, u32[]{:S(2)}, u32[]{:S(2)}) collective-permute-start(bf16[256,512]{1,0:T(8,128)(2,1)} %bitcast.18), channel_id=1, source_target_pairs={{0,2},{2,4},{4,6},{6,7},{7,5},{5,3},{3,1},{1,0},{8,10},{10,12},{12... | collective-permute-start | bytes 786440 | tf_op jit(solution)/shard_map/ppermute | solution.py:50
  4.3 4.7 %collective-permute-done.rest_2_ = bf16[256,512]{1,0:T(8,128)(2,1)S(1)} collective-permute-done((bf16[256,512]{1,0:T(8,128)(2,1)}, bf16[256,512]{1,0:T(8,128)(2,1)S(1)}, u32[]{:S(2)}, u32[]{:S(2)}) %collective-permute-start) | collective-permute-done | bytes 262176 | tf_op jit(solution)/shard_map/ppermute | solution.py:50
  9.0 1.2 %collective-permute-start.8 = (bf16[256,512]{1,0:T(8,128)(2,1)S(1)}, bf16[256,512]{1,0:T(8,128)(2,1)S(1)}, u32[]{:S(2)}, u32[]{:S(2)}) collective-permute-start(bf16[256,512]{1,0:T(8,128)(2,1)S(1)} %collective-permute-done.rest_2_), channel_id=1, source_target_pairs={{0,2},{2,4},{4,6},{6,7},{7,5},{5,3},{3,1},{1,0},{8,10},{10,12},{12... | collective-permute-start | bytes 786440 | tf_op jit(solution)/shard_map/ppermute | solution.py:50
  10.5 4.1 %collective-permute-done.1.rest_3_ = bf16[256,512]{1,0:T(8,128)(2,1)S(1)} collective-permute-done((bf16[256,512]{1,0:T(8,128)(2,1)}, bf16[256,512]{1,0:T(8,128)(2,1)S(1)}, u32[]{:S(2)}, u32[]{:S(2)}) %collective-permute-start.1) | collective-permute-done | bytes 262176 | tf_op jit(solution)/shard_map/ppermute | solution.py:50
  14.6 3.0 %collective-permute-start.4 = (bf16[128,512]{1,0:T(8,128)(2,1)}, bf16[128,512]{1,0:T(8,128)(2,1)S(1)}, u32[]{:S(2)}, u32[]{:S(2)}) collective-permute-start(bf16[128,512]{1,0:T(8,128)(2,1)} %rest_0_), channel_id=1, source_target_pairs={{16,0},{8,24},{17,1},{9,25},{18,2},{10,26},{19,3},{11,27},{20,4},{... | collective-permute-start | bytes 393224 | tf_op jit(solution)/shard_map/ppermute | solution.py:71
  17.6 1.3 %collective-permute-start.10 = (bf16[256,512]{1,0:T(8,128)(2,1)S(1)}, bf16[256,512]{1,0:T(8,128)(2,1)S(1)}, u32[]{:S(2)}, u32[]{:S(2)}) collective-permute-start(bf16[256,512]{1,0:T(8,128)(2,1)S(1)} %collective-permute-done.6.rest_4_), channel_id=1, source_target_pairs={{2,0},{4,2},{6,4},{7,6},{5,7},{3,5},{1,3},{0,1},{10,8},{12,10},{14... | collective-permute-start | bytes 786440 | tf_op jit(solution)/shard_map/ppermute | solution.py:51
  20.1 2.9 %collective-permute-start.2 = (bf16[128,2048]{1,0:T(8,128)(2,1)}, bf16[128,2048]{1,0:T(8,128)(2,1)S(1)}, u32[]{:S(2)}, u32[]{:S(2)}) collective-permute-start(bf16[128,2048]{1,0:T(8,128)(2,1)} %bitcast.24), channel_id=1, source_target_pairs={{0,24},{8,16},{16,8},{24,0},{1,25},{9,17},{17,9},{25,1},{2,26},{10... | collective-permute-start | bytes 1572872 | tf_op jit(solution)/shard_map/ppermute | solution.py:242
  23.0 1.8 %collective-permute-start.9 = (bf16[256,512]{1,0:T(8,128)(2,1)S(1)}, bf16[256,512]{1,0:T(8,128)(2,1)S(1)}, u32[]{:S(2)}, u32[]{:S(2)}) collective-permute-start(bf16[256,512]{1,0:T(8,128)(2,1)S(1)} %collective-permute-done.1.rest_3_), channel_id=1, source_target_pairs={{0,2},{2,4},{4,6},{6,7},{7,5},{5,3},{3,1},{1,0},{8,10},{10,12},{12... | collective-permute-start | bytes 786440 | tf_op jit(solution)/shard_map/ppermute | solution.py:50
  24.9 1.3 %collective-permute-start.12 = (bf16[256,512]{1,0:T(8,128)(2,1)S(1)}, bf16[256,512]{1,0:T(8,128)(2,1)S(1)}, u32[]{:S(2)}, u32[]{:S(2)}) collective-permute-start(bf16[256,512]{1,0:T(8,128)(2,1)S(1)} %collective-permute-done.8.rest_6_), channel_id=1, source_target_pairs={{0,2},{2,4},{4,6},{6,7},{7,5},{5,3},{3,1},{1,0},{8,10},{10,12},{12... | collective-permute-start | bytes 786440 | tf_op jit(solution)/shard_map/ppermute | solution.py:50
  26.7 3.6 %collective-permute-start.5 = (bf16[128,512]{1,0:T(8,128)(2,1)S(1)}, bf16[128,512]{1,0:T(8,128)(2,1)S(1)}, u32[]{:S(2)}, u32[]{:S(2)}) collective-permute-start(bf16[128,512]{1,0:T(8,128)(2,1)S(1)} %collective-permute-done.3.rest_1_), channel_id=1, source_target_pairs={{16,0},{8,24},{17,1},{9,25},{18,2},{10,26},{19,3},{11,27},{20,4},{... | collective-permute-start | bytes 393224 | tf_op jit(solution)/shard_map/ppermute | solution.py:71
  30.3 6.1 %collective-permute-done.5.rest_3_ = bf16[128,512]{1,0:T(8,128)(2,1)S(1)} collective-permute-done((bf16[128,512]{1,0:T(8,128)(2,1)S(1)}, bf16[128,512]{1,0:T(8,128)(2,1)S(1)}, u32[]{:S(2)}, u32[]{:S(2)}) %collective-permute-start.5) | collective-permute-done | bytes 131104 | tf_op jit(solution)/shard_map/ppermute | solution.py:71
  36.4 1.8 %collective-permute-start.14 = (bf16[256,512]{1,0:T(8,128)(2,1)S(1)}, bf16[256,512]{1,0:T(8,128)(2,1)S(1)}, u32[]{:S(2)}, u32[]{:S(2)}) collective-permute-start(bf16[256,512]{1,0:T(8,128)(2,1)S(1)} %collective-permute-done.10.rest_8_), channel_id=1, source_target_pairs={{2,0},{4,2},{6,4},{7,6},{5,7},{3,5},{1,3},{0,1},{10,8},{12,10},{14... | collective-permute-start | bytes 786440 | tf_op jit(solution)/shard_map/ppermute | solution.py:51
  38.2 1.5 %collective-permute-start.16 = (bf16[256,512]{1,0:T(8,128)(2,1)S(1)}, bf16[256,512]{1,0:T(8,128)(2,1)S(1)}, u32[]{:S(2)}, u32[]{:S(2)}) collective-permute-start(bf16[256,512]{1,0:T(8,128)(2,1)S(1)} %collective-permute-done.12.rest_10_), channel_id=1, source_target_pairs={{0,2},{2,4},{4,6},{6,7},{7,5},{5,3},{3,1},{1,0},{8,10},{10,12},{12... | collective-permute-start | bytes 786440 | tf_op jit(solution)/shard_map/ppermute | solution.py:56
  39.7 1.6 %copy-done = bf16[1,512,2048]{2,1,0:T(8,128)(2,1)S(1)} copy-done((bf16[1,512,2048]{2,1,0:T(8,128)(2,1)S(1)}, bf16[1,512,2048]{2,1,0:T(8,128)(2,1)}, u32[]{:S(2)}) %copy-start) | copy-done | bytes 2097176
  44.7 5.6 %collective-permute-done.16.rest_14_ = bf16[256,512]{1,0:T(8,128)(2,1)S(1)} collective-permute-done((bf16[256,512]{1,0:T(8,128)(2,1)S(1)}, bf16[256,512]{1,0:T(8,128)(2,1)S(1)}, u32[]{:S(2)}, u32[]{:S(2)}) %collective-permute-start.16) | collective-permute-done | bytes 262176 | tf_op jit(solution)/shard_map/ppermute | solution.py:56
  50.3 2.2 %first_tick.1 = (bf16[128,2048]{1,0:T(8,128)(2,1)S(1)}, f32[128,512]{1,0:T(8,128)S(1)}, f32[128,512]{1,0:T(8,128)S(1)}, f32[128,512]{1,0:T(8,128)S(1)}, bf16[128,512]{1,0:T(8,128)(2,1)S(1)}) custom-call(bf16[128,2048]{1,0:T(8,128)(2,1)S(1)} %collective-permute-done.2.rows, f32[128,1]{1,0:T(8,128)S(1)} %get-tuple-element.20.score, ...), custom_call_target="tpu_custom_call" | custom-call | flops 1073741824 | bytes 4194304 | tf_op jit(solution)/shard_map/first_tick/pallas_call | solution.py:266
  53.3 1.3 %collective-permute-start.19 = (bf16[128,2048]{1,0:T(8,128)(2,1)S(1)}, bf16[128,2048]{1,0:T(8,128)(2,1)S(1)}, u32[]{:S(2)}, u32[]{:S(2)}) collective-permute-start(bf16[128,2048]{1,0:T(8,128)(2,1)S(1)} %tick.3.held), channel_id=1, source_target_pairs={{16,8},{17,9},{18,10},{19,11},{20,12},{21,13},{22,14},{23,15}} | collective-permute-start | bytes 1572872 | tf_op jit(solution)/shard_map/ppermute | solution.py:297
  54.6 7.5 %collective-permute-start.21 = (bf16[128,512]{1,0:T(8,128)(2,1)S(1)}, bf16[128,512]{1,0:T(8,128)(2,1)S(1)}, u32[]{:S(2)}, u32[]{:S(2)}) collective-permute-start(bf16[128,512]{1,0:T(8,128)(2,1)S(1)} %get-tuple-element.27), channel_id=1, source_target_pairs={{0,8},{8,16},{16,24},{24,0},{1,9},{9,17},{17,25},{25,1},{2,10},{10... | collective-permute-start | bytes 393224 | tf_op jit(solution)/shard_map/ppermute | solution.py:281
  62.2 7.1 %collective-permute-done.19.grad = bf16[128,2048]{1,0:T(8,128)(2,1)S(1)} collective-permute-done((bf16[128,2048]{1,0:T(8,128)(2,1)S(1)}, bf16[128,2048]{1,0:T(8,128)(2,1)S(1)}, u32[]{:S(2)}, u32[]{:S(2)}) %collective-permute-start.19) | collective-permute-done | bytes 524320 | tf_op jit(solution)/shard_map/ppermute | solution.py:297
  69.2 2.2 %tick.4.held.grad = bf16[128,2048]{1,0:T(8,128)(2,1)S(1)} custom-call(bf16[128,2048]{1,0:T(8,128)(2,1)S(1)} %collective-permute-done.19.grad, bf16[128,2048]{1,0:T(8,128)(2,1)S(1)} %tick.3.held, bf16[512,2048]{1,0:T(8,128)(2,1)S(1)} %bitcast.9, bf16[1,2048]{1,0:T(2,128)(2,1)S(1)} %copy-done.4, f32[128,512]{1,0:T(8,128)S(1)} %get-tuple-element.24.a, ...), custom_call_target="tpu_custom_call" | custom-call | flops 805306368 | bytes 4194304 | tf_op jit(solution)/shard_map/tick/pallas_call | solution.py:284
  72.3 1.4 %collective-permute-start.22 = (bf16[256,1408]{1,0:T(8,128)(2,1)S(1)}, bf16[256,1408]{1,0:T(8,128)(2,1)S(1)}, u32[]{:S(2)}, u32[]{:S(2)}) collective-permute-start(bf16[256,1408]{1,0:T(8,128)(2,1)S(1)} %get-tuple-element.29), channel_id=1, source_target_pairs={{0,1},{1,0},{2,3},{3,2},{4,5},{5,4},{6,7},{7,6},{8,9},{9,8},{10,11... | collective-permute-start | bytes 2162696 | tf_op jit(solution)/shard_map/ppermute | solution.py:220
  73.7 1.3 %collective-permute-start.26 = (bf16[128,640]{1,0:T(8,128)(2,1)S(1)}, bf16[128,640]{1,0:T(8,128)(2,1)S(1)}, u32[]{:S(2)}, u32[]{:S(2)}) collective-permute-start(bf16[128,640]{1,0:T(8,128)(2,1)S(1)} %get-tuple-element.31), channel_id=1, source_target_pairs={{0,2},{1,3},{2,4},{3,5},{4,6},{5,7},{6,0},{7,1},{8,10},{9,11},{10,... | collective-permute-start | bytes 491528 | tf_op jit(solution)/shard_map/ppermute | solution.py:222
  75.0 1.2 %collective-permute-start.27 = (bf16[128,640]{1,0:T(8,128)(2,1)S(1)}, bf16[128,640]{1,0:T(8,128)(2,1)S(1)}, u32[]{:S(2)}, u32[]{:S(2)}) collective-permute-start(bf16[128,640]{1,0:T(8,128)(2,1)S(1)} %get-tuple-element.32), channel_id=1, source_target_pairs={{0,4},{1,5},{2,6},{3,7},{4,0},{5,1},{6,2},{7,3},{8,12},{9,13},{10,... | collective-permute-start | bytes 491528 | tf_op jit(solution)/shard_map/ppermute | solution.py:222
  76.2 2.1 %collective-permute-start.28 = (bf16[128,640]{1,0:T(8,128)(2,1)S(1)}, bf16[128,640]{1,0:T(8,128)(2,1)S(1)}, u32[]{:S(2)}, u32[]{:S(2)}) collective-permute-start(bf16[128,640]{1,0:T(8,128)(2,1)S(1)} %get-tuple-element.33), channel_id=1, source_target_pairs={{0,6},{1,7},{2,0},{3,1},{4,2},{5,3},{6,4},{7,5},{8,14},{9,15},{10,... | collective-permute-start | bytes 491528 | tf_op jit(solution)/shard_map/ppermute | solution.py:222
  78.4 1.3 %collective-permute-start.20 = (bf16[128,2048]{1,0:T(8,128)(2,1)S(1)}, bf16[128,2048]{1,0:T(8,128)(2,1)S(1)}, u32[]{:S(2)}, u32[]{:S(2)}) collective-permute-start(bf16[128,2048]{1,0:T(8,128)(2,1)S(1)} %tick.4.held.grad), channel_id=1, source_target_pairs={{8,0},{9,1},{10,2},{11,3},{12,4},{13,5},{14,6},{15,7}} | collective-permute-start | bytes 1572872 | tf_op jit(solution)/shard_map/ppermute | solution.py:297
  79.9 6.9 %collective-permute-done.27 = bf16[128,640]{1,0:T(8,128)(2,1)S(1)} collective-permute-done((bf16[128,640]{1,0:T(8,128)(2,1)S(1)}, bf16[128,640]{1,0:T(8,128)(2,1)S(1)}, u32[]{:S(2)}, u32[]{:S(2)}) %collective-permute-start.27) | collective-permute-done | bytes 163872 | tf_op jit(solution)/shard_map/ppermute | solution.py:222
  87.2 5.8 %collective-permute-start.23 = (bf16[64,1408]{1,0:T(8,128)(2,1)S(1)}, bf16[64,1408]{1,0:T(8,128)(2,1)S(1)}, u32[]{:S(2)}, u32[]{:S(2)}) collective-permute-start(bf16[64,1408]{1,0:T(8,128)(2,1)S(1)} %get-tuple-element.36), channel_id=1, source_target_pairs={{0,2},{1,3},{2,4},{3,5},{4,6},{5,7},{6,0},{7,1},{8,10},{9,11},{10,... | collective-permute-start | bytes 540680 | tf_op jit(solution)/shard_map/ppermute | solution.py:226
  93.0 1.2 %collective-permute-start.24 = (bf16[64,1408]{1,0:T(8,128)(2,1)S(1)}, bf16[64,1408]{1,0:T(8,128)(2,1)S(1)}, u32[]{:S(2)}, u32[]{:S(2)}) collective-permute-start(bf16[64,1408]{1,0:T(8,128)(2,1)S(1)} %get-tuple-element.38), channel_id=1, source_target_pairs={{0,4},{1,5},{2,6},{3,7},{4,0},{5,1},{6,2},{7,3},{8,12},{9,13},{10,... | collective-permute-start | bytes 540680 | tf_op jit(solution)/shard_map/ppermute | solution.py:226
  95.4 2.0 %collective-permute-done.25 = bf16[64,1408]{1,0:T(8,128)(2,1)S(1)} collective-permute-done((bf16[64,1408]{1,0:T(8,128)(2,1)S(1)}, bf16[64,1408]{1,0:T(8,128)(2,1)S(1)}, u32[]{:S(2)}, u32[]{:S(2)}) %collective-permute-start.25) | collective-permute-done | bytes 180256 | tf_op jit(solution)/shard_map/ppermute | solution.py:226
  97.4 3.8 %collective-permute-done.24 = bf16[64,1408]{1,0:T(8,128)(2,1)S(1)} collective-permute-done((bf16[64,1408]{1,0:T(8,128)(2,1)S(1)}, bf16[64,1408]{1,0:T(8,128)(2,1)S(1)}, u32[]{:S(2)}, u32[]{:S(2)}) %collective-permute-start.24) | collective-permute-done | bytes 180256 | tf_op jit(solution)/shard_map/ppermute | solution.py:226
  102.2 4.9 %collective-permute-done.30 = bf16[64,2048]{1,0:T(8,128)(2,1)S(1)} collective-permute-done((bf16[64,2048]{1,0:T(8,128)(2,1)S(1)}, bf16[64,2048]{1,0:T(8,128)(2,1)S(1)}, u32[]{:S(2)}, u32[]{:S(2)}) %collective-permute-start.30) | collective-permute-done | bytes 262176 | tf_op jit(solution)/shard_map/ppermute | solution.py:300
  (58 shorter events, 10.7 us)
Async XLA Ops:
  0.6 8.4 %collective-permute-start = (bf16[256,512]{1,0:T(8,128)(2,1)}, bf16[256,512]{1,0:T(8,128)(2,1)S(1)}, u32[]{:S(2)}, u32[]{:S(2)}) collective-permute-start(bf16[256,512]{1,0:T(8,128)(2,1)} %bitcast.11), channel_id=1, source_target_pairs={{0,2},{2,4},{4,6},{6,7},{7,5},{5,3},{3,1},{1,0},{8,10},{10,12},{12... | collective-permute-start | bytes 786440 | tf_op jit(solution)/shard_map/ppermute | solution.py:50
  2.8 7.4 %collective-permute-start.7 = (bf16[256,512]{1,0:T(8,128)(2,1)}, bf16[256,512]{1,0:T(8,128)(2,1)S(1)}, u32[]{:S(2)}, u32[]{:S(2)}) collective-permute-start(bf16[256,512]{1,0:T(8,128)(2,1)} %bitcast.17), channel_id=1, source_target_pairs={{2,0},{4,2},{6,4},{7,6},{5,7},{3,5},{1,3},{0,1},{10,8},{12,10},{14... | collective-permute-start | bytes 786440 | tf_op jit(solution)/shard_map/ppermute | solution.py:51
  2.8 11.8 %collective-permute-start.1 = (bf16[256,512]{1,0:T(8,128)(2,1)}, bf16[256,512]{1,0:T(8,128)(2,1)S(1)}, u32[]{:S(2)}, u32[]{:S(2)}) collective-permute-start(bf16[256,512]{1,0:T(8,128)(2,1)} %bitcast.18), channel_id=1, source_target_pairs={{0,2},{2,4},{4,6},{6,7},{7,5},{5,3},{3,1},{1,0},{8,10},{10,12},{12... | collective-permute-start | bytes 786440 | tf_op jit(solution)/shard_map/ppermute | solution.py:50
  4.3 13.4 %collective-permute-start.6 = (bf16[256,512]{1,0:T(8,128)(2,1)}, bf16[256,512]{1,0:T(8,128)(2,1)S(1)}, u32[]{:S(2)}, u32[]{:S(2)}) collective-permute-start(bf16[256,512]{1,0:T(8,128)(2,1)} %bitcast.12), channel_id=1, source_target_pairs={{2,0},{4,2},{6,4},{7,6},{5,7},{3,5},{1,3},{0,1},{10,8},{12,10},{14... | collective-permute-start | bytes 786440 | tf_op jit(solution)/shard_map/ppermute | solution.py:51
  9.0 15.9 %collective-permute-start.8 = (bf16[256,512]{1,0:T(8,128)(2,1)S(1)}, bf16[256,512]{1,0:T(8,128)(2,1)S(1)}, u32[]{:S(2)}, u32[]{:S(2)}) collective-permute-start(bf16[256,512]{1,0:T(8,128)(2,1)S(1)} %collective-permute-done.rest_2_), channel_id=1, source_target_pairs={{0,2},{2,4},{4,6},{6,7},{7,5},{5,3},{3,1},{1,0},{8,10},{10,12},{12... | collective-permute-start | bytes 786440 | tf_op jit(solution)/shard_map/ppermute | solution.py:50
  10.2 16.0 %collective-permute-start.11 = (bf16[256,512]{1,0:T(8,128)(2,1)S(1)}, bf16[256,512]{1,0:T(8,128)(2,1)S(1)}, u32[]{:S(2)}, u32[]{:S(2)}) collective-permute-start(bf16[256,512]{1,0:T(8,128)(2,1)S(1)} %collective-permute-done.7.rest_5_), channel_id=1, source_target_pairs={{2,0},{4,2},{6,4},{7,6},{5,7},{3,5},{1,3},{0,1},{10,8},{12,10},{14... | collective-permute-start | bytes 786440 | tf_op jit(solution)/shard_map/ppermute | solution.py:51
  14.6 5.5 %collective-permute-start.4 = (bf16[128,512]{1,0:T(8,128)(2,1)}, bf16[128,512]{1,0:T(8,128)(2,1)S(1)}, u32[]{:S(2)}, u32[]{:S(2)}) collective-permute-start(bf16[128,512]{1,0:T(8,128)(2,1)} %rest_0_), channel_id=1, source_target_pairs={{16,0},{8,24},{17,1},{9,25},{18,2},{10,26},{19,3},{11,27},{20,4},{... | collective-permute-start | bytes 393224 | tf_op jit(solution)/shard_map/ppermute | solution.py:71
  17.6 9.1 %collective-permute-start.10 = (bf16[256,512]{1,0:T(8,128)(2,1)S(1)}, bf16[256,512]{1,0:T(8,128)(2,1)S(1)}, u32[]{:S(2)}, u32[]{:S(2)}) collective-permute-start(bf16[256,512]{1,0:T(8,128)(2,1)S(1)} %collective-permute-done.6.rest_4_), channel_id=1, source_target_pairs={{2,0},{4,2},{6,4},{7,6},{5,7},{3,5},{1,3},{0,1},{10,8},{12,10},{14... | collective-permute-start | bytes 786440 | tf_op jit(solution)/shard_map/ppermute | solution.py:51
  18.9 4.1 %collective-permute-start.3 = (bf16[128,512]{1,0:T(8,128)(2,1)}, bf16[128,512]{1,0:T(8,128)(2,1)S(1)}, u32[]{:S(2)}, u32[]{:S(2)}) collective-permute-start(bf16[128,512]{1,0:T(8,128)(2,1)} %rest_0_), channel_id=1, source_target_pairs={{8,0},{0,8},{24,16},{16,24},{9,1},{1,9},{25,17},{17,25},{10,2},{2,... | collective-permute-start | bytes 393224 | tf_op jit(solution)/shard_map/ppermute | solution.py:71
  20.1 19.6 %collective-permute-start.2 = (bf16[128,2048]{1,0:T(8,128)(2,1)}, bf16[128,2048]{1,0:T(8,128)(2,1)S(1)}, u32[]{:S(2)}, u32[]{:S(2)}) collective-permute-start(bf16[128,2048]{1,0:T(8,128)(2,1)} %bitcast.24), channel_id=1, source_target_pairs={{0,24},{8,16},{16,8},{24,0},{1,25},{9,17},{17,9},{25,1},{2,26},{10... | collective-permute-start | bytes 1572872 | tf_op jit(solution)/shard_map/ppermute | solution.py:242
  23.0 15.1 %collective-permute-start.9 = (bf16[256,512]{1,0:T(8,128)(2,1)S(1)}, bf16[256,512]{1,0:T(8,128)(2,1)S(1)}, u32[]{:S(2)}, u32[]{:S(2)}) collective-permute-start(bf16[256,512]{1,0:T(8,128)(2,1)S(1)} %collective-permute-done.1.rest_3_), channel_id=1, source_target_pairs={{0,2},{2,4},{4,6},{6,7},{7,5},{5,3},{3,1},{1,0},{8,10},{10,12},{12... | collective-permute-start | bytes 786440 | tf_op jit(solution)/shard_map/ppermute | solution.py:50
  24.9 13.4 %collective-permute-start.12 = (bf16[256,512]{1,0:T(8,128)(2,1)S(1)}, bf16[256,512]{1,0:T(8,128)(2,1)S(1)}, u32[]{:S(2)}, u32[]{:S(2)}) collective-permute-start(bf16[256,512]{1,0:T(8,128)(2,1)S(1)} %collective-permute-done.8.rest_6_), channel_id=1, source_target_pairs={{0,2},{2,4},{4,6},{6,7},{7,5},{5,3},{3,1},{1,0},{8,10},{10,12},{12... | collective-permute-start | bytes 786440 | tf_op jit(solution)/shard_map/ppermute | solution.py:50
  26.2 13.5 %collective-permute-start.15 = (bf16[256,512]{1,0:T(8,128)(2,1)S(1)}, bf16[256,512]{1,0:T(8,128)(2,1)S(1)}, u32[]{:S(2)}, u32[]{:S(2)}) collective-permute-start(bf16[256,512]{1,0:T(8,128)(2,1)S(1)} %collective-permute-done.11.rest_9_), channel_id=1, source_target_pairs={{2,0},{4,2},{6,4},{7,6},{5,7},{3,5},{1,3},{0,1},{10,8},{12,10},{14... | collective-permute-start | bytes 786440 | tf_op jit(solution)/shard_map/ppermute | solution.py:51
  26.7 9.7 %collective-permute-start.5 = (bf16[128,512]{1,0:T(8,128)(2,1)S(1)}, bf16[128,512]{1,0:T(8,128)(2,1)S(1)}, u32[]{:S(2)}, u32[]{:S(2)}) collective-permute-start(bf16[128,512]{1,0:T(8,128)(2,1)S(1)} %collective-permute-done.3.rest_1_), channel_id=1, source_target_pairs={{16,0},{8,24},{17,1},{9,25},{18,2},{10,26},{19,3},{11,27},{20,4},{... | collective-permute-start | bytes 393224 | tf_op jit(solution)/shard_map/ppermute | solution.py:71
  36.4 7.5 %collective-permute-start.14 = (bf16[256,512]{1,0:T(8,128)(2,1)S(1)}, bf16[256,512]{1,0:T(8,128)(2,1)S(1)}, u32[]{:S(2)}, u32[]{:S(2)}) collective-permute-start(bf16[256,512]{1,0:T(8,128)(2,1)S(1)} %collective-permute-done.10.rest_8_), channel_id=1, source_target_pairs={{2,0},{4,2},{6,4},{7,6},{5,7},{3,5},{1,3},{0,1},{10,8},{12,10},{14... | collective-permute-start | bytes 786440 | tf_op jit(solution)/shard_map/ppermute | solution.py:51
  38.2 6.5 %collective-permute-start.13 = (bf16[256,512]{1,0:T(8,128)(2,1)S(1)}, bf16[256,512]{1,0:T(8,128)(2,1)S(1)}, u32[]{:S(2)}, u32[]{:S(2)}) collective-permute-start(bf16[256,512]{1,0:T(8,128)(2,1)S(1)} %collective-permute-done.9.rest_7_), channel_id=1, source_target_pairs={{0,2},{2,4},{4,6},{6,7},{7,5},{5,3},{3,1},{1,0},{8,10},{10,12},{12... | collective-permute-start | bytes 786440 | tf_op jit(solution)/shard_map/ppermute | solution.py:50
  38.2 12.1 %collective-permute-start.16 = (bf16[256,512]{1,0:T(8,128)(2,1)S(1)}, bf16[256,512]{1,0:T(8,128)(2,1)S(1)}, u32[]{:S(2)}, u32[]{:S(2)}) collective-permute-start(bf16[256,512]{1,0:T(8,128)(2,1)S(1)} %collective-permute-done.12.rest_10_), channel_id=1, source_target_pairs={{0,2},{2,4},{4,6},{6,7},{7,5},{5,3},{3,1},{1,0},{8,10},{10,12},{12... | collective-permute-start | bytes 786440 | tf_op jit(solution)/shard_map/ppermute | solution.py:56
  39.7 10.6 %collective-permute-start.17 = (bf16[256,512]{1,0:T(8,128)(2,1)S(1)}, bf16[256,512]{1,0:T(8,128)(2,1)S(1)}, u32[]{:S(2)}, u32[]{:S(2)}) collective-permute-start(bf16[256,512]{1,0:T(8,128)(2,1)S(1)} %collective-permute-done.15.rest_13_), channel_id=1, source_target_pairs={{2,0},{4,2},{6,4},{7,6},{5,7},{3,5},{1,3},{0,1},{10,8},{12,10},{14... | collective-permute-start | bytes 786440 | tf_op jit(solution)/shard_map/ppermute | solution.py:56
  52.5 0.7 collective-permute-start.18
  53.3 15.9 %collective-permute-start.19 = (bf16[128,2048]{1,0:T(8,128)(2,1)S(1)}, bf16[128,2048]{1,0:T(8,128)(2,1)S(1)}, u32[]{:S(2)}, u32[]{:S(2)}) collective-permute-start(bf16[128,2048]{1,0:T(8,128)(2,1)S(1)} %tick.3.held), channel_id=1, source_target_pairs={{16,8},{17,9},{18,10},{19,11},{20,12},{21,13},{22,14},{23,15}} | collective-permute-start | bytes 1572872 | tf_op jit(solution)/shard_map/ppermute | solution.py:297
  54.6 16.8 %collective-permute-start.21 = (bf16[128,512]{1,0:T(8,128)(2,1)S(1)}, bf16[128,512]{1,0:T(8,128)(2,1)S(1)}, u32[]{:S(2)}, u32[]{:S(2)}) collective-permute-start(bf16[128,512]{1,0:T(8,128)(2,1)S(1)} %get-tuple-element.27), channel_id=1, source_target_pairs={{0,8},{8,16},{16,24},{24,0},{1,9},{9,17},{17,25},{25,1},{2,10},{10... | collective-permute-start | bytes 393224 | tf_op jit(solution)/shard_map/ppermute | solution.py:281
  72.3 14.6 %collective-permute-start.22 = (bf16[256,1408]{1,0:T(8,128)(2,1)S(1)}, bf16[256,1408]{1,0:T(8,128)(2,1)S(1)}, u32[]{:S(2)}, u32[]{:S(2)}) collective-permute-start(bf16[256,1408]{1,0:T(8,128)(2,1)S(1)} %get-tuple-element.29), channel_id=1, source_target_pairs={{0,1},{1,0},{2,3},{3,2},{4,5},{5,4},{6,7},{7,6},{8,9},{9,8},{10,11... | collective-permute-start | bytes 2162696 | tf_op jit(solution)/shard_map/ppermute | solution.py:220
  73.7 6.2 %collective-permute-start.26 = (bf16[128,640]{1,0:T(8,128)(2,1)S(1)}, bf16[128,640]{1,0:T(8,128)(2,1)S(1)}, u32[]{:S(2)}, u32[]{:S(2)}) collective-permute-start(bf16[128,640]{1,0:T(8,128)(2,1)S(1)} %get-tuple-element.31), channel_id=1, source_target_pairs={{0,2},{1,3},{2,4},{3,5},{4,6},{5,7},{6,0},{7,1},{8,10},{9,11},{10,... | collective-permute-start | bytes 491528 | tf_op jit(solution)/shard_map/ppermute | solution.py:222
  75.0 11.7 %collective-permute-start.27 = (bf16[128,640]{1,0:T(8,128)(2,1)S(1)}, bf16[128,640]{1,0:T(8,128)(2,1)S(1)}, u32[]{:S(2)}, u32[]{:S(2)}) collective-permute-start(bf16[128,640]{1,0:T(8,128)(2,1)S(1)} %get-tuple-element.32), channel_id=1, source_target_pairs={{0,4},{1,5},{2,6},{3,7},{4,0},{5,1},{6,2},{7,3},{8,12},{9,13},{10,... | collective-permute-start | bytes 491528 | tf_op jit(solution)/shard_map/ppermute | solution.py:222
  76.2 10.5 %collective-permute-start.28 = (bf16[128,640]{1,0:T(8,128)(2,1)S(1)}, bf16[128,640]{1,0:T(8,128)(2,1)S(1)}, u32[]{:S(2)}, u32[]{:S(2)}) collective-permute-start(bf16[128,640]{1,0:T(8,128)(2,1)S(1)} %get-tuple-element.33), channel_id=1, source_target_pairs={{0,6},{1,7},{2,0},{3,1},{4,2},{5,3},{6,4},{7,5},{8,14},{9,15},{10,... | collective-permute-start | bytes 491528 | tf_op jit(solution)/shard_map/ppermute | solution.py:222
  78.4 22.9 %collective-permute-start.20 = (bf16[128,2048]{1,0:T(8,128)(2,1)S(1)}, bf16[128,2048]{1,0:T(8,128)(2,1)S(1)}, u32[]{:S(2)}, u32[]{:S(2)}) collective-permute-start(bf16[128,2048]{1,0:T(8,128)(2,1)S(1)} %tick.4.held.grad), channel_id=1, source_target_pairs={{8,0},{9,1},{10,2},{11,3},{12,4},{13,5},{14,6},{15,7}} | collective-permute-start | bytes 1572872 | tf_op jit(solution)/shard_map/ppermute | solution.py:297
  86.8 7.4 %collective-permute-start.29 = (bf16[64,640]{1,0:T(8,128)(2,1)S(1)}, bf16[64,640]{1,0:T(8,128)(2,1)S(1)}, u32[]{:S(2)}, u32[]{:S(2)}) collective-permute-start(bf16[64,640]{1,0:T(8,128)(2,1)S(1)} %slice.45), channel_id=1, source_target_pairs={{0,1},{1,0},{2,3},{3,2},{4,5},{5,4},{6,7},{7,6},{8,9},{9,8},{10,11... | collective-permute-start | bytes 245768 | tf_op jit(solution)/shard_map/ppermute | solution.py:227
  87.1 14.2 %copy-start.5 = (bf16[1,2048]{1,0:T(2,128)(2,1)S(1)}, bf16[1,2048]{1,0:T(2,128)(2,1)}, u32[]{:S(2)}) copy-start(bf16[1,2048]{1,0:T(2,128)(2,1)} %gate_vector.9) | copy-start | bytes 12292
  87.2 8.2 %collective-permute-start.23 = (bf16[64,1408]{1,0:T(8,128)(2,1)S(1)}, bf16[64,1408]{1,0:T(8,128)(2,1)S(1)}, u32[]{:S(2)}, u32[]{:S(2)}) collective-permute-start(bf16[64,1408]{1,0:T(8,128)(2,1)S(1)} %get-tuple-element.36), channel_id=1, source_target_pairs={{0,2},{1,3},{2,4},{3,5},{4,6},{5,7},{6,0},{7,1},{8,10},{9,11},{10,... | collective-permute-start | bytes 540680 | tf_op jit(solution)/shard_map/ppermute | solution.py:226
  92.9 4.4 %collective-permute-start.25 = (bf16[64,1408]{1,0:T(8,128)(2,1)S(1)}, bf16[64,1408]{1,0:T(8,128)(2,1)S(1)}, u32[]{:S(2)}, u32[]{:S(2)}) collective-permute-start(bf16[64,1408]{1,0:T(8,128)(2,1)S(1)} %get-tuple-element.37), channel_id=1, source_target_pairs={{0,6},{1,7},{2,0},{3,1},{4,2},{5,3},{6,4},{7,5},{8,14},{9,15},{10,... | collective-permute-start | bytes 540680 | tf_op jit(solution)/shard_map/ppermute | solution.py:226
  93.0 8.2 %collective-permute-start.24 = (bf16[64,1408]{1,0:T(8,128)(2,1)S(1)}, bf16[64,1408]{1,0:T(8,128)(2,1)S(1)}, u32[]{:S(2)}, u32[]{:S(2)}) collective-permute-start(bf16[64,1408]{1,0:T(8,128)(2,1)S(1)} %get-tuple-element.38), channel_id=1, source_target_pairs={{0,4},{1,5},{2,6},{3,7},{4,0},{5,1},{6,2},{7,3},{8,12},{9,13},{10,... | collective-permute-start | bytes 540680 | tf_op jit(solution)/shard_map/ppermute | solution.py:226
  101.2 5.8 %collective-permute-start.30 = (bf16[64,2048]{1,0:T(8,128)(2,1)S(1)}, bf16[64,2048]{1,0:T(8,128)(2,1)S(1)}, u32[]{:S(2)}, u32[]{:S(2)}) collective-permute-start(bf16[64,2048]{1,0:T(8,128)(2,1)S(1)} %pad_maximum_fusion), channel_id=1, source_target_pairs={{0,24},{8,0},{16,8},{24,16},{1,25},{9,1},{17,9},{25,17},{2,26},{10... | collective-permute-start | bytes 786440 | tf_op jit(solution)/shard_map/ppermute | solution.py:300
  (6 other events, 20.9 us)

commit v3 on v2

v3 whole, which is shorter than its diff:
```python
import functools

import jax
import jax.numpy as jnp
from jax import lax
from jax.experimental import pallas as pl
from jax.experimental.pallas import tpu as pltpu
from jax.sharding import PartitionSpec as P

F32, BF16 = jnp.float32, jnp.bfloat16
PLAIN = (((1,), (0,)), ((), ()))
TURNED = (((1,), (1,)), ((), ()))
VMEM = pl.BlockSpec(memory_space=pltpu.VMEM)
LIMIT = 16 * 2**20


def dot(left, right, dims):
    return lax.dot_general(left, right, dims, preferred_element_type=F32)


def params():
    return pltpu.CompilerParams(vmem_limit_bytes=LIMIT)


def cost(macs, *arrays):
    moved = sum(a.size * a.dtype.itemsize for a in arrays)
    return pl.CostEstimate(flops=2 * macs, bytes_accessed=moved, transcendentals=0)


def ring_place(index, size):
    return jnp.where(index % 2 == 0, index // 2, size - 1 - index // 2)


def ring_member(place, size):
    return jnp.where(place < (size + 1) // 2, 2 * place, 2 * (size - 1 - place) + 1)


def ring_pairs(size):
    order = list(range(0, size, 2)) + list(range(1, size, 2))[::-1]
    ahead = [(order[i], order[(i + 1) % size]) for i in range(size)]
    return ahead, [(b, a) for a, b in ahead]


def gather_ring(arrays, axis, between):
    size = lax.axis_size(axis)
    ahead, back = ring_pairs(size)
    pieces, offsets = [list(arrays)], [0]
    moving = [(v, v) for v in arrays]
    for step in range(1, (size - 1) // 2 + 1):
        moved = []
        for i, (v, w) in enumerate(moving):
            v, w = between(step, i, (v, w))
            both = lax.ppermute(v, axis, ahead), lax.ppermute(w, axis, back)
            moved.append(lax.optimization_barrier(both))
        moving = moved
        pieces += [[v for v, _ in moving], [w for _, w in moving]]
        offsets += [-step, step]
    if size % 2 == 0:
        (v, _), (_, w) = between(size // 2, 0, moving[0]), between(size // 2, 1, moving[1])
        pieces.append([lax.ppermute(v, axis, ahead), lax.ppermute(w, axis, back)])
        offsets.append(size // 2)
    return pieces, offsets


def gather_to_ends(x, axis):
    size = lax.axis_size(axis)
    steps = [1 << place for place in range(size.bit_length() - 1)][::-1]
    needed = [{0, size - 1}]
    for stride in steps[::-1]:
        needed.append(needed[-1] | {i ^ stride for i in needed[-1]})
    held, offsets = [x], [0]
    yield held, offsets
    for stride, wanted in zip(steps, needed[-2::-1]):
        pairs = [(i ^ stride, i) for i in sorted(wanted)]
        held += [lax.ppermute(block, axis, pairs) for block in list(held)]
        offsets += [offset ^ stride for offset in offsets]
        yield held, offsets


def after(values, *others):
    return lax.optimization_barrier((values, others))[0]


def piece_columns(offset, axis, depth):
    if offset is None:
        return slice(0, depth)
    size = lax.axis_size(axis)
    place = (ring_place(lax.axis_index(axis), size) + (offset + size)) % size
    return pl.ds(pl.multiple_of(ring_member(place, size) * depth, depth), depth)


def push_back(grad_ref, back_proj, scales, gate_vector, pieces, columns, out_ref):
    gate_scale, up_scale, logit_scale = scales
    logit = jnp.sum(back_proj * logit_scale[...], axis=1, keepdims=True)
    gate_grad = (back_proj * gate_scale[...]).astype(BF16)
    up_grad = (back_proj * up_scale[...]).astype(BF16)
    for where, (gate, up) in zip(columns, pieces):
        through = dot(gate_grad, gate[...], TURNED) + dot(up_grad, up[...], TURNED)
        out_ref[:, where] = (
            grad_ref[:, where].astype(F32) + through + logit * gate_vector[:, where].astype(F32)
        ).astype(BF16)


def pair_up(refs):
    return [refs[i : i + 2] for i in range(0, len(refs), 2)]


def score_kernel(rows, gate_vector, score):
    logit = jnp.sum(
        rows[...].astype(F32) * gate_vector[...].astype(F32), axis=1, keepdims=True
    )
    score[...] = jax.nn.sigmoid(logit)


def prepare_kernel(offsets, down, *rest):
    blocks, (seeded, back_proj) = rest[:-2], rest[-2:]
    sections = lax.axis_size("section")
    is_last = lax.axis_index("section") == sections - 1
    width = blocks[0].shape[1]

    def lay(flip):
        for offset, block in zip(offsets, blocks):
            place = offset ^ flip
            seeded[:, place * width : (place + 1) * width] = block[...]

    pl.when(is_last)(lambda: lay(sections - 1))
    pl.when(jnp.logical_not(is_last))(lambda: lay(0))
    back_proj[...] = dot(seeded[...], down[...], TURNED)


def first_kernel(offsets, rows, score, back_proj, grad, gate_vector, *rest):
    pieces = pair_up(rest[: 2 * len(offsets)])
    out, gate_scale, up_scale, logit_scale, scored = rest[2 * len(offsets) :]
    depth = pieces[0][0].shape[0]
    columns = [piece_columns(offset, "dp", depth) for offset in offsets]
    gate_pre = up_pre = 0.0
    for where, (gate, up) in zip(columns, pieces):
        block = rows[:, where]
        gate_pre += dot(block, gate[...], PLAIN)
        up_pre += dot(block, up[...], PLAIN)
    gate_sig = jax.nn.sigmoid(gate_pre)
    activated = gate_pre * gate_sig
    hidden = (activated * up_pre).astype(BF16).astype(F32)
    share = score[...]
    gate_scale[...] = share * up_pre * gate_sig * (1.0 + gate_pre * (1.0 - gate_sig))
    up_scale[...] = share * activated
    logit_scale[...] = hidden * (share * (1.0 - share))
    scored[...] = (hidden * share).astype(BF16).T
    scales = gate_scale, up_scale, logit_scale
    section, sections = lax.axis_index("section"), lax.axis_size("section")

    @pl.when(section == sections - 1)
    def _():
        push_back(grad, back_proj[...], scales, gate_vector, pieces, columns, out)

    @pl.when(section < sections - 1)
    def _():
        out[...] = grad[...]


def tick_kernel(offsets, section, grad, held, down, gate_vector, a, b, c, *rest):
    pieces, out = pair_up(rest[:-1]), rest[-1]

    here = lax.axis_index("section") == section

    @pl.when(jnp.logical_not(here))
    def _():
        out[...] = held[...]

    @pl.when(here)
    def _():
        depth = pieces[0][0].shape[0]
        columns = [piece_columns(offset, "dp", depth) for offset in offsets]
        back_proj = dot(grad[...], down[...], TURNED)
        push_back(grad, back_proj, (a, b, c), gate_vector, pieces, columns, out)


def block_rows(bits, rest, units):
    return pl.ds(pl.multiple_of((rest * 4 + 2 * bits[1] + bits[0]) * units, units), units)


def own_bits():
    me = lax.axis_index("dp")
    return me % 2, me // 2 % 2


def split_kernel(scored, *out):
    size = lax.axis_size("dp")
    units = scored.shape[0] // size
    own = own_bits()
    for bit in range(2):
        for second in range(2):
            for rest in range(size // 4):
                bits = (1 - own[0], second) if bit == 0 else (second, 1 - own[1])
                start = (second * (size // 4) + rest) * units
                out[bit][start : start + units, :] = scored[block_rows(bits, rest, units), :]


def products_kernel(scored, grad, *rest):
    theirs, partners, sends, keeps = rest[:2], rest[2:4], rest[4:6], rest[6:]
    size = lax.axis_size("dp")
    units = scored.shape[0] // size
    half, width = sends[0].shape
    own = own_bits()
    for bit in range(2):
        columns = slice(bit * width, (bit + 1) * width)
        mine = grad[:, columns]

        def rows(second):
            bits = (own[0], second) if bit == 0 else (second, own[1])
            blocks = [scored[block_rows(bits, rest, units), :] for rest in range(size // 4)]
            where = pl.ds(pl.multiple_of(second * half, half), half)
            left = jnp.concatenate(blocks, axis=0)
            return dot(left, mine, PLAIN) + dot(theirs[bit][where, :], partners[bit][...], PLAIN)

        sends[bit][...] = rows(1 - own[1 - bit]).astype(BF16)
        keeps[bit][...] = rows(own[1 - bit])


def combine_kernel(bit, count, *refs):
    keeps, gots, outs = refs[:count], refs[count : 2 * count], refs[2 * count :]
    width = keeps[0].shape[1]
    for i, (keep, got) in enumerate(zip(keeps, gots)):
        columns = slice(i * width, (i + 1) * width)
        if bit is None:
            outs[0][:, columns] = (keep[...] + got[...].astype(F32)).astype(BF16)
            continue
        half = keep.shape[0] // 2
        own = lax.axis_index("dp") >> bit & 1

        def rows(which):
            where = pl.ds(pl.multiple_of(which * half, half), half)
            return keep[where, :] + got[where, :].astype(F32)

        outs[0][:, columns] = rows(1 - own).astype(BF16)
        outs[1][:, columns] = rows(own)


def along(bit, *values):
    pairs = [(i, i ^ 1 << bit) for i in range(lax.axis_size("dp"))]
    return [lax.ppermute(v, "dp", pairs) for v in values]


def call(kernel, name, outs, macs, *args):
    return pl.pallas_call(
        kernel,
        out_shape=outs,
        in_specs=[VMEM] * len(args),
        out_specs=[VMEM] * len(outs),
        compiler_params=params(),
        cost_estimate=cost(macs, *args),
        name=name,
    )(*args)


def swap_scored(scored):
    half = jax.ShapeDtypeStruct((scored.shape[0] // 2, scored.shape[1]), BF16)
    to_first, to_second = call(split_kernel, "split", [half] * 2, 0, scored)
    return [*along(0, to_first), *along(1, to_second)]


def reduce_rows(scored, theirs, grad):
    size = lax.axis_size("dp")
    rows, width = scored.shape[0] // 4, grad.shape[1]
    shape = jax.ShapeDtypeStruct
    partners = [*along(0, grad[:, : width // 2]), *along(1, grad[:, width // 2 :])]
    half = (rows, width // 2)
    outs = [shape(half, BF16)] * 2 + [shape(half, F32)] * 2
    macs = 4 * rows * scored.shape[1] * width
    *sends, keep_a, keep_b = call(
        products_kernel, "products", outs, macs, scored, grad, *theirs, *partners
    )
    keeps = [keep_a, keep_b]
    gots = [*along(1, sends[0]), *along(0, sends[1])]
    for bit in range(size.bit_length() - 2, 1, -1):
        rows //= 2
        outs = [shape((rows, width), BF16), shape((rows, width), F32)]
        kernel = functools.partial(combine_kernel, bit, len(keeps))
        send, keep = call(kernel, "combine", outs, 0, *keeps, *gots)
        keeps, gots = [keep], along(bit, send)
    kernel = functools.partial(combine_kernel, None, len(keeps))
    return call(kernel, "total", [shape((rows, width), BF16)], 0, *keeps, *gots)[0]


def on_device(stash, cotangent, gate_weight, up_weight, down_weight, shared_gate):
    sections = lax.axis_size("section")
    replicas = lax.axis_size("dp")
    local_rows, model_width = stash.shape[1:]
    depth = gate_weight.shape[1]
    down_full = down_weight[0]
    hidden_units = down_full.shape[0]

    shape = jax.ShapeDtypeStruct
    small = shape((local_rows, hidden_units), F32)
    cotangents = gather_to_ends(cotangent, "section")
    blocks, block_offsets = next(cotangents)
    own_rows = stash[0]

    def between(step, i, moving):
        nonlocal blocks, own_rows
        if step == 1 and i == 1:
            blocks, _ = next(cotangents, (blocks, None))
        if step == 2 and i == 0:
            own_rows, *moving = after((own_rows, *moving))
            mirrored = [(k, sections - 1 - k) for k in range(sections)]
            own_rows = lax.ppermute(own_rows, "section", mirrored)
        if step == 2 and i == 1:
            moving, blocks = after((moving, blocks))
            blocks, _ = next(cotangents, (list(blocks), None))
        if step == 3 and i == 1:
            moving, blocks = after((moving, blocks))
        if step == replicas // 2 and i == 0:
            moving, own_rows = after((moving, own_rows))
        return moving

    pieces, offsets = gather_ring([gate_weight[0], up_weight[0]], "dp", between)
    for blocks, _ in cotangents:
        pass
    seeded, back_proj = pl.pallas_call(
        functools.partial(prepare_kernel, block_offsets),
        out_shape=[shape((local_rows, model_width), BF16), small],
        in_specs=[VMEM] * (1 + len(blocks)),
        out_specs=[VMEM] * 2,
        compiler_params=params(),
        cost_estimate=cost(local_rows * model_width * hidden_units, down_full),
        name="prepare",
    )(down_full, *blocks)
    score = pl.pallas_call(
        score_kernel,
        out_shape=shape((local_rows, 1), F32),
        in_specs=[VMEM] * 2,
        out_specs=VMEM,
        compiler_params=params(),
        cost_estimate=cost(local_rows * model_width, own_rows),
        name="score",
    )(own_rows, shared_gate)

    if depth % 128:
        size = replicas
        place = ring_place(lax.axis_index("dp"), size)
        joined = [jnp.zeros((depth * replicas, hidden_units), BF16)] * 2
        for offset, piece in zip(offsets, pieces):
            start = ring_member((place + offset + size) % size, size) * depth
            joined = [lax.dynamic_update_slice(j, p, (start, 0)) for j, p in zip(joined, piece)]
        pieces, offsets = [joined], [None]
    flat = [v for piece in pieces for v in piece]

    outgoing, *scales, scored = pl.pallas_call(
        functools.partial(first_kernel, offsets),
        out_shape=[
            shape((local_rows, model_width), BF16),
            small,
            small,
            small,
            shape((hidden_units, local_rows), BF16),
        ],
        in_specs=[VMEM] * (5 + len(flat)),
        out_specs=[VMEM] * 5,
        compiler_params=params(),
        cost_estimate=cost(4 * local_rows * model_width * hidden_units, *flat),
        name="first_tick",
    )(own_rows, score, back_proj, seeded, shared_gate, *flat)
    around = [(i, (i + 1) % sections) for i in range(sections)]
    scored = lax.ppermute(scored, "section", around)

    def tick(section, grad, held):
        return pl.pallas_call(
            functools.partial(tick_kernel, offsets, section),
            out_shape=shape((local_rows, model_width), BF16),
            in_specs=[VMEM] * (7 + len(flat)),
            out_specs=VMEM,
            compiler_params=params(),
            cost_estimate=cost(3 * local_rows * model_width * hidden_units, *flat),
            name="tick",
        )(grad, held, down_full, shared_gate, *scales, *flat)

    for section in range(sections - 2, -1, -1):
        if section == 0:
            reduced = reduce_rows(scored, theirs, outgoing)
        if section == sections - 3:
            outgoing, scored = after((outgoing, scored))
        grad = lax.ppermute(outgoing, "section", [(section + 1, section)])
        if section == max(sections - 3, 0):
            theirs = swap_scored(scored)
        outgoing = tick(section, grad, outgoing)

    reduced = lax.ppermute(reduced, "section", [(b, a) for a, b in around])
    norm_factor = (local_rows * replicas) ** (-0.5)
    return (outgoing[None], (reduced.astype(F32) * norm_factor)[None])


def solution(mesh):
    placed = (
        P("section", "dp", None),
        P("dp", "section"),
        P("section", "dp", None),
        P("section", "dp", None),
        P("section", None, None),
        P("section", None),
    )
    return jax.shard_map(
        on_device,
        mesh=mesh,
        in_specs=placed,
        out_specs=(P("section", "dp", None), P("section", "dp", None)),
        check_vma=False,
    )
```

time: 108 us -> 100 us (0.926)
  starting transfers between devices: 47.7 us -> 36.3 us
  waiting for transfers between devices: 47.8 us -> 53.6 us
  Pallas kernels: 7.09 us -> 5.96 us
    ppermute x28 -> x27, starting transfers between devices: 44.4 us -> 33 us  [the longest x12 9.57 us: gather_ring(): both = (lax.ppermute(v, axis, ahead), lax.ppermute(w, axis, back))]
    ppermute x28 -> x27, waiting for transfers between devices: 40.7 us -> 44 us  [the longest x12 18.4 us: gather_ring(): both = (lax.ppermute(v, axis, ahead), lax.ppermute(w, axis, back))]
    ppermute x3, waiting for transfers between devices: 7.06 us -> 9.6 us  [on_device(): grad = lax.ppermute(outgoing, 'section', [(section + 1, section)])]
    pallas_call x1, Pallas kernels: 2.2 us -> 0.94 us  [on_device(): pl.pallas_call(functools.partial(first_kernel, offsets), out_shape=[shape...]
    unnamed x14 -> x12, local copies, waits for them, and re-layouts: 3.21 us -> 2.51 us
  transfers between devices with their start and end apart: 31 -> 30, of which waited for: 14 -> 17; matrix products, arithmetic and copies ran while one was open for 0% -> 0% of each run, Pallas kernels for 4% -> 2%
where the time goes in v3:
time: 100 us
  waiting for transfers between devices  53.6 us (54%)
  starting transfers between devices  36.3 us (36%)
  Pallas kernels  5.96 us (6%)
  local copies, waits for them, and re-layouts  2.55 us (3%)
    ppermute x12, waiting for transfers between devices, gather_ring(): both = (lax.ppermute(v, axis, ahead), lax.ppermute(w, axis, back))  18.4 us
    ppermute x7, waiting for transfers between devices, along(): return [lax.ppermute(v, 'dp', pairs) for v in values]  16.5 us
    ppermute x3, waiting for transfers between devices, on_device(): grad = lax.ppermute(outgoing, 'section', [(section + 1, section)])  9.6 us
    ppermute x12, starting transfers between devices, gather_ring(): both = (lax.ppermute(v, axis, ahead), lax.ppermute(w, axis, back))  9.57 us
    ppermute x7, starting transfers between devices, along(): return [lax.ppermute(v, 'dp', pairs) for v in values]  6.89 us
    ppermute x3, starting transfers between devices, gather_to_ends(): held += [lax.ppermute(block, axis, pairs) for block in list(held)]  5.74 us
    ppermute x1, starting transfers between devices, between(): own_rows = lax.ppermute(own_rows, 'section', mirrored)  4.99 us
    ppermute x1, waiting for transfers between devices, on_device(): reduced = lax.ppermute(reduced, 'section', [(b, a) for a, b in around])  4.91 us
  transfers between devices with their start and end apart: 30, of which 17 were waited for; matrix products, arithmetic and copies ran while one was open for 0% of the time, Pallas kernels for 2%

profile of v3, /device:TPU:1, one launch (start us, length us, event | category | flops | bytes accessed | tf_op | source)
XLA Modules:
  0.0 100.1 jit_solution(2990950550816666630)
XLA Ops:
  0.6 2.2 %collective-permute-start = (bf16[256,512]{1,0:T(8,128)(2,1)}, bf16[256,512]{1,0:T(8,128)(2,1)S(1)}, u32[]{:S(2)}, u32[]{:S(2)}) collective-permute-start(bf16[256,512]{1,0:T(8,128)(2,1)} %bitcast.11), channel_id=1, source_target_pairs={{0,2},{2,4},{4,6},{6,7},{7,5},{5,3},{3,1},{1,0},{8,10},{10,12},{12... | collective-permute-start | bytes 786440 | tf_op jit(solution)/shard_map/ppermute | solution.py:53
  2.8 1.5 %collective-permute-start.7 = (bf16[256,512]{1,0:T(8,128)(2,1)}, bf16[256,512]{1,0:T(8,128)(2,1)S(1)}, u32[]{:S(2)}, u32[]{:S(2)}) collective-permute-start(bf16[256,512]{1,0:T(8,128)(2,1)} %bitcast.17), channel_id=1, source_target_pairs={{0,2},{2,4},{4,6},{6,7},{7,5},{5,3},{3,1},{1,0},{8,10},{10,12},{12... | collective-permute-start | bytes 786440 | tf_op jit(solution)/shard_map/ppermute | solution.py:53
  4.3 1.4 %collective-permute-start.9 = (bf16[128,512]{1,0:T(8,128)(2,1)}, bf16[128,512]{1,0:T(8,128)(2,1)S(1)}, u32[]{:S(2)}, u32[]{:S(2)}) collective-permute-start(bf16[128,512]{1,0:T(8,128)(2,1)} %rest_0_), channel_id=1, source_target_pairs={{16,0},{24,8},{0,16},{8,24},{17,1},{25,9},{1,17},{9,25},{18,2},{26... | collective-permute-start | bytes 393224 | tf_op jit(solution)/shard_map/ppermute | solution.py:75
  5.7 3.3 %collective-permute-done.rest_2_ = bf16[256,512]{1,0:T(8,128)(2,1)S(1)} collective-permute-done((bf16[256,512]{1,0:T(8,128)(2,1)}, bf16[256,512]{1,0:T(8,128)(2,1)S(1)}, u32[]{:S(2)}, u32[]{:S(2)}) %collective-permute-start) | collective-permute-done | bytes 262176 | tf_op jit(solution)/shard_map/ppermute | solution.py:53
  9.9 1.3 %collective-permute-start.2 = (bf16[256,512]{1,0:T(8,128)(2,1)S(1)}, bf16[256,512]{1,0:T(8,128)(2,1)S(1)}, u32[]{:S(2)}, u32[]{:S(2)}) collective-permute-start(bf16[256,512]{1,0:T(8,128)(2,1)S(1)} %collective-permute-done.rest_2_), channel_id=1, source_target_pairs={{0,2},{2,4},{4,6},{6,7},{7,5},{5,3},{3,1},{1,0},{8,10},{10,12},{12... | collective-permute-start | bytes 786440 | tf_op jit(solution)/shard_map/ppermute | solution.py:53
  11.3 3.3 %collective-permute-done.7.rest_3_ = bf16[256,512]{1,0:T(8,128)(2,1)S(1)} collective-permute-done((bf16[256,512]{1,0:T(8,128)(2,1)}, bf16[256,512]{1,0:T(8,128)(2,1)S(1)}, u32[]{:S(2)}, u32[]{:S(2)}) %collective-permute-start.7) | collective-permute-done | bytes 262176 | tf_op jit(solution)/shard_map/ppermute | solution.py:53
  15.5 1.3 %collective-permute-start.10 = (bf16[256,512]{1,0:T(8,128)(2,1)S(1)}, bf16[256,512]{1,0:T(8,128)(2,1)S(1)}, u32[]{:S(2)}, u32[]{:S(2)}) collective-permute-start(bf16[256,512]{1,0:T(8,128)(2,1)S(1)} %collective-permute-done.7.rest_3_), channel_id=1, source_target_pairs={{0,2},{2,4},{4,6},{6,7},{7,5},{5,3},{3,1},{1,0},{8,10},{10,12},{12... | collective-permute-start | bytes 786440 | tf_op jit(solution)/shard_map/ppermute | solution.py:53
  17.0 5.0 %collective-permute-start.6 = (bf16[128,2048]{1,0:T(8,128)(2,1)}, bf16[128,2048]{1,0:T(8,128)(2,1)S(1)}, u32[]{:S(2)}, u32[]{:S(2)}) collective-permute-start(bf16[128,2048]{1,0:T(8,128)(2,1)} %bitcast.24), channel_id=1, source_target_pairs={{0,24},{8,16},{16,8},{24,0},{1,25},{9,17},{17,9},{25,1},{2,26},{10... | collective-permute-start | bytes 1572872 | tf_op jit(solution)/shard_map/ppermute | solution.py:306
  22.0 2.4 %collective-permute-start.12 = (bf16[128,512]{1,0:T(8,128)(2,1)}, bf16[128,512]{1,0:T(8,128)(2,1)S(1)}, u32[]{:S(2)}, u32[]{:S(2)}) collective-permute-start(bf16[128,512]{1,0:T(8,128)(2,1)} %rest_0_), channel_id=1, source_target_pairs={{8,0},{16,24},{9,1},{17,25},{10,2},{18,26},{11,3},{19,27},{12,4},{... | collective-permute-start | bytes 393224 | tf_op jit(solution)/shard_map/ppermute | solution.py:75
  24.4 2.0 %collective-permute-start.13 = (bf16[128,512]{1,0:T(8,128)(2,1)S(1)}, bf16[128,512]{1,0:T(8,128)(2,1)S(1)}, u32[]{:S(2)}, u32[]{:S(2)}) collective-permute-start(bf16[128,512]{1,0:T(8,128)(2,1)S(1)} %collective-permute-done.9.rest_1_), channel_id=1, source_target_pairs={{8,0},{16,24},{9,1},{17,25},{10,2},{18,26},{11,3},{19,27},{12,4},{... | collective-permute-start | bytes 393224 | tf_op jit(solution)/shard_map/ppermute | solution.py:75
  26.4 1.3 %collective-permute-start.4 = (bf16[256,512]{1,0:T(8,128)(2,1)S(1)}, bf16[256,512]{1,0:T(8,128)(2,1)S(1)}, u32[]{:S(2)}, u32[]{:S(2)}) collective-permute-start(bf16[256,512]{1,0:T(8,128)(2,1)S(1)} %collective-permute-done.2.rest_6_), channel_id=1, source_target_pairs={{0,2},{2,4},{4,6},{6,7},{7,5},{5,3},{3,1},{1,0},{8,10},{10,12},{12... | collective-permute-start | bytes 786440 | tf_op jit(solution)/shard_map/ppermute | solution.py:53
  27.9 1.3 %collective-permute-start.14 = (bf16[256,512]{1,0:T(8,128)(2,1)S(1)}, bf16[256,512]{1,0:T(8,128)(2,1)S(1)}, u32[]{:S(2)}, u32[]{:S(2)}) collective-permute-start(bf16[256,512]{1,0:T(8,128)(2,1)S(1)} %collective-permute-done.10.rest_7_), channel_id=1, source_target_pairs={{0,2},{2,4},{4,6},{6,7},{7,5},{5,3},{3,1},{1,0},{8,10},{10,12},{12... | collective-permute-start | bytes 786440 | tf_op jit(solution)/shard_map/ppermute | solution.py:53
  29.4 4.2 %collective-permute-done.4.rest_10_ = bf16[256,512]{1,0:T(8,128)(2,1)S(1)} collective-permute-done((bf16[256,512]{1,0:T(8,128)(2,1)S(1)}, bf16[256,512]{1,0:T(8,128)(2,1)S(1)}, u32[]{:S(2)}, u32[]{:S(2)}) %collective-permute-start.4) | collective-permute-done | bytes 262176 | tf_op jit(solution)/shard_map/ppermute | solution.py:53
  34.9 4.3 %collective-permute-done.14.rest_11_ = bf16[256,512]{1,0:T(8,128)(2,1)S(1)} collective-permute-done((bf16[256,512]{1,0:T(8,128)(2,1)S(1)}, bf16[256,512]{1,0:T(8,128)(2,1)S(1)}, u32[]{:S(2)}, u32[]{:S(2)}) %collective-permute-start.14) | collective-permute-done | bytes 262176 | tf_op jit(solution)/shard_map/ppermute | solution.py:53
  40.0 1.3 %collective-permute-start.16 = (bf16[256,512]{1,0:T(8,128)(2,1)S(1)}, bf16[256,512]{1,0:T(8,128)(2,1)S(1)}, u32[]{:S(2)}, u32[]{:S(2)}) collective-permute-start(bf16[256,512]{1,0:T(8,128)(2,1)S(1)} %collective-permute-done.4.rest_10_), channel_id=1, source_target_pairs={{0,2},{2,4},{4,6},{6,7},{7,5},{5,3},{3,1},{1,0},{8,10},{10,12},{12... | collective-permute-start | bytes 786440 | tf_op jit(solution)/shard_map/ppermute | solution.py:60
  41.4 1.6 %copy-done = bf16[1,512,2048]{2,1,0:T(8,128)(2,1)S(1)} copy-done((bf16[1,512,2048]{2,1,0:T(8,128)(2,1)S(1)}, bf16[1,512,2048]{2,1,0:T(8,128)(2,1)}, u32[]{:S(2)}) %copy-start) | copy-done | bytes 2097176
  45.7 1.1 %collective-permute-done.17.rest_15_ = bf16[256,512]{1,0:T(8,128)(2,1)S(1)} collective-permute-done((bf16[256,512]{1,0:T(8,128)(2,1)S(1)}, bf16[256,512]{1,0:T(8,128)(2,1)S(1)}, u32[]{:S(2)}, u32[]{:S(2)}) %collective-permute-start.17) | collective-permute-done | bytes 262176 | tf_op jit(solution)/shard_map/ppermute | solution.py:60
  46.8 0.9 first_tick.1
  48.4 4.3 %collective-permute-start.19 = (bf16[512,128]{1,0:T(8,128)(2,1)S(1)}, bf16[512,128]{1,0:T(8,128)(2,1)S(1)}, u32[]{:S(2)}, u32[]{:S(2)}) collective-permute-start(bf16[512,128]{1,0:T(8,128)(2,1)S(1)} %get-tuple-element.75), channel_id=1, source_target_pairs={{0,8},{8,16},{16,24},{24,0},{1,9},{9,17},{17,25},{25,1},{2,10},{10... | collective-permute-start | bytes 393224 | tf_op jit(solution)/shard_map/ppermute | solution.py:364
  52.8 1.9 %collective-permute-done.19.scored = bf16[512,128]{1,0:T(8,128)(2,1)S(1)} collective-permute-done((bf16[512,128]{1,0:T(8,128)(2,1)S(1)}, bf16[512,128]{1,0:T(8,128)(2,1)S(1)}, u32[]{:S(2)}, u32[]{:S(2)}) %collective-permute-start.19) | collective-permute-done | bytes 131104 | tf_op jit(solution)/shard_map/ppermute | solution.py:364
  54.7 1.3 %collective-permute-start.20 = (bf16[128,2048]{1,0:T(8,128)(2,1)S(1)}, bf16[128,2048]{1,0:T(8,128)(2,1)S(1)}, u32[]{:S(2)}, u32[]{:S(2)}) collective-permute-start(bf16[128,2048]{1,0:T(8,128)(2,1)S(1)} %tick.3.held), channel_id=1, source_target_pairs={{16,8},{17,9},{18,10},{19,11},{20,12},{21,13},{22,14},{23,15}} | collective-permute-start | bytes 1572872 | tf_op jit(solution)/shard_map/ppermute | solution.py:382
  56.0 9.6 %collective-permute-done.20.grad = bf16[128,2048]{1,0:T(8,128)(2,1)S(1)} collective-permute-done((bf16[128,2048]{1,0:T(8,128)(2,1)S(1)}, bf16[128,2048]{1,0:T(8,128)(2,1)S(1)}, u32[]{:S(2)}, u32[]{:S(2)}) %collective-permute-start.20) | collective-permute-done | bytes 524320 | tf_op jit(solution)/shard_map/ppermute | solution.py:382
  65.6 2.2 %tick.4.held.grad = bf16[128,2048]{1,0:T(8,128)(2,1)S(1)} custom-call(bf16[128,2048]{1,0:T(8,128)(2,1)S(1)} %collective-permute-done.20.grad, bf16[128,2048]{1,0:T(8,128)(2,1)S(1)} %tick.3.held, bf16[512,2048]{1,0:T(8,128)(2,1)S(1)} %bitcast.9, bf16[1,2048]{1,0:T(2,128)(2,1)S(1)} %copy-done.4, f32[128,512]{1,0:T(8,128)S(1)} %get-tuple-element.72.a, ...), custom_call_target="tpu_custom_call" | custom-call | flops 805306368 | bytes 4194304 | tf_op jit(solution)/shard_map/tick/pallas_call | solution.py:367
  68.2 1.1 %collective-permute-start.25 = (bf16[128,1024]{1,0:T(8,128)(2,1)S(1)}, bf16[128,1024]{1,0:T(8,128)(2,1)S(1)}, u32[]{:S(2)}, u32[]{:S(2)}) collective-permute-start(bf16[128,1024]{1,0:T(8,128)(2,1)S(1)} %get-tuple-element.86), channel_id=1, source_target_pairs={{0,2},{1,3},{2,0},{3,1},{4,6},{5,7},{6,4},{7,5},{8,10},{9,11},{10,... | collective-permute-start | bytes 786440 | tf_op jit(solution)/shard_map/ppermute | solution.py:241
  69.3 1.5 %collective-permute-start.22 = (bf16[256,128]{1,0:T(8,128)(2,1)S(1)}, bf16[256,128]{1,0:T(8,128)(2,1)S(1)}, u32[]{:S(2)}, u32[]{:S(2)}) collective-permute-start(bf16[256,128]{1,0:T(8,128)(2,1)S(1)} %get-tuple-element.78), channel_id=1, source_target_pairs={{0,1},{1,0},{2,3},{3,2},{4,5},{5,4},{6,7},{7,6},{8,9},{9,8},{10,11... | collective-permute-start | bytes 196616 | tf_op jit(solution)/shard_map/ppermute | solution.py:241
  70.9 5.2 %collective-permute-done.22.rest_0_ = bf16[256,128]{1,0:T(8,128)(2,1)S(1)} collective-permute-done((bf16[256,128]{1,0:T(8,128)(2,1)S(1)}, bf16[256,128]{1,0:T(8,128)(2,1)S(1)}, u32[]{:S(2)}, u32[]{:S(2)}) %collective-permute-start.22) | collective-permute-done | bytes 65568 | tf_op jit(solution)/shard_map/ppermute | solution.py:241
  76.9 1.0 %collective-permute-start.26 = (bf16[128,1024]{1,0:T(8,128)(2,1)S(1)}, bf16[128,1024]{1,0:T(8,128)(2,1)S(1)}, u32[]{:S(2)}, u32[]{:S(2)}) collective-permute-start(bf16[128,1024]{1,0:T(8,128)(2,1)S(1)} %get-tuple-element.82), channel_id=1, source_target_pairs={{0,2},{1,3},{2,0},{3,1},{4,6},{5,7},{6,4},{7,5},{8,10},{9,11},{10,... | collective-permute-start | bytes 786440 | tf_op jit(solution)/shard_map/ppermute | solution.py:241
  78.8 1.3 %collective-permute-start.21 = (bf16[128,2048]{1,0:T(8,128)(2,1)S(1)}, bf16[128,2048]{1,0:T(8,128)(2,1)S(1)}, u32[]{:S(2)}, u32[]{:S(2)}) collective-permute-start(bf16[128,2048]{1,0:T(8,128)(2,1)S(1)} %tick.4.held.grad), channel_id=1, source_target_pairs={{8,0},{9,1},{10,2},{11,3},{12,4},{13,5},{14,6},{15,7}} | collective-permute-start | bytes 1572872 | tf_op jit(solution)/shard_map/ppermute | solution.py:382
  80.1 4.2 %collective-permute-done.26.refs_2_ = bf16[128,1024]{1,0:T(8,128)(2,1)S(1)} collective-permute-done((bf16[128,1024]{1,0:T(8,128)(2,1)S(1)}, bf16[128,1024]{1,0:T(8,128)(2,1)S(1)}, u32[]{:S(2)}, u32[]{:S(2)}) %collective-permute-start.26) | collective-permute-done | bytes 262176 | tf_op jit(solution)/shard_map/ppermute | solution.py:241
  84.4 1.9 %collective-permute-start.28 = (bf16[64,2048]{1,0:T(8,128)(2,1)S(1)}, bf16[64,2048]{1,0:T(8,128)(2,1)S(1)}, u32[]{:S(2)}, u32[]{:S(2)}) collective-permute-start(bf16[64,2048]{1,0:T(8,128)(2,1)S(1)} %get-tuple-element.85), channel_id=1, source_target_pairs={{0,4},{1,5},{2,6},{3,7},{4,0},{5,1},{6,2},{7,3},{8,12},{9,13},{10,... | collective-permute-start | bytes 786440 | tf_op jit(solution)/shard_map/ppermute | solution.py:241
  86.3 7.1 %collective-permute-done.28.refs_1_ = bf16[64,2048]{1,0:T(8,128)(2,1)S(1)} collective-permute-done((bf16[64,2048]{1,0:T(8,128)(2,1)S(1)}, bf16[64,2048]{1,0:T(8,128)(2,1)S(1)}, u32[]{:S(2)}, u32[]{:S(2)}) %collective-permute-start.28) | collective-permute-done | bytes 262176 | tf_op jit(solution)/shard_map/ppermute | solution.py:241
  94.4 4.9 %collective-permute-done.29 = bf16[64,2048]{1,0:T(8,128)(2,1)S(1)} collective-permute-done((bf16[64,2048]{1,0:T(8,128)(2,1)S(1)}, bf16[64,2048]{1,0:T(8,128)(2,1)S(1)}, u32[]{:S(2)}, u32[]{:S(2)}) %collective-permute-start.29) | collective-permute-done | bytes 262176 | tf_op jit(solution)/shard_map/ppermute | solution.py:387
  (52 shorter events, 12.1 us)
Async XLA Ops:
  0.6 8.4 %collective-permute-start = (bf16[256,512]{1,0:T(8,128)(2,1)}, bf16[256,512]{1,0:T(8,128)(2,1)S(1)}, u32[]{:S(2)}, u32[]{:S(2)}) collective-permute-start(bf16[256,512]{1,0:T(8,128)(2,1)} %bitcast.11), channel_id=1, source_target_pairs={{0,2},{2,4},{4,6},{6,7},{7,5},{5,3},{3,1},{1,0},{8,10},{10,12},{12... | collective-permute-start | bytes 786440 | tf_op jit(solution)/shard_map/ppermute | solution.py:53
  2.8 7.1 %collective-permute-start.1 = (bf16[256,512]{1,0:T(8,128)(2,1)}, bf16[256,512]{1,0:T(8,128)(2,1)S(1)}, u32[]{:S(2)}, u32[]{:S(2)}) collective-permute-start(bf16[256,512]{1,0:T(8,128)(2,1)} %bitcast.12), channel_id=1, source_target_pairs={{2,0},{4,2},{6,4},{7,6},{5,7},{3,5},{1,3},{0,1},{10,8},{12,10},{14... | collective-permute-start | bytes 786440 | tf_op jit(solution)/shard_map/ppermute | solution.py:53
  2.8 11.8 %collective-permute-start.7 = (bf16[256,512]{1,0:T(8,128)(2,1)}, bf16[256,512]{1,0:T(8,128)(2,1)S(1)}, u32[]{:S(2)}, u32[]{:S(2)}) collective-permute-start(bf16[256,512]{1,0:T(8,128)(2,1)} %bitcast.17), channel_id=1, source_target_pairs={{0,2},{2,4},{4,6},{6,7},{7,5},{5,3},{3,1},{1,0},{8,10},{10,12},{12... | collective-permute-start | bytes 786440 | tf_op jit(solution)/shard_map/ppermute | solution.py:53
  4.3 11.2 %collective-permute-start.8 = (bf16[256,512]{1,0:T(8,128)(2,1)}, bf16[256,512]{1,0:T(8,128)(2,1)S(1)}, u32[]{:S(2)}, u32[]{:S(2)}) collective-permute-start(bf16[256,512]{1,0:T(8,128)(2,1)} %bitcast.18), channel_id=1, source_target_pairs={{2,0},{4,2},{6,4},{7,6},{5,7},{3,5},{1,3},{0,1},{10,8},{12,10},{14... | collective-permute-start | bytes 786440 | tf_op jit(solution)/shard_map/ppermute | solution.py:53
  4.3 11.2 %collective-permute-start.9 = (bf16[128,512]{1,0:T(8,128)(2,1)}, bf16[128,512]{1,0:T(8,128)(2,1)S(1)}, u32[]{:S(2)}, u32[]{:S(2)}) collective-permute-start(bf16[128,512]{1,0:T(8,128)(2,1)} %rest_0_), channel_id=1, source_target_pairs={{16,0},{24,8},{0,16},{8,24},{17,1},{25,9},{1,17},{9,25},{18,2},{26... | collective-permute-start | bytes 393224 | tf_op jit(solution)/shard_map/ppermute | solution.py:75
  9.9 12.1 %collective-permute-start.2 = (bf16[256,512]{1,0:T(8,128)(2,1)S(1)}, bf16[256,512]{1,0:T(8,128)(2,1)S(1)}, u32[]{:S(2)}, u32[]{:S(2)}) collective-permute-start(bf16[256,512]{1,0:T(8,128)(2,1)S(1)} %collective-permute-done.rest_2_), channel_id=1, source_target_pairs={{0,2},{2,4},{4,6},{6,7},{7,5},{5,3},{3,1},{1,0},{8,10},{10,12},{12... | collective-permute-start | bytes 786440 | tf_op jit(solution)/shard_map/ppermute | solution.py:53
  11.2 13.2 %collective-permute-start.3 = (bf16[256,512]{1,0:T(8,128)(2,1)S(1)}, bf16[256,512]{1,0:T(8,128)(2,1)S(1)}, u32[]{:S(2)}, u32[]{:S(2)}) collective-permute-start(bf16[256,512]{1,0:T(8,128)(2,1)S(1)} %collective-permute-done.1.rest_4_), channel_id=1, source_target_pairs={{2,0},{4,2},{6,4},{7,6},{5,7},{3,5},{1,3},{0,1},{10,8},{12,10},{14... | collective-permute-start | bytes 786440 | tf_op jit(solution)/shard_map/ppermute | solution.py:53
  15.5 10.9 %collective-permute-start.10 = (bf16[256,512]{1,0:T(8,128)(2,1)S(1)}, bf16[256,512]{1,0:T(8,128)(2,1)S(1)}, u32[]{:S(2)}, u32[]{:S(2)}) collective-permute-start(bf16[256,512]{1,0:T(8,128)(2,1)S(1)} %collective-permute-done.7.rest_3_), channel_id=1, source_target_pairs={{0,2},{2,4},{4,6},{6,7},{7,5},{5,3},{3,1},{1,0},{8,10},{10,12},{12... | collective-permute-start | bytes 786440 | tf_op jit(solution)/shard_map/ppermute | solution.py:53
  16.8 10.9 %collective-permute-start.11 = (bf16[256,512]{1,0:T(8,128)(2,1)S(1)}, bf16[256,512]{1,0:T(8,128)(2,1)S(1)}, u32[]{:S(2)}, u32[]{:S(2)}) collective-permute-start(bf16[256,512]{1,0:T(8,128)(2,1)S(1)} %collective-permute-done.8.rest_5_), channel_id=1, source_target_pairs={{2,0},{4,2},{6,4},{7,6},{5,7},{3,5},{1,3},{0,1},{10,8},{12,10},{14... | collective-permute-start | bytes 786440 | tf_op jit(solution)/shard_map/ppermute | solution.py:53
  17.0 17.9 %collective-permute-start.6 = (bf16[128,2048]{1,0:T(8,128)(2,1)}, bf16[128,2048]{1,0:T(8,128)(2,1)S(1)}, u32[]{:S(2)}, u32[]{:S(2)}) collective-permute-start(bf16[128,2048]{1,0:T(8,128)(2,1)} %bitcast.24), channel_id=1, source_target_pairs={{0,24},{8,16},{16,8},{24,0},{1,25},{9,17},{17,9},{25,1},{2,26},{10... | collective-permute-start | bytes 1572872 | tf_op jit(solution)/shard_map/ppermute | solution.py:306
  22.0 5.9 %collective-permute-start.12 = (bf16[128,512]{1,0:T(8,128)(2,1)}, bf16[128,512]{1,0:T(8,128)(2,1)S(1)}, u32[]{:S(2)}, u32[]{:S(2)}) collective-permute-start(bf16[128,512]{1,0:T(8,128)(2,1)} %rest_0_), channel_id=1, source_target_pairs={{8,0},{16,24},{9,1},{17,25},{10,2},{18,26},{11,3},{19,27},{12,4},{... | collective-permute-start | bytes 393224 | tf_op jit(solution)/shard_map/ppermute | solution.py:75
  24.4 3.5 %collective-permute-start.13 = (bf16[128,512]{1,0:T(8,128)(2,1)S(1)}, bf16[128,512]{1,0:T(8,128)(2,1)S(1)}, u32[]{:S(2)}, u32[]{:S(2)}) collective-permute-start(bf16[128,512]{1,0:T(8,128)(2,1)S(1)} %collective-permute-done.9.rest_1_), channel_id=1, source_target_pairs={{8,0},{16,24},{9,1},{17,25},{10,2},{18,26},{11,3},{19,27},{12,4},{... | collective-permute-start | bytes 393224 | tf_op jit(solution)/shard_map/ppermute | solution.py:75
  26.4 7.2 %collective-permute-start.4 = (bf16[256,512]{1,0:T(8,128)(2,1)S(1)}, bf16[256,512]{1,0:T(8,128)(2,1)S(1)}, u32[]{:S(2)}, u32[]{:S(2)}) collective-permute-start(bf16[256,512]{1,0:T(8,128)(2,1)S(1)} %collective-permute-done.2.rest_6_), channel_id=1, source_target_pairs={{0,2},{2,4},{4,6},{6,7},{7,5},{5,3},{3,1},{1,0},{8,10},{10,12},{12... | collective-permute-start | bytes 786440 | tf_op jit(solution)/shard_map/ppermute | solution.py:53
  27.7 6.6 %collective-permute-start.5 = (bf16[256,512]{1,0:T(8,128)(2,1)S(1)}, bf16[256,512]{1,0:T(8,128)(2,1)S(1)}, u32[]{:S(2)}, u32[]{:S(2)}) collective-permute-start(bf16[256,512]{1,0:T(8,128)(2,1)S(1)} %collective-permute-done.3.rest_8_), channel_id=1, source_target_pairs={{2,0},{4,2},{6,4},{7,6},{5,7},{3,5},{1,3},{0,1},{10,8},{12,10},{14... | collective-permute-start | bytes 786440 | tf_op jit(solution)/shard_map/ppermute | solution.py:53
  27.9 11.3 %collective-permute-start.14 = (bf16[256,512]{1,0:T(8,128)(2,1)S(1)}, bf16[256,512]{1,0:T(8,128)(2,1)S(1)}, u32[]{:S(2)}, u32[]{:S(2)}) collective-permute-start(bf16[256,512]{1,0:T(8,128)(2,1)S(1)} %collective-permute-done.10.rest_7_), channel_id=1, source_target_pairs={{0,2},{2,4},{4,6},{6,7},{7,5},{5,3},{3,1},{1,0},{8,10},{10,12},{12... | collective-permute-start | bytes 786440 | tf_op jit(solution)/shard_map/ppermute | solution.py:53
  29.2 10.8 %collective-permute-start.15 = (bf16[256,512]{1,0:T(8,128)(2,1)S(1)}, bf16[256,512]{1,0:T(8,128)(2,1)S(1)}, u32[]{:S(2)}, u32[]{:S(2)}) collective-permute-start(bf16[256,512]{1,0:T(8,128)(2,1)S(1)} %collective-permute-done.11.rest_9_), channel_id=1, source_target_pairs={{2,0},{4,2},{6,4},{7,6},{5,7},{3,5},{1,3},{0,1},{10,8},{12,10},{14... | collective-permute-start | bytes 786440 | tf_op jit(solution)/shard_map/ppermute | solution.py:53
  40.0 5.7 %collective-permute-start.16 = (bf16[256,512]{1,0:T(8,128)(2,1)S(1)}, bf16[256,512]{1,0:T(8,128)(2,1)S(1)}, u32[]{:S(2)}, u32[]{:S(2)}) collective-permute-start(bf16[256,512]{1,0:T(8,128)(2,1)S(1)} %collective-permute-done.4.rest_10_), channel_id=1, source_target_pairs={{0,2},{2,4},{4,6},{6,7},{7,5},{5,3},{3,1},{1,0},{8,10},{10,12},{12... | collective-permute-start | bytes 786440 | tf_op jit(solution)/shard_map/ppermute | solution.py:60
  41.3 5.5 %collective-permute-start.17 = (bf16[256,512]{1,0:T(8,128)(2,1)S(1)}, bf16[256,512]{1,0:T(8,128)(2,1)S(1)}, u32[]{:S(2)}, u32[]{:S(2)}) collective-permute-start(bf16[256,512]{1,0:T(8,128)(2,1)S(1)} %collective-permute-done.15.rest_13_), channel_id=1, source_target_pairs={{2,0},{4,2},{6,4},{7,6},{5,7},{3,5},{1,3},{0,1},{10,8},{12,10},{14... | collective-permute-start | bytes 786440 | tf_op jit(solution)/shard_map/ppermute | solution.py:60
  43.9 2.9 %copy-start.3 = (bf16[1,256,512]{2,1,0:T(8,128)(2,1)S(1)}, bf16[1,256,512]{2,1,0:T(8,128)(2,1)}, u32[]{:S(2)}) copy-start(bf16[1,256,512]{2,1,0:T(8,128)(2,1)} %param.9) | copy-start | bytes 786436
  46.8 6.0 %copy-start.1 = (bf16[1,512,2048]{2,1,0:T(8,128)(2,1)S(1)}, bf16[1,512,2048]{2,1,0:T(8,128)(2,1)}, u32[]{:S(2)}) copy-start(bf16[1,512,2048]{2,1,0:T(8,128)(2,1)} %param.10) | copy-start | bytes 6291460
  47.7 5.0 %collective-permute-start.18 = (bf16[128,2048]{1,0:T(8,128)(2,1)S(1)}, bf16[128,2048]{1,0:T(8,128)(2,1)S(1)}, u32[]{:S(2)}, u32[]{:S(2)}) collective-permute-start(bf16[128,2048]{1,0:T(8,128)(2,1)S(1)} %get-tuple-element.71.held), channel_id=1, source_target_pairs={{24,16},{25,17},{26,18},{27,19},{28,20},{29,21},{30,22},{31,23}} | collective-permute-start | bytes 1572872 | tf_op jit(solution)/shard_map/ppermute | solution.py:382
  48.4 6.3 %collective-permute-start.19 = (bf16[512,128]{1,0:T(8,128)(2,1)S(1)}, bf16[512,128]{1,0:T(8,128)(2,1)S(1)}, u32[]{:S(2)}, u32[]{:S(2)}) collective-permute-start(bf16[512,128]{1,0:T(8,128)(2,1)S(1)} %get-tuple-element.75), channel_id=1, source_target_pairs={{0,8},{8,16},{16,24},{24,0},{1,9},{9,17},{17,25},{25,1},{2,10},{10... | collective-permute-start | bytes 393224 | tf_op jit(solution)/shard_map/ppermute | solution.py:364
  54.7 10.9 %collective-permute-start.20 = (bf16[128,2048]{1,0:T(8,128)(2,1)S(1)}, bf16[128,2048]{1,0:T(8,128)(2,1)S(1)}, u32[]{:S(2)}, u32[]{:S(2)}) collective-permute-start(bf16[128,2048]{1,0:T(8,128)(2,1)S(1)} %tick.3.held), channel_id=1, source_target_pairs={{16,8},{17,9},{18,10},{19,11},{20,12},{21,13},{22,14},{23,15}} | collective-permute-start | bytes 1572872 | tf_op jit(solution)/shard_map/ppermute | solution.py:382
  67.9 8.3 %collective-permute-start.24 = (bf16[128,1024]{1,0:T(8,128)(2,1)S(1)}, bf16[128,1024]{1,0:T(8,128)(2,1)S(1)}, u32[]{:S(2)}, u32[]{:S(2)}) collective-permute-start(bf16[128,1024]{1,0:T(8,128)(2,1)S(1)} %get-tuple-element.87), channel_id=1, source_target_pairs={{0,1},{1,0},{2,3},{3,2},{4,5},{5,4},{6,7},{7,6},{8,9},{9,8},{10,11... | collective-permute-start | bytes 786440 | tf_op jit(solution)/shard_map/ppermute | solution.py:241
  68.2 7.9 %collective-permute-start.25 = (bf16[128,1024]{1,0:T(8,128)(2,1)S(1)}, bf16[128,1024]{1,0:T(8,128)(2,1)S(1)}, u32[]{:S(2)}, u32[]{:S(2)}) collective-permute-start(bf16[128,1024]{1,0:T(8,128)(2,1)S(1)} %get-tuple-element.86), channel_id=1, source_target_pairs={{0,2},{1,3},{2,0},{3,1},{4,6},{5,7},{6,4},{7,5},{8,10},{9,11},{10,... | collective-permute-start | bytes 786440 | tf_op jit(solution)/shard_map/ppermute | solution.py:241
  69.3 6.8 %collective-permute-start.22 = (bf16[256,128]{1,0:T(8,128)(2,1)S(1)}, bf16[256,128]{1,0:T(8,128)(2,1)S(1)}, u32[]{:S(2)}, u32[]{:S(2)}) collective-permute-start(bf16[256,128]{1,0:T(8,128)(2,1)S(1)} %get-tuple-element.78), channel_id=1, source_target_pairs={{0,1},{1,0},{2,3},{3,2},{4,5},{5,4},{6,7},{7,6},{8,9},{9,8},{10,11... | collective-permute-start | bytes 196616 | tf_op jit(solution)/shard_map/ppermute | solution.py:241
  70.8 5.4 %collective-permute-start.23 = (bf16[256,128]{1,0:T(8,128)(2,1)S(1)}, bf16[256,128]{1,0:T(8,128)(2,1)S(1)}, u32[]{:S(2)}, u32[]{:S(2)}) collective-permute-start(bf16[256,128]{1,0:T(8,128)(2,1)S(1)} %get-tuple-element.79), channel_id=1, source_target_pairs={{0,2},{1,3},{2,0},{3,1},{4,6},{5,7},{6,4},{7,5},{8,10},{9,11},{10,... | collective-permute-start | bytes 196616 | tf_op jit(solution)/shard_map/ppermute | solution.py:241
  76.9 7.4 %collective-permute-start.26 = (bf16[128,1024]{1,0:T(8,128)(2,1)S(1)}, bf16[128,1024]{1,0:T(8,128)(2,1)S(1)}, u32[]{:S(2)}, u32[]{:S(2)}) collective-permute-start(bf16[128,1024]{1,0:T(8,128)(2,1)S(1)} %get-tuple-element.82), channel_id=1, source_target_pairs={{0,2},{1,3},{2,0},{3,1},{4,6},{5,7},{6,4},{7,5},{8,10},{9,11},{10,... | collective-permute-start | bytes 786440 | tf_op jit(solution)/shard_map/ppermute | solution.py:241
  77.9 6.4 %collective-permute-start.27 = (bf16[128,1024]{1,0:T(8,128)(2,1)S(1)}, bf16[128,1024]{1,0:T(8,128)(2,1)S(1)}, u32[]{:S(2)}, u32[]{:S(2)}) collective-permute-start(bf16[128,1024]{1,0:T(8,128)(2,1)S(1)} %get-tuple-element.83), channel_id=1, source_target_pairs={{0,1},{1,0},{2,3},{3,2},{4,5},{5,4},{6,7},{7,6},{8,9},{9,8},{10,11... | collective-permute-start | bytes 786440 | tf_op jit(solution)/shard_map/ppermute | solution.py:241
  78.8 14.7 %collective-permute-start.21 = (bf16[128,2048]{1,0:T(8,128)(2,1)S(1)}, bf16[128,2048]{1,0:T(8,128)(2,1)S(1)}, u32[]{:S(2)}, u32[]{:S(2)}) collective-permute-start(bf16[128,2048]{1,0:T(8,128)(2,1)S(1)} %tick.4.held.grad), channel_id=1, source_target_pairs={{8,0},{9,1},{10,2},{11,3},{12,4},{13,5},{14,6},{15,7}} | collective-permute-start | bytes 1572872 | tf_op jit(solution)/shard_map/ppermute | solution.py:382
  84.4 9.0 %collective-permute-start.28 = (bf16[64,2048]{1,0:T(8,128)(2,1)S(1)}, bf16[64,2048]{1,0:T(8,128)(2,1)S(1)}, u32[]{:S(2)}, u32[]{:S(2)}) collective-permute-start(bf16[64,2048]{1,0:T(8,128)(2,1)S(1)} %get-tuple-element.85), channel_id=1, source_target_pairs={{0,4},{1,5},{2,6},{3,7},{4,0},{5,1},{6,2},{7,3},{8,12},{9,13},{10,... | collective-permute-start | bytes 786440 | tf_op jit(solution)/shard_map/ppermute | solution.py:241
  93.4 5.8 %collective-permute-start.29 = (bf16[64,2048]{1,0:T(8,128)(2,1)S(1)}, bf16[64,2048]{1,0:T(8,128)(2,1)S(1)}, u32[]{:S(2)}, u32[]{:S(2)}) collective-permute-start(bf16[64,2048]{1,0:T(8,128)(2,1)S(1)} %total.1), channel_id=1, source_target_pairs={{8,0},{16,8},{24,16},{0,24},{9,1},{17,9},{25,17},{1,25},{10,2},{18... | collective-permute-start | bytes 786440 | tf_op jit(solution)/shard_map/ppermute | solution.py:387
  (4 other events, 6.2 us)

commit v4 on v3

--- a/solution.py
+++ b/solution.py
@@ -218,22 +218,23 @@
 
 
 def combine_kernel(bit, count, *refs):
-    keeps, gots, outs = refs[:count], refs[count : 2 * count], refs[2 * count :]
+    keeps, gots, (send, kept) = refs[:count], refs[count : 2 * count], refs[2 * count :]
     width = keeps[0].shape[1]
+    half = send.shape[0]
+    own = lax.axis_index("dp") >> bit & 1
     for i, (keep, got) in enumerate(zip(keeps, gots)):
         columns = slice(i * width, (i + 1) * width)
-        if bit is None:
-            outs[0][:, columns] = (keep[...] + got[...].astype(F32)).astype(BF16)
-            continue
-        half = keep.shape[0] // 2
-        own = lax.axis_index("dp") >> bit & 1
 
         def rows(which):
             where = pl.ds(pl.multiple_of(which * half, half), half)
             return keep[where, :] + got[where, :].astype(F32)
 
-        outs[0][:, columns] = rows(1 - own).astype(BF16)
-        outs[1][:, columns] = rows(own)
+        send[:, columns] = rows(1 - own).astype(BF16)
+        kept[:, columns] = rows(own).astype(kept.dtype)
+
+
+def finish_kernel(factor, first, second, out):
+    out[...] = (first[...].astype(F32) + second[...].astype(F32)) * factor
 
 
 def along(bit, *values):
@@ -274,12 +275,22 @@
     gots = [*along(1, sends[0]), *along(0, sends[1])]
     for bit in range(size.bit_length() - 2, 1, -1):
         rows //= 2
-        outs = [shape((rows, width), BF16), shape((rows, width), F32)]
+        outs = [shape((rows, width), BF16), shape((rows, width), BF16 if bit == 2 else F32)]
         kernel = functools.partial(combine_kernel, bit, len(keeps))
         send, keep = call(kernel, "combine", outs, 0, *keeps, *gots)
+        if bit == 2:
+            return send, keep
         keeps, gots = [keep], along(bit, send)
-    kernel = functools.partial(combine_kernel, None, len(keeps))
-    return call(kernel, "total", [shape((rows, width), BF16)], 0, *keeps, *gots)[0]
+
+
+def to_layer(value, flip):
+    sections, size = lax.axis_size("section"), lax.axis_size("dp")
+    pairs = [
+        (s * size + d, (s - 1) % sections * size + (d ^ flip))
+        for s in range(sections)
+        for d in range(size)
+    ]
+    return lax.ppermute(value, ("section", "dp"), pairs)
 
 
 def on_device(stash, cotangent, gate_weight, up_weight, down_weight, shared_gate):
@@ -374,19 +385,23 @@
             name="tick",
         )(grad, held, down_full, shared_gate, *scales, *flat)
 
+    swap = [(i, i ^ 1) for i in range(sections)]
     for section in range(sections - 2, -1, -1):
         if section == 0:
             reduced = reduce_rows(scored, theirs, outgoing)
         if section == sections - 3:
             outgoing, scored = after((outgoing, scored))
-        grad = lax.ppermute(outgoing, "section", [(section + 1, section)])
+        pairs = swap if section == sections - 2 else [(section + 1, section)]
+        grad = lax.ppermute(outgoing, "section", pairs)
         if section == max(sections - 3, 0):
-            theirs = swap_scored(scored)
+            grad, theirs = after((grad, swap_scored(scored)))
         outgoing = tick(section, grad, outgoing)
 
-    reduced = lax.ppermute(reduced, "section", [(b, a) for a, b in around])
-    norm_factor = (local_rows * replicas) ** (-0.5)
-    return (outgoing[None], (reduced.astype(F32) * norm_factor)[None])
+    send, keep = reduced
+    kernel = functools.partial(finish_kernel, (local_rows * replicas) ** (-0.5))
+    outs = [shape(keep.shape, F32)]
+    summed = call(kernel, "finish", outs, 0, to_layer(send, 4), to_layer(keep, 0))[0]
+    return (outgoing[None], summed[None])
 
 
 def solution(mesh):

time: 100 us -> 97.3 us (0.973)
  waiting for transfers between devices: 53.6 us -> 51.9 us
  starting transfers between devices: 36.3 us -> 35 us
    ppermute x7 -> x6, waiting for transfers between devices: 16.5 us -> 8.26 us  [along(): return [lax.ppermute(v, 'dp', pairs) for v in values]]
    ppermute x4 -> x5, waiting for transfers between devices: 14.5 us -> 22 us  [the longest x2 14.8 us: to_layer(): return lax.ppermute(value, ('section', 'dp'), pairs)]
    ppermute x1, starting transfers between devices: 4.31 us -> 0.5 us  [on_device(): scored = lax.ppermute(scored, 'section', around)]
    ppermute x4 -> x5, starting transfers between devices: 3.34 us -> 6 us  [the longest x3 5.88 us: on_device(): grad = lax.ppermute(outgoing, 'section', pairs)]
    ppermute x1, waiting for transfers between devices: 1.9 us -> 0.86 us  [on_device(): scored = lax.ppermute(scored, 'section', around)]
    ppermute x7 -> x6, starting transfers between devices: 6.89 us -> 6.76 us  [along(): return [lax.ppermute(v, 'dp', pairs) for v in values]]
  transfers between devices with their start and end apart: 30 -> 30, of which waited for: 17 -> 21; matrix products, arithmetic and copies ran while one was open for 0% -> 0% of each run, Pallas kernels for 2% -> 3%
where the time goes in v4:
time: 97.3 us; the launch traced here: 97.1 us
  waiting for transfers between devices  51.9 us (53%)
  starting transfers between devices  35 us (36%)
  Pallas kernels  6.78 us (7%)
  local copies, waits for them, and re-layouts  2.55 us (3%)
    ppermute x12, waiting for transfers between devices, gather_ring(): both = (lax.ppermute(v, axis, ahead), lax.ppermute(w, axis, back))  18.4 us
    ppermute x2, waiting for transfers between devices, to_layer(): return lax.ppermute(value, ('section', 'dp'), pairs)  14.8 us
    ppermute x12, starting transfers between devices, gather_ring(): both = (lax.ppermute(v, axis, ahead), lax.ppermute(w, axis, back))  9.57 us
    ppermute x6, waiting for transfers between devices, along(): return [lax.ppermute(v, 'dp', pairs) for v in values]  8.26 us
    ppermute x3, waiting for transfers between devices, on_device(): grad = lax.ppermute(outgoing, 'section', pairs)  7.24 us
    ppermute x6, starting transfers between devices, along(): return [lax.ppermute(v, 'dp', pairs) for v in values]  6.76 us
    ppermute x3, starting transfers between devices, on_device(): grad = lax.ppermute(outgoing, 'section', pairs)  5.88 us
    ppermute x3, starting transfers between devices, gather_to_ends(): held += [lax.ppermute(block, axis, pairs) for block in list(held)]  5.74 us
  transfers between devices with their start and end apart: 30, of which 21 were waited for; matrix products, arithmetic and copies ran while one was open for 0% of the time, Pallas kernels for 3%

profile of v4, /device:TPU:1, one launch (start us, length us, event | category | flops | bytes accessed | tf_op | source)
XLA Modules:
  0.0 97.1 jit_solution(15268225579232680894)
XLA Ops:
  0.6 2.2 %collective-permute-start = (bf16[256,512]{1,0:T(8,128)(2,1)}, bf16[256,512]{1,0:T(8,128)(2,1)S(1)}, u32[]{:S(2)}, u32[]{:S(2)}) collective-permute-start(bf16[256,512]{1,0:T(8,128)(2,1)} %bitcast.10), channel_id=1, source_target_pairs={{0,2},{2,4},{4,6},{6,7},{7,5},{5,3},{3,1},{1,0},{8,10},{10,12},{12... | collective-permute-start | bytes 786440 | tf_op jit(solution)/shard_map/ppermute | solution.py:53
  2.8 1.5 %collective-permute-start.7 = (bf16[256,512]{1,0:T(8,128)(2,1)}, bf16[256,512]{1,0:T(8,128)(2,1)S(1)}, u32[]{:S(2)}, u32[]{:S(2)}) collective-permute-start(bf16[256,512]{1,0:T(8,128)(2,1)} %bitcast.16), channel_id=1, source_target_pairs={{0,2},{2,4},{4,6},{6,7},{7,5},{5,3},{3,1},{1,0},{8,10},{10,12},{12... | collective-permute-start | bytes 786440 | tf_op jit(solution)/shard_map/ppermute | solution.py:53
  4.3 1.4 %collective-permute-start.9 = (bf16[128,512]{1,0:T(8,128)(2,1)}, bf16[128,512]{1,0:T(8,128)(2,1)S(1)}, u32[]{:S(2)}, u32[]{:S(2)}) collective-permute-start(bf16[128,512]{1,0:T(8,128)(2,1)} %rest_0_), channel_id=1, source_target_pairs={{16,0},{24,8},{0,16},{8,24},{17,1},{25,9},{1,17},{9,25},{18,2},{26... | collective-permute-start | bytes 393224 | tf_op jit(solution)/shard_map/ppermute | solution.py:75
  5.7 3.3 %collective-permute-done.rest_2_ = bf16[256,512]{1,0:T(8,128)(2,1)S(1)} collective-permute-done((bf16[256,512]{1,0:T(8,128)(2,1)}, bf16[256,512]{1,0:T(8,128)(2,1)S(1)}, u32[]{:S(2)}, u32[]{:S(2)}) %collective-permute-start) | collective-permute-done | bytes 262176 | tf_op jit(solution)/shard_map/ppermute | solution.py:53
  9.9 1.3 %collective-permute-start.2 = (bf16[256,512]{1,0:T(8,128)(2,1)S(1)}, bf16[256,512]{1,0:T(8,128)(2,1)S(1)}, u32[]{:S(2)}, u32[]{:S(2)}) collective-permute-start(bf16[256,512]{1,0:T(8,128)(2,1)S(1)} %collective-permute-done.rest_2_), channel_id=1, source_target_pairs={{0,2},{2,4},{4,6},{6,7},{7,5},{5,3},{3,1},{1,0},{8,10},{10,12},{12... | collective-permute-start | bytes 786440 | tf_op jit(solution)/shard_map/ppermute | solution.py:53
  11.3 3.3 %collective-permute-done.7.rest_3_ = bf16[256,512]{1,0:T(8,128)(2,1)S(1)} collective-permute-done((bf16[256,512]{1,0:T(8,128)(2,1)}, bf16[256,512]{1,0:T(8,128)(2,1)S(1)}, u32[]{:S(2)}, u32[]{:S(2)}) %collective-permute-start.7) | collective-permute-done | bytes 262176 | tf_op jit(solution)/shard_map/ppermute | solution.py:53
  15.5 1.3 %collective-permute-start.10 = (bf16[256,512]{1,0:T(8,128)(2,1)S(1)}, bf16[256,512]{1,0:T(8,128)(2,1)S(1)}, u32[]{:S(2)}, u32[]{:S(2)}) collective-permute-start(bf16[256,512]{1,0:T(8,128)(2,1)S(1)} %collective-permute-done.7.rest_3_), channel_id=1, source_target_pairs={{0,2},{2,4},{4,6},{6,7},{7,5},{5,3},{3,1},{1,0},{8,10},{10,12},{12... | collective-permute-start | bytes 786440 | tf_op jit(solution)/shard_map/ppermute | solution.py:53
  17.0 5.0 %collective-permute-start.6 = (bf16[128,2048]{1,0:T(8,128)(2,1)}, bf16[128,2048]{1,0:T(8,128)(2,1)S(1)}, u32[]{:S(2)}, u32[]{:S(2)}) collective-permute-start(bf16[128,2048]{1,0:T(8,128)(2,1)} %bitcast.24), channel_id=1, source_target_pairs={{0,24},{8,16},{16,8},{24,0},{1,25},{9,17},{17,9},{25,1},{2,26},{10... | collective-permute-start | bytes 1572872 | tf_op jit(solution)/shard_map/ppermute | solution.py:317
  22.0 2.4 %collective-permute-start.12 = (bf16[128,512]{1,0:T(8,128)(2,1)}, bf16[128,512]{1,0:T(8,128)(2,1)S(1)}, u32[]{:S(2)}, u32[]{:S(2)}) collective-permute-start(bf16[128,512]{1,0:T(8,128)(2,1)} %rest_0_), channel_id=1, source_target_pairs={{8,0},{16,24},{9,1},{17,25},{10,2},{18,26},{11,3},{19,27},{12,4},{... | collective-permute-start | bytes 393224 | tf_op jit(solution)/shard_map/ppermute | solution.py:75
  24.4 2.0 %collective-permute-start.13 = (bf16[128,512]{1,0:T(8,128)(2,1)S(1)}, bf16[128,512]{1,0:T(8,128)(2,1)S(1)}, u32[]{:S(2)}, u32[]{:S(2)}) collective-permute-start(bf16[128,512]{1,0:T(8,128)(2,1)S(1)} %collective-permute-done.9.rest_1_), channel_id=1, source_target_pairs={{8,0},{16,24},{9,1},{17,25},{10,2},{18,26},{11,3},{19,27},{12,4},{... | collective-permute-start | bytes 393224 | tf_op jit(solution)/shard_map/ppermute | solution.py:75
  26.4 1.3 %collective-permute-start.4 = (bf16[256,512]{1,0:T(8,128)(2,1)S(1)}, bf16[256,512]{1,0:T(8,128)(2,1)S(1)}, u32[]{:S(2)}, u32[]{:S(2)}) collective-permute-start(bf16[256,512]{1,0:T(8,128)(2,1)S(1)} %collective-permute-done.2.rest_6_), channel_id=1, source_target_pairs={{0,2},{2,4},{4,6},{6,7},{7,5},{5,3},{3,1},{1,0},{8,10},{10,12},{12... | collective-permute-start | bytes 786440 | tf_op jit(solution)/shard_map/ppermute | solution.py:53
  27.9 1.3 %collective-permute-start.14 = (bf16[256,512]{1,0:T(8,128)(2,1)S(1)}, bf16[256,512]{1,0:T(8,128)(2,1)S(1)}, u32[]{:S(2)}, u32[]{:S(2)}) collective-permute-start(bf16[256,512]{1,0:T(8,128)(2,1)S(1)} %collective-permute-done.10.rest_7_), channel_id=1, source_target_pairs={{0,2},{2,4},{4,6},{6,7},{7,5},{5,3},{3,1},{1,0},{8,10},{10,12},{12... | collective-permute-start | bytes 786440 | tf_op jit(solution)/shard_map/ppermute | solution.py:53
  29.4 4.2 %collective-permute-done.4.rest_10_ = bf16[256,512]{1,0:T(8,128)(2,1)S(1)} collective-permute-done((bf16[256,512]{1,0:T(8,128)(2,1)S(1)}, bf16[256,512]{1,0:T(8,128)(2,1)S(1)}, u32[]{:S(2)}, u32[]{:S(2)}) %collective-permute-start.4) | collective-permute-done | bytes 262176 | tf_op jit(solution)/shard_map/ppermute | solution.py:53
  34.9 4.3 %collective-permute-done.14.rest_11_ = bf16[256,512]{1,0:T(8,128)(2,1)S(1)} collective-permute-done((bf16[256,512]{1,0:T(8,128)(2,1)S(1)}, bf16[256,512]{1,0:T(8,128)(2,1)S(1)}, u32[]{:S(2)}, u32[]{:S(2)}) %collective-permute-start.14) | collective-permute-done | bytes 262176 | tf_op jit(solution)/shard_map/ppermute | solution.py:53
  40.0 1.3 %collective-permute-start.16 = (bf16[256,512]{1,0:T(8,128)(2,1)S(1)}, bf16[256,512]{1,0:T(8,128)(2,1)S(1)}, u32[]{:S(2)}, u32[]{:S(2)}) collective-permute-start(bf16[256,512]{1,0:T(8,128)(2,1)S(1)} %collective-permute-done.4.rest_10_), channel_id=1, source_target_pairs={{0,2},{2,4},{4,6},{6,7},{7,5},{5,3},{3,1},{1,0},{8,10},{10,12},{12... | collective-permute-start | bytes 786440 | tf_op jit(solution)/shard_map/ppermute | solution.py:60
  41.4 1.6 %copy-done = bf16[1,512,2048]{2,1,0:T(8,128)(2,1)S(1)} copy-done((bf16[1,512,2048]{2,1,0:T(8,128)(2,1)S(1)}, bf16[1,512,2048]{2,1,0:T(8,128)(2,1)}, u32[]{:S(2)}) %copy-start) | copy-done | bytes 2097176
  45.7 1.1 %collective-permute-done.17.rest_15_ = bf16[256,512]{1,0:T(8,128)(2,1)S(1)} collective-permute-done((bf16[256,512]{1,0:T(8,128)(2,1)S(1)}, bf16[256,512]{1,0:T(8,128)(2,1)S(1)}, u32[]{:S(2)}, u32[]{:S(2)}) %collective-permute-start.17) | collective-permute-done | bytes 262176 | tf_op jit(solution)/shard_map/ppermute | solution.py:60
  47.7 3.3 %collective-permute-start.18 = (bf16[128,2048]{1,0:T(8,128)(2,1)S(1)}, bf16[128,2048]{1,0:T(8,128)(2,1)S(1)}, u32[]{:S(2)}, u32[]{:S(2)}) collective-permute-start(bf16[128,2048]{1,0:T(8,128)(2,1)S(1)} %get-tuple-element.74.held), channel_id=1, source_target_pairs={{0,8},{8,0},{16,24},{24,16},{1,9},{9,1},{17,25},{25,17},{2,10},{10... | collective-permute-start | bytes 1572872 | tf_op jit(solution)/shard_map/ppermute | solution.py:395
  51.5 1.0 %collective-permute-done.18.grad = bf16[128,2048]{1,0:T(8,128)(2,1)S(1)} collective-permute-done((bf16[128,2048]{1,0:T(8,128)(2,1)S(1)}, bf16[128,2048]{1,0:T(8,128)(2,1)S(1)}, u32[]{:S(2)}, u32[]{:S(2)}) %collective-permute-start.18) | collective-permute-done | bytes 524320 | tf_op jit(solution)/shard_map/ppermute | solution.py:395
  53.5 1.3 %collective-permute-start.20 = (bf16[128,2048]{1,0:T(8,128)(2,1)S(1)}, bf16[128,2048]{1,0:T(8,128)(2,1)S(1)}, u32[]{:S(2)}, u32[]{:S(2)}) collective-permute-start(bf16[128,2048]{1,0:T(8,128)(2,1)S(1)} %tick.3.held), channel_id=1, source_target_pairs={{16,8},{17,9},{18,10},{19,11},{20,12},{21,13},{22,14},{23,15}} | collective-permute-start | bytes 1572872 | tf_op jit(solution)/shard_map/ppermute | solution.py:395
  55.0 1.2 %collective-permute-start.22 = (bf16[256,128]{1,0:T(8,128)(2,1)S(1)}, bf16[256,128]{1,0:T(8,128)(2,1)S(1)}, u32[]{:S(2)}, u32[]{:S(2)}) collective-permute-start(bf16[256,128]{1,0:T(8,128)(2,1)S(1)} %get-tuple-element.82), channel_id=1, source_target_pairs={{0,2},{1,3},{2,0},{3,1},{4,6},{5,7},{6,4},{7,5},{8,10},{9,11},{10,... | collective-permute-start | bytes 196616 | tf_op jit(solution)/shard_map/ppermute | solution.py:242
  56.2 1.7 %collective-permute-done.21.rest_0_ = bf16[256,128]{1,0:T(8,128)(2,1)S(1)} collective-permute-done((bf16[256,128]{1,0:T(8,128)(2,1)S(1)}, bf16[256,128]{1,0:T(8,128)(2,1)S(1)}, u32[]{:S(2)}, u32[]{:S(2)}) %collective-permute-start.21) | collective-permute-done | bytes 65568 | tf_op jit(solution)/shard_map/ppermute | solution.py:242
  58.1 6.2 %collective-permute-done.20.grad = bf16[128,2048]{1,0:T(8,128)(2,1)S(1)} collective-permute-done((bf16[128,2048]{1,0:T(8,128)(2,1)S(1)}, bf16[128,2048]{1,0:T(8,128)(2,1)S(1)}, u32[]{:S(2)}, u32[]{:S(2)}) %collective-permute-start.20) | collective-permute-done | bytes 524320 | tf_op jit(solution)/shard_map/ppermute | solution.py:395
  64.3 2.2 %tick.4.held.grad = bf16[128,2048]{1,0:T(8,128)(2,1)S(1)} custom-call(bf16[128,2048]{1,0:T(8,128)(2,1)S(1)} %collective-permute-done.20.grad, bf16[128,2048]{1,0:T(8,128)(2,1)S(1)} %tick.3.held, bf16[512,2048]{1,0:T(8,128)(2,1)S(1)} %bitcast.8, bf16[1,2048]{1,0:T(2,128)(2,1)S(1)} %copy-done.4, f32[128,512]{1,0:T(8,128)S(1)} %get-tuple-element.75.a, ...), custom_call_target="tpu_custom_call" | custom-call | flops 805306368 | bytes 4194304 | tf_op jit(solution)/shard_map/tick/pallas_call | solution.py:378
  66.7 1.4 %collective-permute-start.25 = (bf16[128,1024]{1,0:T(8,128)(2,1)S(1)}, bf16[128,1024]{1,0:T(8,128)(2,1)S(1)}, u32[]{:S(2)}, u32[]{:S(2)}) collective-permute-start(bf16[128,1024]{1,0:T(8,128)(2,1)S(1)} %get-tuple-element.92), channel_id=1, source_target_pairs={{0,2},{1,3},{2,0},{3,1},{4,6},{5,7},{6,4},{7,5},{8,10},{9,11},{10,... | collective-permute-start | bytes 786440 | tf_op jit(solution)/shard_map/ppermute | solution.py:242
  68.1 1.3 %collective-permute-start.23 = (bf16[128,2048]{1,0:T(8,128)(2,1)S(1)}, bf16[128,2048]{1,0:T(8,128)(2,1)S(1)}, u32[]{:S(2)}, u32[]{:S(2)}) collective-permute-start(bf16[128,2048]{1,0:T(8,128)(2,1)S(1)} %tick.4.held.grad), channel_id=1, source_target_pairs={{8,0},{9,1},{10,2},{11,3},{12,4},{13,5},{14,6},{15,7}} | collective-permute-start | bytes 1572872 | tf_op jit(solution)/shard_map/ppermute | solution.py:395
  69.4 2.5 %collective-permute-done.24.rest_2_ = bf16[128,1024]{1,0:T(8,128)(2,1)S(1)} collective-permute-done((bf16[128,1024]{1,0:T(8,128)(2,1)S(1)}, bf16[128,1024]{1,0:T(8,128)(2,1)S(1)}, u32[]{:S(2)}, u32[]{:S(2)}) %collective-permute-start.24) | collective-permute-done | bytes 262176 | tf_op jit(solution)/shard_map/ppermute | solution.py:242
  72.7 1.4 %collective-permute-start.26 = (bf16[128,1024]{1,0:T(8,128)(2,1)S(1)}, bf16[128,1024]{1,0:T(8,128)(2,1)S(1)}, u32[]{:S(2)}, u32[]{:S(2)}) collective-permute-start(bf16[128,1024]{1,0:T(8,128)(2,1)S(1)} %get-tuple-element.88), channel_id=1, source_target_pairs={{0,2},{1,3},{2,0},{3,1},{4,6},{5,7},{6,4},{7,5},{8,10},{9,11},{10,... | collective-permute-start | bytes 786440 | tf_op jit(solution)/shard_map/ppermute | solution.py:242
  74.1 2.5 %collective-permute-start.27 = (bf16[128,1024]{1,0:T(8,128)(2,1)S(1)}, bf16[128,1024]{1,0:T(8,128)(2,1)S(1)}, u32[]{:S(2)}, u32[]{:S(2)}) collective-permute-start(bf16[128,1024]{1,0:T(8,128)(2,1)S(1)} %get-tuple-element.89), channel_id=1, source_target_pairs={{0,1},{1,0},{2,3},{3,2},{4,5},{5,4},{6,7},{7,6},{8,9},{9,8},{10,11... | collective-permute-start | bytes 786440 | tf_op jit(solution)/shard_map/ppermute | solution.py:242
  76.6 1.8 %collective-permute-done.26.refs_2_ = bf16[128,1024]{1,0:T(8,128)(2,1)S(1)} collective-permute-done((bf16[128,1024]{1,0:T(8,128)(2,1)S(1)}, bf16[128,1024]{1,0:T(8,128)(2,1)S(1)}, u32[]{:S(2)}, u32[]{:S(2)}) %collective-permute-start.26) | collective-permute-done | bytes 262176 | tf_op jit(solution)/shard_map/ppermute | solution.py:242
  78.4 2.0 %collective-permute-done.27.refs_3_ = bf16[128,1024]{1,0:T(8,128)(2,1)S(1)} collective-permute-done((bf16[128,1024]{1,0:T(8,128)(2,1)S(1)}, bf16[128,1024]{1,0:T(8,128)(2,1)S(1)}, u32[]{:S(2)}, u32[]{:S(2)}) %collective-permute-start.27) | collective-permute-done | bytes 262176 | tf_op jit(solution)/shard_map/ppermute | solution.py:242
  81.4 14.8 %collective-permute-done.28.first = bf16[64,2048]{1,0:T(8,128)(2,1)S(1)} collective-permute-done((bf16[64,2048]{1,0:T(8,128)(2,1)S(1)}, bf16[64,2048]{1,0:T(8,128)(2,1)S(1)}, u32[]{:S(2)}, u32[]{:S(2)}) %collective-permute-start.28) | collective-permute-done | bytes 262176 | tf_op jit(solution)/shard_map/ppermute | solution.py:293
  (51 shorter events, 12.9 us)
Async XLA Ops:
  0.6 8.4 %collective-permute-start = (bf16[256,512]{1,0:T(8,128)(2,1)}, bf16[256,512]{1,0:T(8,128)(2,1)S(1)}, u32[]{:S(2)}, u32[]{:S(2)}) collective-permute-start(bf16[256,512]{1,0:T(8,128)(2,1)} %bitcast.10), channel_id=1, source_target_pairs={{0,2},{2,4},{4,6},{6,7},{7,5},{5,3},{3,1},{1,0},{8,10},{10,12},{12... | collective-permute-start | bytes 786440 | tf_op jit(solution)/shard_map/ppermute | solution.py:53
  2.8 7.1 %collective-permute-start.1 = (bf16[256,512]{1,0:T(8,128)(2,1)}, bf16[256,512]{1,0:T(8,128)(2,1)S(1)}, u32[]{:S(2)}, u32[]{:S(2)}) collective-permute-start(bf16[256,512]{1,0:T(8,128)(2,1)} %bitcast.11), channel_id=1, source_target_pairs={{2,0},{4,2},{6,4},{7,6},{5,7},{3,5},{1,3},{0,1},{10,8},{12,10},{14... | collective-permute-start | bytes 786440 | tf_op jit(solution)/shard_map/ppermute | solution.py:53
  2.8 11.8 %collective-permute-start.7 = (bf16[256,512]{1,0:T(8,128)(2,1)}, bf16[256,512]{1,0:T(8,128)(2,1)S(1)}, u32[]{:S(2)}, u32[]{:S(2)}) collective-permute-start(bf16[256,512]{1,0:T(8,128)(2,1)} %bitcast.16), channel_id=1, source_target_pairs={{0,2},{2,4},{4,6},{6,7},{7,5},{5,3},{3,1},{1,0},{8,10},{10,12},{12... | collective-permute-start | bytes 786440 | tf_op jit(solution)/shard_map/ppermute | solution.py:53
  4.3 11.2 %collective-permute-start.8 = (bf16[256,512]{1,0:T(8,128)(2,1)}, bf16[256,512]{1,0:T(8,128)(2,1)S(1)}, u32[]{:S(2)}, u32[]{:S(2)}) collective-permute-start(bf16[256,512]{1,0:T(8,128)(2,1)} %bitcast.17), channel_id=1, source_target_pairs={{2,0},{4,2},{6,4},{7,6},{5,7},{3,5},{1,3},{0,1},{10,8},{12,10},{14... | collective-permute-start | bytes 786440 | tf_op jit(solution)/shard_map/ppermute | solution.py:53
  4.3 11.2 %collective-permute-start.9 = (bf16[128,512]{1,0:T(8,128)(2,1)}, bf16[128,512]{1,0:T(8,128)(2,1)S(1)}, u32[]{:S(2)}, u32[]{:S(2)}) collective-permute-start(bf16[128,512]{1,0:T(8,128)(2,1)} %rest_0_), channel_id=1, source_target_pairs={{16,0},{24,8},{0,16},{8,24},{17,1},{25,9},{1,17},{9,25},{18,2},{26... | collective-permute-start | bytes 393224 | tf_op jit(solution)/shard_map/ppermute | solution.py:75
  9.9 12.1 %collective-permute-start.2 = (bf16[256,512]{1,0:T(8,128)(2,1)S(1)}, bf16[256,512]{1,0:T(8,128)(2,1)S(1)}, u32[]{:S(2)}, u32[]{:S(2)}) collective-permute-start(bf16[256,512]{1,0:T(8,128)(2,1)S(1)} %collective-permute-done.rest_2_), channel_id=1, source_target_pairs={{0,2},{2,4},{4,6},{6,7},{7,5},{5,3},{3,1},{1,0},{8,10},{10,12},{12... | collective-permute-start | bytes 786440 | tf_op jit(solution)/shard_map/ppermute | solution.py:53
  11.2 13.2 %collective-permute-start.3 = (bf16[256,512]{1,0:T(8,128)(2,1)S(1)}, bf16[256,512]{1,0:T(8,128)(2,1)S(1)}, u32[]{:S(2)}, u32[]{:S(2)}) collective-permute-start(bf16[256,512]{1,0:T(8,128)(2,1)S(1)} %collective-permute-done.1.rest_4_), channel_id=1, source_target_pairs={{2,0},{4,2},{6,4},{7,6},{5,7},{3,5},{1,3},{0,1},{10,8},{12,10},{14... | collective-permute-start | bytes 786440 | tf_op jit(solution)/shard_map/ppermute | solution.py:53
  15.5 10.9 %collective-permute-start.10 = (bf16[256,512]{1,0:T(8,128)(2,1)S(1)}, bf16[256,512]{1,0:T(8,128)(2,1)S(1)}, u32[]{:S(2)}, u32[]{:S(2)}) collective-permute-start(bf16[256,512]{1,0:T(8,128)(2,1)S(1)} %collective-permute-done.7.rest_3_), channel_id=1, source_target_pairs={{0,2},{2,4},{4,6},{6,7},{7,5},{5,3},{3,1},{1,0},{8,10},{10,12},{12... | collective-permute-start | bytes 786440 | tf_op jit(solution)/shard_map/ppermute | solution.py:53
  16.8 10.9 %collective-permute-start.11 = (bf16[256,512]{1,0:T(8,128)(2,1)S(1)}, bf16[256,512]{1,0:T(8,128)(2,1)S(1)}, u32[]{:S(2)}, u32[]{:S(2)}) collective-permute-start(bf16[256,512]{1,0:T(8,128)(2,1)S(1)} %collective-permute-done.8.rest_5_), channel_id=1, source_target_pairs={{2,0},{4,2},{6,4},{7,6},{5,7},{3,5},{1,3},{0,1},{10,8},{12,10},{14... | collective-permute-start | bytes 786440 | tf_op jit(solution)/shard_map/ppermute | solution.py:53
  17.0 17.9 %collective-permute-start.6 = (bf16[128,2048]{1,0:T(8,128)(2,1)}, bf16[128,2048]{1,0:T(8,128)(2,1)S(1)}, u32[]{:S(2)}, u32[]{:S(2)}) collective-permute-start(bf16[128,2048]{1,0:T(8,128)(2,1)} %bitcast.24), channel_id=1, source_target_pairs={{0,24},{8,16},{16,8},{24,0},{1,25},{9,17},{17,9},{25,1},{2,26},{10... | collective-permute-start | bytes 1572872 | tf_op jit(solution)/shard_map/ppermute | solution.py:317
  22.0 5.9 %collective-permute-start.12 = (bf16[128,512]{1,0:T(8,128)(2,1)}, bf16[128,512]{1,0:T(8,128)(2,1)S(1)}, u32[]{:S(2)}, u32[]{:S(2)}) collective-permute-start(bf16[128,512]{1,0:T(8,128)(2,1)} %rest_0_), channel_id=1, source_target_pairs={{8,0},{16,24},{9,1},{17,25},{10,2},{18,26},{11,3},{19,27},{12,4},{... | collective-permute-start | bytes 393224 | tf_op jit(solution)/shard_map/ppermute | solution.py:75
  24.4 3.5 %collective-permute-start.13 = (bf16[128,512]{1,0:T(8,128)(2,1)S(1)}, bf16[128,512]{1,0:T(8,128)(2,1)S(1)}, u32[]{:S(2)}, u32[]{:S(2)}) collective-permute-start(bf16[128,512]{1,0:T(8,128)(2,1)S(1)} %collective-permute-done.9.rest_1_), channel_id=1, source_target_pairs={{8,0},{16,24},{9,1},{17,25},{10,2},{18,26},{11,3},{19,27},{12,4},{... | collective-permute-start | bytes 393224 | tf_op jit(solution)/shard_map/ppermute | solution.py:75
  26.4 7.2 %collective-permute-start.4 = (bf16[256,512]{1,0:T(8,128)(2,1)S(1)}, bf16[256,512]{1,0:T(8,128)(2,1)S(1)}, u32[]{:S(2)}, u32[]{:S(2)}) collective-permute-start(bf16[256,512]{1,0:T(8,128)(2,1)S(1)} %collective-permute-done.2.rest_6_), channel_id=1, source_target_pairs={{0,2},{2,4},{4,6},{6,7},{7,5},{5,3},{3,1},{1,0},{8,10},{10,12},{12... | collective-permute-start | bytes 786440 | tf_op jit(solution)/shard_map/ppermute | solution.py:53
  27.7 6.6 %collective-permute-start.5 = (bf16[256,512]{1,0:T(8,128)(2,1)S(1)}, bf16[256,512]{1,0:T(8,128)(2,1)S(1)}, u32[]{:S(2)}, u32[]{:S(2)}) collective-permute-start(bf16[256,512]{1,0:T(8,128)(2,1)S(1)} %collective-permute-done.3.rest_8_), channel_id=1, source_target_pairs={{2,0},{4,2},{6,4},{7,6},{5,7},{3,5},{1,3},{0,1},{10,8},{12,10},{14... | collective-permute-start | bytes 786440 | tf_op jit(solution)/shard_map/ppermute | solution.py:53
  27.9 11.3 %collective-permute-start.14 = (bf16[256,512]{1,0:T(8,128)(2,1)S(1)}, bf16[256,512]{1,0:T(8,128)(2,1)S(1)}, u32[]{:S(2)}, u32[]{:S(2)}) collective-permute-start(bf16[256,512]{1,0:T(8,128)(2,1)S(1)} %collective-permute-done.10.rest_7_), channel_id=1, source_target_pairs={{0,2},{2,4},{4,6},{6,7},{7,5},{5,3},{3,1},{1,0},{8,10},{10,12},{12... | collective-permute-start | bytes 786440 | tf_op jit(solution)/shard_map/ppermute | solution.py:53
  29.2 10.8 %collective-permute-start.15 = (bf16[256,512]{1,0:T(8,128)(2,1)S(1)}, bf16[256,512]{1,0:T(8,128)(2,1)S(1)}, u32[]{:S(2)}, u32[]{:S(2)}) collective-permute-start(bf16[256,512]{1,0:T(8,128)(2,1)S(1)} %collective-permute-done.11.rest_9_), channel_id=1, source_target_pairs={{2,0},{4,2},{6,4},{7,6},{5,7},{3,5},{1,3},{0,1},{10,8},{12,10},{14... | collective-permute-start | bytes 786440 | tf_op jit(solution)/shard_map/ppermute | solution.py:53
  40.0 5.7 %collective-permute-start.16 = (bf16[256,512]{1,0:T(8,128)(2,1)S(1)}, bf16[256,512]{1,0:T(8,128)(2,1)S(1)}, u32[]{:S(2)}, u32[]{:S(2)}) collective-permute-start(bf16[256,512]{1,0:T(8,128)(2,1)S(1)} %collective-permute-done.4.rest_10_), channel_id=1, source_target_pairs={{0,2},{2,4},{4,6},{6,7},{7,5},{5,3},{3,1},{1,0},{8,10},{10,12},{12... | collective-permute-start | bytes 786440 | tf_op jit(solution)/shard_map/ppermute | solution.py:60
  41.3 5.5 %collective-permute-start.17 = (bf16[256,512]{1,0:T(8,128)(2,1)S(1)}, bf16[256,512]{1,0:T(8,128)(2,1)S(1)}, u32[]{:S(2)}, u32[]{:S(2)}) collective-permute-start(bf16[256,512]{1,0:T(8,128)(2,1)S(1)} %collective-permute-done.15.rest_13_), channel_id=1, source_target_pairs={{2,0},{4,2},{6,4},{7,6},{5,7},{3,5},{1,3},{0,1},{10,8},{12,10},{14... | collective-permute-start | bytes 786440 | tf_op jit(solution)/shard_map/ppermute | solution.py:60
  43.9 2.9 %copy-start.3 = (bf16[1,256,512]{2,1,0:T(8,128)(2,1)S(1)}, bf16[1,256,512]{2,1,0:T(8,128)(2,1)}, u32[]{:S(2)}) copy-start(bf16[1,256,512]{2,1,0:T(8,128)(2,1)} %param.9) | copy-start | bytes 786436
  46.8 5.8 %copy-start.1 = (bf16[1,512,2048]{2,1,0:T(8,128)(2,1)S(1)}, bf16[1,512,2048]{2,1,0:T(8,128)(2,1)}, u32[]{:S(2)}) copy-start(bf16[1,512,2048]{2,1,0:T(8,128)(2,1)} %param.10) | copy-start | bytes 6291460
  47.7 4.8 %collective-permute-start.18 = (bf16[128,2048]{1,0:T(8,128)(2,1)S(1)}, bf16[128,2048]{1,0:T(8,128)(2,1)S(1)}, u32[]{:S(2)}, u32[]{:S(2)}) collective-permute-start(bf16[128,2048]{1,0:T(8,128)(2,1)S(1)} %get-tuple-element.74.held), channel_id=1, source_target_pairs={{0,8},{8,0},{16,24},{24,16},{1,9},{9,1},{17,25},{25,17},{2,10},{10... | collective-permute-start | bytes 1572872 | tf_op jit(solution)/shard_map/ppermute | solution.py:395
  51.0 2.4 %collective-permute-start.19 = (bf16[512,128]{1,0:T(8,128)(2,1)S(1)}, bf16[512,128]{1,0:T(8,128)(2,1)S(1)}, u32[]{:S(2)}, u32[]{:S(2)}) collective-permute-start(bf16[512,128]{1,0:T(8,128)(2,1)S(1)} %get-tuple-element.78), channel_id=1, source_target_pairs={{0,8},{8,16},{16,24},{24,0},{1,9},{9,17},{17,25},{25,1},{2,10},{10... | collective-permute-start | bytes 393224 | tf_op jit(solution)/shard_map/ppermute | solution.py:375
  53.5 10.9 %collective-permute-start.20 = (bf16[128,2048]{1,0:T(8,128)(2,1)S(1)}, bf16[128,2048]{1,0:T(8,128)(2,1)S(1)}, u32[]{:S(2)}, u32[]{:S(2)}) collective-permute-start(bf16[128,2048]{1,0:T(8,128)(2,1)S(1)} %tick.3.held), channel_id=1, source_target_pairs={{16,8},{17,9},{18,10},{19,11},{20,12},{21,13},{22,14},{23,15}} | collective-permute-start | bytes 1572872 | tf_op jit(solution)/shard_map/ppermute | solution.py:395
  54.8 3.2 %collective-permute-start.21 = (bf16[256,128]{1,0:T(8,128)(2,1)S(1)}, bf16[256,128]{1,0:T(8,128)(2,1)S(1)}, u32[]{:S(2)}, u32[]{:S(2)}) collective-permute-start(bf16[256,128]{1,0:T(8,128)(2,1)S(1)} %get-tuple-element.81), channel_id=1, source_target_pairs={{0,1},{1,0},{2,3},{3,2},{4,5},{5,4},{6,7},{7,6},{8,9},{9,8},{10,11... | collective-permute-start | bytes 196616 | tf_op jit(solution)/shard_map/ppermute | solution.py:242
  55.0 3.1 %collective-permute-start.22 = (bf16[256,128]{1,0:T(8,128)(2,1)S(1)}, bf16[256,128]{1,0:T(8,128)(2,1)S(1)}, u32[]{:S(2)}, u32[]{:S(2)}) collective-permute-start(bf16[256,128]{1,0:T(8,128)(2,1)S(1)} %get-tuple-element.82), channel_id=1, source_target_pairs={{0,2},{1,3},{2,0},{3,1},{4,6},{5,7},{6,4},{7,5},{8,10},{9,11},{10,... | collective-permute-start | bytes 196616 | tf_op jit(solution)/shard_map/ppermute | solution.py:242
  66.6 5.3 %collective-permute-start.24 = (bf16[128,1024]{1,0:T(8,128)(2,1)S(1)}, bf16[128,1024]{1,0:T(8,128)(2,1)S(1)}, u32[]{:S(2)}, u32[]{:S(2)}) collective-permute-start(bf16[128,1024]{1,0:T(8,128)(2,1)S(1)} %get-tuple-element.93), channel_id=1, source_target_pairs={{0,1},{1,0},{2,3},{3,2},{4,5},{5,4},{6,7},{7,6},{8,9},{9,8},{10,11... | collective-permute-start | bytes 786440 | tf_op jit(solution)/shard_map/ppermute | solution.py:242
  66.7 5.3 %collective-permute-start.25 = (bf16[128,1024]{1,0:T(8,128)(2,1)S(1)}, bf16[128,1024]{1,0:T(8,128)(2,1)S(1)}, u32[]{:S(2)}, u32[]{:S(2)}) collective-permute-start(bf16[128,1024]{1,0:T(8,128)(2,1)S(1)} %get-tuple-element.92), channel_id=1, source_target_pairs={{0,2},{1,3},{2,0},{3,1},{4,6},{5,7},{6,4},{7,5},{8,10},{9,11},{10,... | collective-permute-start | bytes 786440 | tf_op jit(solution)/shard_map/ppermute | solution.py:242
  68.1 12.5 %collective-permute-start.23 = (bf16[128,2048]{1,0:T(8,128)(2,1)S(1)}, bf16[128,2048]{1,0:T(8,128)(2,1)S(1)}, u32[]{:S(2)}, u32[]{:S(2)}) collective-permute-start(bf16[128,2048]{1,0:T(8,128)(2,1)S(1)} %tick.4.held.grad), channel_id=1, source_target_pairs={{8,0},{9,1},{10,2},{11,3},{12,4},{13,5},{14,6},{15,7}} | collective-permute-start | bytes 1572872 | tf_op jit(solution)/shard_map/ppermute | solution.py:395
  72.7 5.7 %collective-permute-start.26 = (bf16[128,1024]{1,0:T(8,128)(2,1)S(1)}, bf16[128,1024]{1,0:T(8,128)(2,1)S(1)}, u32[]{:S(2)}, u32[]{:S(2)}) collective-permute-start(bf16[128,1024]{1,0:T(8,128)(2,1)S(1)} %get-tuple-element.88), channel_id=1, source_target_pairs={{0,2},{1,3},{2,0},{3,1},{4,6},{5,7},{6,4},{7,5},{8,10},{9,11},{10,... | collective-permute-start | bytes 786440 | tf_op jit(solution)/shard_map/ppermute | solution.py:242
  74.1 6.3 %collective-permute-start.27 = (bf16[128,1024]{1,0:T(8,128)(2,1)S(1)}, bf16[128,1024]{1,0:T(8,128)(2,1)S(1)}, u32[]{:S(2)}, u32[]{:S(2)}) collective-permute-start(bf16[128,1024]{1,0:T(8,128)(2,1)S(1)} %get-tuple-element.89), channel_id=1, source_target_pairs={{0,1},{1,0},{2,3},{3,2},{4,5},{5,4},{6,7},{7,6},{8,9},{9,8},{10,11... | collective-permute-start | bytes 786440 | tf_op jit(solution)/shard_map/ppermute | solution.py:242
  80.4 15.8 %collective-permute-start.28 = (bf16[64,2048]{1,0:T(8,128)(2,1)S(1)}, bf16[64,2048]{1,0:T(8,128)(2,1)S(1)}, u32[]{:S(2)}, u32[]{:S(2)}) collective-permute-start(bf16[64,2048]{1,0:T(8,128)(2,1)S(1)} %get-tuple-element.90), channel_id=1, source_target_pairs={{0,28},{1,29},{2,30},{3,31},{4,24},{5,25},{6,26},{7,27},{8,4},{9,5... | collective-permute-start | bytes 786440 | tf_op jit(solution)/shard_map/ppermute | solution.py:293
  80.5 15.7 %collective-permute-start.29 = (bf16[64,2048]{1,0:T(8,128)(2,1)S(1)}, bf16[64,2048]{1,0:T(8,128)(2,1)S(1)}, u32[]{:S(2)}, u32[]{:S(2)}) collective-permute-start(bf16[64,2048]{1,0:T(8,128)(2,1)S(1)} %get-tuple-element.91), channel_id=1, source_target_pairs={{0,24},{1,25},{2,26},{3,27},{4,28},{5,29},{6,30},{7,31},{8,0},{9,1... | collective-permute-start | bytes 786440 | tf_op jit(solution)/shard_map/ppermute | solution.py:293
  (4 other events, 6.2 us)

commit v5 on v4

--- a/solution.py
+++ b/solution.py
@@ -89,16 +89,23 @@
     return pl.ds(pl.multiple_of(ring_member(place, size) * depth, depth), depth)
 
 
-def push_back(grad_ref, back_proj, scales, gate_vector, pieces, columns, out_ref):
+def push_back(grad_ref, back_proj, scales, gate_vector, turned, pieces, columns, out_ref):
     gate_scale, up_scale, logit_scale = scales
     logit = jnp.sum(back_proj * logit_scale[...], axis=1, keepdims=True)
     gate_grad = (back_proj * gate_scale[...]).astype(BF16)
     up_grad = (back_proj * up_scale[...]).astype(BF16)
-    for where, (gate, up) in zip(columns, pieces):
-        through = dot(gate_grad, gate[...], TURNED) + dot(up_grad, up[...], TURNED)
+    for i, (where, (gate, up)) in enumerate(zip(columns, pieces)):
+        dims = PLAIN if i < turned else TURNED
+        through = dot(gate_grad, gate[...], dims) + dot(up_grad, up[...], dims)
         out_ref[:, where] = (
             grad_ref[:, where].astype(F32) + through + logit * gate_vector[:, where].astype(F32)
         ).astype(BF16)
+
+
+def turn_kernel(*refs):
+    half = len(refs) // 2
+    for value, out in zip(refs[:half], refs[half:]):
+        out[...] = value[...].T
 
 
 def pair_up(refs):
@@ -128,9 +135,10 @@
     back_proj[...] = dot(seeded[...], down[...], TURNED)
 
 
-def first_kernel(offsets, rows, score, back_proj, grad, gate_vector, *rest):
-    pieces = pair_up(rest[: 2 * len(offsets)])
-    out, gate_scale, up_scale, logit_scale, scored = rest[2 * len(offsets) :]
+def first_kernel(offsets, turned, rows, score, back_proj, grad, gate_vector, *rest):
+    pieces, rest = pair_up(rest[: 2 * len(offsets)]), rest[2 * len(offsets) :]
+    turned_pieces, rest = pair_up(rest[: 2 * turned]), rest[2 * turned :]
+    out, gate_scale, up_scale, logit_scale, scored = rest
     depth = pieces[0][0].shape[0]
     columns = [piece_columns(offset, "dp", depth) for offset in offsets]
     gate_pre = up_pre = 0.0
@@ -151,14 +159,15 @@
 
     @pl.when(section == sections - 1)
     def _():
-        push_back(grad, back_proj[...], scales, gate_vector, pieces, columns, out)
+        back = turned_pieces + pieces[turned:]
+        push_back(grad, back_proj[...], scales, gate_vector, turned, back, columns, out)
 
     @pl.when(section < sections - 1)
     def _():
         out[...] = grad[...]
 
 
-def tick_kernel(offsets, section, grad, held, down, gate_vector, a, b, c, *rest):
+def tick_kernel(offsets, turned, section, grad, held, down, gate_vector, a, b, c, *rest):
     pieces, out = pair_up(rest[:-1]), rest[-1]
 
     here = lax.axis_index("section") == section
@@ -169,10 +178,10 @@
 
     @pl.when(here)
     def _():
-        depth = pieces[0][0].shape[0]
+        depth = pieces[0][0].shape[1 if turned else 0]
         columns = [piece_columns(offset, "dp", depth) for offset in offsets]
-        back_proj = dot(grad[...], down[...], TURNED)
-        push_back(grad, back_proj, (a, b, c), gate_vector, pieces, columns, out)
+        back_proj = dot(grad[...], down[...], PLAIN if turned else TURNED)
+        push_back(grad, back_proj, (a, b, c), gate_vector, turned, pieces, columns, out)
 
 
 def block_rows(bits, rest, units):
@@ -327,6 +336,13 @@
     pieces, offsets = gather_ring([gate_weight[0], up_weight[0]], "dp", between)
     for blocks, _ in cotangents:
         pass
+    turned = 0 if depth % 128 else len(pieces) - 1
+    down_back = down_full
+    if turned:
+        outs = [shape(down_full.shape[::-1], BF16)]
+        down_back = call(turn_kernel, "turn_down", outs, 0, down_full)[0]
+    outs = [shape((hidden_units, depth), BF16)] * 2
+    turned_pieces = [call(turn_kernel, "turn", outs, 0, *piece) for piece in pieces[:turned]]
     seeded, back_proj = pl.pallas_call(
         functools.partial(prepare_kernel, block_offsets),
         out_shape=[shape((local_rows, model_width), BF16), small],
@@ -355,9 +371,11 @@
             joined = [lax.dynamic_update_slice(j, p, (start, 0)) for j, p in zip(joined, piece)]
         pieces, offsets = [joined], [None]
     flat = [v for piece in pieces for v in piece]
+    flat_turned = [v for piece in turned_pieces for v in piece]
+    flat_back = flat_turned + flat[2 * turned :]
 
     outgoing, *scales, scored = pl.pallas_call(
-        functools.partial(first_kernel, offsets),
+        functools.partial(first_kernel, offsets, turned),
         out_shape=[
             shape((local_rows, model_width), BF16),
             small,
@@ -365,25 +383,25 @@
             small,
             shape((hidden_units, local_rows), BF16),
         ],
-        in_specs=[VMEM] * (5 + len(flat)),
+        in_specs=[VMEM] * (5 + len(flat) + 2 * turned),
         out_specs=[VMEM] * 5,
         compiler_params=params(),
         cost_estimate=cost(4 * local_rows * model_width * hidden_units, *flat),
         name="first_tick",
-    )(own_rows, score, back_proj, seeded, shared_gate, *flat)
+    )(own_rows, score, back_proj, seeded, shared_gate, *flat, *flat_turned)
     around = [(i, (i + 1) % sections) for i in range(sections)]
     scored = lax.ppermute(scored, "section", around)
 
     def tick(section, grad, held):
         return pl.pallas_call(
-            functools.partial(tick_kernel, offsets, section),
+            functools.partial(tick_kernel, offsets, turned, section),
             out_shape=shape((local_rows, model_width), BF16),
             in_specs=[VMEM] * (7 + len(flat)),
             out_specs=VMEM,
             compiler_params=params(),
             cost_estimate=cost(3 * local_rows * model_width * hidden_units, *flat),
             name="tick",
-        )(grad, held, down_full, shared_gate, *scales, *flat)
+        )(grad, held, down_back, shared_gate, *scales, *flat_back)
 
     swap = [(i, i ^ 1) for i in range(sections)]
     for section in range(sections - 2, -1, -1):

time: 97.3 us -> 97 us (level)
  waiting for transfers between devices: 51.9 us -> 49.3 us
  starting transfers between devices: 35 us -> 36.1 us
    ppermute x6, waiting for transfers between devices: 8.26 us -> 12.8 us  [along(): return [lax.ppermute(v, 'dp', pairs) for v in values]]
    ppermute x2, waiting for transfers between devices: 14.8 us -> 11.5 us  [to_layer(): return lax.ppermute(value, ('section', 'dp'), pairs)]
    pallas_call x4 -> x12, Pallas kernels: 1.68 us -> 3.57 us  [call(): pl.pallas_call(kernel, out_shape=outs, in_specs=[VMEM] * len(args), out_s...]
    ppermute x3, waiting for transfers between devices: 7.24 us -> 5.68 us  [on_device(): grad = lax.ppermute(outgoing, 'section', pairs)]
    ppermute x3, starting transfers between devices: 5.74 us -> 7 us  [gather_to_ends(): held += [lax.ppermute(block, axis, pairs) for block in list(held)]]
    ppermute x2, starting transfers between devices: 0.12 us -> 1.25 us  [to_layer(): return lax.ppermute(value, ('section', 'dp'), pairs)]
    pallas_call x4, Pallas kernels: 4.08 us -> 3.06 us  [the longest x3 2.14 us: tick(): pl.pallas_call(functools.partial(tick_kernel, offsets, turned, section),...]
    unnamed x12 -> x14, local copies, waits for them, and re-layouts: 2.51 us -> 1.93 us
  transfers between devices with their start and end apart: 30 -> 30, of which waited for: 21 -> 18; matrix products, arithmetic and copies ran while one was open for 0% -> 0% of each run, Pallas kernels for 3% -> 5%
where the time goes in v5:
time: 97 us; the launch traced here: 96 us
  waiting for transfers between devices  49.3 us (51%)
  starting transfers between devices  36.1 us (37%)
  Pallas kernels  7.68 us (8%)
  local copies, waits for them, and re-layouts  1.96 us (2%)
    ppermute x12, waiting for transfers between devices, gather_ring(): both = (lax.ppermute(v, axis, ahead), lax.ppermute(w, axis, back))  17.9 us
    ppermute x6, waiting for transfers between devices, along(): return [lax.ppermute(v, 'dp', pairs) for v in values]  12.8 us
    ppermute x2, waiting for transfers between devices, to_layer(): return lax.ppermute(value, ('section', 'dp'), pairs)  11.5 us
    ppermute x12, starting transfers between devices, gather_ring(): both = (lax.ppermute(v, axis, ahead), lax.ppermute(w, axis, back))  9.61 us
    ppermute x3, starting transfers between devices, gather_to_ends(): held += [lax.ppermute(block, axis, pairs) for block in list(held)]  7 us
    ppermute x6, starting transfers between devices, along(): return [lax.ppermute(v, 'dp', pairs) for v in values]  5.98 us
    ppermute x3, starting transfers between devices, on_device(): grad = lax.ppermute(outgoing, 'section', pairs)  5.8 us
    ppermute x3, waiting for transfers between devices, on_device(): grad = lax.ppermute(outgoing, 'section', pairs)  5.68 us
  transfers between devices with their start and end apart: 30, of which 18 were waited for; matrix products, arithmetic and copies ran while one was open for 0% of the time, Pallas kernels for 5%

profile of v5, /device:TPU:1, one launch (start us, length us, event | category | flops | bytes accessed | tf_op | source)
XLA Modules:
  0.0 96.0 jit_solution(5245605817143908572)
XLA Ops:
  0.6 2.1 %collective-permute-start.1 = (bf16[256,512]{1,0:T(8,128)(2,1)}, bf16[256,512]{1,0:T(8,128)(2,1)S(1)}, u32[]{:S(2)}, u32[]{:S(2)}) collective-permute-start(bf16[256,512]{1,0:T(8,128)(2,1)} %bitcast.8), channel_id=1, source_target_pairs={{2,0},{4,2},{6,4},{7,6},{5,7},{3,5},{1,3},{0,1},{10,8},{12,10},{14... | collective-permute-start | bytes 786440 | tf_op jit(solution)/shard_map/ppermute | solution.py:53
  2.9 1.3 %collective-permute-start.8 = (bf16[256,512]{1,0:T(8,128)(2,1)}, bf16[256,512]{1,0:T(8,128)(2,1)S(1)}, u32[]{:S(2)}, u32[]{:S(2)}) collective-permute-start(bf16[256,512]{1,0:T(8,128)(2,1)} %bitcast.12), channel_id=1, source_target_pairs={{2,0},{4,2},{6,4},{7,6},{5,7},{3,5},{1,3},{0,1},{10,8},{12,10},{14... | collective-permute-start | bytes 786440 | tf_op jit(solution)/shard_map/ppermute | solution.py:53
  4.4 1.3 %collective-permute-start.9 = (bf16[128,512]{1,0:T(8,128)(2,1)}, bf16[128,512]{1,0:T(8,128)(2,1)S(1)}, u32[]{:S(2)}, u32[]{:S(2)}) collective-permute-start(bf16[128,512]{1,0:T(8,128)(2,1)} %rest_0_), channel_id=1, source_target_pairs={{16,0},{24,8},{0,16},{8,24},{17,1},{25,9},{1,17},{9,25},{18,2},{26... | collective-permute-start | bytes 393224 | tf_op jit(solution)/shard_map/ppermute | solution.py:75
  5.7 3.4 %collective-permute-done.1.refs_0_.rest_4_ = bf16[256,512]{1,0:T(8,128)(2,1)S(1)} collective-permute-done((bf16[256,512]{1,0:T(8,128)(2,1)}, bf16[256,512]{1,0:T(8,128)(2,1)S(1)}, u32[]{:S(2)}, u32[]{:S(2)}) %collective-permute-start.1) | collective-permute-done | bytes 262176 | tf_op jit(solution)/shard_map/ppermute | solution.py:53
  10.3 1.0 %collective-permute-start.3 = (bf16[256,512]{1,0:T(8,128)(2,1)S(1)}, bf16[256,512]{1,0:T(8,128)(2,1)S(1)}, u32[]{:S(2)}, u32[]{:S(2)}) collective-permute-start(bf16[256,512]{1,0:T(8,128)(2,1)S(1)} %collective-permute-done.1.refs_0_.rest_4_), channel_id=1, source_target_pairs={{2,0},{4,2},{6,4},{7,6},{5,7},{3,5},{1,3},{0,1},{10,8},{12,10},{14... | collective-permute-start | bytes 786440 | tf_op jit(solution)/shard_map/ppermute | solution.py:53
  11.3 3.4 %collective-permute-done.8.refs_1_.rest_5_ = bf16[256,512]{1,0:T(8,128)(2,1)S(1)} collective-permute-done((bf16[256,512]{1,0:T(8,128)(2,1)}, bf16[256,512]{1,0:T(8,128)(2,1)S(1)}, u32[]{:S(2)}, u32[]{:S(2)}) %collective-permute-start.8) | collective-permute-done | bytes 262176 | tf_op jit(solution)/shard_map/ppermute | solution.py:53
  15.9 1.0 %collective-permute-start.11 = (bf16[256,512]{1,0:T(8,128)(2,1)S(1)}, bf16[256,512]{1,0:T(8,128)(2,1)S(1)}, u32[]{:S(2)}, u32[]{:S(2)}) collective-permute-start(bf16[256,512]{1,0:T(8,128)(2,1)S(1)} %collective-permute-done.8.refs_1_.rest_5_), channel_id=1, source_target_pairs={{2,0},{4,2},{6,4},{7,6},{5,7},{3,5},{1,3},{0,1},{10,8},{12,10},{14... | collective-permute-start | bytes 786440 | tf_op jit(solution)/shard_map/ppermute | solution.py:53
  16.9 5.0 %collective-permute-start.6 = (bf16[128,2048]{1,0:T(8,128)(2,1)}, bf16[128,2048]{1,0:T(8,128)(2,1)S(1)}, u32[]{:S(2)}, u32[]{:S(2)}) collective-permute-start(bf16[128,2048]{1,0:T(8,128)(2,1)} %bitcast.18), channel_id=1, source_target_pairs={{0,24},{8,16},{16,8},{24,0},{1,25},{9,17},{17,9},{25,1},{2,26},{10... | collective-permute-start | bytes 1572872 | tf_op jit(solution)/shard_map/ppermute | solution.py:326
  21.9 4.4 %collective-permute-start.12 = (bf16[128,512]{1,0:T(8,128)(2,1)}, bf16[128,512]{1,0:T(8,128)(2,1)S(1)}, u32[]{:S(2)}, u32[]{:S(2)}) collective-permute-start(bf16[128,512]{1,0:T(8,128)(2,1)} %rest_0_), channel_id=1, source_target_pairs={{8,0},{16,24},{9,1},{17,25},{10,2},{18,26},{11,3},{19,27},{12,4},{... | collective-permute-start | bytes 393224 | tf_op jit(solution)/shard_map/ppermute | solution.py:75
  26.3 1.3 %collective-permute-start.13 = (bf16[128,512]{1,0:T(8,128)(2,1)S(1)}, bf16[128,512]{1,0:T(8,128)(2,1)S(1)}, u32[]{:S(2)}, u32[]{:S(2)}) collective-permute-start(bf16[128,512]{1,0:T(8,128)(2,1)S(1)} %collective-permute-done.9.rest_1_), channel_id=1, source_target_pairs={{8,0},{16,24},{9,1},{17,25},{10,2},{18,26},{11,3},{19,27},{12,4},{... | collective-permute-start | bytes 393224 | tf_op jit(solution)/shard_map/ppermute | solution.py:75
  27.7 1.4 %collective-permute-start.5 = (bf16[256,512]{1,0:T(8,128)(2,1)S(1)}, bf16[256,512]{1,0:T(8,128)(2,1)S(1)}, u32[]{:S(2)}, u32[]{:S(2)}) collective-permute-start(bf16[256,512]{1,0:T(8,128)(2,1)S(1)} %collective-permute-done.3.refs_0_.rest_8_), channel_id=1, source_target_pairs={{2,0},{4,2},{6,4},{7,6},{5,7},{3,5},{1,3},{0,1},{10,8},{12,10},{14... | collective-permute-start | bytes 786440 | tf_op jit(solution)/shard_map/ppermute | solution.py:53
  29.3 1.3 %collective-permute-start.15 = (bf16[256,512]{1,0:T(8,128)(2,1)S(1)}, bf16[256,512]{1,0:T(8,128)(2,1)S(1)}, u32[]{:S(2)}, u32[]{:S(2)}) collective-permute-start(bf16[256,512]{1,0:T(8,128)(2,1)S(1)} %collective-permute-done.11.refs_1_.rest_9_), channel_id=1, source_target_pairs={{2,0},{4,2},{6,4},{7,6},{5,7},{3,5},{1,3},{0,1},{10,8},{12,10},{14... | collective-permute-start | bytes 786440 | tf_op jit(solution)/shard_map/ppermute | solution.py:53
  30.6 4.0 %collective-permute-done.4.refs_0_.rest_10_ = bf16[256,512]{1,0:T(8,128)(2,1)S(1)} collective-permute-done((bf16[256,512]{1,0:T(8,128)(2,1)S(1)}, bf16[256,512]{1,0:T(8,128)(2,1)S(1)}, u32[]{:S(2)}, u32[]{:S(2)}) %collective-permute-start.4) | collective-permute-done | bytes 262176 | tf_op jit(solution)/shard_map/ppermute | solution.py:53
  34.6 5.6 %collective-permute-done.14.refs_1_.rest_11_ = bf16[256,512]{1,0:T(8,128)(2,1)S(1)} collective-permute-done((bf16[256,512]{1,0:T(8,128)(2,1)S(1)}, bf16[256,512]{1,0:T(8,128)(2,1)S(1)}, u32[]{:S(2)}, u32[]{:S(2)}) %collective-permute-start.14) | collective-permute-done | bytes 262176 | tf_op jit(solution)/shard_map/ppermute | solution.py:53
  40.3 1.3 %collective-permute-start.17 = (bf16[256,512]{1,0:T(8,128)(2,1)S(1)}, bf16[256,512]{1,0:T(8,128)(2,1)S(1)}, u32[]{:S(2)}, u32[]{:S(2)}) collective-permute-start(bf16[256,512]{1,0:T(8,128)(2,1)S(1)} %collective-permute-done.15.refs_1_.rest_13_), channel_id=1, source_target_pairs={{2,0},{4,2},{6,4},{7,6},{5,7},{3,5},{1,3},{0,1},{10,8},{12,10},{14... | collective-permute-start | bytes 786440 | tf_op jit(solution)/shard_map/ppermute | solution.py:60
  41.7 0.9 copy-done.1
  42.7 0.9 copy-done.3
  47.1 0.9 first_tick.1
  48.1 3.2 %collective-permute-start.18 = (bf16[128,2048]{1,0:T(8,128)(2,1)S(1)}, bf16[128,2048]{1,0:T(8,128)(2,1)S(1)}, u32[]{:S(2)}, u32[]{:S(2)}) collective-permute-start(bf16[128,2048]{1,0:T(8,128)(2,1)S(1)} %get-tuple-element.102.held), channel_id=1, source_target_pairs={{0,8},{8,0},{16,24},{24,16},{1,9},{9,1},{17,25},{25,17},{2,10},{10... | collective-permute-start | bytes 1572872 | tf_op jit(solution)/shard_map/ppermute | solution.py:413
  53.3 1.3 %collective-permute-start.20 = (bf16[128,2048]{1,0:T(8,128)(2,1)S(1)}, bf16[128,2048]{1,0:T(8,128)(2,1)S(1)}, u32[]{:S(2)}, u32[]{:S(2)}) collective-permute-start(bf16[128,2048]{1,0:T(8,128)(2,1)S(1)} %tick.3.held), channel_id=1, source_target_pairs={{16,8},{17,9},{18,10},{19,11},{20,12},{21,13},{22,14},{23,15}} | collective-permute-start | bytes 1572872 | tf_op jit(solution)/shard_map/ppermute | solution.py:413
  54.6 1.4 %collective-permute-start.21 = (bf16[256,128]{1,0:T(8,128)(2,1)S(1)}, bf16[256,128]{1,0:T(8,128)(2,1)S(1)}, u32[]{:S(2)}, u32[]{:S(2)}) collective-permute-start(bf16[256,128]{1,0:T(8,128)(2,1)S(1)} %get-tuple-element.109), channel_id=1, source_target_pairs={{0,1},{1,0},{2,3},{3,2},{4,5},{5,4},{6,7},{7,6},{8,9},{9,8},{10,11... | collective-permute-start | bytes 196616 | tf_op jit(solution)/shard_map/ppermute | solution.py:251
  55.9 1.3 %collective-permute-start.22 = (bf16[256,128]{1,0:T(8,128)(2,1)S(1)}, bf16[256,128]{1,0:T(8,128)(2,1)S(1)}, u32[]{:S(2)}, u32[]{:S(2)}) collective-permute-start(bf16[256,128]{1,0:T(8,128)(2,1)S(1)} %get-tuple-element.110), channel_id=1, source_target_pairs={{0,2},{1,3},{2,0},{3,1},{4,6},{5,7},{6,4},{7,5},{8,10},{9,11},{10,... | collective-permute-start | bytes 196616 | tf_op jit(solution)/shard_map/ppermute | solution.py:251
  57.8 1.3 %collective-permute-done.22.rest_1_ = bf16[256,128]{1,0:T(8,128)(2,1)S(1)} collective-permute-done((bf16[256,128]{1,0:T(8,128)(2,1)S(1)}, bf16[256,128]{1,0:T(8,128)(2,1)S(1)}, u32[]{:S(2)}, u32[]{:S(2)}) %collective-permute-start.22) | collective-permute-done | bytes 65568 | tf_op jit(solution)/shard_map/ppermute | solution.py:251
  59.1 4.8 %collective-permute-done.20.grad = bf16[128,2048]{1,0:T(8,128)(2,1)S(1)} collective-permute-done((bf16[128,2048]{1,0:T(8,128)(2,1)S(1)}, bf16[128,2048]{1,0:T(8,128)(2,1)S(1)}, u32[]{:S(2)}, u32[]{:S(2)}) %collective-permute-start.20) | collective-permute-done | bytes 524320 | tf_op jit(solution)/shard_map/ppermute | solution.py:413
  63.8 1.3 %tick.4.held.grad = bf16[128,2048]{1,0:T(8,128)(2,1)S(1)} custom-call(bf16[128,2048]{1,0:T(8,128)(2,1)S(1)} %collective-permute-done.20.grad, bf16[128,2048]{1,0:T(8,128)(2,1)S(1)} %tick.3.held, bf16[2048,512]{1,0:T(8,128)(2,1)S(1)} %turn_down.1.down, bf16[1,2048]{1,0:T(2,128)(2,1)S(1)} %copy-done.5, f32[128,512]{1,0:T(8,128)S(1)} %get-tuple-element.103.a, ...), custom_call_target="tpu_custom_call" | custom-call | flops 805306368 | bytes 4194304 | tf_op jit(solution)/shard_map/tick/pallas_call | solution.py:396
  65.4 2.4 %collective-permute-start.24 = (bf16[128,1024]{1,0:T(8,128)(2,1)S(1)}, bf16[128,1024]{1,0:T(8,128)(2,1)S(1)}, u32[]{:S(2)}, u32[]{:S(2)}) collective-permute-start(bf16[128,1024]{1,0:T(8,128)(2,1)S(1)} %get-tuple-element.121), channel_id=1, source_target_pairs={{0,1},{1,0},{2,3},{3,2},{4,5},{5,4},{6,7},{7,6},{8,9},{9,8},{10,11... | collective-permute-start | bytes 786440 | tf_op jit(solution)/shard_map/ppermute | solution.py:251
  67.8 1.3 %collective-permute-start.23 = (bf16[128,2048]{1,0:T(8,128)(2,1)S(1)}, bf16[128,2048]{1,0:T(8,128)(2,1)S(1)}, u32[]{:S(2)}, u32[]{:S(2)}) collective-permute-start(bf16[128,2048]{1,0:T(8,128)(2,1)S(1)} %tick.4.held.grad), channel_id=1, source_target_pairs={{8,0},{9,1},{10,2},{11,3},{12,4},{13,5},{14,6},{15,7}} | collective-permute-start | bytes 1572872 | tf_op jit(solution)/shard_map/ppermute | solution.py:413
  69.1 1.9 %collective-permute-done.25.rest_3_ = bf16[128,1024]{1,0:T(8,128)(2,1)S(1)} collective-permute-done((bf16[128,1024]{1,0:T(8,128)(2,1)S(1)}, bf16[128,1024]{1,0:T(8,128)(2,1)S(1)}, u32[]{:S(2)}, u32[]{:S(2)}) %collective-permute-start.25) | collective-permute-done | bytes 262176 | tf_op jit(solution)/shard_map/ppermute | solution.py:251
  71.0 1.6 %collective-permute-done.24.rest_2_ = bf16[128,1024]{1,0:T(8,128)(2,1)S(1)} collective-permute-done((bf16[128,1024]{1,0:T(8,128)(2,1)S(1)}, bf16[128,1024]{1,0:T(8,128)(2,1)S(1)}, u32[]{:S(2)}, u32[]{:S(2)}) %collective-permute-start.24) | collective-permute-done | bytes 262176 | tf_op jit(solution)/shard_map/ppermute | solution.py:251
  74.0 7.0 %collective-permute-done.26.refs_2_ = bf16[128,1024]{1,0:T(8,128)(2,1)S(1)} collective-permute-done((bf16[128,1024]{1,0:T(8,128)(2,1)S(1)}, bf16[128,1024]{1,0:T(8,128)(2,1)S(1)}, u32[]{:S(2)}, u32[]{:S(2)}) %collective-permute-start.26) | collective-permute-done | bytes 262176 | tf_op jit(solution)/shard_map/ppermute | solution.py:251
  81.6 1.2 %collective-permute-start.28 = (bf16[64,2048]{1,0:T(8,128)(2,1)S(1)}, bf16[64,2048]{1,0:T(8,128)(2,1)S(1)}, u32[]{:S(2)}, u32[]{:S(2)}) collective-permute-start(bf16[64,2048]{1,0:T(8,128)(2,1)S(1)} %get-tuple-element.118), channel_id=1, source_target_pairs={{0,28},{1,29},{2,30},{3,31},{4,24},{5,25},{6,26},{7,27},{8,4},{9,5... | collective-permute-start | bytes 786440 | tf_op jit(solution)/shard_map/ppermute | solution.py:302
  83.7 11.5 %collective-permute-done.28.first = bf16[64,2048]{1,0:T(8,128)(2,1)S(1)} collective-permute-done((bf16[64,2048]{1,0:T(8,128)(2,1)S(1)}, bf16[64,2048]{1,0:T(8,128)(2,1)S(1)}, u32[]{:S(2)}, u32[]{:S(2)}) %collective-permute-start.28) | collective-permute-done | bytes 262176 | tf_op jit(solution)/shard_map/ppermute | solution.py:302
  (61 shorter events, 12.9 us)
Async XLA Ops:
  0.6 44.0 %copy-start = (bf16[1,512,2048]{2,1,0:T(8,128)(2,1)S(1)}, bf16[1,512,2048]{2,1,0:T(8,128)(2,1)}, u32[]{:S(2)}) copy-start(bf16[1,512,2048]{2,1,0:T(8,128)(2,1)} %param.10) | copy-start | bytes 6291460
  0.6 8.4 %collective-permute-start.1 = (bf16[256,512]{1,0:T(8,128)(2,1)}, bf16[256,512]{1,0:T(8,128)(2,1)S(1)}, u32[]{:S(2)}, u32[]{:S(2)}) collective-permute-start(bf16[256,512]{1,0:T(8,128)(2,1)} %bitcast.8), channel_id=1, source_target_pairs={{2,0},{4,2},{6,4},{7,6},{5,7},{3,5},{1,3},{0,1},{10,8},{12,10},{14... | collective-permute-start | bytes 786440 | tf_op jit(solution)/shard_map/ppermute | solution.py:53
  2.8 7.1 %collective-permute-start = (bf16[256,512]{1,0:T(8,128)(2,1)}, bf16[256,512]{1,0:T(8,128)(2,1)S(1)}, u32[]{:S(2)}, u32[]{:S(2)}) collective-permute-start(bf16[256,512]{1,0:T(8,128)(2,1)} %bitcast.9), channel_id=1, source_target_pairs={{0,2},{2,4},{4,6},{6,7},{7,5},{5,3},{3,1},{1,0},{8,10},{10,12},{12... | collective-permute-start | bytes 786440 | tf_op jit(solution)/shard_map/ppermute | solution.py:53
  2.9 11.8 %collective-permute-start.8 = (bf16[256,512]{1,0:T(8,128)(2,1)}, bf16[256,512]{1,0:T(8,128)(2,1)S(1)}, u32[]{:S(2)}, u32[]{:S(2)}) collective-permute-start(bf16[256,512]{1,0:T(8,128)(2,1)} %bitcast.12), channel_id=1, source_target_pairs={{2,0},{4,2},{6,4},{7,6},{5,7},{3,5},{1,3},{0,1},{10,8},{12,10},{14... | collective-permute-start | bytes 786440 | tf_op jit(solution)/shard_map/ppermute | solution.py:53
  4.2 11.2 %collective-permute-start.7 = (bf16[256,512]{1,0:T(8,128)(2,1)}, bf16[256,512]{1,0:T(8,128)(2,1)S(1)}, u32[]{:S(2)}, u32[]{:S(2)}) collective-permute-start(bf16[256,512]{1,0:T(8,128)(2,1)} %bitcast.13), channel_id=1, source_target_pairs={{0,2},{2,4},{4,6},{6,7},{7,5},{5,3},{3,1},{1,0},{8,10},{10,12},{12... | collective-permute-start | bytes 786440 | tf_op jit(solution)/shard_map/ppermute | solution.py:53
  4.4 11.1 %collective-permute-start.9 = (bf16[128,512]{1,0:T(8,128)(2,1)}, bf16[128,512]{1,0:T(8,128)(2,1)S(1)}, u32[]{:S(2)}, u32[]{:S(2)}) collective-permute-start(bf16[128,512]{1,0:T(8,128)(2,1)} %rest_0_), channel_id=1, source_target_pairs={{16,0},{24,8},{0,16},{8,24},{17,1},{25,9},{1,17},{9,25},{18,2},{26... | collective-permute-start | bytes 393224 | tf_op jit(solution)/shard_map/ppermute | solution.py:75
  9.8 12.1 %collective-permute-start.2 = (bf16[256,512]{1,0:T(8,128)(2,1)S(1)}, bf16[256,512]{1,0:T(8,128)(2,1)S(1)}, u32[]{:S(2)}, u32[]{:S(2)}) collective-permute-start(bf16[256,512]{1,0:T(8,128)(2,1)S(1)} %collective-permute-done.refs_0_.rest_2_), channel_id=1, source_target_pairs={{0,2},{2,4},{4,6},{6,7},{7,5},{5,3},{3,1},{1,0},{8,10},{10,12},{12... | collective-permute-start | bytes 786440 | tf_op jit(solution)/shard_map/ppermute | solution.py:53
  10.3 16.0 %collective-permute-start.3 = (bf16[256,512]{1,0:T(8,128)(2,1)S(1)}, bf16[256,512]{1,0:T(8,128)(2,1)S(1)}, u32[]{:S(2)}, u32[]{:S(2)}) collective-permute-start(bf16[256,512]{1,0:T(8,128)(2,1)S(1)} %collective-permute-done.1.refs_0_.rest_4_), channel_id=1, source_target_pairs={{2,0},{4,2},{6,4},{7,6},{5,7},{3,5},{1,3},{0,1},{10,8},{12,10},{14... | collective-permute-start | bytes 786440 | tf_op jit(solution)/shard_map/ppermute | solution.py:53
  15.4 12.2 %collective-permute-start.10 = (bf16[256,512]{1,0:T(8,128)(2,1)S(1)}, bf16[256,512]{1,0:T(8,128)(2,1)S(1)}, u32[]{:S(2)}, u32[]{:S(2)}) collective-permute-start(bf16[256,512]{1,0:T(8,128)(2,1)S(1)} %collective-permute-done.7.refs_1_.rest_3_), channel_id=1, source_target_pairs={{0,2},{2,4},{4,6},{6,7},{7,5},{5,3},{3,1},{1,0},{8,10},{10,12},{12... | collective-permute-start | bytes 786440 | tf_op jit(solution)/shard_map/ppermute | solution.py:53
  15.9 11.8 %collective-permute-start.11 = (bf16[256,512]{1,0:T(8,128)(2,1)S(1)}, bf16[256,512]{1,0:T(8,128)(2,1)S(1)}, u32[]{:S(2)}, u32[]{:S(2)}) collective-permute-start(bf16[256,512]{1,0:T(8,128)(2,1)S(1)} %collective-permute-done.8.refs_1_.rest_5_), channel_id=1, source_target_pairs={{2,0},{4,2},{6,4},{7,6},{5,7},{3,5},{1,3},{0,1},{10,8},{12,10},{14... | collective-permute-start | bytes 786440 | tf_op jit(solution)/shard_map/ppermute | solution.py:53
  16.9 24.6 %collective-permute-start.6 = (bf16[128,2048]{1,0:T(8,128)(2,1)}, bf16[128,2048]{1,0:T(8,128)(2,1)S(1)}, u32[]{:S(2)}, u32[]{:S(2)}) collective-permute-start(bf16[128,2048]{1,0:T(8,128)(2,1)} %bitcast.18), channel_id=1, source_target_pairs={{0,24},{8,16},{16,8},{24,0},{1,25},{9,17},{17,9},{25,1},{2,26},{10... | collective-permute-start | bytes 1572872 | tf_op jit(solution)/shard_map/ppermute | solution.py:326
  21.9 7.2 %collective-permute-start.12 = (bf16[128,512]{1,0:T(8,128)(2,1)}, bf16[128,512]{1,0:T(8,128)(2,1)S(1)}, u32[]{:S(2)}, u32[]{:S(2)}) collective-permute-start(bf16[128,512]{1,0:T(8,128)(2,1)} %rest_0_), channel_id=1, source_target_pairs={{8,0},{16,24},{9,1},{17,25},{10,2},{18,26},{11,3},{19,27},{12,4},{... | collective-permute-start | bytes 393224 | tf_op jit(solution)/shard_map/ppermute | solution.py:75
  26.3 2.8 %collective-permute-start.13 = (bf16[128,512]{1,0:T(8,128)(2,1)S(1)}, bf16[128,512]{1,0:T(8,128)(2,1)S(1)}, u32[]{:S(2)}, u32[]{:S(2)}) collective-permute-start(bf16[128,512]{1,0:T(8,128)(2,1)S(1)} %collective-permute-done.9.rest_1_), channel_id=1, source_target_pairs={{8,0},{16,24},{9,1},{17,25},{10,2},{18,26},{11,3},{19,27},{12,4},{... | collective-permute-start | bytes 393224 | tf_op jit(solution)/shard_map/ppermute | solution.py:75
  27.6 7.0 %collective-permute-start.4 = (bf16[256,512]{1,0:T(8,128)(2,1)S(1)}, bf16[256,512]{1,0:T(8,128)(2,1)S(1)}, u32[]{:S(2)}, u32[]{:S(2)}) collective-permute-start(bf16[256,512]{1,0:T(8,128)(2,1)S(1)} %collective-permute-done.2.refs_0_.rest_6_), channel_id=1, source_target_pairs={{0,2},{2,4},{4,6},{6,7},{7,5},{5,3},{3,1},{1,0},{8,10},{10,12},{12... | collective-permute-start | bytes 786440 | tf_op jit(solution)/shard_map/ppermute | solution.py:53
  27.7 6.9 %collective-permute-start.5 = (bf16[256,512]{1,0:T(8,128)(2,1)S(1)}, bf16[256,512]{1,0:T(8,128)(2,1)S(1)}, u32[]{:S(2)}, u32[]{:S(2)}) collective-permute-start(bf16[256,512]{1,0:T(8,128)(2,1)S(1)} %collective-permute-done.3.refs_0_.rest_8_), channel_id=1, source_target_pairs={{2,0},{4,2},{6,4},{7,6},{5,7},{3,5},{1,3},{0,1},{10,8},{12,10},{14... | collective-permute-start | bytes 786440 | tf_op jit(solution)/shard_map/ppermute | solution.py:53
  29.2 11.1 %collective-permute-start.14 = (bf16[256,512]{1,0:T(8,128)(2,1)S(1)}, bf16[256,512]{1,0:T(8,128)(2,1)S(1)}, u32[]{:S(2)}, u32[]{:S(2)}) collective-permute-start(bf16[256,512]{1,0:T(8,128)(2,1)S(1)} %collective-permute-done.10.refs_1_.rest_7_), channel_id=1, source_target_pairs={{0,2},{2,4},{4,6},{6,7},{7,5},{5,3},{3,1},{1,0},{8,10},{10,12},{12... | collective-permute-start | bytes 786440 | tf_op jit(solution)/shard_map/ppermute | solution.py:53
  29.3 11.0 %collective-permute-start.15 = (bf16[256,512]{1,0:T(8,128)(2,1)S(1)}, bf16[256,512]{1,0:T(8,128)(2,1)S(1)}, u32[]{:S(2)}, u32[]{:S(2)}) collective-permute-start(bf16[256,512]{1,0:T(8,128)(2,1)S(1)} %collective-permute-done.11.refs_1_.rest_9_), channel_id=1, source_target_pairs={{2,0},{4,2},{6,4},{7,6},{5,7},{3,5},{1,3},{0,1},{10,8},{12,10},{14... | collective-permute-start | bytes 786440 | tf_op jit(solution)/shard_map/ppermute | solution.py:53
  40.3 6.0 %collective-permute-start.17 = (bf16[256,512]{1,0:T(8,128)(2,1)S(1)}, bf16[256,512]{1,0:T(8,128)(2,1)S(1)}, u32[]{:S(2)}, u32[]{:S(2)}) collective-permute-start(bf16[256,512]{1,0:T(8,128)(2,1)S(1)} %collective-permute-done.15.refs_1_.rest_13_), channel_id=1, source_target_pairs={{2,0},{4,2},{6,4},{7,6},{5,7},{3,5},{1,3},{0,1},{10,8},{12,10},{14... | collective-permute-start | bytes 786440 | tf_op jit(solution)/shard_map/ppermute | solution.py:60
  41.6 5.6 %collective-permute-start.16 = (bf16[256,512]{1,0:T(8,128)(2,1)S(1)}, bf16[256,512]{1,0:T(8,128)(2,1)S(1)}, u32[]{:S(2)}, u32[]{:S(2)}) collective-permute-start(bf16[256,512]{1,0:T(8,128)(2,1)S(1)} %collective-permute-done.4.refs_0_.rest_10_), channel_id=1, source_target_pairs={{0,2},{2,4},{4,6},{6,7},{7,5},{5,3},{3,1},{1,0},{8,10},{10,12},{12... | collective-permute-start | bytes 786440 | tf_op jit(solution)/shard_map/ppermute | solution.py:60
  44.6 2.5 %copy-start.2 = (bf16[1,256,512]{2,1,0:T(8,128)(2,1)S(1)}, bf16[1,256,512]{2,1,0:T(8,128)(2,1)}, u32[]{:S(2)}) copy-start(bf16[1,256,512]{2,1,0:T(8,128)(2,1)} %param.8) | copy-start | bytes 786436
  48.1 4.7 %collective-permute-start.18 = (bf16[128,2048]{1,0:T(8,128)(2,1)S(1)}, bf16[128,2048]{1,0:T(8,128)(2,1)S(1)}, u32[]{:S(2)}, u32[]{:S(2)}) collective-permute-start(bf16[128,2048]{1,0:T(8,128)(2,1)S(1)} %get-tuple-element.102.held), channel_id=1, source_target_pairs={{0,8},{8,0},{16,24},{24,16},{1,9},{9,1},{17,25},{25,17},{2,10},{10... | collective-permute-start | bytes 1572872 | tf_op jit(solution)/shard_map/ppermute | solution.py:413
  51.3 2.0 %collective-permute-start.19 = (bf16[512,128]{1,0:T(8,128)(2,1)S(1)}, bf16[512,128]{1,0:T(8,128)(2,1)S(1)}, u32[]{:S(2)}, u32[]{:S(2)}) collective-permute-start(bf16[512,128]{1,0:T(8,128)(2,1)S(1)} %get-tuple-element.106), channel_id=1, source_target_pairs={{0,8},{8,16},{16,24},{24,0},{1,9},{9,17},{17,25},{25,1},{2,10},{10... | collective-permute-start | bytes 393224 | tf_op jit(solution)/shard_map/ppermute | solution.py:393
  53.3 10.6 %collective-permute-start.20 = (bf16[128,2048]{1,0:T(8,128)(2,1)S(1)}, bf16[128,2048]{1,0:T(8,128)(2,1)S(1)}, u32[]{:S(2)}, u32[]{:S(2)}) collective-permute-start(bf16[128,2048]{1,0:T(8,128)(2,1)S(1)} %tick.3.held), channel_id=1, source_target_pairs={{16,8},{17,9},{18,10},{19,11},{20,12},{21,13},{22,14},{23,15}} | collective-permute-start | bytes 1572872 | tf_op jit(solution)/shard_map/ppermute | solution.py:413
  54.6 3.2 %collective-permute-start.21 = (bf16[256,128]{1,0:T(8,128)(2,1)S(1)}, bf16[256,128]{1,0:T(8,128)(2,1)S(1)}, u32[]{:S(2)}, u32[]{:S(2)}) collective-permute-start(bf16[256,128]{1,0:T(8,128)(2,1)S(1)} %get-tuple-element.109), channel_id=1, source_target_pairs={{0,1},{1,0},{2,3},{3,2},{4,5},{5,4},{6,7},{7,6},{8,9},{9,8},{10,11... | collective-permute-start | bytes 196616 | tf_op jit(solution)/shard_map/ppermute | solution.py:251
  55.9 3.1 %collective-permute-start.22 = (bf16[256,128]{1,0:T(8,128)(2,1)S(1)}, bf16[256,128]{1,0:T(8,128)(2,1)S(1)}, u32[]{:S(2)}, u32[]{:S(2)}) collective-permute-start(bf16[256,128]{1,0:T(8,128)(2,1)S(1)} %get-tuple-element.110), channel_id=1, source_target_pairs={{0,2},{1,3},{2,0},{3,1},{4,6},{5,7},{6,4},{7,5},{8,10},{9,11},{10,... | collective-permute-start | bytes 196616 | tf_op jit(solution)/shard_map/ppermute | solution.py:251
  65.2 5.9 %collective-permute-start.25 = (bf16[128,1024]{1,0:T(8,128)(2,1)S(1)}, bf16[128,1024]{1,0:T(8,128)(2,1)S(1)}, u32[]{:S(2)}, u32[]{:S(2)}) collective-permute-start(bf16[128,1024]{1,0:T(8,128)(2,1)S(1)} %get-tuple-element.120), channel_id=1, source_target_pairs={{0,2},{1,3},{2,0},{3,1},{4,6},{5,7},{6,4},{7,5},{8,10},{9,11},{10,... | collective-permute-start | bytes 786440 | tf_op jit(solution)/shard_map/ppermute | solution.py:251
  65.4 7.2 %collective-permute-start.24 = (bf16[128,1024]{1,0:T(8,128)(2,1)S(1)}, bf16[128,1024]{1,0:T(8,128)(2,1)S(1)}, u32[]{:S(2)}, u32[]{:S(2)}) collective-permute-start(bf16[128,1024]{1,0:T(8,128)(2,1)S(1)} %get-tuple-element.121), channel_id=1, source_target_pairs={{0,1},{1,0},{2,3},{3,2},{4,5},{5,4},{6,7},{7,6},{8,9},{9,8},{10,11... | collective-permute-start | bytes 786440 | tf_op jit(solution)/shard_map/ppermute | solution.py:251
  67.8 15.0 %collective-permute-start.23 = (bf16[128,2048]{1,0:T(8,128)(2,1)S(1)}, bf16[128,2048]{1,0:T(8,128)(2,1)S(1)}, u32[]{:S(2)}, u32[]{:S(2)}) collective-permute-start(bf16[128,2048]{1,0:T(8,128)(2,1)S(1)} %tick.4.held.grad), channel_id=1, source_target_pairs={{8,0},{9,1},{10,2},{11,3},{12,4},{13,5},{14,6},{15,7}} | collective-permute-start | bytes 1572872 | tf_op jit(solution)/shard_map/ppermute | solution.py:413
  73.3 7.7 %collective-permute-start.26 = (bf16[128,1024]{1,0:T(8,128)(2,1)S(1)}, bf16[128,1024]{1,0:T(8,128)(2,1)S(1)}, u32[]{:S(2)}, u32[]{:S(2)}) collective-permute-start(bf16[128,1024]{1,0:T(8,128)(2,1)S(1)} %get-tuple-element.116), channel_id=1, source_target_pairs={{0,2},{1,3},{2,0},{3,1},{4,6},{5,7},{6,4},{7,5},{8,10},{9,11},{10,... | collective-permute-start | bytes 786440 | tf_op jit(solution)/shard_map/ppermute | solution.py:251
  73.5 7.9 %collective-permute-start.27 = (bf16[128,1024]{1,0:T(8,128)(2,1)S(1)}, bf16[128,1024]{1,0:T(8,128)(2,1)S(1)}, u32[]{:S(2)}, u32[]{:S(2)}) collective-permute-start(bf16[128,1024]{1,0:T(8,128)(2,1)S(1)} %get-tuple-element.117), channel_id=1, source_target_pairs={{0,1},{1,0},{2,3},{3,2},{4,5},{5,4},{6,7},{7,6},{8,9},{9,8},{10,11... | collective-permute-start | bytes 786440 | tf_op jit(solution)/shard_map/ppermute | solution.py:251
  81.6 13.6 %collective-permute-start.28 = (bf16[64,2048]{1,0:T(8,128)(2,1)S(1)}, bf16[64,2048]{1,0:T(8,128)(2,1)S(1)}, u32[]{:S(2)}, u32[]{:S(2)}) collective-permute-start(bf16[64,2048]{1,0:T(8,128)(2,1)S(1)} %get-tuple-element.118), channel_id=1, source_target_pairs={{0,28},{1,29},{2,30},{3,31},{4,24},{5,25},{6,26},{7,27},{8,4},{9,5... | collective-permute-start | bytes 786440 | tf_op jit(solution)/shard_map/ppermute | solution.py:302
  82.8 12.3 %collective-permute-start.29 = (bf16[64,2048]{1,0:T(8,128)(2,1)S(1)}, bf16[64,2048]{1,0:T(8,128)(2,1)S(1)}, u32[]{:S(2)}, u32[]{:S(2)}) collective-permute-start(bf16[64,2048]{1,0:T(8,128)(2,1)S(1)} %get-tuple-element.119), channel_id=1, source_target_pairs={{0,24},{1,25},{2,26},{3,27},{4,28},{5,29},{6,30},{7,31},{8,0},{9,1... | collective-permute-start | bytes 786440 | tf_op jit(solution)/shard_map/ppermute | solution.py:302
  (5 other events, 6.9 us)

commit v6 on v5

--- a/solution.py
+++ b/solution.py
@@ -62,16 +62,13 @@
     return pieces, offsets
 
 
-def gather_to_ends(x, axis):
+def gather_blocks(x, axis):
     size = lax.axis_size(axis)
-    steps = [1 << place for place in range(size.bit_length() - 1)][::-1]
-    needed = [{0, size - 1}]
-    for stride in steps[::-1]:
-        needed.append(needed[-1] | {i ^ stride for i in needed[-1]})
     held, offsets = [x], [0]
     yield held, offsets
-    for stride, wanted in zip(steps, needed[-2::-1]):
-        pairs = [(i ^ stride, i) for i in sorted(wanted)]
+    for place in range(size.bit_length() - 1)[::-1]:
+        stride = 1 << place
+        pairs = [(i, i ^ stride) for i in range(size)]
         held += [lax.ppermute(block, axis, pairs) for block in list(held)]
         offsets += [offset ^ stride for offset in offsets]
         yield held, offsets
@@ -312,25 +309,27 @@
 
     shape = jax.ShapeDtypeStruct
     small = shape((local_rows, hidden_units), F32)
-    cotangents = gather_to_ends(cotangent, "section")
+    cotangents = gather_blocks(cotangent, "section")
     blocks, block_offsets = next(cotangents)
     own_rows = stash[0]
 
+    last_step = replicas // 2
+
     def between(step, i, moving):
         nonlocal blocks, own_rows
+        if step == 1 and i == 0:
+            mirrored = [(k, sections - 1 - k) for k in range(sections)]
+            own_rows = lax.ppermute(own_rows, "section", mirrored)
         if step == 1 and i == 1:
             blocks, _ = next(cotangents, (blocks, None))
         if step == 2 and i == 0:
-            own_rows, *moving = after((own_rows, *moving))
-            mirrored = [(k, sections - 1 - k) for k in range(sections)]
-            own_rows = lax.ppermute(own_rows, "section", mirrored)
-        if step == 2 and i == 1:
             moving, blocks = after((moving, blocks))
+        if step == last_step - 1 and i == 0:
             blocks, _ = next(cotangents, (list(blocks), None))
-        if step == 3 and i == 1:
+        if step == last_step - 1 and i == 1:
+            moving, own_rows = after((moving, own_rows))
+        if step == last_step and i == 0:
             moving, blocks = after((moving, blocks))
-        if step == replicas // 2 and i == 0:
-            moving, own_rows = after((moving, own_rows))
         return moving
 
     pieces, offsets = gather_ring([gate_weight[0], up_weight[0]], "dp", between)
@@ -409,10 +408,10 @@
             reduced = reduce_rows(scored, theirs, outgoing)
         if section == sections - 3:
             outgoing, scored = after((outgoing, scored))
-        pairs = swap if section == sections - 2 else [(section + 1, section)]
+        pairs = swap if section % 2 == 0 else [(section + 1, section)]
         grad = lax.ppermute(outgoing, "section", pairs)
         if section == max(sections - 3, 0):
-            grad, theirs = after((grad, swap_scored(scored)))
+            theirs = swap_scored(scored)
         outgoing = tick(section, grad, outgoing)
 
     send, keep = reduced

time: 97 us -> 93 us (0.959)
  starting transfers between devices: 36.1 us -> 29.9 us
  waiting for transfers between devices: 49.3 us -> 52.5 us
    ppermute x3, waiting for transfers between devices: 5.68 us -> 10.3 us  [on_device(): grad = lax.ppermute(outgoing, 'section', pairs)]
    ppermute x6, waiting for transfers between devices: 12.8 us -> 8.6 us  [along(): return [lax.ppermute(v, 'dp', pairs) for v in values]]
    ppermute x3, starting transfers between devices: 5.8 us -> 3.14 us  [on_device(): grad = lax.ppermute(outgoing, 'section', pairs)]
    ppermute x2, waiting for transfers between devices: 11.5 us -> 13.3 us  [to_layer(): return lax.ppermute(value, ('section', 'dp'), pairs)]
    ppermute x12, waiting for transfers between devices: 17.9 us -> 16.4 us  [gather_ring(): both = (lax.ppermute(v, axis, ahead), lax.ppermute(w, axis, back))]
    ppermute x1, starting transfers between devices: 4.99 us -> 3.63 us  [between(): own_rows = lax.ppermute(own_rows, 'section', mirrored)]
    ppermute x2, waiting for transfers between devices: 1.04 us -> 2.21 us  [gather_ring(): pieces.append([lax.ppermute(v, axis, ahead), lax.ppermute(w, axis, back)])]
    ppermute x6, starting transfers between devices: 5.98 us -> 4.81 us  [along(): return [lax.ppermute(v, 'dp', pairs) for v in values]]
  transfers between devices with their start and end apart: 30 -> 30, of which waited for: 18 -> 20; matrix products, arithmetic and copies ran while one was open for 0% -> 0% of each run, Pallas kernels for 5% -> 5%
where the time goes in v6:
time: 93 us; the launch traced here: 92.9 us
  waiting for transfers between devices  52.5 us (56%)
  starting transfers between devices  29.9 us (32%)
  Pallas kernels  7.68 us (8%)
  local copies, waits for them, and re-layouts  1.96 us (2%)
    ppermute x12, waiting for transfers between devices, gather_ring(): both = (lax.ppermute(v, axis, ahead), lax.ppermute(w, axis, back))  16.4 us
    ppermute x2, waiting for transfers between devices, to_layer(): return lax.ppermute(value, ('section', 'dp'), pairs)  13.3 us
    ppermute x3, waiting for transfers between devices, on_device(): grad = lax.ppermute(outgoing, 'section', pairs)  10.3 us
    ppermute x12, starting transfers between devices, gather_ring(): both = (lax.ppermute(v, axis, ahead), lax.ppermute(w, axis, back))  9.58 us
    ppermute x6, waiting for transfers between devices, along(): return [lax.ppermute(v, 'dp', pairs) for v in values]  8.6 us
    ppermute x3, starting transfers between devices, gather_blocks(): held += [lax.ppermute(block, axis, pairs) for block in list(held)]  7.54 us
    ppermute x6, starting transfers between devices, along(): return [lax.ppermute(v, 'dp', pairs) for v in values]  4.81 us
    ppermute x1, starting transfers between devices, between(): own_rows = lax.ppermute(own_rows, 'section', mirrored)  3.63 us
  transfers between devices with their start and end apart: 30, of which 20 were waited for; matrix products, arithmetic and copies ran while one was open for 0% of the time, Pallas kernels for 5%

profile of v6, /device:TPU:1, one launch (start us, length us, event | category | flops | bytes accessed | tf_op | source)
XLA Modules:
  0.0 92.9 jit_solution(9114263443947157836)
XLA Ops:
  0.6 2.1 %collective-permute-start.6 = (bf16[256,512]{1,0:T(8,128)(2,1)}, bf16[256,512]{1,0:T(8,128)(2,1)S(1)}, u32[]{:S(2)}, u32[]{:S(2)}) collective-permute-start(bf16[256,512]{1,0:T(8,128)(2,1)} %bitcast.8), channel_id=1, source_target_pairs={{2,0},{4,2},{6,4},{7,6},{5,7},{3,5},{1,3},{0,1},{10,8},{12,10},{14... | collective-permute-start | bytes 786440 | tf_op jit(solution)/shard_map/ppermute | solution.py:53
  2.9 1.3 %collective-permute-start.7 = (bf16[128,512]{1,0:T(8,128)(2,1)}, bf16[128,512]{1,0:T(8,128)(2,1)S(1)}, u32[]{:S(2)}, u32[]{:S(2)}) collective-permute-start(bf16[128,512]{1,0:T(8,128)(2,1)} %rest_0_), channel_id=1, source_target_pairs={{0,16},{8,24},{16,0},{24,8},{1,17},{9,25},{17,1},{25,9},{2,18},{10... | collective-permute-start | bytes 393224 | tf_op jit(solution)/shard_map/ppermute | solution.py:72
  4.2 1.2 %collective-permute-start.1 = (bf16[256,512]{1,0:T(8,128)(2,1)}, bf16[256,512]{1,0:T(8,128)(2,1)S(1)}, u32[]{:S(2)}, u32[]{:S(2)}) collective-permute-start(bf16[256,512]{1,0:T(8,128)(2,1)} %bitcast.12), channel_id=1, source_target_pairs={{2,0},{4,2},{6,4},{7,6},{5,7},{3,5},{1,3},{0,1},{10,8},{12,10},{14... | collective-permute-start | bytes 786440 | tf_op jit(solution)/shard_map/ppermute | solution.py:53
  5.7 3.4 %collective-permute-done.6.refs_0_.rest_4_ = bf16[256,512]{1,0:T(8,128)(2,1)S(1)} collective-permute-done((bf16[256,512]{1,0:T(8,128)(2,1)}, bf16[256,512]{1,0:T(8,128)(2,1)S(1)}, u32[]{:S(2)}, u32[]{:S(2)}) %collective-permute-start.6) | collective-permute-done | bytes 262176 | tf_op jit(solution)/shard_map/ppermute | solution.py:53
  9.1 3.6 %collective-permute-start.4 = (bf16[128,2048]{1,0:T(8,128)(2,1)}, bf16[128,2048]{1,0:T(8,128)(2,1)S(1)}, u32[]{:S(2)}, u32[]{:S(2)}) collective-permute-start(bf16[128,2048]{1,0:T(8,128)(2,1)} %bitcast.18), channel_id=1, source_target_pairs={{0,24},{8,16},{16,8},{24,0},{1,25},{9,17},{17,9},{25,1},{2,26},{10... | collective-permute-start | bytes 1572872 | tf_op jit(solution)/shard_map/ppermute | solution.py:322
  12.7 1.3 %collective-permute-start.8 = (bf16[256,512]{1,0:T(8,128)(2,1)S(1)}, bf16[256,512]{1,0:T(8,128)(2,1)S(1)}, u32[]{:S(2)}, u32[]{:S(2)}) collective-permute-start(bf16[256,512]{1,0:T(8,128)(2,1)S(1)} %collective-permute-done.5.refs_0_.rest_2_), channel_id=1, source_target_pairs={{0,2},{2,4},{4,6},{6,7},{7,5},{5,3},{3,1},{1,0},{8,10},{10,12},{12... | collective-permute-start | bytes 786440 | tf_op jit(solution)/shard_map/ppermute | solution.py:53
  15.9 1.0 %collective-permute-start.3 = (bf16[256,512]{1,0:T(8,128)(2,1)S(1)}, bf16[256,512]{1,0:T(8,128)(2,1)S(1)}, u32[]{:S(2)}, u32[]{:S(2)}) collective-permute-start(bf16[256,512]{1,0:T(8,128)(2,1)S(1)} %collective-permute-done.1.refs_1_.rest_5_), channel_id=1, source_target_pairs={{2,0},{4,2},{6,4},{7,6},{5,7},{3,5},{1,3},{0,1},{10,8},{12,10},{14... | collective-permute-start | bytes 786440 | tf_op jit(solution)/shard_map/ppermute | solution.py:53
  16.9 4.2 %collective-permute-done.8.refs_0_.rest_6_ = bf16[256,512]{1,0:T(8,128)(2,1)S(1)} collective-permute-done((bf16[256,512]{1,0:T(8,128)(2,1)S(1)}, bf16[256,512]{1,0:T(8,128)(2,1)S(1)}, u32[]{:S(2)}, u32[]{:S(2)}) %collective-permute-start.8) | collective-permute-done | bytes 262176 | tf_op jit(solution)/shard_map/ppermute | solution.py:53
  21.1 1.0 %collective-permute-done.9.refs_0_.rest_8_ = bf16[256,512]{1,0:T(8,128)(2,1)S(1)} collective-permute-done((bf16[256,512]{1,0:T(8,128)(2,1)S(1)}, bf16[256,512]{1,0:T(8,128)(2,1)S(1)}, u32[]{:S(2)}, u32[]{:S(2)}) %collective-permute-start.9) | collective-permute-done | bytes 262176 | tf_op jit(solution)/shard_map/ppermute | solution.py:53
  22.1 1.4 %collective-permute-start.10 = (bf16[256,512]{1,0:T(8,128)(2,1)S(1)}, bf16[256,512]{1,0:T(8,128)(2,1)S(1)}, u32[]{:S(2)}, u32[]{:S(2)}) collective-permute-start(bf16[256,512]{1,0:T(8,128)(2,1)S(1)} %collective-permute-done.8.refs_0_.rest_6_), channel_id=1, source_target_pairs={{0,2},{2,4},{4,6},{6,7},{7,5},{5,3},{3,1},{1,0},{8,10},{10,12},{12... | collective-permute-start | bytes 786440 | tf_op jit(solution)/shard_map/ppermute | solution.py:53
  23.5 3.2 %collective-permute-done.2.refs_1_.rest_7_ = bf16[256,512]{1,0:T(8,128)(2,1)S(1)} collective-permute-done((bf16[256,512]{1,0:T(8,128)(2,1)S(1)}, bf16[256,512]{1,0:T(8,128)(2,1)S(1)}, u32[]{:S(2)}, u32[]{:S(2)}) %collective-permute-start.2) | collective-permute-done | bytes 262176 | tf_op jit(solution)/shard_map/ppermute | solution.py:53
  26.7 1.0 %collective-permute-done.3.refs_1_.rest_9_ = bf16[256,512]{1,0:T(8,128)(2,1)S(1)} collective-permute-done((bf16[256,512]{1,0:T(8,128)(2,1)S(1)}, bf16[256,512]{1,0:T(8,128)(2,1)S(1)}, u32[]{:S(2)}, u32[]{:S(2)}) %collective-permute-start.3) | collective-permute-done | bytes 262176 | tf_op jit(solution)/shard_map/ppermute | solution.py:53
  27.7 1.4 %collective-permute-start.14 = (bf16[256,512]{1,0:T(8,128)(2,1)S(1)}, bf16[256,512]{1,0:T(8,128)(2,1)S(1)}, u32[]{:S(2)}, u32[]{:S(2)}) collective-permute-start(bf16[256,512]{1,0:T(8,128)(2,1)S(1)} %collective-permute-done.2.refs_1_.rest_7_), channel_id=1, source_target_pairs={{0,2},{2,4},{4,6},{6,7},{7,5},{5,3},{3,1},{1,0},{8,10},{10,12},{12... | collective-permute-start | bytes 786440 | tf_op jit(solution)/shard_map/ppermute | solution.py:53
  29.1 2.9 %collective-permute-start.12 = (bf16[128,512]{1,0:T(8,128)(2,1)}, bf16[128,512]{1,0:T(8,128)(2,1)S(1)}, u32[]{:S(2)}, u32[]{:S(2)}) collective-permute-start(bf16[128,512]{1,0:T(8,128)(2,1)} %rest_0_), channel_id=1, source_target_pairs={{0,8},{8,0},{16,24},{24,16},{1,9},{9,1},{17,25},{25,17},{2,10},{10... | collective-permute-start | bytes 393224 | tf_op jit(solution)/shard_map/ppermute | solution.py:72
  32.3 3.3 %collective-permute-start.13 = (bf16[128,512]{1,0:T(8,128)(2,1)S(1)}, bf16[128,512]{1,0:T(8,128)(2,1)S(1)}, u32[]{:S(2)}, u32[]{:S(2)}) collective-permute-start(bf16[128,512]{1,0:T(8,128)(2,1)S(1)} %collective-permute-done.7.rest_1_), channel_id=1, source_target_pairs={{0,8},{8,0},{16,24},{24,16},{1,9},{9,1},{17,25},{25,17},{2,10},{10... | collective-permute-start | bytes 393224 | tf_op jit(solution)/shard_map/ppermute | solution.py:72
  35.6 1.0 %collective-permute-done.13.rest_3_ = bf16[128,512]{1,0:T(8,128)(2,1)S(1)} collective-permute-done((bf16[128,512]{1,0:T(8,128)(2,1)S(1)}, bf16[128,512]{1,0:T(8,128)(2,1)S(1)}, u32[]{:S(2)}, u32[]{:S(2)}) %collective-permute-start.13) | collective-permute-done | bytes 131104 | tf_op jit(solution)/shard_map/ppermute | solution.py:72
  36.6 1.3 %collective-permute-done.14.refs_1_.rest_11_ = bf16[256,512]{1,0:T(8,128)(2,1)S(1)} collective-permute-done((bf16[256,512]{1,0:T(8,128)(2,1)S(1)}, bf16[256,512]{1,0:T(8,128)(2,1)S(1)}, u32[]{:S(2)}, u32[]{:S(2)}) %collective-permute-start.14) | collective-permute-done | bytes 262176 | tf_op jit(solution)/shard_map/ppermute | solution.py:53
  37.9 0.9 %collective-permute-done.15.refs_1_.rest_13_ = bf16[256,512]{1,0:T(8,128)(2,1)S(1)} collective-permute-done((bf16[256,512]{1,0:T(8,128)(2,1)S(1)}, bf16[256,512]{1,0:T(8,128)(2,1)S(1)}, u32[]{:S(2)}, u32[]{:S(2)}) %collective-permute-start.15) | collective-permute-done | bytes 262176 | tf_op jit(solution)/shard_map/ppermute | solution.py:53
  39.2 0.9 %copy-done.1 = bf16[1,256,512]{2,1,0:T(8,128)(2,1)S(1)} copy-done((bf16[1,256,512]{2,1,0:T(8,128)(2,1)S(1)}, bf16[1,256,512]{2,1,0:T(8,128)(2,1)}, u32[]{:S(2)}) %copy-start.1) | copy-done | bytes 262168
  40.2 0.9 %copy-done.3 = bf16[1,256,512]{2,1,0:T(8,128)(2,1)S(1)} copy-done((bf16[1,256,512]{2,1,0:T(8,128)(2,1)S(1)}, bf16[1,256,512]{2,1,0:T(8,128)(2,1)}, u32[]{:S(2)}) %copy-start.3) | copy-done | bytes 262168
  44.3 1.5 %collective-permute-done.17.rest_15_ = bf16[256,512]{1,0:T(8,128)(2,1)S(1)} collective-permute-done((bf16[256,512]{1,0:T(8,128)(2,1)S(1)}, bf16[256,512]{1,0:T(8,128)(2,1)S(1)}, u32[]{:S(2)}, u32[]{:S(2)}) %collective-permute-start.17) | collective-permute-done | bytes 262176 | tf_op jit(solution)/shard_map/ppermute | solution.py:60
  46.7 1.9 %collective-permute-start.18 = (bf16[128,2048]{1,0:T(8,128)(2,1)S(1)}, bf16[128,2048]{1,0:T(8,128)(2,1)S(1)}, u32[]{:S(2)}, u32[]{:S(2)}) collective-permute-start(bf16[128,2048]{1,0:T(8,128)(2,1)S(1)} %get-tuple-element.93.held), channel_id=1, source_target_pairs={{0,8},{8,0},{16,24},{24,16},{1,9},{9,1},{17,25},{25,17},{2,10},{10... | collective-permute-start | bytes 1572872 | tf_op jit(solution)/shard_map/ppermute | solution.py:412
  50.7 1.3 %collective-permute-start.20 = (bf16[128,2048]{1,0:T(8,128)(2,1)S(1)}, bf16[128,2048]{1,0:T(8,128)(2,1)S(1)}, u32[]{:S(2)}, u32[]{:S(2)}) collective-permute-start(bf16[128,2048]{1,0:T(8,128)(2,1)S(1)} %tick.3.held), channel_id=1, source_target_pairs={{16,8},{17,9},{18,10},{19,11},{20,12},{21,13},{22,14},{23,15}} | collective-permute-start | bytes 1572872 | tf_op jit(solution)/shard_map/ppermute | solution.py:412
  52.0 9.6 %collective-permute-done.20.grad = bf16[128,2048]{1,0:T(8,128)(2,1)S(1)} collective-permute-done((bf16[128,2048]{1,0:T(8,128)(2,1)S(1)}, bf16[128,2048]{1,0:T(8,128)(2,1)S(1)}, u32[]{:S(2)}, u32[]{:S(2)}) %collective-permute-start.20) | collective-permute-done | bytes 524320 | tf_op jit(solution)/shard_map/ppermute | solution.py:412
  61.6 1.3 %tick.4.held.grad = bf16[128,2048]{1,0:T(8,128)(2,1)S(1)} custom-call(bf16[128,2048]{1,0:T(8,128)(2,1)S(1)} %collective-permute-done.20.grad, bf16[128,2048]{1,0:T(8,128)(2,1)S(1)} %tick.3.held, bf16[2048,512]{1,0:T(8,128)(2,1)S(1)} %turn_down.1.down, bf16[1,2048]{1,0:T(2,128)(2,1)S(1)} %copy-done.5, f32[128,512]{1,0:T(8,128)S(1)} %get-tuple-element.94.a, ...), custom_call_target="tpu_custom_call" | custom-call | flops 805306368 | bytes 4194304 | tf_op jit(solution)/shard_map/tick/pallas_call | solution.py:395
  62.9 1.1 %collective-permute-start.25 = (bf16[128,1024]{1,0:T(8,128)(2,1)S(1)}, bf16[128,1024]{1,0:T(8,128)(2,1)S(1)}, u32[]{:S(2)}, u32[]{:S(2)}) collective-permute-start(bf16[128,1024]{1,0:T(8,128)(2,1)S(1)} %get-tuple-element.108), channel_id=1, source_target_pairs={{0,2},{1,3},{2,0},{3,1},{4,6},{5,7},{6,4},{7,5},{8,10},{9,11},{10,... | collective-permute-start | bytes 786440 | tf_op jit(solution)/shard_map/ppermute | solution.py:248
  64.0 1.3 %collective-permute-start.24 = (bf16[128,1024]{1,0:T(8,128)(2,1)S(1)}, bf16[128,1024]{1,0:T(8,128)(2,1)S(1)}, u32[]{:S(2)}, u32[]{:S(2)}) collective-permute-start(bf16[128,1024]{1,0:T(8,128)(2,1)S(1)} %get-tuple-element.109), channel_id=1, source_target_pairs={{0,1},{1,0},{2,3},{3,2},{4,5},{5,4},{6,7},{7,6},{8,9},{9,8},{10,11... | collective-permute-start | bytes 786440 | tf_op jit(solution)/shard_map/ppermute | solution.py:248
  66.0 3.9 %collective-permute-done.22.rest_0_ = bf16[256,128]{1,0:T(8,128)(2,1)S(1)} collective-permute-done((bf16[256,128]{1,0:T(8,128)(2,1)S(1)}, bf16[256,128]{1,0:T(8,128)(2,1)S(1)}, u32[]{:S(2)}, u32[]{:S(2)}) %collective-permute-start.22) | collective-permute-done | bytes 65568 | tf_op jit(solution)/shard_map/ppermute | solution.py:248
  71.2 1.2 %collective-permute-start.27 = (bf16[128,1024]{1,0:T(8,128)(2,1)S(1)}, bf16[128,1024]{1,0:T(8,128)(2,1)S(1)}, u32[]{:S(2)}, u32[]{:S(2)}) collective-permute-start(bf16[128,1024]{1,0:T(8,128)(2,1)S(1)} %get-tuple-element.105), channel_id=1, source_target_pairs={{0,1},{1,0},{2,3},{3,2},{4,5},{5,4},{6,7},{7,6},{8,9},{9,8},{10,11... | collective-permute-start | bytes 786440 | tf_op jit(solution)/shard_map/ppermute | solution.py:248
  72.4 3.5 %collective-permute-done.26.refs_2_ = bf16[128,1024]{1,0:T(8,128)(2,1)S(1)} collective-permute-done((bf16[128,1024]{1,0:T(8,128)(2,1)S(1)}, bf16[128,1024]{1,0:T(8,128)(2,1)S(1)}, u32[]{:S(2)}, u32[]{:S(2)}) %collective-permute-start.26) | collective-permute-done | bytes 262176 | tf_op jit(solution)/shard_map/ppermute | solution.py:248
  75.9 1.2 %collective-permute-done.27.refs_3_ = bf16[128,1024]{1,0:T(8,128)(2,1)S(1)} collective-permute-done((bf16[128,1024]{1,0:T(8,128)(2,1)S(1)}, bf16[128,1024]{1,0:T(8,128)(2,1)S(1)}, u32[]{:S(2)}, u32[]{:S(2)}) %collective-permute-start.27) | collective-permute-done | bytes 262176 | tf_op jit(solution)/shard_map/ppermute | solution.py:248
  78.7 13.3 %collective-permute-done.28.first = bf16[64,2048]{1,0:T(8,128)(2,1)S(1)} collective-permute-done((bf16[64,2048]{1,0:T(8,128)(2,1)S(1)}, bf16[64,2048]{1,0:T(8,128)(2,1)S(1)}, u32[]{:S(2)}, u32[]{:S(2)}) %collective-permute-start.28) | collective-permute-done | bytes 262176 | tf_op jit(solution)/shard_map/ppermute | solution.py:299
  (61 shorter events, 13.5 us)
Async XLA Ops:
  0.6 8.4 %collective-permute-start.6 = (bf16[256,512]{1,0:T(8,128)(2,1)}, bf16[256,512]{1,0:T(8,128)(2,1)S(1)}, u32[]{:S(2)}, u32[]{:S(2)}) collective-permute-start(bf16[256,512]{1,0:T(8,128)(2,1)} %bitcast.8), channel_id=1, source_target_pairs={{2,0},{4,2},{6,4},{7,6},{5,7},{3,5},{1,3},{0,1},{10,8},{12,10},{14... | collective-permute-start | bytes 786440 | tf_op jit(solution)/shard_map/ppermute | solution.py:53
  2.8 9.9 %collective-permute-start.5 = (bf16[256,512]{1,0:T(8,128)(2,1)}, bf16[256,512]{1,0:T(8,128)(2,1)S(1)}, u32[]{:S(2)}, u32[]{:S(2)}) collective-permute-start(bf16[256,512]{1,0:T(8,128)(2,1)} %bitcast.9), channel_id=1, source_target_pairs={{0,2},{2,4},{4,6},{6,7},{7,5},{5,3},{3,1},{1,0},{8,10},{10,12},{12... | collective-permute-start | bytes 786440 | tf_op jit(solution)/shard_map/ppermute | solution.py:53
  2.9 9.8 %collective-permute-start.7 = (bf16[128,512]{1,0:T(8,128)(2,1)}, bf16[128,512]{1,0:T(8,128)(2,1)S(1)}, u32[]{:S(2)}, u32[]{:S(2)}) collective-permute-start(bf16[128,512]{1,0:T(8,128)(2,1)} %rest_0_), channel_id=1, source_target_pairs={{0,16},{8,24},{16,0},{24,8},{1,17},{9,25},{17,1},{25,9},{2,18},{10... | collective-permute-start | bytes 393224 | tf_op jit(solution)/shard_map/ppermute | solution.py:72
  4.2 10.5 %collective-permute-start.1 = (bf16[256,512]{1,0:T(8,128)(2,1)}, bf16[256,512]{1,0:T(8,128)(2,1)S(1)}, u32[]{:S(2)}, u32[]{:S(2)}) collective-permute-start(bf16[256,512]{1,0:T(8,128)(2,1)} %bitcast.12), channel_id=1, source_target_pairs={{2,0},{4,2},{6,4},{7,6},{5,7},{3,5},{1,3},{0,1},{10,8},{12,10},{14... | collective-permute-start | bytes 786440 | tf_op jit(solution)/shard_map/ppermute | solution.py:53
  5.4 10.0 %collective-permute-start = (bf16[256,512]{1,0:T(8,128)(2,1)}, bf16[256,512]{1,0:T(8,128)(2,1)S(1)}, u32[]{:S(2)}, u32[]{:S(2)}) collective-permute-start(bf16[256,512]{1,0:T(8,128)(2,1)} %bitcast.13), channel_id=1, source_target_pairs={{0,2},{2,4},{4,6},{6,7},{7,5},{5,3},{3,1},{1,0},{8,10},{10,12},{12... | collective-permute-start | bytes 786440 | tf_op jit(solution)/shard_map/ppermute | solution.py:53
  9.1 33.6 %copy-start = (bf16[1,512,2048]{2,1,0:T(8,128)(2,1)S(1)}, bf16[1,512,2048]{2,1,0:T(8,128)(2,1)}, u32[]{:S(2)}) copy-start(bf16[1,512,2048]{2,1,0:T(8,128)(2,1)} %param.10) | copy-start | bytes 6291460
  9.1 18.6 %collective-permute-start.4 = (bf16[128,2048]{1,0:T(8,128)(2,1)}, bf16[128,2048]{1,0:T(8,128)(2,1)S(1)}, u32[]{:S(2)}, u32[]{:S(2)}) collective-permute-start(bf16[128,2048]{1,0:T(8,128)(2,1)} %bitcast.18), channel_id=1, source_target_pairs={{0,24},{8,16},{16,8},{24,0},{1,25},{9,17},{17,9},{25,1},{2,26},{10... | collective-permute-start | bytes 1572872 | tf_op jit(solution)/shard_map/ppermute | solution.py:322
  12.7 8.4 %collective-permute-start.8 = (bf16[256,512]{1,0:T(8,128)(2,1)S(1)}, bf16[256,512]{1,0:T(8,128)(2,1)S(1)}, u32[]{:S(2)}, u32[]{:S(2)}) collective-permute-start(bf16[256,512]{1,0:T(8,128)(2,1)S(1)} %collective-permute-done.5.refs_0_.rest_2_), channel_id=1, source_target_pairs={{0,2},{2,4},{4,6},{6,7},{7,5},{5,3},{3,1},{1,0},{8,10},{10,12},{12... | collective-permute-start | bytes 786440 | tf_op jit(solution)/shard_map/ppermute | solution.py:53
  14.0 8.1 %collective-permute-start.9 = (bf16[256,512]{1,0:T(8,128)(2,1)S(1)}, bf16[256,512]{1,0:T(8,128)(2,1)S(1)}, u32[]{:S(2)}, u32[]{:S(2)}) collective-permute-start(bf16[256,512]{1,0:T(8,128)(2,1)S(1)} %collective-permute-done.6.refs_0_.rest_4_), channel_id=1, source_target_pairs={{2,0},{4,2},{6,4},{7,6},{5,7},{3,5},{1,3},{0,1},{10,8},{12,10},{14... | collective-permute-start | bytes 786440 | tf_op jit(solution)/shard_map/ppermute | solution.py:53
  15.4 11.2 %collective-permute-start.2 = (bf16[256,512]{1,0:T(8,128)(2,1)S(1)}, bf16[256,512]{1,0:T(8,128)(2,1)S(1)}, u32[]{:S(2)}, u32[]{:S(2)}) collective-permute-start(bf16[256,512]{1,0:T(8,128)(2,1)S(1)} %collective-permute-done.refs_1_.rest_3_), channel_id=1, source_target_pairs={{0,2},{2,4},{4,6},{6,7},{7,5},{5,3},{3,1},{1,0},{8,10},{10,12},{12... | collective-permute-start | bytes 786440 | tf_op jit(solution)/shard_map/ppermute | solution.py:53
  15.9 11.8 %collective-permute-start.3 = (bf16[256,512]{1,0:T(8,128)(2,1)S(1)}, bf16[256,512]{1,0:T(8,128)(2,1)S(1)}, u32[]{:S(2)}, u32[]{:S(2)}) collective-permute-start(bf16[256,512]{1,0:T(8,128)(2,1)S(1)} %collective-permute-done.1.refs_1_.rest_5_), channel_id=1, source_target_pairs={{2,0},{4,2},{6,4},{7,6},{5,7},{3,5},{1,3},{0,1},{10,8},{12,10},{14... | collective-permute-start | bytes 786440 | tf_op jit(solution)/shard_map/ppermute | solution.py:53
  22.1 10.2 %collective-permute-start.10 = (bf16[256,512]{1,0:T(8,128)(2,1)S(1)}, bf16[256,512]{1,0:T(8,128)(2,1)S(1)}, u32[]{:S(2)}, u32[]{:S(2)}) collective-permute-start(bf16[256,512]{1,0:T(8,128)(2,1)S(1)} %collective-permute-done.8.refs_0_.rest_6_), channel_id=1, source_target_pairs={{0,2},{2,4},{4,6},{6,7},{7,5},{5,3},{3,1},{1,0},{8,10},{10,12},{12... | collective-permute-start | bytes 786440 | tf_op jit(solution)/shard_map/ppermute | solution.py:53
  23.5 12.1 %collective-permute-start.11 = (bf16[256,512]{1,0:T(8,128)(2,1)S(1)}, bf16[256,512]{1,0:T(8,128)(2,1)S(1)}, u32[]{:S(2)}, u32[]{:S(2)}) collective-permute-start(bf16[256,512]{1,0:T(8,128)(2,1)S(1)} %collective-permute-done.9.refs_0_.rest_8_), channel_id=1, source_target_pairs={{2,0},{4,2},{6,4},{7,6},{5,7},{3,5},{1,3},{0,1},{10,8},{12,10},{14... | collective-permute-start | bytes 786440 | tf_op jit(solution)/shard_map/ppermute | solution.py:53
  27.7 10.2 %collective-permute-start.14 = (bf16[256,512]{1,0:T(8,128)(2,1)S(1)}, bf16[256,512]{1,0:T(8,128)(2,1)S(1)}, u32[]{:S(2)}, u32[]{:S(2)}) collective-permute-start(bf16[256,512]{1,0:T(8,128)(2,1)S(1)} %collective-permute-done.2.refs_1_.rest_7_), channel_id=1, source_target_pairs={{0,2},{2,4},{4,6},{6,7},{7,5},{5,3},{3,1},{1,0},{8,10},{10,12},{12... | collective-permute-start | bytes 786440 | tf_op jit(solution)/shard_map/ppermute | solution.py:53
  29.1 9.7 %collective-permute-start.15 = (bf16[256,512]{1,0:T(8,128)(2,1)S(1)}, bf16[256,512]{1,0:T(8,128)(2,1)S(1)}, u32[]{:S(2)}, u32[]{:S(2)}) collective-permute-start(bf16[256,512]{1,0:T(8,128)(2,1)S(1)} %collective-permute-done.3.refs_1_.rest_9_), channel_id=1, source_target_pairs={{2,0},{4,2},{6,4},{7,6},{5,7},{3,5},{1,3},{0,1},{10,8},{12,10},{14... | collective-permute-start | bytes 786440 | tf_op jit(solution)/shard_map/ppermute | solution.py:53
  29.1 6.5 %collective-permute-start.12 = (bf16[128,512]{1,0:T(8,128)(2,1)}, bf16[128,512]{1,0:T(8,128)(2,1)S(1)}, u32[]{:S(2)}, u32[]{:S(2)}) collective-permute-start(bf16[128,512]{1,0:T(8,128)(2,1)} %rest_0_), channel_id=1, source_target_pairs={{0,8},{8,0},{16,24},{24,16},{1,9},{9,1},{17,25},{25,17},{2,10},{10... | collective-permute-start | bytes 393224 | tf_op jit(solution)/shard_map/ppermute | solution.py:72
  32.3 4.3 %collective-permute-start.13 = (bf16[128,512]{1,0:T(8,128)(2,1)S(1)}, bf16[128,512]{1,0:T(8,128)(2,1)S(1)}, u32[]{:S(2)}, u32[]{:S(2)}) collective-permute-start(bf16[128,512]{1,0:T(8,128)(2,1)S(1)} %collective-permute-done.7.rest_1_), channel_id=1, source_target_pairs={{0,8},{8,0},{16,24},{24,16},{1,9},{9,1},{17,25},{25,17},{2,10},{10... | collective-permute-start | bytes 393224 | tf_op jit(solution)/shard_map/ppermute | solution.py:72
  36.6 7.7 %collective-permute-start.16 = (bf16[256,512]{1,0:T(8,128)(2,1)S(1)}, bf16[256,512]{1,0:T(8,128)(2,1)S(1)}, u32[]{:S(2)}, u32[]{:S(2)}) collective-permute-start(bf16[256,512]{1,0:T(8,128)(2,1)S(1)} %collective-permute-done.10.refs_0_.rest_10_), channel_id=1, source_target_pairs={{0,2},{2,4},{4,6},{6,7},{7,5},{5,3},{3,1},{1,0},{8,10},{10,12},{12... | collective-permute-start | bytes 786440 | tf_op jit(solution)/shard_map/ppermute | solution.py:60
  38.8 7.0 %collective-permute-start.17 = (bf16[256,512]{1,0:T(8,128)(2,1)S(1)}, bf16[256,512]{1,0:T(8,128)(2,1)S(1)}, u32[]{:S(2)}, u32[]{:S(2)}) collective-permute-start(bf16[256,512]{1,0:T(8,128)(2,1)S(1)} %collective-permute-done.15.refs_1_.rest_13_), channel_id=1, source_target_pairs={{2,0},{4,2},{6,4},{7,6},{5,7},{3,5},{1,3},{0,1},{10,8},{12,10},{14... | collective-permute-start | bytes 786440 | tf_op jit(solution)/shard_map/ppermute | solution.py:60
  42.1 3.7 %copy-start.2 = (bf16[1,256,512]{2,1,0:T(8,128)(2,1)S(1)}, bf16[1,256,512]{2,1,0:T(8,128)(2,1)}, u32[]{:S(2)}) copy-start(bf16[1,256,512]{2,1,0:T(8,128)(2,1)} %param.8) | copy-start | bytes 786436
  46.7 3.4 %collective-permute-start.18 = (bf16[128,2048]{1,0:T(8,128)(2,1)S(1)}, bf16[128,2048]{1,0:T(8,128)(2,1)S(1)}, u32[]{:S(2)}, u32[]{:S(2)}) collective-permute-start(bf16[128,2048]{1,0:T(8,128)(2,1)S(1)} %get-tuple-element.93.held), channel_id=1, source_target_pairs={{0,8},{8,0},{16,24},{24,16},{1,9},{9,1},{17,25},{25,17},{2,10},{10... | collective-permute-start | bytes 1572872 | tf_op jit(solution)/shard_map/ppermute | solution.py:412
  48.6 2.1 %collective-permute-start.19 = (bf16[512,128]{1,0:T(8,128)(2,1)S(1)}, bf16[512,128]{1,0:T(8,128)(2,1)S(1)}, u32[]{:S(2)}, u32[]{:S(2)}) collective-permute-start(bf16[512,128]{1,0:T(8,128)(2,1)S(1)} %get-tuple-element.97), channel_id=1, source_target_pairs={{0,8},{8,16},{16,24},{24,0},{1,9},{9,17},{17,25},{25,1},{2,10},{10... | collective-permute-start | bytes 393224 | tf_op jit(solution)/shard_map/ppermute | solution.py:392
  50.7 10.9 %collective-permute-start.20 = (bf16[128,2048]{1,0:T(8,128)(2,1)S(1)}, bf16[128,2048]{1,0:T(8,128)(2,1)S(1)}, u32[]{:S(2)}, u32[]{:S(2)}) collective-permute-start(bf16[128,2048]{1,0:T(8,128)(2,1)S(1)} %tick.3.held), channel_id=1, source_target_pairs={{16,8},{17,9},{18,10},{19,11},{20,12},{21,13},{22,14},{23,15}} | collective-permute-start | bytes 1572872 | tf_op jit(solution)/shard_map/ppermute | solution.py:412
  62.9 7.0 %collective-permute-start.25 = (bf16[128,1024]{1,0:T(8,128)(2,1)S(1)}, bf16[128,1024]{1,0:T(8,128)(2,1)S(1)}, u32[]{:S(2)}, u32[]{:S(2)}) collective-permute-start(bf16[128,1024]{1,0:T(8,128)(2,1)S(1)} %get-tuple-element.108), channel_id=1, source_target_pairs={{0,2},{1,3},{2,0},{3,1},{4,6},{5,7},{6,4},{7,5},{8,10},{9,11},{10,... | collective-permute-start | bytes 786440 | tf_op jit(solution)/shard_map/ppermute | solution.py:248
  64.0 5.9 %collective-permute-start.24 = (bf16[128,1024]{1,0:T(8,128)(2,1)S(1)}, bf16[128,1024]{1,0:T(8,128)(2,1)S(1)}, u32[]{:S(2)}, u32[]{:S(2)}) collective-permute-start(bf16[128,1024]{1,0:T(8,128)(2,1)S(1)} %get-tuple-element.109), channel_id=1, source_target_pairs={{0,1},{1,0},{2,3},{3,2},{4,5},{5,4},{6,7},{7,6},{8,9},{9,8},{10,11... | collective-permute-start | bytes 786440 | tf_op jit(solution)/shard_map/ppermute | solution.py:248
  65.3 4.6 %collective-permute-start.22 = (bf16[256,128]{1,0:T(8,128)(2,1)S(1)}, bf16[256,128]{1,0:T(8,128)(2,1)S(1)}, u32[]{:S(2)}, u32[]{:S(2)}) collective-permute-start(bf16[256,128]{1,0:T(8,128)(2,1)S(1)} %get-tuple-element.100), channel_id=1, source_target_pairs={{0,1},{1,0},{2,3},{3,2},{4,5},{5,4},{6,7},{7,6},{8,9},{9,8},{10,11... | collective-permute-start | bytes 196616 | tf_op jit(solution)/shard_map/ppermute | solution.py:248
  65.5 4.4 %collective-permute-start.23 = (bf16[256,128]{1,0:T(8,128)(2,1)S(1)}, bf16[256,128]{1,0:T(8,128)(2,1)S(1)}, u32[]{:S(2)}, u32[]{:S(2)}) collective-permute-start(bf16[256,128]{1,0:T(8,128)(2,1)S(1)} %get-tuple-element.101), channel_id=1, source_target_pairs={{0,2},{1,3},{2,0},{3,1},{4,6},{5,7},{6,4},{7,5},{8,10},{9,11},{10,... | collective-permute-start | bytes 196616 | tf_op jit(solution)/shard_map/ppermute | solution.py:248
  66.0 11.8 %collective-permute-start.21 = (bf16[128,2048]{1,0:T(8,128)(2,1)S(1)}, bf16[128,2048]{1,0:T(8,128)(2,1)S(1)}, u32[]{:S(2)}, u32[]{:S(2)}) collective-permute-start(bf16[128,2048]{1,0:T(8,128)(2,1)S(1)} %tick.4.held.grad), channel_id=1, source_target_pairs={{0,8},{8,0},{16,24},{24,16},{1,9},{9,1},{17,25},{25,17},{2,10},{10... | collective-permute-start | bytes 1572872 | tf_op jit(solution)/shard_map/ppermute | solution.py:412
  70.6 5.3 %collective-permute-start.26 = (bf16[128,1024]{1,0:T(8,128)(2,1)S(1)}, bf16[128,1024]{1,0:T(8,128)(2,1)S(1)}, u32[]{:S(2)}, u32[]{:S(2)}) collective-permute-start(bf16[128,1024]{1,0:T(8,128)(2,1)S(1)} %get-tuple-element.104), channel_id=1, source_target_pairs={{0,2},{1,3},{2,0},{3,1},{4,6},{5,7},{6,4},{7,5},{8,10},{9,11},{10,... | collective-permute-start | bytes 786440 | tf_op jit(solution)/shard_map/ppermute | solution.py:248
  71.2 5.9 %collective-permute-start.27 = (bf16[128,1024]{1,0:T(8,128)(2,1)S(1)}, bf16[128,1024]{1,0:T(8,128)(2,1)S(1)}, u32[]{:S(2)}, u32[]{:S(2)}) collective-permute-start(bf16[128,1024]{1,0:T(8,128)(2,1)S(1)} %get-tuple-element.105), channel_id=1, source_target_pairs={{0,1},{1,0},{2,3},{3,2},{4,5},{5,4},{6,7},{7,6},{8,9},{9,8},{10,11... | collective-permute-start | bytes 786440 | tf_op jit(solution)/shard_map/ppermute | solution.py:248
  77.2 14.8 %collective-permute-start.28 = (bf16[64,2048]{1,0:T(8,128)(2,1)S(1)}, bf16[64,2048]{1,0:T(8,128)(2,1)S(1)}, u32[]{:S(2)}, u32[]{:S(2)}) collective-permute-start(bf16[64,2048]{1,0:T(8,128)(2,1)S(1)} %get-tuple-element.106), channel_id=1, source_target_pairs={{0,28},{1,29},{2,30},{3,31},{4,24},{5,25},{6,26},{7,27},{8,4},{9,5... | collective-permute-start | bytes 786440 | tf_op jit(solution)/shard_map/ppermute | solution.py:299
  77.8 14.2 %collective-permute-start.29 = (bf16[64,2048]{1,0:T(8,128)(2,1)S(1)}, bf16[64,2048]{1,0:T(8,128)(2,1)S(1)}, u32[]{:S(2)}, u32[]{:S(2)}) collective-permute-start(bf16[64,2048]{1,0:T(8,128)(2,1)S(1)} %get-tuple-element.107), channel_id=1, source_target_pairs={{0,24},{1,25},{2,26},{3,27},{4,28},{5,29},{6,30},{7,31},{8,0},{9,1... | collective-permute-start | bytes 786440 | tf_op jit(solution)/shard_map/ppermute | solution.py:299
  (5 other events, 8.2 us)

commit v7 on v6

--- a/solution.py
+++ b/solution.py
@@ -181,25 +181,31 @@
         push_back(grad, back_proj, (a, b, c), gate_vector, turned, pieces, columns, out)
 
 
-def block_rows(bits, rest, units):
-    return pl.ds(pl.multiple_of((rest * 4 + 2 * bits[1] + bits[0]) * units, units), units)
-
-
-def own_bits():
-    me = lax.axis_index("dp")
-    return me % 2, me // 2 % 2
+def orders(size):
+    top = size.bit_length() - 2
+    return [0, 1, *range(top, 1, -1)], [top, 0, *range(top - 1, 0, -1)]
+
+
+def own_bit(bit):
+    return lax.axis_index("dp") >> bit & 1
+
+
+def block_rows(order, first, second, rest, units):
+    place = (first << order[0]) + (second << order[1])
+    for i, bit in enumerate(order[2:]):
+        place += (rest >> len(order) - 3 - i & 1) << bit
+    return pl.ds(pl.multiple_of(place * units, units), units)
 
 
 def split_kernel(scored, *out):
     size = lax.axis_size("dp")
     units = scored.shape[0] // size
-    own = own_bits()
-    for bit in range(2):
+    for order, half in zip(orders(size), out):
         for second in range(2):
             for rest in range(size // 4):
-                bits = (1 - own[0], second) if bit == 0 else (second, 1 - own[1])
                 start = (second * (size // 4) + rest) * units
-                out[bit][start : start + units, :] = scored[block_rows(bits, rest, units), :]
+                rows = block_rows(order, 1 - own_bit(order[0]), second, rest, units)
+                half[start : start + units, :] = scored[rows, :]
 
 
 def products_kernel(scored, grad, *rest):
@@ -207,45 +213,53 @@
     size = lax.axis_size("dp")
     units = scored.shape[0] // size
     half, width = sends[0].shape
-    own = own_bits()
-    for bit in range(2):
-        columns = slice(bit * width, (bit + 1) * width)
-        mine = grad[:, columns]
+    for i, order in enumerate(orders(size)):
+        mine = grad[:, i * width : (i + 1) * width]
 
         def rows(second):
-            bits = (own[0], second) if bit == 0 else (second, own[1])
-            blocks = [scored[block_rows(bits, rest, units), :] for rest in range(size // 4)]
+            own = own_bit(order[0])
+            blocks = [
+                scored[block_rows(order, own, second, rest, units), :] for rest in range(size // 4)
+            ]
             where = pl.ds(pl.multiple_of(second * half, half), half)
             left = jnp.concatenate(blocks, axis=0)
-            return dot(left, mine, PLAIN) + dot(theirs[bit][where, :], partners[bit][...], PLAIN)
-
-        sends[bit][...] = rows(1 - own[1 - bit]).astype(BF16)
-        keeps[bit][...] = rows(own[1 - bit])
-
-
-def combine_kernel(bit, count, *refs):
-    keeps, gots, (send, kept) = refs[:count], refs[count : 2 * count], refs[2 * count :]
-    width = keeps[0].shape[1]
-    half = send.shape[0]
-    own = lax.axis_index("dp") >> bit & 1
-    for i, (keep, got) in enumerate(zip(keeps, gots)):
-        columns = slice(i * width, (i + 1) * width)
+            return dot(left, mine, PLAIN) + dot(theirs[i][where, :], partners[i][...], PLAIN)
+
+        sends[i][...] = rows(1 - own_bit(order[1])).astype(BF16)
+        keeps[i][...] = rows(own_bit(order[1]))
+
+
+def combine_kernel(stage, *refs):
+    keeps, gots, sends, kept = refs[:2], refs[2:4], refs[4:6], refs[6:]
+    half, width = sends[0].shape
+    for i, order in enumerate(orders(lax.axis_size("dp"))):
+        own = own_bit(order[stage])
 
         def rows(which):
             where = pl.ds(pl.multiple_of(which * half, half), half)
-            return keep[where, :] + got[where, :].astype(F32)
-
-        send[:, columns] = rows(1 - own).astype(BF16)
-        kept[:, columns] = rows(own).astype(kept.dtype)
-
-
-def finish_kernel(factor, first, second, out):
-    out[...] = (first[...].astype(F32) + second[...].astype(F32)) * factor
-
-
-def along(bit, *values):
-    pairs = [(i, i ^ 1 << bit) for i in range(lax.axis_size("dp"))]
-    return [lax.ppermute(v, "dp", pairs) for v in values]
+            return keeps[i][where, :] + gots[i][where, :].astype(F32)
+
+        sends[i][...] = rows(1 - own).astype(BF16)
+        if len(kept) == 2:
+            kept[i][...] = rows(own)
+        else:
+            kept[0][:, i * width : (i + 1) * width] = rows(own).astype(BF16)
+
+
+def finish_kernel(factor, first, second, keep, out):
+    width = first.shape[1]
+    for i, got in enumerate((first, second)):
+        columns = slice(i * width, (i + 1) * width)
+        out[:, columns] = (got[...].astype(F32) + keep[:, columns].astype(F32)) * factor
+
+
+def along(stage, values):
+    size = lax.axis_size("dp")
+    found = []
+    for order, value in zip(orders(size), values):
+        pairs = [(i, i ^ 1 << order[stage]) for i in range(size)]
+        found.append(lax.ppermute(value, "dp", pairs))
+    return found
 
 
 def call(kernel, name, outs, macs, *args):
@@ -262,31 +276,28 @@
 
 def swap_scored(scored):
     half = jax.ShapeDtypeStruct((scored.shape[0] // 2, scored.shape[1]), BF16)
-    to_first, to_second = call(split_kernel, "split", [half] * 2, 0, scored)
-    return [*along(0, to_first), *along(1, to_second)]
+    return along(0, call(split_kernel, "split", [half] * 2, 0, scored))
 
 
 def reduce_rows(scored, theirs, grad):
-    size = lax.axis_size("dp")
+    stages = lax.axis_size("dp").bit_length() - 1
     rows, width = scored.shape[0] // 4, grad.shape[1]
     shape = jax.ShapeDtypeStruct
-    partners = [*along(0, grad[:, : width // 2]), *along(1, grad[:, width // 2 :])]
+    partners = along(0, (grad[:, : width // 2], grad[:, width // 2 :]))
     half = (rows, width // 2)
     outs = [shape(half, BF16)] * 2 + [shape(half, F32)] * 2
     macs = 4 * rows * scored.shape[1] * width
-    *sends, keep_a, keep_b = call(
-        products_kernel, "products", outs, macs, scored, grad, *theirs, *partners
-    )
-    keeps = [keep_a, keep_b]
-    gots = [*along(1, sends[0]), *along(0, sends[1])]
-    for bit in range(size.bit_length() - 2, 1, -1):
+    found = call(products_kernel, "products", outs, macs, scored, grad, *theirs, *partners)
+    for stage in range(2, stages):
+        gots = along(stage - 1, found[:2])
         rows //= 2
-        outs = [shape((rows, width), BF16), shape((rows, width), BF16 if bit == 2 else F32)]
-        kernel = functools.partial(combine_kernel, bit, len(keeps))
-        send, keep = call(kernel, "combine", outs, 0, *keeps, *gots)
-        if bit == 2:
-            return send, keep
-        keeps, gots = [keep], along(bit, send)
+        half = (rows, width // 2)
+        outs = [shape(half, BF16)] * 2 + [shape(half, F32)] * 2
+        if stage == stages - 1:
+            outs[2:] = [shape((rows, width), BF16)]
+        kernel = functools.partial(combine_kernel, stage)
+        found = call(kernel, "combine", outs, 0, *found[2:], *gots)
+    return found
 
 
 def to_layer(value, flip):
@@ -408,16 +419,17 @@
             reduced = reduce_rows(scored, theirs, outgoing)
         if section == sections - 3:
             outgoing, scored = after((outgoing, scored))
-        pairs = swap if section % 2 == 0 else [(section + 1, section)]
+        pairs = swap if section == sections - 2 else [(section + 1, section)]
         grad = lax.ppermute(outgoing, "section", pairs)
         if section == max(sections - 3, 0):
             theirs = swap_scored(scored)
         outgoing = tick(section, grad, outgoing)
 
-    send, keep = reduced
+    first, second, keep = reduced
+    flips = [1 << order[-1] for order in orders(replicas)]
+    terms = to_layer(first, flips[0]), to_layer(second, flips[1]), to_layer(keep, 0)
     kernel = functools.partial(finish_kernel, (local_rows * replicas) ** (-0.5))
-    outs = [shape(keep.shape, F32)]
-    summed = call(kernel, "finish", outs, 0, to_layer(send, 4), to_layer(keep, 0))[0]
+    summed = call(kernel, "finish", [shape(keep.shape, F32)], 0, *terms)[0]
     return (outgoing[None], summed[None])
 
 

time: 93 us -> 92.3 us (level)
  waiting for transfers between devices: 52.5 us -> 46.8 us
  starting transfers between devices: 29.9 us -> 34.8 us
    ppermute x2 -> x3, waiting for transfers between devices: 13.3 us -> 6.51 us  [to_layer(): return lax.ppermute(value, ('section', 'dp'), pairs)]
    ppermute x2 -> x3, starting transfers between devices: 0.64 us -> 3.54 us  [to_layer(): return lax.ppermute(value, ('section', 'dp'), pairs)]
    ppermute x3, starting transfers between devices: 3.14 us -> 4.45 us  [on_device(): grad = lax.ppermute(outgoing, 'section', pairs)]
    ppermute x6, waiting for transfers between devices: 8.6 us -> 9.8 us  [along(): found.append(lax.ppermute(value, 'dp', pairs))]
  transfers between devices with their start and end apart: 30 -> 31, of which waited for: 20 -> 21; matrix products, arithmetic and copies ran while one was open for 0% -> 0% of each run, Pallas kernels for 5% -> 5%
where the time goes in v7:
time: 92.3 us; the launch traced here: 92.1 us
  waiting for transfers between devices  46.8 us (51%)
  starting transfers between devices  34.8 us (38%)
  Pallas kernels  7.68 us (8%)
  local copies, waits for them, and re-layouts  1.96 us (2%)
    ppermute x12, waiting for transfers between devices, gather_ring(): both = (lax.ppermute(v, axis, ahead), lax.ppermute(w, axis, back))  16.4 us
    ppermute x3, waiting for transfers between devices, on_device(): grad = lax.ppermute(outgoing, 'section', pairs)  10.3 us
    ppermute x6, waiting for transfers between devices, along(): found.append(lax.ppermute(value, 'dp', pairs))  9.8 us
    ppermute x12, starting transfers between devices, gather_ring(): both = (lax.ppermute(v, axis, ahead), lax.ppermute(w, axis, back))  9.58 us
    ppermute x3, starting transfers between devices, gather_blocks(): held += [lax.ppermute(block, axis, pairs) for block in list(held)]  7.54 us
    ppermute x3, waiting for transfers between devices, to_layer(): return lax.ppermute(value, ('section', 'dp'), pairs)  6.51 us
    ppermute x6, starting transfers between devices, along(): found.append(lax.ppermute(value, 'dp', pairs))  5.44 us
    ppermute x3, starting transfers between devices, on_device(): grad = lax.ppermute(outgoing, 'section', pairs)  4.45 us
  transfers between devices with their start and end apart: 31, of which 21 were waited for; matrix products, arithmetic and copies ran while one was open for 0% of the time, Pallas kernels for 5%

profile of v7, /device:TPU:1, one launch (start us, length us, event | category | flops | bytes accessed | tf_op | source)
XLA Modules:
  0.0 92.1 jit_solution(10578338712344459973)
XLA Ops:
  0.6 2.1 %collective-permute-start.6 = (bf16[256,512]{1,0:T(8,128)(2,1)}, bf16[256,512]{1,0:T(8,128)(2,1)S(1)}, u32[]{:S(2)}, u32[]{:S(2)}) collective-permute-start(bf16[256,512]{1,0:T(8,128)(2,1)} %bitcast.8), channel_id=1, source_target_pairs={{2,0},{4,2},{6,4},{7,6},{5,7},{3,5},{1,3},{0,1},{10,8},{12,10},{14... | collective-permute-start | bytes 786440 | tf_op jit(solution)/shard_map/ppermute | solution.py:53
  2.9 1.3 %collective-permute-start.7 = (bf16[128,512]{1,0:T(8,128)(2,1)}, bf16[128,512]{1,0:T(8,128)(2,1)S(1)}, u32[]{:S(2)}, u32[]{:S(2)}) collective-permute-start(bf16[128,512]{1,0:T(8,128)(2,1)} %rest_0_), channel_id=1, source_target_pairs={{0,16},{8,24},{16,0},{24,8},{1,17},{9,25},{17,1},{25,9},{2,18},{10... | collective-permute-start | bytes 393224 | tf_op jit(solution)/shard_map/ppermute | solution.py:72
  4.2 1.2 %collective-permute-start.1 = (bf16[256,512]{1,0:T(8,128)(2,1)}, bf16[256,512]{1,0:T(8,128)(2,1)S(1)}, u32[]{:S(2)}, u32[]{:S(2)}) collective-permute-start(bf16[256,512]{1,0:T(8,128)(2,1)} %bitcast.12), channel_id=1, source_target_pairs={{2,0},{4,2},{6,4},{7,6},{5,7},{3,5},{1,3},{0,1},{10,8},{12,10},{14... | collective-permute-start | bytes 786440 | tf_op jit(solution)/shard_map/ppermute | solution.py:53
  5.7 3.4 %collective-permute-done.6.refs_0_.rest_4_ = bf16[256,512]{1,0:T(8,128)(2,1)S(1)} collective-permute-done((bf16[256,512]{1,0:T(8,128)(2,1)}, bf16[256,512]{1,0:T(8,128)(2,1)S(1)}, u32[]{:S(2)}, u32[]{:S(2)}) %collective-permute-start.6) | collective-permute-done | bytes 262176 | tf_op jit(solution)/shard_map/ppermute | solution.py:53
  9.1 3.6 %collective-permute-start.4 = (bf16[128,2048]{1,0:T(8,128)(2,1)}, bf16[128,2048]{1,0:T(8,128)(2,1)S(1)}, u32[]{:S(2)}, u32[]{:S(2)}) collective-permute-start(bf16[128,2048]{1,0:T(8,128)(2,1)} %bitcast.18), channel_id=1, source_target_pairs={{0,24},{8,16},{16,8},{24,0},{1,25},{9,17},{17,9},{25,1},{2,26},{10... | collective-permute-start | bytes 1572872 | tf_op jit(solution)/shard_map/ppermute | solution.py:333
  12.7 1.3 %collective-permute-start.8 = (bf16[256,512]{1,0:T(8,128)(2,1)S(1)}, bf16[256,512]{1,0:T(8,128)(2,1)S(1)}, u32[]{:S(2)}, u32[]{:S(2)}) collective-permute-start(bf16[256,512]{1,0:T(8,128)(2,1)S(1)} %collective-permute-done.5.refs_0_.rest_2_), channel_id=1, source_target_pairs={{0,2},{2,4},{4,6},{6,7},{7,5},{5,3},{3,1},{1,0},{8,10},{10,12},{12... | collective-permute-start | bytes 786440 | tf_op jit(solution)/shard_map/ppermute | solution.py:53
  15.9 1.0 %collective-permute-start.3 = (bf16[256,512]{1,0:T(8,128)(2,1)S(1)}, bf16[256,512]{1,0:T(8,128)(2,1)S(1)}, u32[]{:S(2)}, u32[]{:S(2)}) collective-permute-start(bf16[256,512]{1,0:T(8,128)(2,1)S(1)} %collective-permute-done.1.refs_1_.rest_5_), channel_id=1, source_target_pairs={{2,0},{4,2},{6,4},{7,6},{5,7},{3,5},{1,3},{0,1},{10,8},{12,10},{14... | collective-permute-start | bytes 786440 | tf_op jit(solution)/shard_map/ppermute | solution.py:53
  16.9 4.2 %collective-permute-done.8.refs_0_.rest_6_ = bf16[256,512]{1,0:T(8,128)(2,1)S(1)} collective-permute-done((bf16[256,512]{1,0:T(8,128)(2,1)S(1)}, bf16[256,512]{1,0:T(8,128)(2,1)S(1)}, u32[]{:S(2)}, u32[]{:S(2)}) %collective-permute-start.8) | collective-permute-done | bytes 262176 | tf_op jit(solution)/shard_map/ppermute | solution.py:53
  21.1 1.0 %collective-permute-done.9.refs_0_.rest_8_ = bf16[256,512]{1,0:T(8,128)(2,1)S(1)} collective-permute-done((bf16[256,512]{1,0:T(8,128)(2,1)S(1)}, bf16[256,512]{1,0:T(8,128)(2,1)S(1)}, u32[]{:S(2)}, u32[]{:S(2)}) %collective-permute-start.9) | collective-permute-done | bytes 262176 | tf_op jit(solution)/shard_map/ppermute | solution.py:53
  22.1 1.4 %collective-permute-start.10 = (bf16[256,512]{1,0:T(8,128)(2,1)S(1)}, bf16[256,512]{1,0:T(8,128)(2,1)S(1)}, u32[]{:S(2)}, u32[]{:S(2)}) collective-permute-start(bf16[256,512]{1,0:T(8,128)(2,1)S(1)} %collective-permute-done.8.refs_0_.rest_6_), channel_id=1, source_target_pairs={{0,2},{2,4},{4,6},{6,7},{7,5},{5,3},{3,1},{1,0},{8,10},{10,12},{12... | collective-permute-start | bytes 786440 | tf_op jit(solution)/shard_map/ppermute | solution.py:53
  23.5 3.2 %collective-permute-done.2.refs_1_.rest_7_ = bf16[256,512]{1,0:T(8,128)(2,1)S(1)} collective-permute-done((bf16[256,512]{1,0:T(8,128)(2,1)S(1)}, bf16[256,512]{1,0:T(8,128)(2,1)S(1)}, u32[]{:S(2)}, u32[]{:S(2)}) %collective-permute-start.2) | collective-permute-done | bytes 262176 | tf_op jit(solution)/shard_map/ppermute | solution.py:53
  26.7 1.0 %collective-permute-done.3.refs_1_.rest_9_ = bf16[256,512]{1,0:T(8,128)(2,1)S(1)} collective-permute-done((bf16[256,512]{1,0:T(8,128)(2,1)S(1)}, bf16[256,512]{1,0:T(8,128)(2,1)S(1)}, u32[]{:S(2)}, u32[]{:S(2)}) %collective-permute-start.3) | collective-permute-done | bytes 262176 | tf_op jit(solution)/shard_map/ppermute | solution.py:53
  27.7 1.4 %collective-permute-start.14 = (bf16[256,512]{1,0:T(8,128)(2,1)S(1)}, bf16[256,512]{1,0:T(8,128)(2,1)S(1)}, u32[]{:S(2)}, u32[]{:S(2)}) collective-permute-start(bf16[256,512]{1,0:T(8,128)(2,1)S(1)} %collective-permute-done.2.refs_1_.rest_7_), channel_id=1, source_target_pairs={{0,2},{2,4},{4,6},{6,7},{7,5},{5,3},{3,1},{1,0},{8,10},{10,12},{12... | collective-permute-start | bytes 786440 | tf_op jit(solution)/shard_map/ppermute | solution.py:53
  29.1 2.9 %collective-permute-start.12 = (bf16[128,512]{1,0:T(8,128)(2,1)}, bf16[128,512]{1,0:T(8,128)(2,1)S(1)}, u32[]{:S(2)}, u32[]{:S(2)}) collective-permute-start(bf16[128,512]{1,0:T(8,128)(2,1)} %rest_0_), channel_id=1, source_target_pairs={{0,8},{8,0},{16,24},{24,16},{1,9},{9,1},{17,25},{25,17},{2,10},{10... | collective-permute-start | bytes 393224 | tf_op jit(solution)/shard_map/ppermute | solution.py:72
  32.3 3.3 %collective-permute-start.13 = (bf16[128,512]{1,0:T(8,128)(2,1)S(1)}, bf16[128,512]{1,0:T(8,128)(2,1)S(1)}, u32[]{:S(2)}, u32[]{:S(2)}) collective-permute-start(bf16[128,512]{1,0:T(8,128)(2,1)S(1)} %collective-permute-done.7.rest_1_), channel_id=1, source_target_pairs={{0,8},{8,0},{16,24},{24,16},{1,9},{9,1},{17,25},{25,17},{2,10},{10... | collective-permute-start | bytes 393224 | tf_op jit(solution)/shard_map/ppermute | solution.py:72
  35.6 1.0 %collective-permute-done.13.rest_3_ = bf16[128,512]{1,0:T(8,128)(2,1)S(1)} collective-permute-done((bf16[128,512]{1,0:T(8,128)(2,1)S(1)}, bf16[128,512]{1,0:T(8,128)(2,1)S(1)}, u32[]{:S(2)}, u32[]{:S(2)}) %collective-permute-start.13) | collective-permute-done | bytes 131104 | tf_op jit(solution)/shard_map/ppermute | solution.py:72
  36.6 1.3 %collective-permute-done.14.refs_1_.rest_11_ = bf16[256,512]{1,0:T(8,128)(2,1)S(1)} collective-permute-done((bf16[256,512]{1,0:T(8,128)(2,1)S(1)}, bf16[256,512]{1,0:T(8,128)(2,1)S(1)}, u32[]{:S(2)}, u32[]{:S(2)}) %collective-permute-start.14) | collective-permute-done | bytes 262176 | tf_op jit(solution)/shard_map/ppermute | solution.py:53
  37.9 0.9 %collective-permute-done.15.refs_1_.rest_13_ = bf16[256,512]{1,0:T(8,128)(2,1)S(1)} collective-permute-done((bf16[256,512]{1,0:T(8,128)(2,1)S(1)}, bf16[256,512]{1,0:T(8,128)(2,1)S(1)}, u32[]{:S(2)}, u32[]{:S(2)}) %collective-permute-start.15) | collective-permute-done | bytes 262176 | tf_op jit(solution)/shard_map/ppermute | solution.py:53
  39.2 0.9 %copy-done.1 = bf16[1,256,512]{2,1,0:T(8,128)(2,1)S(1)} copy-done((bf16[1,256,512]{2,1,0:T(8,128)(2,1)S(1)}, bf16[1,256,512]{2,1,0:T(8,128)(2,1)}, u32[]{:S(2)}) %copy-start.1) | copy-done | bytes 262168
  40.2 0.9 %copy-done.3 = bf16[1,256,512]{2,1,0:T(8,128)(2,1)S(1)} copy-done((bf16[1,256,512]{2,1,0:T(8,128)(2,1)S(1)}, bf16[1,256,512]{2,1,0:T(8,128)(2,1)}, u32[]{:S(2)}) %copy-start.3) | copy-done | bytes 262168
  44.3 1.5 %collective-permute-done.17.rest_15_ = bf16[256,512]{1,0:T(8,128)(2,1)S(1)} collective-permute-done((bf16[256,512]{1,0:T(8,128)(2,1)S(1)}, bf16[256,512]{1,0:T(8,128)(2,1)S(1)}, u32[]{:S(2)}, u32[]{:S(2)}) %collective-permute-start.17) | collective-permute-done | bytes 262176 | tf_op jit(solution)/shard_map/ppermute | solution.py:60
  46.7 1.9 %collective-permute-start.18 = (bf16[128,2048]{1,0:T(8,128)(2,1)S(1)}, bf16[128,2048]{1,0:T(8,128)(2,1)S(1)}, u32[]{:S(2)}, u32[]{:S(2)}) collective-permute-start(bf16[128,2048]{1,0:T(8,128)(2,1)S(1)} %get-tuple-element.94.held), channel_id=1, source_target_pairs={{0,8},{8,0},{16,24},{24,16},{1,9},{9,1},{17,25},{25,17},{2,10},{10... | collective-permute-start | bytes 1572872 | tf_op jit(solution)/shard_map/ppermute | solution.py:423
  50.7 1.3 %collective-permute-start.20 = (bf16[128,2048]{1,0:T(8,128)(2,1)S(1)}, bf16[128,2048]{1,0:T(8,128)(2,1)S(1)}, u32[]{:S(2)}, u32[]{:S(2)}) collective-permute-start(bf16[128,2048]{1,0:T(8,128)(2,1)S(1)} %tick.3.held), channel_id=1, source_target_pairs={{16,8},{17,9},{18,10},{19,11},{20,12},{21,13},{22,14},{23,15}} | collective-permute-start | bytes 1572872 | tf_op jit(solution)/shard_map/ppermute | solution.py:423
  52.0 9.6 %collective-permute-done.20.grad = bf16[128,2048]{1,0:T(8,128)(2,1)S(1)} collective-permute-done((bf16[128,2048]{1,0:T(8,128)(2,1)S(1)}, bf16[128,2048]{1,0:T(8,128)(2,1)S(1)}, u32[]{:S(2)}, u32[]{:S(2)}) %collective-permute-start.20) | collective-permute-done | bytes 524320 | tf_op jit(solution)/shard_map/ppermute | solution.py:423
  61.6 1.3 %tick.4.held.grad = bf16[128,2048]{1,0:T(8,128)(2,1)S(1)} custom-call(bf16[128,2048]{1,0:T(8,128)(2,1)S(1)} %collective-permute-done.20.grad, bf16[128,2048]{1,0:T(8,128)(2,1)S(1)} %tick.3.held, bf16[2048,512]{1,0:T(8,128)(2,1)S(1)} %turn_down.1.down, bf16[1,2048]{1,0:T(2,128)(2,1)S(1)} %copy-done.5, f32[128,512]{1,0:T(8,128)S(1)} %get-tuple-element.95.a, ...), custom_call_target="tpu_custom_call" | custom-call | flops 805306368 | bytes 4194304 | tf_op jit(solution)/shard_map/tick/pallas_call | solution.py:406
  62.9 2.4 %collective-permute-start.25 = (bf16[128,1024]{1,0:T(8,128)(2,1)S(1)}, bf16[128,1024]{1,0:T(8,128)(2,1)S(1)}, u32[]{:S(2)}, u32[]{:S(2)}) collective-permute-start(bf16[128,1024]{1,0:T(8,128)(2,1)S(1)} %get-tuple-element.110), channel_id=1, source_target_pairs={{0,4},{1,5},{2,6},{3,7},{4,0},{5,1},{6,2},{7,3},{8,12},{9,13},{10,... | collective-permute-start | bytes 786440 | tf_op jit(solution)/shard_map/ppermute | solution.py:261
  65.3 1.0 %collective-permute-start.24 = (bf16[128,1024]{1,0:T(8,128)(2,1)S(1)}, bf16[128,1024]{1,0:T(8,128)(2,1)S(1)}, u32[]{:S(2)}, u32[]{:S(2)}) collective-permute-start(bf16[128,1024]{1,0:T(8,128)(2,1)S(1)} %get-tuple-element.111), channel_id=1, source_target_pairs={{0,1},{1,0},{2,3},{3,2},{4,5},{5,4},{6,7},{7,6},{8,9},{9,8},{10,11... | collective-permute-start | bytes 786440 | tf_op jit(solution)/shard_map/ppermute | solution.py:261
  66.9 1.3 %collective-permute-start.21 = (bf16[128,2048]{1,0:T(8,128)(2,1)S(1)}, bf16[128,2048]{1,0:T(8,128)(2,1)S(1)}, u32[]{:S(2)}, u32[]{:S(2)}) collective-permute-start(bf16[128,2048]{1,0:T(8,128)(2,1)S(1)} %tick.4.held.grad), channel_id=1, source_target_pairs={{8,0},{9,1},{10,2},{11,3},{12,4},{13,5},{14,6},{15,7}} | collective-permute-start | bytes 1572872 | tf_op jit(solution)/shard_map/ppermute | solution.py:423
  68.2 4.5 %collective-permute-done.22.rest_0_ = bf16[256,128]{1,0:T(8,128)(2,1)S(1)} collective-permute-done((bf16[256,128]{1,0:T(8,128)(2,1)S(1)}, bf16[256,128]{1,0:T(8,128)(2,1)S(1)}, u32[]{:S(2)}, u32[]{:S(2)}) %collective-permute-start.22) | collective-permute-done | bytes 65568 | tf_op jit(solution)/shard_map/ppermute | solution.py:261
  75.5 3.8 %collective-permute-done.26.refs_2_ = bf16[128,1024]{1,0:T(8,128)(2,1)S(1)} collective-permute-done((bf16[128,1024]{1,0:T(8,128)(2,1)S(1)}, bf16[128,1024]{1,0:T(8,128)(2,1)S(1)}, u32[]{:S(2)}, u32[]{:S(2)}) %collective-permute-start.26) | collective-permute-done | bytes 262176 | tf_op jit(solution)/shard_map/ppermute | solution.py:261
  80.4 3.4 %collective-permute-start.29 = (bf16[64,1024]{1,0:T(8,128)(2,1)S(1)}, bf16[64,1024]{1,0:T(8,128)(2,1)S(1)}, u32[]{:S(2)}, u32[]{:S(2)}) collective-permute-start(bf16[64,1024]{1,0:T(8,128)(2,1)S(1)} %get-tuple-element.108), channel_id=1, source_target_pairs={{0,26},{1,27},{2,24},{3,25},{4,30},{5,31},{6,28},{7,29},{8,2},{9,3... | collective-permute-start | bytes 393224 | tf_op jit(solution)/shard_map/ppermute | solution.py:310
  84.7 6.5 %collective-permute-done.28.first = bf16[64,1024]{1,0:T(8,128)(2,1)S(1)} collective-permute-done((bf16[64,1024]{1,0:T(8,128)(2,1)S(1)}, bf16[64,1024]{1,0:T(8,128)(2,1)S(1)}, u32[]{:S(2)}, u32[]{:S(2)}) %collective-permute-start.28) | collective-permute-done | bytes 131104 | tf_op jit(solution)/shard_map/ppermute | solution.py:310
  (63 shorter events, 15.2 us)
Async XLA Ops:
  0.6 8.4 %collective-permute-start.6 = (bf16[256,512]{1,0:T(8,128)(2,1)}, bf16[256,512]{1,0:T(8,128)(2,1)S(1)}, u32[]{:S(2)}, u32[]{:S(2)}) collective-permute-start(bf16[256,512]{1,0:T(8,128)(2,1)} %bitcast.8), channel_id=1, source_target_pairs={{2,0},{4,2},{6,4},{7,6},{5,7},{3,5},{1,3},{0,1},{10,8},{12,10},{14... | collective-permute-start | bytes 786440 | tf_op jit(solution)/shard_map/ppermute | solution.py:53
  2.8 9.9 %collective-permute-start.5 = (bf16[256,512]{1,0:T(8,128)(2,1)}, bf16[256,512]{1,0:T(8,128)(2,1)S(1)}, u32[]{:S(2)}, u32[]{:S(2)}) collective-permute-start(bf16[256,512]{1,0:T(8,128)(2,1)} %bitcast.9), channel_id=1, source_target_pairs={{0,2},{2,4},{4,6},{6,7},{7,5},{5,3},{3,1},{1,0},{8,10},{10,12},{12... | collective-permute-start | bytes 786440 | tf_op jit(solution)/shard_map/ppermute | solution.py:53
  2.9 9.8 %collective-permute-start.7 = (bf16[128,512]{1,0:T(8,128)(2,1)}, bf16[128,512]{1,0:T(8,128)(2,1)S(1)}, u32[]{:S(2)}, u32[]{:S(2)}) collective-permute-start(bf16[128,512]{1,0:T(8,128)(2,1)} %rest_0_), channel_id=1, source_target_pairs={{0,16},{8,24},{16,0},{24,8},{1,17},{9,25},{17,1},{25,9},{2,18},{10... | collective-permute-start | bytes 393224 | tf_op jit(solution)/shard_map/ppermute | solution.py:72
  4.2 10.5 %collective-permute-start.1 = (bf16[256,512]{1,0:T(8,128)(2,1)}, bf16[256,512]{1,0:T(8,128)(2,1)S(1)}, u32[]{:S(2)}, u32[]{:S(2)}) collective-permute-start(bf16[256,512]{1,0:T(8,128)(2,1)} %bitcast.12), channel_id=1, source_target_pairs={{2,0},{4,2},{6,4},{7,6},{5,7},{3,5},{1,3},{0,1},{10,8},{12,10},{14... | collective-permute-start | bytes 786440 | tf_op jit(solution)/shard_map/ppermute | solution.py:53
  5.4 10.0 %collective-permute-start = (bf16[256,512]{1,0:T(8,128)(2,1)}, bf16[256,512]{1,0:T(8,128)(2,1)S(1)}, u32[]{:S(2)}, u32[]{:S(2)}) collective-permute-start(bf16[256,512]{1,0:T(8,128)(2,1)} %bitcast.13), channel_id=1, source_target_pairs={{0,2},{2,4},{4,6},{6,7},{7,5},{5,3},{3,1},{1,0},{8,10},{10,12},{12... | collective-permute-start | bytes 786440 | tf_op jit(solution)/shard_map/ppermute | solution.py:53
  9.1 33.6 %copy-start = (bf16[1,512,2048]{2,1,0:T(8,128)(2,1)S(1)}, bf16[1,512,2048]{2,1,0:T(8,128)(2,1)}, u32[]{:S(2)}) copy-start(bf16[1,512,2048]{2,1,0:T(8,128)(2,1)} %param.10) | copy-start | bytes 6291460
  9.1 18.6 %collective-permute-start.4 = (bf16[128,2048]{1,0:T(8,128)(2,1)}, bf16[128,2048]{1,0:T(8,128)(2,1)S(1)}, u32[]{:S(2)}, u32[]{:S(2)}) collective-permute-start(bf16[128,2048]{1,0:T(8,128)(2,1)} %bitcast.18), channel_id=1, source_target_pairs={{0,24},{8,16},{16,8},{24,0},{1,25},{9,17},{17,9},{25,1},{2,26},{10... | collective-permute-start | bytes 1572872 | tf_op jit(solution)/shard_map/ppermute | solution.py:333
  12.7 8.4 %collective-permute-start.8 = (bf16[256,512]{1,0:T(8,128)(2,1)S(1)}, bf16[256,512]{1,0:T(8,128)(2,1)S(1)}, u32[]{:S(2)}, u32[]{:S(2)}) collective-permute-start(bf16[256,512]{1,0:T(8,128)(2,1)S(1)} %collective-permute-done.5.refs_0_.rest_2_), channel_id=1, source_target_pairs={{0,2},{2,4},{4,6},{6,7},{7,5},{5,3},{3,1},{1,0},{8,10},{10,12},{12... | collective-permute-start | bytes 786440 | tf_op jit(solution)/shard_map/ppermute | solution.py:53
  14.0 8.1 %collective-permute-start.9 = (bf16[256,512]{1,0:T(8,128)(2,1)S(1)}, bf16[256,512]{1,0:T(8,128)(2,1)S(1)}, u32[]{:S(2)}, u32[]{:S(2)}) collective-permute-start(bf16[256,512]{1,0:T(8,128)(2,1)S(1)} %collective-permute-done.6.refs_0_.rest_4_), channel_id=1, source_target_pairs={{2,0},{4,2},{6,4},{7,6},{5,7},{3,5},{1,3},{0,1},{10,8},{12,10},{14... | collective-permute-start | bytes 786440 | tf_op jit(solution)/shard_map/ppermute | solution.py:53
  15.4 11.2 %collective-permute-start.2 = (bf16[256,512]{1,0:T(8,128)(2,1)S(1)}, bf16[256,512]{1,0:T(8,128)(2,1)S(1)}, u32[]{:S(2)}, u32[]{:S(2)}) collective-permute-start(bf16[256,512]{1,0:T(8,128)(2,1)S(1)} %collective-permute-done.refs_1_.rest_3_), channel_id=1, source_target_pairs={{0,2},{2,4},{4,6},{6,7},{7,5},{5,3},{3,1},{1,0},{8,10},{10,12},{12... | collective-permute-start | bytes 786440 | tf_op jit(solution)/shard_map/ppermute | solution.py:53
  15.9 11.8 %collective-permute-start.3 = (bf16[256,512]{1,0:T(8,128)(2,1)S(1)}, bf16[256,512]{1,0:T(8,128)(2,1)S(1)}, u32[]{:S(2)}, u32[]{:S(2)}) collective-permute-start(bf16[256,512]{1,0:T(8,128)(2,1)S(1)} %collective-permute-done.1.refs_1_.rest_5_), channel_id=1, source_target_pairs={{2,0},{4,2},{6,4},{7,6},{5,7},{3,5},{1,3},{0,1},{10,8},{12,10},{14... | collective-permute-start | bytes 786440 | tf_op jit(solution)/shard_map/ppermute | solution.py:53
  22.1 10.2 %collective-permute-start.10 = (bf16[256,512]{1,0:T(8,128)(2,1)S(1)}, bf16[256,512]{1,0:T(8,128)(2,1)S(1)}, u32[]{:S(2)}, u32[]{:S(2)}) collective-permute-start(bf16[256,512]{1,0:T(8,128)(2,1)S(1)} %collective-permute-done.8.refs_0_.rest_6_), channel_id=1, source_target_pairs={{0,2},{2,4},{4,6},{6,7},{7,5},{5,3},{3,1},{1,0},{8,10},{10,12},{12... | collective-permute-start | bytes 786440 | tf_op jit(solution)/shard_map/ppermute | solution.py:53
  23.5 12.1 %collective-permute-start.11 = (bf16[256,512]{1,0:T(8,128)(2,1)S(1)}, bf16[256,512]{1,0:T(8,128)(2,1)S(1)}, u32[]{:S(2)}, u32[]{:S(2)}) collective-permute-start(bf16[256,512]{1,0:T(8,128)(2,1)S(1)} %collective-permute-done.9.refs_0_.rest_8_), channel_id=1, source_target_pairs={{2,0},{4,2},{6,4},{7,6},{5,7},{3,5},{1,3},{0,1},{10,8},{12,10},{14... | collective-permute-start | bytes 786440 | tf_op jit(solution)/shard_map/ppermute | solution.py:53
  27.7 10.2 %collective-permute-start.14 = (bf16[256,512]{1,0:T(8,128)(2,1)S(1)}, bf16[256,512]{1,0:T(8,128)(2,1)S(1)}, u32[]{:S(2)}, u32[]{:S(2)}) collective-permute-start(bf16[256,512]{1,0:T(8,128)(2,1)S(1)} %collective-permute-done.2.refs_1_.rest_7_), channel_id=1, source_target_pairs={{0,2},{2,4},{4,6},{6,7},{7,5},{5,3},{3,1},{1,0},{8,10},{10,12},{12... | collective-permute-start | bytes 786440 | tf_op jit(solution)/shard_map/ppermute | solution.py:53
  29.1 9.7 %collective-permute-start.15 = (bf16[256,512]{1,0:T(8,128)(2,1)S(1)}, bf16[256,512]{1,0:T(8,128)(2,1)S(1)}, u32[]{:S(2)}, u32[]{:S(2)}) collective-permute-start(bf16[256,512]{1,0:T(8,128)(2,1)S(1)} %collective-permute-done.3.refs_1_.rest_9_), channel_id=1, source_target_pairs={{2,0},{4,2},{6,4},{7,6},{5,7},{3,5},{1,3},{0,1},{10,8},{12,10},{14... | collective-permute-start | bytes 786440 | tf_op jit(solution)/shard_map/ppermute | solution.py:53
  29.1 6.5 %collective-permute-start.12 = (bf16[128,512]{1,0:T(8,128)(2,1)}, bf16[128,512]{1,0:T(8,128)(2,1)S(1)}, u32[]{:S(2)}, u32[]{:S(2)}) collective-permute-start(bf16[128,512]{1,0:T(8,128)(2,1)} %rest_0_), channel_id=1, source_target_pairs={{0,8},{8,0},{16,24},{24,16},{1,9},{9,1},{17,25},{25,17},{2,10},{10... | collective-permute-start | bytes 393224 | tf_op jit(solution)/shard_map/ppermute | solution.py:72
  32.3 4.3 %collective-permute-start.13 = (bf16[128,512]{1,0:T(8,128)(2,1)S(1)}, bf16[128,512]{1,0:T(8,128)(2,1)S(1)}, u32[]{:S(2)}, u32[]{:S(2)}) collective-permute-start(bf16[128,512]{1,0:T(8,128)(2,1)S(1)} %collective-permute-done.7.rest_1_), channel_id=1, source_target_pairs={{0,8},{8,0},{16,24},{24,16},{1,9},{9,1},{17,25},{25,17},{2,10},{10... | collective-permute-start | bytes 393224 | tf_op jit(solution)/shard_map/ppermute | solution.py:72
  36.6 7.7 %collective-permute-start.16 = (bf16[256,512]{1,0:T(8,128)(2,1)S(1)}, bf16[256,512]{1,0:T(8,128)(2,1)S(1)}, u32[]{:S(2)}, u32[]{:S(2)}) collective-permute-start(bf16[256,512]{1,0:T(8,128)(2,1)S(1)} %collective-permute-done.10.refs_0_.rest_10_), channel_id=1, source_target_pairs={{0,2},{2,4},{4,6},{6,7},{7,5},{5,3},{3,1},{1,0},{8,10},{10,12},{12... | collective-permute-start | bytes 786440 | tf_op jit(solution)/shard_map/ppermute | solution.py:60
  38.8 7.0 %collective-permute-start.17 = (bf16[256,512]{1,0:T(8,128)(2,1)S(1)}, bf16[256,512]{1,0:T(8,128)(2,1)S(1)}, u32[]{:S(2)}, u32[]{:S(2)}) collective-permute-start(bf16[256,512]{1,0:T(8,128)(2,1)S(1)} %collective-permute-done.15.refs_1_.rest_13_), channel_id=1, source_target_pairs={{2,0},{4,2},{6,4},{7,6},{5,7},{3,5},{1,3},{0,1},{10,8},{12,10},{14... | collective-permute-start | bytes 786440 | tf_op jit(solution)/shard_map/ppermute | solution.py:60
  46.7 3.4 %collective-permute-start.18 = (bf16[128,2048]{1,0:T(8,128)(2,1)S(1)}, bf16[128,2048]{1,0:T(8,128)(2,1)S(1)}, u32[]{:S(2)}, u32[]{:S(2)}) collective-permute-start(bf16[128,2048]{1,0:T(8,128)(2,1)S(1)} %get-tuple-element.94.held), channel_id=1, source_target_pairs={{0,8},{8,0},{16,24},{24,16},{1,9},{9,1},{17,25},{25,17},{2,10},{10... | collective-permute-start | bytes 1572872 | tf_op jit(solution)/shard_map/ppermute | solution.py:423
  48.6 2.1 %collective-permute-start.19 = (bf16[512,128]{1,0:T(8,128)(2,1)S(1)}, bf16[512,128]{1,0:T(8,128)(2,1)S(1)}, u32[]{:S(2)}, u32[]{:S(2)}) collective-permute-start(bf16[512,128]{1,0:T(8,128)(2,1)S(1)} %get-tuple-element.98), channel_id=1, source_target_pairs={{0,8},{8,16},{16,24},{24,0},{1,9},{9,17},{17,25},{25,1},{2,10},{10... | collective-permute-start | bytes 393224 | tf_op jit(solution)/shard_map/ppermute | solution.py:403
  50.7 10.9 %collective-permute-start.20 = (bf16[128,2048]{1,0:T(8,128)(2,1)S(1)}, bf16[128,2048]{1,0:T(8,128)(2,1)S(1)}, u32[]{:S(2)}, u32[]{:S(2)}) collective-permute-start(bf16[128,2048]{1,0:T(8,128)(2,1)S(1)} %tick.3.held), channel_id=1, source_target_pairs={{16,8},{17,9},{18,10},{19,11},{20,12},{21,13},{22,14},{23,15}} | collective-permute-start | bytes 1572872 | tf_op jit(solution)/shard_map/ppermute | solution.py:423
  62.9 10.5 %collective-permute-start.25 = (bf16[128,1024]{1,0:T(8,128)(2,1)S(1)}, bf16[128,1024]{1,0:T(8,128)(2,1)S(1)}, u32[]{:S(2)}, u32[]{:S(2)}) collective-permute-start(bf16[128,1024]{1,0:T(8,128)(2,1)S(1)} %get-tuple-element.110), channel_id=1, source_target_pairs={{0,4},{1,5},{2,6},{3,7},{4,0},{5,1},{6,2},{7,3},{8,12},{9,13},{10,... | collective-permute-start | bytes 786440 | tf_op jit(solution)/shard_map/ppermute | solution.py:261
  65.3 8.1 %collective-permute-start.24 = (bf16[128,1024]{1,0:T(8,128)(2,1)S(1)}, bf16[128,1024]{1,0:T(8,128)(2,1)S(1)}, u32[]{:S(2)}, u32[]{:S(2)}) collective-permute-start(bf16[128,1024]{1,0:T(8,128)(2,1)S(1)} %get-tuple-element.111), channel_id=1, source_target_pairs={{0,1},{1,0},{2,3},{3,2},{4,5},{5,4},{6,7},{7,6},{8,9},{9,8},{10,11... | collective-permute-start | bytes 786440 | tf_op jit(solution)/shard_map/ppermute | solution.py:261
  66.3 6.5 %collective-permute-start.22 = (bf16[256,128]{1,0:T(8,128)(2,1)S(1)}, bf16[256,128]{1,0:T(8,128)(2,1)S(1)}, u32[]{:S(2)}, u32[]{:S(2)}) collective-permute-start(bf16[256,128]{1,0:T(8,128)(2,1)S(1)} %get-tuple-element.101), channel_id=1, source_target_pairs={{0,1},{1,0},{2,3},{3,2},{4,5},{5,4},{6,7},{7,6},{8,9},{9,8},{10,11... | collective-permute-start | bytes 196616 | tf_op jit(solution)/shard_map/ppermute | solution.py:261
  66.9 6.5 %collective-permute-start.23 = (bf16[256,128]{1,0:T(8,128)(2,1)S(1)}, bf16[256,128]{1,0:T(8,128)(2,1)S(1)}, u32[]{:S(2)}, u32[]{:S(2)}) collective-permute-start(bf16[256,128]{1,0:T(8,128)(2,1)S(1)} %get-tuple-element.102), channel_id=1, source_target_pairs={{0,4},{1,5},{2,6},{3,7},{4,0},{5,1},{6,2},{7,3},{8,12},{9,13},{10,... | collective-permute-start | bytes 196616 | tf_op jit(solution)/shard_map/ppermute | solution.py:261
  66.9 16.9 %collective-permute-start.21 = (bf16[128,2048]{1,0:T(8,128)(2,1)S(1)}, bf16[128,2048]{1,0:T(8,128)(2,1)S(1)}, u32[]{:S(2)}, u32[]{:S(2)}) collective-permute-start(bf16[128,2048]{1,0:T(8,128)(2,1)S(1)} %tick.4.held.grad), channel_id=1, source_target_pairs={{8,0},{9,1},{10,2},{11,3},{12,4},{13,5},{14,6},{15,7}} | collective-permute-start | bytes 1572872 | tf_op jit(solution)/shard_map/ppermute | solution.py:423
  74.1 5.3 %collective-permute-start.26 = (bf16[128,1024]{1,0:T(8,128)(2,1)S(1)}, bf16[128,1024]{1,0:T(8,128)(2,1)S(1)}, u32[]{:S(2)}, u32[]{:S(2)}) collective-permute-start(bf16[128,1024]{1,0:T(8,128)(2,1)S(1)} %get-tuple-element.105), channel_id=1, source_target_pairs={{0,2},{1,3},{2,0},{3,1},{4,6},{5,7},{6,4},{7,5},{8,10},{9,11},{10,... | collective-permute-start | bytes 786440 | tf_op jit(solution)/shard_map/ppermute | solution.py:261
  75.0 5.2 %collective-permute-start.27 = (bf16[128,1024]{1,0:T(8,128)(2,1)S(1)}, bf16[128,1024]{1,0:T(8,128)(2,1)S(1)}, u32[]{:S(2)}, u32[]{:S(2)}) collective-permute-start(bf16[128,1024]{1,0:T(8,128)(2,1)S(1)} %get-tuple-element.106), channel_id=1, source_target_pairs={{0,1},{1,0},{2,3},{3,2},{4,5},{5,4},{6,7},{7,6},{8,9},{9,8},{10,11... | collective-permute-start | bytes 786440 | tf_op jit(solution)/shard_map/ppermute | solution.py:261
  80.3 10.9 %collective-permute-start.30 = (bf16[64,2048]{1,0:T(8,128)(2,1)S(1)}, bf16[64,2048]{1,0:T(8,128)(2,1)S(1)}, u32[]{:S(2)}, u32[]{:S(2)}) collective-permute-start(bf16[64,2048]{1,0:T(8,128)(2,1)S(1)} %get-tuple-element.109), channel_id=1, source_target_pairs={{0,24},{1,25},{2,26},{3,27},{4,28},{5,29},{6,30},{7,31},{8,0},{9,1... | collective-permute-start | bytes 786440 | tf_op jit(solution)/shard_map/ppermute | solution.py:310
  80.4 10.8 %collective-permute-start.28 = (bf16[64,1024]{1,0:T(8,128)(2,1)S(1)}, bf16[64,1024]{1,0:T(8,128)(2,1)S(1)}, u32[]{:S(2)}, u32[]{:S(2)}) collective-permute-start(bf16[64,1024]{1,0:T(8,128)(2,1)S(1)} %get-tuple-element.107), channel_id=1, source_target_pairs={{0,28},{1,29},{2,30},{3,31},{4,24},{5,25},{6,26},{7,27},{8,4},{9,5... | collective-permute-start | bytes 393224 | tf_op jit(solution)/shard_map/ppermute | solution.py:310
  80.4 10.8 %collective-permute-start.29 = (bf16[64,1024]{1,0:T(8,128)(2,1)S(1)}, bf16[64,1024]{1,0:T(8,128)(2,1)S(1)}, u32[]{:S(2)}, u32[]{:S(2)}) collective-permute-start(bf16[64,1024]{1,0:T(8,128)(2,1)S(1)} %get-tuple-element.108), channel_id=1, source_target_pairs={{0,26},{1,27},{2,24},{3,25},{4,30},{5,31},{6,28},{7,29},{8,2},{9,3... | collective-permute-start | bytes 393224 | tf_op jit(solution)/shard_map/ppermute | solution.py:310
  (6 other events, 11.9 us)

commit v8 on v7

--- a/solution.py
+++ b/solution.py
@@ -346,7 +346,7 @@
     pieces, offsets = gather_ring([gate_weight[0], up_weight[0]], "dp", between)
     for blocks, _ in cotangents:
         pass
-    turned = 0 if depth % 128 else len(pieces) - 1
+    turned = 0 if depth % 128 else len(pieces)
     down_back = down_full
     if turned:
         outs = [shape(down_full.shape[::-1], BF16)]

time: 92.3 us -> 92.5 us (level)
    pallas_call x12 -> x13, Pallas kernels: 3.57 us -> 3.73 us  [call(): pl.pallas_call(kernel, out_shape=outs, in_specs=[VMEM] * len(args), out_s...]
where the time goes in v8:
time: 92.5 us; the launch traced here: 92.3 us
  waiting for transfers between devices  46.8 us (51%)
  starting transfers between devices  34.9 us (38%)
  Pallas kernels  7.78 us (8%)
  local copies, waits for them, and re-layouts  1.96 us (2%)
    ppermute x12, waiting for transfers between devices, gather_ring(): both = (lax.ppermute(v, axis, ahead), lax.ppermute(w, axis, back))  16.4 us
    ppermute x3, waiting for transfers between devices, on_device(): grad = lax.ppermute(outgoing, 'section', pairs)  10.3 us
    ppermute x6, waiting for transfers between devices, along(): found.append(lax.ppermute(value, 'dp', pairs))  9.74 us
    ppermute x12, starting transfers between devices, gather_ring(): both = (lax.ppermute(v, axis, ahead), lax.ppermute(w, axis, back))  9.58 us
    ppermute x3, starting transfers between devices, gather_blocks(): held += [lax.ppermute(block, axis, pairs) for block in list(held)]  7.54 us
    ppermute x3, waiting for transfers between devices, to_layer(): return lax.ppermute(value, ('section', 'dp'), pairs)  6.47 us
    ppermute x6, starting transfers between devices, along(): found.append(lax.ppermute(value, 'dp', pairs))  5.4 us
    ppermute x3, starting transfers between devices, on_device(): grad = lax.ppermute(outgoing, 'section', pairs)  4.45 us
  transfers between devices with their start and end apart: 31, of which 21 were waited for; matrix products, arithmetic and copies ran while one was open for 0% of the time, Pallas kernels for 5%

profile of v8, /device:TPU:1, one launch (start us, length us, event | category | flops | bytes accessed | tf_op | source)
XLA Modules:
  0.0 92.3 jit_solution(17423287103834642187)
XLA Ops:
  0.6 2.1 %collective-permute-start.6 = (bf16[256,512]{1,0:T(8,128)(2,1)}, bf16[256,512]{1,0:T(8,128)(2,1)S(1)}, u32[]{:S(2)}, u32[]{:S(2)}) collective-permute-start(bf16[256,512]{1,0:T(8,128)(2,1)} %bitcast.8), channel_id=1, source_target_pairs={{2,0},{4,2},{6,4},{7,6},{5,7},{3,5},{1,3},{0,1},{10,8},{12,10},{14... | collective-permute-start | bytes 786440 | tf_op jit(solution)/shard_map/ppermute | solution.py:53
  2.9 1.3 %collective-permute-start.7 = (bf16[128,512]{1,0:T(8,128)(2,1)}, bf16[128,512]{1,0:T(8,128)(2,1)S(1)}, u32[]{:S(2)}, u32[]{:S(2)}) collective-permute-start(bf16[128,512]{1,0:T(8,128)(2,1)} %rest_0_), channel_id=1, source_target_pairs={{0,16},{8,24},{16,0},{24,8},{1,17},{9,25},{17,1},{25,9},{2,18},{10... | collective-permute-start | bytes 393224 | tf_op jit(solution)/shard_map/ppermute | solution.py:72
  4.2 1.2 %collective-permute-start.1 = (bf16[256,512]{1,0:T(8,128)(2,1)}, bf16[256,512]{1,0:T(8,128)(2,1)S(1)}, u32[]{:S(2)}, u32[]{:S(2)}) collective-permute-start(bf16[256,512]{1,0:T(8,128)(2,1)} %bitcast.12), channel_id=1, source_target_pairs={{2,0},{4,2},{6,4},{7,6},{5,7},{3,5},{1,3},{0,1},{10,8},{12,10},{14... | collective-permute-start | bytes 786440 | tf_op jit(solution)/shard_map/ppermute | solution.py:53
  5.7 3.4 %collective-permute-done.6.refs_0_.rest_4_ = bf16[256,512]{1,0:T(8,128)(2,1)S(1)} collective-permute-done((bf16[256,512]{1,0:T(8,128)(2,1)}, bf16[256,512]{1,0:T(8,128)(2,1)S(1)}, u32[]{:S(2)}, u32[]{:S(2)}) %collective-permute-start.6) | collective-permute-done | bytes 262176 | tf_op jit(solution)/shard_map/ppermute | solution.py:53
  9.1 3.6 %collective-permute-start.4 = (bf16[128,2048]{1,0:T(8,128)(2,1)}, bf16[128,2048]{1,0:T(8,128)(2,1)S(1)}, u32[]{:S(2)}, u32[]{:S(2)}) collective-permute-start(bf16[128,2048]{1,0:T(8,128)(2,1)} %bitcast.18), channel_id=1, source_target_pairs={{0,24},{8,16},{16,8},{24,0},{1,25},{9,17},{17,9},{25,1},{2,26},{10... | collective-permute-start | bytes 1572872 | tf_op jit(solution)/shard_map/ppermute | solution.py:333
  12.7 1.3 %collective-permute-start.8 = (bf16[256,512]{1,0:T(8,128)(2,1)S(1)}, bf16[256,512]{1,0:T(8,128)(2,1)S(1)}, u32[]{:S(2)}, u32[]{:S(2)}) collective-permute-start(bf16[256,512]{1,0:T(8,128)(2,1)S(1)} %collective-permute-done.5.refs_0_.rest_2_), channel_id=1, source_target_pairs={{0,2},{2,4},{4,6},{6,7},{7,5},{5,3},{3,1},{1,0},{8,10},{10,12},{12... | collective-permute-start | bytes 786440 | tf_op jit(solution)/shard_map/ppermute | solution.py:53
  15.9 1.0 %collective-permute-start.3 = (bf16[256,512]{1,0:T(8,128)(2,1)S(1)}, bf16[256,512]{1,0:T(8,128)(2,1)S(1)}, u32[]{:S(2)}, u32[]{:S(2)}) collective-permute-start(bf16[256,512]{1,0:T(8,128)(2,1)S(1)} %collective-permute-done.1.refs_1_.rest_5_), channel_id=1, source_target_pairs={{2,0},{4,2},{6,4},{7,6},{5,7},{3,5},{1,3},{0,1},{10,8},{12,10},{14... | collective-permute-start | bytes 786440 | tf_op jit(solution)/shard_map/ppermute | solution.py:53
  16.9 4.2 %collective-permute-done.8.refs_0_.rest_6_ = bf16[256,512]{1,0:T(8,128)(2,1)S(1)} collective-permute-done((bf16[256,512]{1,0:T(8,128)(2,1)S(1)}, bf16[256,512]{1,0:T(8,128)(2,1)S(1)}, u32[]{:S(2)}, u32[]{:S(2)}) %collective-permute-start.8) | collective-permute-done | bytes 262176 | tf_op jit(solution)/shard_map/ppermute | solution.py:53
  21.1 1.0 %collective-permute-done.9.refs_0_.rest_8_ = bf16[256,512]{1,0:T(8,128)(2,1)S(1)} collective-permute-done((bf16[256,512]{1,0:T(8,128)(2,1)S(1)}, bf16[256,512]{1,0:T(8,128)(2,1)S(1)}, u32[]{:S(2)}, u32[]{:S(2)}) %collective-permute-start.9) | collective-permute-done | bytes 262176 | tf_op jit(solution)/shard_map/ppermute | solution.py:53
  22.1 1.4 %collective-permute-start.10 = (bf16[256,512]{1,0:T(8,128)(2,1)S(1)}, bf16[256,512]{1,0:T(8,128)(2,1)S(1)}, u32[]{:S(2)}, u32[]{:S(2)}) collective-permute-start(bf16[256,512]{1,0:T(8,128)(2,1)S(1)} %collective-permute-done.8.refs_0_.rest_6_), channel_id=1, source_target_pairs={{0,2},{2,4},{4,6},{6,7},{7,5},{5,3},{3,1},{1,0},{8,10},{10,12},{12... | collective-permute-start | bytes 786440 | tf_op jit(solution)/shard_map/ppermute | solution.py:53
  23.5 3.2 %collective-permute-done.2.refs_1_.rest_7_ = bf16[256,512]{1,0:T(8,128)(2,1)S(1)} collective-permute-done((bf16[256,512]{1,0:T(8,128)(2,1)S(1)}, bf16[256,512]{1,0:T(8,128)(2,1)S(1)}, u32[]{:S(2)}, u32[]{:S(2)}) %collective-permute-start.2) | collective-permute-done | bytes 262176 | tf_op jit(solution)/shard_map/ppermute | solution.py:53
  26.7 1.0 %collective-permute-done.3.refs_1_.rest_9_ = bf16[256,512]{1,0:T(8,128)(2,1)S(1)} collective-permute-done((bf16[256,512]{1,0:T(8,128)(2,1)S(1)}, bf16[256,512]{1,0:T(8,128)(2,1)S(1)}, u32[]{:S(2)}, u32[]{:S(2)}) %collective-permute-start.3) | collective-permute-done | bytes 262176 | tf_op jit(solution)/shard_map/ppermute | solution.py:53
  27.7 1.4 %collective-permute-start.14 = (bf16[256,512]{1,0:T(8,128)(2,1)S(1)}, bf16[256,512]{1,0:T(8,128)(2,1)S(1)}, u32[]{:S(2)}, u32[]{:S(2)}) collective-permute-start(bf16[256,512]{1,0:T(8,128)(2,1)S(1)} %collective-permute-done.2.refs_1_.rest_7_), channel_id=1, source_target_pairs={{0,2},{2,4},{4,6},{6,7},{7,5},{5,3},{3,1},{1,0},{8,10},{10,12},{12... | collective-permute-start | bytes 786440 | tf_op jit(solution)/shard_map/ppermute | solution.py:53
  29.1 2.9 %collective-permute-start.12 = (bf16[128,512]{1,0:T(8,128)(2,1)}, bf16[128,512]{1,0:T(8,128)(2,1)S(1)}, u32[]{:S(2)}, u32[]{:S(2)}) collective-permute-start(bf16[128,512]{1,0:T(8,128)(2,1)} %rest_0_), channel_id=1, source_target_pairs={{0,8},{8,0},{16,24},{24,16},{1,9},{9,1},{17,25},{25,17},{2,10},{10... | collective-permute-start | bytes 393224 | tf_op jit(solution)/shard_map/ppermute | solution.py:72
  32.3 3.3 %collective-permute-start.13 = (bf16[128,512]{1,0:T(8,128)(2,1)S(1)}, bf16[128,512]{1,0:T(8,128)(2,1)S(1)}, u32[]{:S(2)}, u32[]{:S(2)}) collective-permute-start(bf16[128,512]{1,0:T(8,128)(2,1)S(1)} %collective-permute-done.7.rest_1_), channel_id=1, source_target_pairs={{0,8},{8,0},{16,24},{24,16},{1,9},{9,1},{17,25},{25,17},{2,10},{10... | collective-permute-start | bytes 393224 | tf_op jit(solution)/shard_map/ppermute | solution.py:72
  35.6 1.0 %collective-permute-done.13.rest_3_ = bf16[128,512]{1,0:T(8,128)(2,1)S(1)} collective-permute-done((bf16[128,512]{1,0:T(8,128)(2,1)S(1)}, bf16[128,512]{1,0:T(8,128)(2,1)S(1)}, u32[]{:S(2)}, u32[]{:S(2)}) %collective-permute-start.13) | collective-permute-done | bytes 131104 | tf_op jit(solution)/shard_map/ppermute | solution.py:72
  36.6 1.3 %collective-permute-done.14.refs_1_.rest_11_ = bf16[256,512]{1,0:T(8,128)(2,1)S(1)} collective-permute-done((bf16[256,512]{1,0:T(8,128)(2,1)S(1)}, bf16[256,512]{1,0:T(8,128)(2,1)S(1)}, u32[]{:S(2)}, u32[]{:S(2)}) %collective-permute-start.14) | collective-permute-done | bytes 262176 | tf_op jit(solution)/shard_map/ppermute | solution.py:53
  39.2 0.9 %copy-done.1 = bf16[1,256,512]{2,1,0:T(8,128)(2,1)S(1)} copy-done((bf16[1,256,512]{2,1,0:T(8,128)(2,1)S(1)}, bf16[1,256,512]{2,1,0:T(8,128)(2,1)}, u32[]{:S(2)}) %copy-start.1) | copy-done | bytes 262168
  40.2 0.9 %copy-done.3 = bf16[1,256,512]{2,1,0:T(8,128)(2,1)S(1)} copy-done((bf16[1,256,512]{2,1,0:T(8,128)(2,1)S(1)}, bf16[1,256,512]{2,1,0:T(8,128)(2,1)}, u32[]{:S(2)}) %copy-start.3) | copy-done | bytes 262168
  44.3 1.5 %collective-permute-done.17.refs_1_.rest_15_ = bf16[256,512]{1,0:T(8,128)(2,1)S(1)} collective-permute-done((bf16[256,512]{1,0:T(8,128)(2,1)S(1)}, bf16[256,512]{1,0:T(8,128)(2,1)S(1)}, u32[]{:S(2)}, u32[]{:S(2)}) %collective-permute-start.17) | collective-permute-done | bytes 262176 | tf_op jit(solution)/shard_map/ppermute | solution.py:60
  46.0 1.0 %first_tick.1 = (bf16[128,2048]{1,0:T(8,128)(2,1)S(1)}, f32[128,512]{1,0:T(8,128)S(1)}, f32[128,512]{1,0:T(8,128)S(1)}, f32[128,512]{1,0:T(8,128)S(1)}, bf16[512,128]{1,0:T(8,128)(2,1)S(1)}) custom-call(bf16[128,2048]{1,0:T(8,128)(2,1)S(1)} %collective-permute-done.4.rows, f32[128,1]{1,0:T(8,128)S(1)} %score.1, f32[128,512]{1,0:T(8,128)S(1)} %get-tuple-element.75.back_proj, ...), custom_call_target="tpu_custom_call" | custom-call | flops 1073741824 | bytes 4194304 | tf_op jit(solution)/shard_map/first_tick/pallas_call | solution.py:387
  47.0 1.9 %collective-permute-start.18 = (bf16[128,2048]{1,0:T(8,128)(2,1)S(1)}, bf16[128,2048]{1,0:T(8,128)(2,1)S(1)}, u32[]{:S(2)}, u32[]{:S(2)}) collective-permute-start(bf16[128,2048]{1,0:T(8,128)(2,1)S(1)} %get-tuple-element.98.held), channel_id=1, source_target_pairs={{0,8},{8,0},{16,24},{24,16},{1,9},{9,1},{17,25},{25,17},{2,10},{10... | collective-permute-start | bytes 1572872 | tf_op jit(solution)/shard_map/ppermute | solution.py:423
  51.0 1.3 %collective-permute-start.20 = (bf16[128,2048]{1,0:T(8,128)(2,1)S(1)}, bf16[128,2048]{1,0:T(8,128)(2,1)S(1)}, u32[]{:S(2)}, u32[]{:S(2)}) collective-permute-start(bf16[128,2048]{1,0:T(8,128)(2,1)S(1)} %tick.3.held), channel_id=1, source_target_pairs={{16,8},{17,9},{18,10},{19,11},{20,12},{21,13},{22,14},{23,15}} | collective-permute-start | bytes 1572872 | tf_op jit(solution)/shard_map/ppermute | solution.py:423
  52.3 9.6 %collective-permute-done.20.grad = bf16[128,2048]{1,0:T(8,128)(2,1)S(1)} collective-permute-done((bf16[128,2048]{1,0:T(8,128)(2,1)S(1)}, bf16[128,2048]{1,0:T(8,128)(2,1)S(1)}, u32[]{:S(2)}, u32[]{:S(2)}) %collective-permute-start.20) | collective-permute-done | bytes 524320 | tf_op jit(solution)/shard_map/ppermute | solution.py:423
  61.8 1.2 %tick.4.held.grad = bf16[128,2048]{1,0:T(8,128)(2,1)S(1)} custom-call(bf16[128,2048]{1,0:T(8,128)(2,1)S(1)} %collective-permute-done.20.grad, bf16[128,2048]{1,0:T(8,128)(2,1)S(1)} %tick.3.held, bf16[2048,512]{1,0:T(8,128)(2,1)S(1)} %turn_down.1.down, bf16[1,2048]{1,0:T(2,128)(2,1)S(1)} %copy-done.5, f32[128,512]{1,0:T(8,128)S(1)} %get-tuple-element.99.a, ...), custom_call_target="tpu_custom_call" | custom-call | flops 805306368 | bytes 4194304 | tf_op jit(solution)/shard_map/tick/pallas_call | solution.py:406
  63.1 2.4 %collective-permute-start.25 = (bf16[128,1024]{1,0:T(8,128)(2,1)S(1)}, bf16[128,1024]{1,0:T(8,128)(2,1)S(1)}, u32[]{:S(2)}, u32[]{:S(2)}) collective-permute-start(bf16[128,1024]{1,0:T(8,128)(2,1)S(1)} %get-tuple-element.114), channel_id=1, source_target_pairs={{0,4},{1,5},{2,6},{3,7},{4,0},{5,1},{6,2},{7,3},{8,12},{9,13},{10,... | collective-permute-start | bytes 786440 | tf_op jit(solution)/shard_map/ppermute | solution.py:261
  65.4 1.0 %collective-permute-start.24 = (bf16[128,1024]{1,0:T(8,128)(2,1)S(1)}, bf16[128,1024]{1,0:T(8,128)(2,1)S(1)}, u32[]{:S(2)}, u32[]{:S(2)}) collective-permute-start(bf16[128,1024]{1,0:T(8,128)(2,1)S(1)} %get-tuple-element.115), channel_id=1, source_target_pairs={{0,1},{1,0},{2,3},{3,2},{4,5},{5,4},{6,7},{7,6},{8,9},{9,8},{10,11... | collective-permute-start | bytes 786440 | tf_op jit(solution)/shard_map/ppermute | solution.py:261
  67.1 1.3 %collective-permute-start.21 = (bf16[128,2048]{1,0:T(8,128)(2,1)S(1)}, bf16[128,2048]{1,0:T(8,128)(2,1)S(1)}, u32[]{:S(2)}, u32[]{:S(2)}) collective-permute-start(bf16[128,2048]{1,0:T(8,128)(2,1)S(1)} %tick.4.held.grad), channel_id=1, source_target_pairs={{8,0},{9,1},{10,2},{11,3},{12,4},{13,5},{14,6},{15,7}} | collective-permute-start | bytes 1572872 | tf_op jit(solution)/shard_map/ppermute | solution.py:423
  68.4 4.4 %collective-permute-done.22.rest_0_ = bf16[256,128]{1,0:T(8,128)(2,1)S(1)} collective-permute-done((bf16[256,128]{1,0:T(8,128)(2,1)S(1)}, bf16[256,128]{1,0:T(8,128)(2,1)S(1)}, u32[]{:S(2)}, u32[]{:S(2)}) %collective-permute-start.22) | collective-permute-done | bytes 65568 | tf_op jit(solution)/shard_map/ppermute | solution.py:261
  75.7 3.9 %collective-permute-done.26.refs_2_ = bf16[128,1024]{1,0:T(8,128)(2,1)S(1)} collective-permute-done((bf16[128,1024]{1,0:T(8,128)(2,1)S(1)}, bf16[128,1024]{1,0:T(8,128)(2,1)S(1)}, u32[]{:S(2)}, u32[]{:S(2)}) %collective-permute-start.26) | collective-permute-done | bytes 262176 | tf_op jit(solution)/shard_map/ppermute | solution.py:261
  80.5 3.6 %collective-permute-start.29 = (bf16[64,1024]{1,0:T(8,128)(2,1)S(1)}, bf16[64,1024]{1,0:T(8,128)(2,1)S(1)}, u32[]{:S(2)}, u32[]{:S(2)}) collective-permute-start(bf16[64,1024]{1,0:T(8,128)(2,1)S(1)} %get-tuple-element.112), channel_id=1, source_target_pairs={{0,26},{1,27},{2,24},{3,25},{4,30},{5,31},{6,28},{7,29},{8,2},{9,3... | collective-permute-start | bytes 393224 | tf_op jit(solution)/shard_map/ppermute | solution.py:310
  84.9 6.5 %collective-permute-done.28.first = bf16[64,1024]{1,0:T(8,128)(2,1)S(1)} collective-permute-done((bf16[64,1024]{1,0:T(8,128)(2,1)S(1)}, bf16[64,1024]{1,0:T(8,128)(2,1)S(1)}, u32[]{:S(2)}, u32[]{:S(2)}) %collective-permute-start.28) | collective-permute-done | bytes 131104 | tf_op jit(solution)/shard_map/ppermute | solution.py:310
  (64 shorter events, 15.4 us)
Async XLA Ops:
  0.6 8.4 %collective-permute-start.6 = (bf16[256,512]{1,0:T(8,128)(2,1)}, bf16[256,512]{1,0:T(8,128)(2,1)S(1)}, u32[]{:S(2)}, u32[]{:S(2)}) collective-permute-start(bf16[256,512]{1,0:T(8,128)(2,1)} %bitcast.8), channel_id=1, source_target_pairs={{2,0},{4,2},{6,4},{7,6},{5,7},{3,5},{1,3},{0,1},{10,8},{12,10},{14... | collective-permute-start | bytes 786440 | tf_op jit(solution)/shard_map/ppermute | solution.py:53
  2.8 9.9 %collective-permute-start.5 = (bf16[256,512]{1,0:T(8,128)(2,1)}, bf16[256,512]{1,0:T(8,128)(2,1)S(1)}, u32[]{:S(2)}, u32[]{:S(2)}) collective-permute-start(bf16[256,512]{1,0:T(8,128)(2,1)} %bitcast.9), channel_id=1, source_target_pairs={{0,2},{2,4},{4,6},{6,7},{7,5},{5,3},{3,1},{1,0},{8,10},{10,12},{12... | collective-permute-start | bytes 786440 | tf_op jit(solution)/shard_map/ppermute | solution.py:53
  2.9 9.8 %collective-permute-start.7 = (bf16[128,512]{1,0:T(8,128)(2,1)}, bf16[128,512]{1,0:T(8,128)(2,1)S(1)}, u32[]{:S(2)}, u32[]{:S(2)}) collective-permute-start(bf16[128,512]{1,0:T(8,128)(2,1)} %rest_0_), channel_id=1, source_target_pairs={{0,16},{8,24},{16,0},{24,8},{1,17},{9,25},{17,1},{25,9},{2,18},{10... | collective-permute-start | bytes 393224 | tf_op jit(solution)/shard_map/ppermute | solution.py:72
  4.2 10.5 %collective-permute-start.1 = (bf16[256,512]{1,0:T(8,128)(2,1)}, bf16[256,512]{1,0:T(8,128)(2,1)S(1)}, u32[]{:S(2)}, u32[]{:S(2)}) collective-permute-start(bf16[256,512]{1,0:T(8,128)(2,1)} %bitcast.12), channel_id=1, source_target_pairs={{2,0},{4,2},{6,4},{7,6},{5,7},{3,5},{1,3},{0,1},{10,8},{12,10},{14... | collective-permute-start | bytes 786440 | tf_op jit(solution)/shard_map/ppermute | solution.py:53
  5.4 10.0 %collective-permute-start = (bf16[256,512]{1,0:T(8,128)(2,1)}, bf16[256,512]{1,0:T(8,128)(2,1)S(1)}, u32[]{:S(2)}, u32[]{:S(2)}) collective-permute-start(bf16[256,512]{1,0:T(8,128)(2,1)} %bitcast.13), channel_id=1, source_target_pairs={{0,2},{2,4},{4,6},{6,7},{7,5},{5,3},{3,1},{1,0},{8,10},{10,12},{12... | collective-permute-start | bytes 786440 | tf_op jit(solution)/shard_map/ppermute | solution.py:53
  9.1 33.6 %copy-start = (bf16[1,512,2048]{2,1,0:T(8,128)(2,1)S(1)}, bf16[1,512,2048]{2,1,0:T(8,128)(2,1)}, u32[]{:S(2)}) copy-start(bf16[1,512,2048]{2,1,0:T(8,128)(2,1)} %param.10) | copy-start | bytes 6291460
  9.1 18.6 %collective-permute-start.4 = (bf16[128,2048]{1,0:T(8,128)(2,1)}, bf16[128,2048]{1,0:T(8,128)(2,1)S(1)}, u32[]{:S(2)}, u32[]{:S(2)}) collective-permute-start(bf16[128,2048]{1,0:T(8,128)(2,1)} %bitcast.18), channel_id=1, source_target_pairs={{0,24},{8,16},{16,8},{24,0},{1,25},{9,17},{17,9},{25,1},{2,26},{10... | collective-permute-start | bytes 1572872 | tf_op jit(solution)/shard_map/ppermute | solution.py:333
  12.7 8.4 %collective-permute-start.8 = (bf16[256,512]{1,0:T(8,128)(2,1)S(1)}, bf16[256,512]{1,0:T(8,128)(2,1)S(1)}, u32[]{:S(2)}, u32[]{:S(2)}) collective-permute-start(bf16[256,512]{1,0:T(8,128)(2,1)S(1)} %collective-permute-done.5.refs_0_.rest_2_), channel_id=1, source_target_pairs={{0,2},{2,4},{4,6},{6,7},{7,5},{5,3},{3,1},{1,0},{8,10},{10,12},{12... | collective-permute-start | bytes 786440 | tf_op jit(solution)/shard_map/ppermute | solution.py:53
  14.0 8.1 %collective-permute-start.9 = (bf16[256,512]{1,0:T(8,128)(2,1)S(1)}, bf16[256,512]{1,0:T(8,128)(2,1)S(1)}, u32[]{:S(2)}, u32[]{:S(2)}) collective-permute-start(bf16[256,512]{1,0:T(8,128)(2,1)S(1)} %collective-permute-done.6.refs_0_.rest_4_), channel_id=1, source_target_pairs={{2,0},{4,2},{6,4},{7,6},{5,7},{3,5},{1,3},{0,1},{10,8},{12,10},{14... | collective-permute-start | bytes 786440 | tf_op jit(solution)/shard_map/ppermute | solution.py:53
  15.4 11.2 %collective-permute-start.2 = (bf16[256,512]{1,0:T(8,128)(2,1)S(1)}, bf16[256,512]{1,0:T(8,128)(2,1)S(1)}, u32[]{:S(2)}, u32[]{:S(2)}) collective-permute-start(bf16[256,512]{1,0:T(8,128)(2,1)S(1)} %collective-permute-done.refs_1_.rest_3_), channel_id=1, source_target_pairs={{0,2},{2,4},{4,6},{6,7},{7,5},{5,3},{3,1},{1,0},{8,10},{10,12},{12... | collective-permute-start | bytes 786440 | tf_op jit(solution)/shard_map/ppermute | solution.py:53
  15.9 11.8 %collective-permute-start.3 = (bf16[256,512]{1,0:T(8,128)(2,1)S(1)}, bf16[256,512]{1,0:T(8,128)(2,1)S(1)}, u32[]{:S(2)}, u32[]{:S(2)}) collective-permute-start(bf16[256,512]{1,0:T(8,128)(2,1)S(1)} %collective-permute-done.1.refs_1_.rest_5_), channel_id=1, source_target_pairs={{2,0},{4,2},{6,4},{7,6},{5,7},{3,5},{1,3},{0,1},{10,8},{12,10},{14... | collective-permute-start | bytes 786440 | tf_op jit(solution)/shard_map/ppermute | solution.py:53
  22.1 10.2 %collective-permute-start.10 = (bf16[256,512]{1,0:T(8,128)(2,1)S(1)}, bf16[256,512]{1,0:T(8,128)(2,1)S(1)}, u32[]{:S(2)}, u32[]{:S(2)}) collective-permute-start(bf16[256,512]{1,0:T(8,128)(2,1)S(1)} %collective-permute-done.8.refs_0_.rest_6_), channel_id=1, source_target_pairs={{0,2},{2,4},{4,6},{6,7},{7,5},{5,3},{3,1},{1,0},{8,10},{10,12},{12... | collective-permute-start | bytes 786440 | tf_op jit(solution)/shard_map/ppermute | solution.py:53
  23.5 12.1 %collective-permute-start.11 = (bf16[256,512]{1,0:T(8,128)(2,1)S(1)}, bf16[256,512]{1,0:T(8,128)(2,1)S(1)}, u32[]{:S(2)}, u32[]{:S(2)}) collective-permute-start(bf16[256,512]{1,0:T(8,128)(2,1)S(1)} %collective-permute-done.9.refs_0_.rest_8_), channel_id=1, source_target_pairs={{2,0},{4,2},{6,4},{7,6},{5,7},{3,5},{1,3},{0,1},{10,8},{12,10},{14... | collective-permute-start | bytes 786440 | tf_op jit(solution)/shard_map/ppermute | solution.py:53
  27.7 10.2 %collective-permute-start.14 = (bf16[256,512]{1,0:T(8,128)(2,1)S(1)}, bf16[256,512]{1,0:T(8,128)(2,1)S(1)}, u32[]{:S(2)}, u32[]{:S(2)}) collective-permute-start(bf16[256,512]{1,0:T(8,128)(2,1)S(1)} %collective-permute-done.2.refs_1_.rest_7_), channel_id=1, source_target_pairs={{0,2},{2,4},{4,6},{6,7},{7,5},{5,3},{3,1},{1,0},{8,10},{10,12},{12... | collective-permute-start | bytes 786440 | tf_op jit(solution)/shard_map/ppermute | solution.py:53
  29.1 9.7 %collective-permute-start.15 = (bf16[256,512]{1,0:T(8,128)(2,1)S(1)}, bf16[256,512]{1,0:T(8,128)(2,1)S(1)}, u32[]{:S(2)}, u32[]{:S(2)}) collective-permute-start(bf16[256,512]{1,0:T(8,128)(2,1)S(1)} %collective-permute-done.3.refs_1_.rest_9_), channel_id=1, source_target_pairs={{2,0},{4,2},{6,4},{7,6},{5,7},{3,5},{1,3},{0,1},{10,8},{12,10},{14... | collective-permute-start | bytes 786440 | tf_op jit(solution)/shard_map/ppermute | solution.py:53
  29.1 6.5 %collective-permute-start.12 = (bf16[128,512]{1,0:T(8,128)(2,1)}, bf16[128,512]{1,0:T(8,128)(2,1)S(1)}, u32[]{:S(2)}, u32[]{:S(2)}) collective-permute-start(bf16[128,512]{1,0:T(8,128)(2,1)} %rest_0_), channel_id=1, source_target_pairs={{0,8},{8,0},{16,24},{24,16},{1,9},{9,1},{17,25},{25,17},{2,10},{10... | collective-permute-start | bytes 393224 | tf_op jit(solution)/shard_map/ppermute | solution.py:72
  32.3 4.3 %collective-permute-start.13 = (bf16[128,512]{1,0:T(8,128)(2,1)S(1)}, bf16[128,512]{1,0:T(8,128)(2,1)S(1)}, u32[]{:S(2)}, u32[]{:S(2)}) collective-permute-start(bf16[128,512]{1,0:T(8,128)(2,1)S(1)} %collective-permute-done.7.rest_1_), channel_id=1, source_target_pairs={{0,8},{8,0},{16,24},{24,16},{1,9},{9,1},{17,25},{25,17},{2,10},{10... | collective-permute-start | bytes 393224 | tf_op jit(solution)/shard_map/ppermute | solution.py:72
  36.6 7.7 %collective-permute-start.16 = (bf16[256,512]{1,0:T(8,128)(2,1)S(1)}, bf16[256,512]{1,0:T(8,128)(2,1)S(1)}, u32[]{:S(2)}, u32[]{:S(2)}) collective-permute-start(bf16[256,512]{1,0:T(8,128)(2,1)S(1)} %collective-permute-done.10.refs_0_.rest_10_), channel_id=1, source_target_pairs={{0,2},{2,4},{4,6},{6,7},{7,5},{5,3},{3,1},{1,0},{8,10},{10,12},{12... | collective-permute-start | bytes 786440 | tf_op jit(solution)/shard_map/ppermute | solution.py:60
  38.8 7.0 %collective-permute-start.17 = (bf16[256,512]{1,0:T(8,128)(2,1)S(1)}, bf16[256,512]{1,0:T(8,128)(2,1)S(1)}, u32[]{:S(2)}, u32[]{:S(2)}) collective-permute-start(bf16[256,512]{1,0:T(8,128)(2,1)S(1)} %collective-permute-done.15.refs_1_.rest_13_), channel_id=1, source_target_pairs={{2,0},{4,2},{6,4},{7,6},{5,7},{3,5},{1,3},{0,1},{10,8},{12,10},{14... | collective-permute-start | bytes 786440 | tf_op jit(solution)/shard_map/ppermute | solution.py:60
  47.0 3.4 %collective-permute-start.18 = (bf16[128,2048]{1,0:T(8,128)(2,1)S(1)}, bf16[128,2048]{1,0:T(8,128)(2,1)S(1)}, u32[]{:S(2)}, u32[]{:S(2)}) collective-permute-start(bf16[128,2048]{1,0:T(8,128)(2,1)S(1)} %get-tuple-element.98.held), channel_id=1, source_target_pairs={{0,8},{8,0},{16,24},{24,16},{1,9},{9,1},{17,25},{25,17},{2,10},{10... | collective-permute-start | bytes 1572872 | tf_op jit(solution)/shard_map/ppermute | solution.py:423
  48.8 2.1 %collective-permute-start.19 = (bf16[512,128]{1,0:T(8,128)(2,1)S(1)}, bf16[512,128]{1,0:T(8,128)(2,1)S(1)}, u32[]{:S(2)}, u32[]{:S(2)}) collective-permute-start(bf16[512,128]{1,0:T(8,128)(2,1)S(1)} %get-tuple-element.102), channel_id=1, source_target_pairs={{0,8},{8,16},{16,24},{24,0},{1,9},{9,17},{17,25},{25,1},{2,10},{10... | collective-permute-start | bytes 393224 | tf_op jit(solution)/shard_map/ppermute | solution.py:403
  51.0 10.9 %collective-permute-start.20 = (bf16[128,2048]{1,0:T(8,128)(2,1)S(1)}, bf16[128,2048]{1,0:T(8,128)(2,1)S(1)}, u32[]{:S(2)}, u32[]{:S(2)}) collective-permute-start(bf16[128,2048]{1,0:T(8,128)(2,1)S(1)} %tick.3.held), channel_id=1, source_target_pairs={{16,8},{17,9},{18,10},{19,11},{20,12},{21,13},{22,14},{23,15}} | collective-permute-start | bytes 1572872 | tf_op jit(solution)/shard_map/ppermute | solution.py:423
  63.1 10.5 %collective-permute-start.25 = (bf16[128,1024]{1,0:T(8,128)(2,1)S(1)}, bf16[128,1024]{1,0:T(8,128)(2,1)S(1)}, u32[]{:S(2)}, u32[]{:S(2)}) collective-permute-start(bf16[128,1024]{1,0:T(8,128)(2,1)S(1)} %get-tuple-element.114), channel_id=1, source_target_pairs={{0,4},{1,5},{2,6},{3,7},{4,0},{5,1},{6,2},{7,3},{8,12},{9,13},{10,... | collective-permute-start | bytes 786440 | tf_op jit(solution)/shard_map/ppermute | solution.py:261
  65.4 8.1 %collective-permute-start.24 = (bf16[128,1024]{1,0:T(8,128)(2,1)S(1)}, bf16[128,1024]{1,0:T(8,128)(2,1)S(1)}, u32[]{:S(2)}, u32[]{:S(2)}) collective-permute-start(bf16[128,1024]{1,0:T(8,128)(2,1)S(1)} %get-tuple-element.115), channel_id=1, source_target_pairs={{0,1},{1,0},{2,3},{3,2},{4,5},{5,4},{6,7},{7,6},{8,9},{9,8},{10,11... | collective-permute-start | bytes 786440 | tf_op jit(solution)/shard_map/ppermute | solution.py:261
  66.5 6.3 %collective-permute-start.22 = (bf16[256,128]{1,0:T(8,128)(2,1)S(1)}, bf16[256,128]{1,0:T(8,128)(2,1)S(1)}, u32[]{:S(2)}, u32[]{:S(2)}) collective-permute-start(bf16[256,128]{1,0:T(8,128)(2,1)S(1)} %get-tuple-element.105), channel_id=1, source_target_pairs={{0,1},{1,0},{2,3},{3,2},{4,5},{5,4},{6,7},{7,6},{8,9},{9,8},{10,11... | collective-permute-start | bytes 196616 | tf_op jit(solution)/shard_map/ppermute | solution.py:261
  67.0 6.5 %collective-permute-start.23 = (bf16[256,128]{1,0:T(8,128)(2,1)S(1)}, bf16[256,128]{1,0:T(8,128)(2,1)S(1)}, u32[]{:S(2)}, u32[]{:S(2)}) collective-permute-start(bf16[256,128]{1,0:T(8,128)(2,1)S(1)} %get-tuple-element.106), channel_id=1, source_target_pairs={{0,4},{1,5},{2,6},{3,7},{4,0},{5,1},{6,2},{7,3},{8,12},{9,13},{10,... | collective-permute-start | bytes 196616 | tf_op jit(solution)/shard_map/ppermute | solution.py:261
  67.1 17.0 %collective-permute-start.21 = (bf16[128,2048]{1,0:T(8,128)(2,1)S(1)}, bf16[128,2048]{1,0:T(8,128)(2,1)S(1)}, u32[]{:S(2)}, u32[]{:S(2)}) collective-permute-start(bf16[128,2048]{1,0:T(8,128)(2,1)S(1)} %tick.4.held.grad), channel_id=1, source_target_pairs={{8,0},{9,1},{10,2},{11,3},{12,4},{13,5},{14,6},{15,7}} | collective-permute-start | bytes 1572872 | tf_op jit(solution)/shard_map/ppermute | solution.py:423
  74.3 5.3 %collective-permute-start.26 = (bf16[128,1024]{1,0:T(8,128)(2,1)S(1)}, bf16[128,1024]{1,0:T(8,128)(2,1)S(1)}, u32[]{:S(2)}, u32[]{:S(2)}) collective-permute-start(bf16[128,1024]{1,0:T(8,128)(2,1)S(1)} %get-tuple-element.109), channel_id=1, source_target_pairs={{0,2},{1,3},{2,0},{3,1},{4,6},{5,7},{6,4},{7,5},{8,10},{9,11},{10,... | collective-permute-start | bytes 786440 | tf_op jit(solution)/shard_map/ppermute | solution.py:261
  75.1 5.2 %collective-permute-start.27 = (bf16[128,1024]{1,0:T(8,128)(2,1)S(1)}, bf16[128,1024]{1,0:T(8,128)(2,1)S(1)}, u32[]{:S(2)}, u32[]{:S(2)}) collective-permute-start(bf16[128,1024]{1,0:T(8,128)(2,1)S(1)} %get-tuple-element.110), channel_id=1, source_target_pairs={{0,1},{1,0},{2,3},{3,2},{4,5},{5,4},{6,7},{7,6},{8,9},{9,8},{10,11... | collective-permute-start | bytes 786440 | tf_op jit(solution)/shard_map/ppermute | solution.py:261
  80.4 11.0 %collective-permute-start.30 = (bf16[64,2048]{1,0:T(8,128)(2,1)S(1)}, bf16[64,2048]{1,0:T(8,128)(2,1)S(1)}, u32[]{:S(2)}, u32[]{:S(2)}) collective-permute-start(bf16[64,2048]{1,0:T(8,128)(2,1)S(1)} %get-tuple-element.113), channel_id=1, source_target_pairs={{0,24},{1,25},{2,26},{3,27},{4,28},{5,29},{6,30},{7,31},{8,0},{9,1... | collective-permute-start | bytes 786440 | tf_op jit(solution)/shard_map/ppermute | solution.py:310
  80.4 11.0 %collective-permute-start.28 = (bf16[64,1024]{1,0:T(8,128)(2,1)S(1)}, bf16[64,1024]{1,0:T(8,128)(2,1)S(1)}, u32[]{:S(2)}, u32[]{:S(2)}) collective-permute-start(bf16[64,1024]{1,0:T(8,128)(2,1)S(1)} %get-tuple-element.111), channel_id=1, source_target_pairs={{0,28},{1,29},{2,30},{3,31},{4,24},{5,25},{6,26},{7,27},{8,4},{9,5... | collective-permute-start | bytes 393224 | tf_op jit(solution)/shard_map/ppermute | solution.py:310
  80.5 10.9 %collective-permute-start.29 = (bf16[64,1024]{1,0:T(8,128)(2,1)S(1)}, bf16[64,1024]{1,0:T(8,128)(2,1)S(1)}, u32[]{:S(2)}, u32[]{:S(2)}) collective-permute-start(bf16[64,1024]{1,0:T(8,128)(2,1)S(1)} %get-tuple-element.112), channel_id=1, source_target_pairs={{0,26},{1,27},{2,24},{3,25},{4,30},{5,31},{6,28},{7,29},{8,2},{9,3... | collective-permute-start | bytes 393224 | tf_op jit(solution)/shard_map/ppermute | solution.py:310
  (6 other events, 11.9 us)
